TPU v7x, 32 devices: a whole 2x2x4 slice. The times are simulated.
32 devices in a mesh: seq: 16 (over z, y, core), head: 2 (over x).
Axes of the slice: x: 2, y: 2, z: 4, core: 2. Of those that a mesh axis runs over, the one named last changes fastest.
Arguments:
- queries: bfloat16 [2048, 4096], P(('seq', 'head')), may hold values from -16 to 16
- keys: bfloat16 [2048, 4096], P(('seq', 'head')), may hold values from -16 to 16
- values: bfloat16 [2048, 4096], P(('seq', 'head')), may hold values from -6 to 6
- out_grad: bfloat16 [2048, 4096], P(('seq', 'head')), may hold values from -6 to 6
Outputs:
- attended: bfloat16 [2048, 4096], P(('seq', 'head'))
- query_grad: bfloat16 [2048, 4096], P(('seq', 'head'))
- key_grad: bfloat16 [2048, 4096], P(('seq', 'head'))
- value_gradient_array: bfloat16 [2048, 4096], P(('seq', 'head'))
All inputs are finite; a program needn't handle non-finite values.
Results may differ from a plain program's by a relative error of at most 0.034.
The roundings to bfloat16 on the way count: a program that leaves them out, or rounds other values in their place, can miss the bound.
Values may be sent and summed in bfloat16 or wider, within the bound.
No kernel may reach another device: no remote copies, remote signals or barrier semaphores. Data moves between devices by JAX's collectives and lax.ppermute only.
A program may use at most 128 MiB of HBM per device.

v0:
```python
import jax
import jax.numpy as jnp
from jax import lax
from jax.sharding import PartitionSpec as P

HD = 128
M = 256
PINV_ITERS = 6


precise_setting = lax.Precision.HIGHEST


def newton_inverse(matrix):
    identity = jnp.eye(matrix.shape[0], dtype=matrix.dtype)
    factor = lax.stop_gradient(1.0 / jnp.max(jnp.sum(matrix, axis=0)))
    iterate = matrix.T * factor
    for sweep_index in range(PINV_ITERS):
        product = jnp.matmul(matrix, iterate, precision=precise_setting)
        inner_term = jnp.matmul(product, 7.0 * identity - product, precision=precise_setting)
        inner_term = jnp.matmul(product, 15.0 * identity - inner_term, precision=precise_setting)
        iterate = 0.25 * jnp.matmul(
            iterate, 13.0 * identity - inner_term, precision=precise_setting
        )
    return iterate


def share_heads(own_matrix, head_count):
    seq_index = lax.axis_index("seq")
    slot_mask = (jnp.arange(head_count, dtype=jnp.int32) == seq_index).astype(jnp.float32)
    return lax.psum(slot_mask[:, None, None] * own_matrix[None], "seq")


def body(queries, keys, values, out_grad):
    query_rows, key_rows, value_rows, grad_rows = (
        lax.all_to_all(queries, "head", split_axis=1, concat_axis=0, tiled=True),
        lax.all_to_all(keys, "head", split_axis=1, concat_axis=0, tiled=True),
        lax.all_to_all(values, "head", split_axis=1, concat_axis=0, tiled=True),
        lax.all_to_all(out_grad, "head", split_axis=1, concat_axis=0, tiled=True),
    )
    tok_rows = query_rows.shape[0]
    head_count = query_rows.shape[1] // HD
    local_marks = M // lax.axis_size("seq")
    segment_len = tok_rows // local_marks
    score_scale = HD ** (-0.5)
    seq_index = lax.axis_index("seq")

    def landmark(matrix):
        summed = jnp.sum(
            matrix.reshape(local_marks, segment_len, matrix.shape[1]), axis=1, dtype=jnp.float32
        )
        return (summed / segment_len).astype(jnp.bfloat16)

    mark_queries, mark_keys = (
        lax.all_gather(landmark(query_rows), "seq", axis=0, tiled=True),
        lax.all_gather(landmark(key_rows), "seq", axis=0, tiled=True),
    )
    query_per_head = query_rows.reshape(tok_rows, head_count, HD)
    key_per_head = key_rows.reshape(tok_rows, head_count, HD)
    value_per_head = value_rows.reshape(tok_rows, head_count, HD)
    gradient_per_head = grad_rows.reshape(tok_rows, head_count, HD)
    landmark_query_heads = mark_queries.reshape(M, head_count, HD)
    landmark_key_heads = mark_keys.reshape(M, head_count, HD)
    key_score = (
        jnp.einsum(
            "pcv,gcv->cpg", landmark_query_heads, key_per_head, preferred_element_type=jnp.float32
        )
        * score_scale
    )
    key_max = lax.pmax(jnp.max(key_score, axis=-1), "seq")
    key_exp = jnp.exp(key_score - key_max[..., None])
    partial_num = jnp.einsum(
        "akq,qay->aky",
        key_exp.astype(jnp.bfloat16),
        value_per_head,
        preferred_element_type=jnp.float32,
    )
    key_total, numerator = lax.psum((jnp.sum(key_exp, axis=-1), partial_num), "seq")
    landmark_value_rows = numerator / key_total[..., None]
    token_prob = jax.nn.softmax(
        jnp.einsum(
            "jti,cti->tjc", query_per_head, landmark_key_heads, preferred_element_type=jnp.float32
        )
        * score_scale,
        axis=-1,
    )
    token_probability_lowered = token_prob.astype(jnp.bfloat16)
    mark_prob = jax.nn.softmax(
        jnp.einsum(
            "jou,iou->oji",
            landmark_query_heads,
            landmark_key_heads,
            preferred_element_type=jnp.float32,
        )
        * score_scale,
        axis=-1,
    )
    own_head = seq_index % head_count
    own_mark = lax.dynamic_index_in_dim(mark_prob, own_head, 0, keepdims=False)
    own_inverse, pull_back = jax.vjp(newton_inverse, own_mark)
    pseudo_inverse_matrix = share_heads(own_inverse, head_count)
    mixing_matrix = jnp.einsum(
        "jvy,jys->jvs", pseudo_inverse_matrix, landmark_value_rows, precision=precise_setting
    )
    mixing_matrix_lowered = mixing_matrix.astype(jnp.bfloat16)
    attended = jnp.einsum(
        "yvo,yor->vyr",
        token_probability_lowered,
        mixing_matrix_lowered,
        preferred_element_type=jnp.float32,
    ).astype(jnp.bfloat16)
    token_grad = jnp.einsum(
        "fag,aog->afo", gradient_per_head, mixing_matrix_lowered, preferred_element_type=jnp.float32
    )
    partial_mix = jnp.einsum(
        "klz,lkr->kzr",
        token_probability_lowered,
        gradient_per_head,
        preferred_element_type=jnp.float32,
    )
    mixing_matrix_gradient = lax.psum(partial_mix, "seq")
    token_score_gradient = (
        token_prob * (token_grad - jnp.sum(token_grad * token_prob, axis=-1, keepdims=True))
    ).astype(jnp.bfloat16)
    direct_qgrad = (
        jnp.einsum(
            "ufg,guc->fuc",
            token_score_gradient,
            landmark_key_heads,
            preferred_element_type=jnp.float32,
        )
        * score_scale
    )
    mark_kgrad_f = (
        jnp.einsum(
            "xgi,gxy->ixy", token_score_gradient, query_per_head, preferred_element_type=jnp.float32
        )
        * score_scale
    )
    pseudo_inverse_gradient = jnp.einsum(
        "ktu,kyu->kty", mixing_matrix_gradient, landmark_value_rows, precision=precise_setting
    )
    landmark_value_gradient = jnp.einsum(
        "lrb,lrz->lbz", pseudo_inverse_matrix, mixing_matrix_gradient, precision=precise_setting
    )
    own_igrad = lax.dynamic_index_in_dim(pseudo_inverse_gradient, own_head, 0, keepdims=False)
    (own_mgrad,) = pull_back(own_igrad)
    mark_grad = share_heads(own_mgrad, head_count)
    mark_sgrad = mark_prob * (mark_grad - jnp.sum(mark_grad * mark_prob, axis=-1, keepdims=True))
    first_mark = seq_index * local_marks
    score_gradient_rows = lax.dynamic_slice_in_dim(mark_sgrad, first_mark, local_marks, 1)
    score_gradient_columns = lax.dynamic_slice_in_dim(mark_sgrad, first_mark, local_marks, 2)
    own_qgrad_a = (
        jnp.einsum(
            "txs,ste->xte",
            score_gradient_rows,
            landmark_key_heads.astype(jnp.float32),
            precision=precise_setting,
        )
        * score_scale
    )
    own_kgrad_a = (
        jnp.einsum(
            "eaj,aev->jev",
            score_gradient_columns,
            landmark_query_heads.astype(jnp.float32),
            precision=precise_setting,
        )
        * score_scale
    )
    landmark_value_lowered = landmark_value_gradient.astype(jnp.bfloat16)
    key_prob = key_exp / key_total[..., None]
    key_probability_lowered = key_prob.astype(jnp.bfloat16)
    value_gradient_array = jnp.einsum(
        "zct,zcj->tzj",
        key_probability_lowered,
        landmark_value_lowered,
        preferred_element_type=jnp.float32,
    )
    key_direct_gradient = jnp.einsum(
        "exb,geb->exg", landmark_value_lowered, value_per_head, preferred_element_type=jnp.float32
    )
    row_total = lax.psum(jnp.sum(key_prob * key_direct_gradient, axis=-1), "seq")
    key_score_gradient = (key_prob * (key_direct_gradient - row_total[..., None])).astype(
        jnp.bfloat16
    )
    direct_kgrad = (
        jnp.einsum(
            "pbo,bpx->opx",
            key_score_gradient,
            landmark_query_heads,
            preferred_element_type=jnp.float32,
        )
        * score_scale
    )
    mark_qgrad_b = (
        jnp.einsum(
            "cbj,jcp->bcp", key_score_gradient, key_per_head, preferred_element_type=jnp.float32
        )
        * score_scale
    )
    own_kgrad_f, own_qgrad_b = (
        lax.psum_scatter(mark_kgrad_f, "seq", scatter_dimension=0, tiled=True),
        lax.psum_scatter(mark_qgrad_b, "seq", scatter_dimension=0, tiled=True),
    )
    mark_qtotal = (own_qgrad_a + own_qgrad_b) / segment_len
    mark_ktotal = (own_kgrad_a + own_kgrad_f) / segment_len
    query_grad = (
        direct_qgrad.reshape(local_marks, segment_len, head_count, HD) + mark_qtotal[:, None]
    )
    key_grad = direct_kgrad.reshape(local_marks, segment_len, head_count, HD) + mark_ktotal[:, None]
    width = head_count * HD
    results = (
        attended.reshape(tok_rows, width),
        query_grad.astype(jnp.bfloat16).reshape(tok_rows, width),
        key_grad.astype(jnp.bfloat16).reshape(tok_rows, width),
        value_gradient_array.astype(jnp.bfloat16).reshape(tok_rows, width),
    )
    attended_out, query_out, key_out, value_out = (
        lax.all_to_all(results[0], "head", split_axis=0, concat_axis=1, tiled=True),
        lax.all_to_all(results[1], "head", split_axis=0, concat_axis=1, tiled=True),
        lax.all_to_all(results[2], "head", split_axis=0, concat_axis=1, tiled=True),
        lax.all_to_all(results[3], "head", split_axis=0, concat_axis=1, tiled=True),
    )
    return (attended_out, query_out, key_out, value_out)


def solution(mesh):
    return jax.shard_map(
        body,
        mesh=mesh,
        in_specs=(
            P(("seq", "head"), None),
            P(("seq", "head"), None),
            P(("seq", "head"), None),
            P(("seq", "head"), None),
        ),
        out_specs=(
            P(("seq", "head"), None),
            P(("seq", "head"), None),
            P(("seq", "head"), None),
            P(("seq", "head"), None),
        ),
        check_vma=False,
    )
```

profile of v0, /device:TPU:0, one launch (start us, length us, event | category | flops | bytes accessed | tf_op | source)
XLA Modules:
  0.0 752.8 jit_solution(6352479212902944426)
XLA Ops:
  8.4 12.0 %all_to_all.134 = bf16[64,2,2048]{2,0,1:T(8,128)(2,1)S(1)} all-to-all(bf16[64,2,2048]{2,0,1:T(8,128)(2,1)S(1)} %bitcast.321), channel_id=1, replica_groups=mesh['seq'=16,'head'=2] {'head'}, dimensions={1} | all-to-all | bytes 1048576 | tf_op jit(solution)/shard_map/all_to_all | solution.py:37
  21.5 9.6 %all_to_all.135 = bf16[64,2,2048]{2,0,1:T(8,128)(2,1)S(1)} all-to-all(bf16[64,2,2048]{2,0,1:T(8,128)(2,1)S(1)} %bitcast.322), channel_id=1, replica_groups=mesh['seq'=16,'head'=2] {'head'}, dimensions={1} | all-to-all | bytes 1048576 | tf_op jit(solution)/shard_map/all_to_all | solution.py:36
  37.3 5.7 all-to-all-done.2
  49.3 3.8 all-to-all-done.4
  54.0 5.9 all-gather.5.cloned.1.call-done
  64.9 34.0 %all-gather.3.cloned.1.call-done = bf16[256,2048]{1,0:T(8,128)(2,1)} async-done(((bf16[16,2048]{1,0:T(8,128)(2,1)}), bf16[256,2048]{1,0:T(8,128)(2,1)}) %all-gather.3.cloned.1.call-update) | async-done | bytes 1048592 | tf_op jit(solution)/shard_map/all_gather | solution.py:55
  105.8 59.9 %pmax.7 = f32[16,256]{1,0:T(8,128)S(1)} all-reduce(f32[16,256]{1,0:T(8,128)S(1)} %get-tuple-element.14), channel_id=1, replica_groups=mesh['seq'=16,'head'=2] {'seq'}, use_global_device_ids=true, to_apply=%region_8.0 | all-reduce | flops 4096 | bytes 32768 | tf_op jit(solution)/shard_map/pmax | solution.py:70
  181.3 7.8 %fusion.58 = f32[16,256,128]{2,1,0:T(8,128)} fusion(bf16[128,16,128]{2,1,0:T(8,128)(2,1)} %bitcast.327, f32[16,128]{1,0:T(8,128)S(1)} %get-tuple-element.16, f32[16,256,128]{1,2,0:T(8,128)} %copy-done.20), kind=kOutput, calls=%fused_computation.138 | convolution fusion | flops 136841472 | bytes 4726784 | tf_op jit(solution)/shard_map/klz,lkr->kzr/dot_general | solution.py:115
  202.1 58.9 %psum.44 = f32[16,256]{1,0:T(8,128)S(1)} all-reduce(f32[16,256]{1,0:T(8,128)S(1)} %fusion.19), channel_id=1, replica_groups=mesh['seq'=16,'head'=2] {'seq'}, use_global_device_ids=true, to_apply=%region_11.12 | all-reduce | flops 4096 | bytes 32768 | tf_op jit(solution)/shard_map/psum | solution.py:78
  261.1 40.6 %all-reduce.7.cloned.1.call-done = (f32[16,256,128]{1,2,0:T(8,128)}, f32[16,256,128]{2,1,0:T(8,128)}) async-done(((f32[16,256,128]{1,2,0:T(8,128)}, f32[16,256,128]{2,1,0:T(8,128)}), (f32[16,256,128]{1,2,0:T(8,128)}, f32[16,256,128]{2,1,0:T(8,128)})) %all-reduce.7.cloned.1.call-update) | async-done | bytes 4194320 | tf_op jit(solution)/shard_map/psum | solution.py:78
  301.6 6.3 fusion.57
  332.9 5.3 broadcast_multiply_fusion
  338.2 169.4 %all-reduce.5.cloned.1.call-done = (f32[16,256,256]{1,2,0:T(8,128)}, f32[16,256,256]{1,2,0:T(8,128)}) async-done(((f32[16,256,256]{1,2,0:T(8,128)}, f32[16,256,256]{1,2,0:T(8,128)}), (f32[16,256,256]{1,2,0:T(8,128)}, f32[16,256,256]{1,2,0:T(8,128)})) %all-reduce.5.cloned.1.call-update) | async-done | bytes 8388624 | tf_op jit(solution)/shard_map/psum | solution.py:31
  507.7 6.7 convolution_convert_fusion
  516.3 60.2 %psum.47 = f32[16,256]{1,0:T(8,128)S(1)} all-reduce(f32[16,256]{1,0:T(8,128)S(1)} %get-tuple-element.20), channel_id=1, replica_groups=mesh['seq'=16,'head'=2] {'seq'}, use_global_device_ids=true, to_apply=%region_19.20 | all-reduce | flops 4096 | bytes 32768 | tf_op jit(solution)/shard_map/psum | solution.py:183
  585.1 9.8 %convolution_convert_fusion.1 = bf16[16,256,128]{2,1,0:T(8,128)(2,1)S(1)} fusion(f32[16,256,256]{1,2,0:T(8,128)} %get-tuple-element.4, f32[16,256,128]{1,2,0:T(8,128)} %get-tuple-element.6, f32[16,256]{1,0:T(8,128)S(1)} %psum.44), kind=kOutput, calls=%fused_computation.30 | convolution fusion | flops 1611661312 | bytes 7356416 | tf_op jit(solution)/shard_map/jvy,jys->jvs/dot_general | solution.py:102
  602.6 7.4 fusion.21
  614.2 4.4 all-to-all-start.3
  637.9 4.4 multiply_reduce_fusion
  646.5 3.9 fusion.45
  650.5 57.6 %reduce-scatter.5.cloned.1.call-done = f32[16,16,128]{2,1,0:T(8,128)} async-done(((f32[256,16,128]{2,1,0:T(8,128)}), f32[16,16,128]{2,1,0:T(8,128)}) %reduce-scatter.5.cloned.1.call-update) | async-done | bytes 131088 | tf_op jit(solution)/shard_map/reduce_scatter | solution.py:203
  713.8 4.2 all-to-all-start.7
  720.1 4.7 all-to-all-done.7
  729.2 5.7 all-to-all-done.6
  (287 shorter events, 148.2 us)
Async XLA Ops:
  7.2 14.2 %copy-start.63 = (bf16[64,4096]{1,0:T(8,128)(2,1)S(1)}, bf16[64,4096]{1,0:T(8,128)(2,1)}, u32[]{:S(2)}) copy-start(bf16[64,4096]{1,0:T(8,128)(2,1)} %param.4) | copy-start | bytes 1572868
  7.2 52.7 %all-gather.5.cloned.1.call-start = ((), (), s32[]{:S(2)}) async-start(), calls=%async_computation.11 | async-start | bytes 1114112 | tf_op jit(solution)/shard_map/all_gather | solution.py:56
  20.3 11.7 %copy-start.64 = (bf16[64,4096]{1,0:T(8,128)(2,1)S(1)}, bf16[64,4096]{1,0:T(8,128)(2,1)}, u32[]{:S(2)}) copy-start(bf16[64,4096]{1,0:T(8,128)(2,1)} %param.6) | copy-start | bytes 1572868
  21.3 77.6 %all-gather.3.cloned.1.call-start = ((), (), s32[]{:S(2)}) async-start(), calls=%async_computation.10 | async-start | bytes 1114112 | tf_op jit(solution)/shard_map/all_gather | solution.py:55
  21.4 15.0 %copy-start.65 = (bf16[64,4096]{1,0:T(8,128)(2,1)S(1)}, bf16[64,4096]{1,0:T(8,128)(2,1)}, u32[]{:S(2)}) copy-start(bf16[64,4096]{1,0:T(8,128)(2,1)} %param.7) | copy-start | bytes 1572868
  32.9 10.1 %all-to-all-start.2 = ((bf16[64,2,2048]{2,0,1:T(8,128)(2,1)}), bf16[64,2,2048]{2,0,1:T(8,128)(2,1)S(1)}, u32[]{:S(2)}, u32[]{:S(2)}) async-start(bf16[64,2,2048]{2,0,1:T(8,128)(2,1)} %bitcast.296), calls=%async_computation.2 | async-start | bytes 1048576 | tf_op jit(solution)/shard_map/all_to_all | solution.py:38
  43.0 10.1 %all-to-all-start.4 = ((bf16[64,2,2048]{2,0,1:T(8,128)(2,1)}), bf16[64,2,2048]{2,0,1:T(8,128)(2,1)S(1)}, u32[]{:S(2)}, u32[]{:S(2)}) async-start(bf16[64,2,2048]{2,0,1:T(8,128)(2,1)} %bitcast.295), calls=%async_computation.4 | async-start | bytes 1048576 | tf_op jit(solution)/shard_map/all_to_all | solution.py:39
  46.5 255.1 %all-reduce.7.cloned.1.call-start = ((), (), s32[]{:S(2)}) async-start(), calls=%async_computation.15 | async-start | bytes 8388608 | tf_op jit(solution)/shard_map/psum | solution.py:78
  192.1 315.5 %all-reduce.5.cloned.1.call-start = ((), (), s32[]{:S(2)}) async-start(), calls=%async_computation.14 | async-start | bytes 16777216 | tf_op jit(solution)/shard_map/psum | solution.py:31
  301.6 6.3 copy-start.29
  301.6 6.9 copy-start.60
  301.6 7.4 copy-start.56
  338.2 308.3 %reduce-scatter.3.cloned.1.call-start = ((), (), s32[]{:S(2)}) async-start(), calls=%async_computation.12 | async-start | bytes 2228224 | tf_op jit(solution)/shard_map/reduce_scatter | solution.py:204
  507.7 6.7 copy-start.61
  584.6 123.5 %reduce-scatter.5.cloned.1.call-start = ((), (), s32[]{:S(2)}) async-start(), calls=%async_computation.13 | async-start | bytes 2228224 | tf_op jit(solution)/shard_map/reduce_scatter | solution.py:203
  585.0 9.9 %copy-start.21 = (f32[16,128,256]{2,1,0:T(8,128)S(1)}, f32[16,128,256]{2,1,0:T(8,128)}, u32[]{:S(2)}) copy-start(f32[16,128,256]{2,1,0:T(8,128)} %get-tuple-element.17) | copy-start | bytes 6291460
  585.0 9.9 %copy-start.66 = (bf16[16,8,16,128]{3,2,1,0:T(8,128)(2,1)S(1)}, bf16[16,8,16,128]{3,2,1,0:T(8,128)(2,1)}, u32[]{:S(2)}) copy-start(bf16[16,8,16,128]{3,2,1,0:T(8,128)(2,1)} %copy.219) | copy-start | bytes 1572868
  614.2 99.5 %all-to-all-start.3 = ((bf16[2,64,2048]{2,1,0:T(8,128)(2,1)}), bf16[2,64,2048]{2,1,0:T(8,128)(2,1)}, u32[]{:S(2)}, u32[]{:S(2)}) async-start(bf16[2,64,2048]{2,1,0:T(8,128)(2,1)} %all_to_all.109), calls=%async_computation.3 | async-start | bytes 1048576 | tf_op jit(solution)/shard_map/all_to_all | solution.py:220
  627.3 5.1 copy-start.19
  637.9 6.0 copy-start.1
  711.3 6.7 copy-start.36
  713.8 11.0 %all-to-all-start.7 = ((bf16[2,64,2048]{2,1,0:T(8,128)(2,1)}), bf16[2,64,2048]{2,1,0:T(8,128)(2,1)}, u32[]{:S(2)}, u32[]{:S(2)}) async-start(bf16[2,64,2048]{2,1,0:T(8,128)(2,1)} %all_to_all.122), calls=%async_computation.9 | async-start | bytes 1048576 | tf_op jit(solution)/shard_map/all_to_all | solution.py:223
  724.8 10.1 %all-to-all-start.6 = ((bf16[2,64,2048]{2,1,0:T(8,128)(2,1)}), bf16[2,64,2048]{2,1,0:T(8,128)(2,1)S(1)}, u32[]{:S(2)}, u32[]{:S(2)}) async-start(bf16[2,64,2048]{2,1,0:T(8,128)(2,1)} %add_convert_fusion), calls=%async_computation.8 | async-start | bytes 1048576 | tf_op jit(solution)/shard_map/all_to_all | solution.py:222
  734.9 10.1 %all-to-all-start.5 = ((bf16[2,64,2048]{2,1,0:T(8,128)(2,1)}), bf16[2,64,2048]{2,1,0:T(8,128)(2,1)S(1)}, u32[]{:S(2)}, u32[]{:S(2)}) async-start(bf16[2,64,2048]{2,1,0:T(8,128)(2,1)} %add_convert_fusion.1), calls=%async_computation.6 | async-start | bytes 1048576 | tf_op jit(solution)/shard_map/all_to_all | solution.py:221
  (56 other events, 119.5 us)
Sparse Core Ops, SparseCore 0:
  21.5 38.3 all-gather.4
  62.0 36.8 all-gather.2
  192.3 109.2 all-reduce.6
  338.3 169.3 all-reduce.4
  584.7 58.7 reduce-scatter.2
  647.5 60.5 reduce-scatter.4
where the time goes:
time: 759 us; the launch traced here: 753 us
  waiting for transfers between devices  329 us (43%)
  blocking collectives  201 us (26%)
  matrix products  103 us (14%)
  local copies, waits for them, and re-layouts  53.3 us (7%)
  other arithmetic  26 us (3%)
  starting transfers between devices  23.6 us (3%)
  between operations  16.5 us (2%)
    psum x1, waiting for transfers between devices, share_heads(): return lax.psum(slot_mask[:, None, None] * own_matrix[None], 'seq')  169 us
    psum x1, blocking collectives, body(): lax.psum(jnp.sum(key_prob * key_direct_gradient, axis=-1), 'seq')  60.2 us
    pmax x1, blocking collectives, body(): key_max = lax.pmax(jnp.max(key_score, axis=-1), 'seq')  59.9 us
    psum x1, blocking collectives, body(): lax.psum((jnp.sum(key_exp, axis=-1), partial_num), 'seq')  58.9 us
    reduce_scatter x1, waiting for transfers between devices, body(): lax.psum_scatter(mark_kgrad_f, 'seq', scatter_dimension=0, tiled=True)  57.6 us
    psum x1, waiting for transfers between devices, body(): lax.psum((jnp.sum(key_exp, axis=-1), partial_num), 'seq')  40.6 us
    all_gather x1, waiting for transfers between devices, body(): lax.all_gather(landmark(query_rows), 'seq', axis=0, tiled=True)  34 us
  transfers between devices with their start and end apart: 12, of which 10 were waited for; matrix products, arithmetic and copies ran while one was open for 11% of the time, Pallas kernels for 0%

commit v1 on v0

--- a/solution.py
+++ b/solution.py
@@ -1,11 +1,18 @@
 import jax
 import jax.numpy as jnp
 from jax import lax
+from jax.experimental import pallas as pl
+from jax.experimental.pallas import tpu as pltpu
 from jax.sharding import PartitionSpec as P
 
 HD = 128
 M = 256
 PINV_ITERS = 6
+CHUNK = 256
+VMEM_LIMIT = 40 * 2**20
+FORWARD_FLOPS = 10 * 10**9
+MIXING_FLOPS = 2 * 10**9
+GRADIENT_FLOPS = 14 * 10**9
 
 
 precise_setting = lax.Precision.HIGHEST
@@ -31,7 +38,7 @@
     return lax.psum(slot_mask[:, None, None] * own_matrix[None], "seq")
 
 
-def body(queries, keys, values, out_grad):
+def shared_body(queries, keys, values, out_grad):
     query_rows, key_rows, value_rows, grad_rows = (
         lax.all_to_all(queries, "head", split_axis=1, concat_axis=0, tiled=True),
         lax.all_to_all(keys, "head", split_axis=1, concat_axis=0, tiled=True),
@@ -225,21 +232,512 @@
     return (attended_out, query_out, key_out, value_out)
 
 
+def dims_of(rows):
+    tokens = rows.shape[0] * rows.shape[2]
+    return tokens, rows.shape[2], tokens // CHUNK
+
+
+def halves(matrix):
+    high = matrix.astype(jnp.bfloat16)
+    return high, (matrix - high.astype(jnp.float32)).astype(jnp.bfloat16)
+
+
+def wide_dot(left, right):
+    return jnp.dot(left, right, preferred_element_type=jnp.float32)
+
+
+def wide_dot_nt(left, right):
+    return lax.dot_general(
+        left, right, (((1,), (1,)), ((), ())), preferred_element_type=jnp.float32
+    )
+
+
+def split_dot(left, right):
+    left_high, left_low = left
+    right_high, right_low = right
+    return wide_dot(
+        jnp.concatenate([left_high, left_high, left_low], axis=1),
+        jnp.concatenate([right_high, right_low, right_high], axis=0),
+    )
+
+
+def split_dot_nt(left, right):
+    left_high, left_low = left
+    right_high, right_low = right
+    return wide_dot_nt(
+        jnp.concatenate([left_high, left_high, left_low], axis=1),
+        jnp.concatenate([right_high, right_low, right_high], axis=1),
+    )
+
+
+def identity_matrix():
+    return (
+        lax.broadcasted_iota(jnp.int32, (M, M), 0) == lax.broadcasted_iota(jnp.int32, (M, M), 1)
+    ).astype(jnp.float32)
+
+
+def chunk_of(ref, slot, index):
+    rows = ref.shape[2]
+    per = CHUNK // rows
+    return ref[pl.ds(index * per, per), slot].reshape(CHUNK, HD)
+
+
+def store_chunk(ref, slot, index, value):
+    rows = ref.shape[2]
+    per = CHUNK // rows
+    ref[pl.ds(index * per, per), slot] = value.reshape(per, rows, HD)
+
+
+def columns(index):
+    return pl.ds(pl.multiple_of(index * CHUNK, CHUNK), CHUNK)
+
+
+def pack_kernel(first_ref, second_ref, out_ref):
+    for head in range(out_ref.shape[0]):
+        out_ref[head, 0] = first_ref[:, head * HD : (head + 1) * HD]
+        out_ref[head, 1] = second_ref[:, head * HD : (head + 1) * HD]
+
+
+def unpack_kernel(packed_ref, first_ref, second_ref):
+    for head in range(packed_ref.shape[0]):
+        first_ref[:, head * HD : (head + 1) * HD] = packed_ref[head, 0]
+        second_ref[:, head * HD : (head + 1) * HD] = packed_ref[head, 1]
+
+
+def forward_kernel(
+    qk_ref,
+    mark_q_ref,
+    mark_k_ref,
+    mark_prob_ref,
+    factor_ref,
+    token_prob_ref,
+    token_low_ref,
+    token_turned_ref,
+    key_prob_ref,
+    key_plow_ref,
+    key_turned_ref,
+    total_inverse_ref,
+    columns_turned_ref,
+    pair_ref,
+    weight_ref,
+    growth_ref,
+    inverse_ref,
+    inverse_turned_ref,
+    last_growth_ref,
+    power_s,
+    iterate_s,
+):
+    tokens, rows, chunks = dims_of(qk_ref)
+    segment_len = tokens // M
+    marks_per = CHUNK // segment_len
+    score_scale = HD ** (-0.5)
+    member = (
+        lax.broadcasted_iota(jnp.int32, (marks_per, CHUNK), 1) // segment_len
+        == lax.broadcasted_iota(jnp.int32, (marks_per, CHUNK), 0)
+    ).astype(jnp.bfloat16)
+    for index in range(chunks):
+        both = jnp.concatenate([chunk_of(qk_ref, 0, index), chunk_of(qk_ref, 1, index)], axis=1)
+        mean = (wide_dot(member, both) / segment_len).astype(jnp.bfloat16)
+        mark_q_ref[index * marks_per : (index + 1) * marks_per] = mean[:, :HD]
+        mark_k_ref[index * marks_per : (index + 1) * marks_per] = mean[:, HD:]
+    landmark_q, landmark_k = mark_q_ref[...], mark_k_ref[...]
+
+    mark_score = wide_dot_nt(landmark_q, landmark_k) * score_scale
+    mark_exp = jnp.exp(mark_score - jnp.max(mark_score, axis=1, keepdims=True))
+    mark_prob = mark_exp / jnp.sum(mark_exp, axis=1, keepdims=True)
+    mark_prob_ref[...] = mark_prob
+    factor = 1.0 / jnp.max(jnp.sum(mark_prob, axis=0, keepdims=True), axis=1, keepdims=True)
+    factor_ref[...] = jnp.broadcast_to(factor, factor_ref.shape)
+    mark_halves = halves(mark_prob)
+    power_s[...] = split_dot_nt(mark_halves, mark_halves) * factor
+    iterate_s[0:M] = mark_prob.T * factor
+    iterate_s[M:] = identity_matrix()
+
+    def newton(sweep, carry):
+        power = power_s[...]
+        power_high, power_low = halves(power)
+        square = split_dot((power_high, power_low), (power_high, power_low))
+        square_halves = halves(square)
+        pair = (
+            jnp.concatenate([power_high, square_halves[0]], axis=0),
+            jnp.concatenate([power_low, square_halves[1]], axis=0),
+        )
+        pair_ref[sweep, 0], pair_ref[sweep, 1] = pair
+        higher = split_dot(pair, square_halves)
+        cube, fourth = higher[:M], higher[M:]
+        weight = halves(
+            0.25 * (13.0 * identity_matrix() - 15.0 * power + 7.0 * square - cube)
+        )
+        power_s[...] = 0.25 * (13.0 * power - 15.0 * square + 7.0 * cube - fourth)
+        weight_ref[sweep, 0], weight_ref[sweep, 1] = weight
+        iterate = halves(iterate_s[...])
+        growth_ref[sweep, 0], growth_ref[sweep, 1] = iterate[0][M:], iterate[1][M:]
+        iterate_s[...] = split_dot(iterate, weight)
+        return carry
+
+    lax.fori_loop(0, PINV_ITERS, newton, 0)
+    inverse = iterate_s[0:M]
+    inverse_ref[0], inverse_ref[1] = halves(inverse)
+    inverse_turned_ref[0], inverse_turned_ref[1] = halves(inverse.T)
+    last_growth_ref[0], last_growth_ref[1] = halves(iterate_s[M:])
+
+    def scores(index, key_max):
+        query_chunk, key_chunk = chunk_of(qk_ref, 0, index), chunk_of(qk_ref, 1, index)
+        place = columns(index)
+        columns_turned_ref[0, :, place] = query_chunk.T
+        columns_turned_ref[1, :, place] = key_chunk.T
+        score = wide_dot_nt(query_chunk, landmark_k) * score_scale
+        grown = jnp.exp(score - jnp.max(score, axis=1, keepdims=True))
+        prob = grown / jnp.sum(grown, axis=1, keepdims=True)
+        token_prob_ref[place] = prob
+        low = prob.astype(jnp.bfloat16)
+        token_low_ref[place] = low
+        token_turned_ref[:, place] = low.T
+        key_score = wide_dot_nt(key_chunk, landmark_q) * score_scale
+        key_prob_ref[place] = key_score
+        return jnp.maximum(key_max, jnp.max(key_score, axis=0, keepdims=True))
+
+    key_max = lax.fori_loop(0, chunks, scores, jnp.full((1, M), -jnp.inf, jnp.float32))
+
+    def grow(index, key_total):
+        place = columns(index)
+        grown = jnp.exp(key_prob_ref[place] - key_max)
+        key_prob_ref[place] = grown
+        key_turned_ref[:, place] = grown.astype(jnp.bfloat16).T
+        return key_total + jnp.sum(grown, axis=0, keepdims=True)
+
+    key_total = lax.fori_loop(0, chunks, grow, jnp.zeros((1, M), jnp.float32))
+    total_inverse = 1.0 / key_total
+    total_inverse_ref[...] = jnp.broadcast_to(total_inverse, (HD, M)).T
+
+    def normalise(index, carry):
+        place = columns(index)
+        prob = key_prob_ref[place] * total_inverse
+        key_prob_ref[place] = prob
+        key_plow_ref[place] = prob.astype(jnp.bfloat16)
+        return carry
+
+    lax.fori_loop(0, chunks, normalise, 0)
+
+
+def mixing_kernel(
+    vg_ref,
+    token_low_ref,
+    token_turned_ref,
+    key_plow_ref,
+    key_turned_ref,
+    total_inverse_ref,
+    inverse_ref,
+    inverse_turned_ref,
+    out_ref,
+    mixing_low_ref,
+    mixing_grad_ref,
+    mark_values_ref,
+    values_low_ref,
+):
+    tokens, rows, chunks = dims_of(vg_ref)
+    values = vg_ref[:, 0].reshape(tokens, HD)
+    out_grad = vg_ref[:, 1].reshape(tokens, HD)
+    landmark_values = wide_dot(key_turned_ref[...], values) * total_inverse_ref[...]
+    mixing_grad = wide_dot(token_turned_ref[...], out_grad)
+    mark_values_ref[...] = landmark_values
+    mixing_grad_ref[...] = mixing_grad
+    mixing_low = split_dot(
+        (inverse_ref[0], inverse_ref[1]), halves(landmark_values)
+    ).astype(jnp.bfloat16)
+    values_low = split_dot(
+        (inverse_turned_ref[0], inverse_turned_ref[1]), halves(mixing_grad)
+    ).astype(jnp.bfloat16)
+    mixing_low_ref[...] = mixing_low
+    values_low_ref[...] = values_low
+
+    def emit(index, carry):
+        place = columns(index)
+        store_chunk(
+            out_ref, 0, index, wide_dot(token_low_ref[place], mixing_low).astype(jnp.bfloat16)
+        )
+        store_chunk(
+            out_ref, 1, index, wide_dot(key_plow_ref[place], values_low).astype(jnp.bfloat16)
+        )
+        return carry
+
+    lax.fori_loop(0, chunks, emit, 0)
+
+
+def gradient_kernel(
+    vg_ref,
+    mark_q_ref,
+    mark_k_ref,
+    mark_prob_ref,
+    factor_ref,
+    token_prob_ref,
+    key_prob_ref,
+    columns_turned_ref,
+    pair_ref,
+    weight_ref,
+    growth_ref,
+    last_growth_ref,
+    mixing_low_ref,
+    mixing_grad_ref,
+    mark_values_ref,
+    values_low_ref,
+    out_ref,
+    power_s,
+    growth_s,
+    direct_s,
+    kept_s,
+):
+    tokens, rows, chunks = dims_of(vg_ref)
+    segment_len = tokens // M
+    marks_per = CHUNK // segment_len
+    score_scale = HD ** (-0.5)
+    landmark_q, landmark_k = mark_q_ref[...], mark_k_ref[...]
+    mark_prob = mark_prob_ref[...]
+    mark_halves = halves(mark_prob)
+    factor = factor_ref[0:1, 0:1]
+    inverse_grad = split_dot_nt(halves(mixing_grad_ref[...]), halves(mark_values_ref[...]))
+    inverse_grad_halves = halves(inverse_grad)
+    toward = split_dot(mark_halves, inverse_grad_halves) * factor
+    power_s[...] = 0.5 * (toward + toward.T)
+    growth_s[...] = jnp.zeros((M, M), jnp.float32)
+
+    def newton(sweep, carry):
+        power = power_s[...]
+        pair = (pair_ref[sweep, 0], pair_ref[sweep, 1])
+        first = split_dot(pair, halves(power))
+        square = first[:M] + first[:M].T
+        second = split_dot(pair, halves(square))
+        cube = first[M:].T + second[:M]
+        fourth = second[M:] + second[M:].T
+        weight = halves(0.25 * (7.0 * square - 15.0 * power - cube))
+        power_s[...] = 0.25 * (13.0 * power - 15.0 * square + 7.0 * cube - fourth)
+        grown_high, grown_low = halves(growth_s[...])
+        held_high, held_low = growth_ref[sweep, 0], growth_ref[sweep, 1]
+        held_weight_high, held_weight_low = weight_ref[sweep, 0], weight_ref[sweep, 1]
+        growth_s[...] = wide_dot(
+            jnp.concatenate(
+                [grown_high, grown_high, grown_low, held_high, held_high, held_low], axis=1
+            ),
+            jnp.concatenate(
+                [
+                    held_weight_high,
+                    held_weight_low,
+                    held_weight_high,
+                    weight[0],
+                    weight[1],
+                    weight[0],
+                ],
+                axis=0,
+            ),
+        )
+        return carry
+
+    lax.fori_loop(0, PINV_ITERS, newton, 0)
+    growth = growth_s[...]
+    mark_grad = factor * (
+        split_dot_nt((last_growth_ref[0], last_growth_ref[1]), inverse_grad_halves)
+        + split_dot(halves(growth + growth.T), mark_halves)
+    )
+    mark_sgrad = mark_prob * (mark_grad - jnp.sum(mark_grad * mark_prob, axis=1, keepdims=True))
+
+    def marks_dot(left, right):
+        high, low = halves(left)
+        return wide_dot(
+            jnp.concatenate([high, low], axis=1), jnp.concatenate([right, right], axis=0)
+        )
+
+    mark_qgrad_a = marks_dot(mark_sgrad, landmark_k)
+    mark_kgrad_a = marks_dot(mark_sgrad.T, landmark_q)
+
+    values_low = values_low_ref[...]
+
+    def key_rows(index, row_total):
+        place = columns(index)
+        key_dgrad = wide_dot_nt(chunk_of(vg_ref, 0, index), values_low)
+        kept_s[place] = key_dgrad
+        return row_total + jnp.sum(key_prob_ref[place] * key_dgrad, axis=0, keepdims=True)
+
+    row_total = lax.fori_loop(0, chunks, key_rows, jnp.zeros((1, M), jnp.float32))
+
+    def key_side(index, total):
+        place = columns(index)
+        key_sgrad = (key_prob_ref[place] * (kept_s[place] - row_total)).astype(jnp.bfloat16)
+        direct_s[place] = wide_dot(key_sgrad, landmark_q) * score_scale
+        return total + wide_dot(columns_turned_ref[1, :, place], key_sgrad)
+
+    mark_qgrad_b = lax.fori_loop(0, chunks, key_side, jnp.zeros((HD, M), jnp.float32))
+    mark_qtotal = (mark_qgrad_a + mark_qgrad_b.T) * (score_scale / segment_len)
+    mixing_low = mixing_low_ref[...]
+
+    def spread(direct, marks):
+        wide = jnp.broadcast_to(marks[:, None], (marks_per, segment_len, HD))
+        return (direct + wide.reshape(CHUNK, HD)).astype(jnp.bfloat16)
+
+    kept_s[0:M, 0:HD] = mark_qtotal
+
+    def token_side(index, total):
+        place = columns(index)
+        prob = token_prob_ref[place]
+        token_grad = wide_dot_nt(chunk_of(vg_ref, 1, index), mixing_low)
+        token_sgrad = (
+            prob * (token_grad - jnp.sum(token_grad * prob, axis=1, keepdims=True))
+        ).astype(jnp.bfloat16)
+        direct = wide_dot(token_sgrad, landmark_k) * score_scale
+        marks = kept_s[pl.ds(pl.multiple_of(index * marks_per, marks_per), marks_per), 0:HD]
+        store_chunk(out_ref, 0, index, spread(direct, marks))
+        return total + wide_dot(columns_turned_ref[0, :, place], token_sgrad)
+
+    mark_kgrad_f = lax.fori_loop(0, chunks, token_side, jnp.zeros((HD, M), jnp.float32))
+    kept_s[0:M, 0:HD] = (mark_kgrad_a + mark_kgrad_f.T) * (score_scale / segment_len)
+
+    def finish(index, carry):
+        marks = kept_s[pl.ds(pl.multiple_of(index * marks_per, marks_per), marks_per), 0:HD]
+        store_chunk(out_ref, 1, index, spread(direct_s[columns(index)], marks))
+        return carry
+
+    lax.fori_loop(0, chunks, finish, 0)
+
+
+def kernel_call(kernel, out_shape, scratch, flops, operands):
+    moved = sum(x.size * x.dtype.itemsize for x in operands)
+    in_vmem = pl.BlockSpec(memory_space=pltpu.VMEM)
+    return pl.pallas_call(
+        kernel,
+        out_shape=out_shape,
+        in_specs=[in_vmem] * len(operands),
+        out_specs=jax.tree.map(lambda _: in_vmem, out_shape),
+        scratch_shapes=scratch,
+        compiler_params=pltpu.CompilerParams(vmem_limit_bytes=VMEM_LIMIT),
+        cost_estimate=pl.CostEstimate(flops=flops, bytes_accessed=moved, transcendentals=0),
+    )(*operands)
+
+
+def pack(first, second):
+    rows, width = first.shape
+    shape = jax.ShapeDtypeStruct((width // HD, 2, rows, HD), first.dtype)
+    return kernel_call(pack_kernel, shape, [], 0, (first, second))
+
+
+def unpack(packed):
+    heads, _, rows, _ = packed.shape
+    shape = jax.ShapeDtypeStruct((rows, heads * HD), packed.dtype)
+    return kernel_call(unpack_kernel, (shape, shape), [], 0, (packed,))
+
+
+def forward_part(qk):
+    tokens = qk.shape[0] * qk.shape[2]
+
+    def low(*shape):
+        return jax.ShapeDtypeStruct(shape, jnp.bfloat16)
+
+    def wide(*shape):
+        return jax.ShapeDtypeStruct(shape, jnp.float32)
+
+    shapes = dict(
+        mark_q=low(M, HD),
+        mark_k=low(M, HD),
+        mark_prob=wide(M, M),
+        factor=wide(8, HD),
+        token_prob=wide(tokens, M),
+        token_low=low(tokens, M),
+        token_turned=low(M, tokens),
+        key_prob=wide(tokens, M),
+        key_plow=low(tokens, M),
+        key_turned=low(M, tokens),
+        total_inverse=wide(M, HD),
+        columns_turned=low(2, HD, tokens),
+        pair=low(PINV_ITERS, 2, 2 * M, M),
+        weight=low(PINV_ITERS, 2, M, M),
+        growth=low(PINV_ITERS, 2, M, M),
+        inverse=low(2, M, M),
+        inverse_turned=low(2, M, M),
+        last_growth=low(2, M, M),
+    )
+    scratch = [pltpu.VMEM((M, M), jnp.float32), pltpu.VMEM((2 * M, M), jnp.float32)]
+    results = kernel_call(
+        forward_kernel, tuple(shapes.values()), scratch, FORWARD_FLOPS, (qk,)
+    )
+    return dict(zip(shapes, results))
+
+
+def mixing_part(vg, kept):
+    names = (
+        "token_low",
+        "token_turned",
+        "key_plow",
+        "key_turned",
+        "total_inverse",
+        "inverse",
+        "inverse_turned",
+    )
+    shapes = (
+        jax.ShapeDtypeStruct(vg.shape, jnp.bfloat16),
+        jax.ShapeDtypeStruct((M, HD), jnp.bfloat16),
+        jax.ShapeDtypeStruct((M, HD), jnp.float32),
+        jax.ShapeDtypeStruct((M, HD), jnp.float32),
+        jax.ShapeDtypeStruct((M, HD), jnp.bfloat16),
+    )
+    return kernel_call(
+        mixing_kernel, shapes, [], MIXING_FLOPS, (vg, *(kept[name] for name in names))
+    )
+
+
+def gradient_part(vg, kept, mixed):
+    names = (
+        "mark_q",
+        "mark_k",
+        "mark_prob",
+        "factor",
+        "token_prob",
+        "key_prob",
+        "columns_turned",
+        "pair",
+        "weight",
+        "growth",
+        "last_growth",
+    )
+    tokens = vg.shape[0] * vg.shape[2]
+    scratch = [
+        pltpu.VMEM((M, M), jnp.float32),
+        pltpu.VMEM((M, M), jnp.float32),
+        pltpu.VMEM((tokens, HD), jnp.float32),
+        pltpu.VMEM((tokens, M), jnp.float32),
+    ]
+    return kernel_call(
+        gradient_kernel,
+        jax.ShapeDtypeStruct(vg.shape, jnp.bfloat16),
+        scratch,
+        GRADIENT_FLOPS,
+        (vg, *(kept[name] for name in names), *mixed),
+    )
+
+
+def exchange(packed):
+    return lax.all_to_all(packed, ("seq", "head"), split_axis=0, concat_axis=0, tiled=True)
+
+
+def body(queries, keys, values, out_grad):
+    qk = exchange(pack(queries, keys))
+    vg = exchange(pack(values, out_grad))
+    kept = forward_part(qk)
+    first_results, *mixed = mixing_part(vg, kept)
+    second_results = gradient_part(vg, kept, mixed)
+    attended, value_gradient_array = unpack(exchange(first_results))
+    query_grad, key_grad = unpack(exchange(second_results))
+    return attended, query_grad, key_grad, value_gradient_array
+
+
 def solution(mesh):
-    return jax.shard_map(
-        body,
-        mesh=mesh,
-        in_specs=(
-            P(("seq", "head"), None),
-            P(("seq", "head"), None),
-            P(("seq", "head"), None),
-            P(("seq", "head"), None),
-        ),
-        out_specs=(
-            P(("seq", "head"), None),
-            P(("seq", "head"), None),
-            P(("seq", "head"), None),
-            P(("seq", "head"), None),
-        ),
-        check_vma=False,
-    )
+    placement = P(("seq", "head"), None)
+
+    def layer(queries, keys, values, out_grad):
+        one_head_each = queries.shape[1] // HD == mesh.size and queries.shape[0] % CHUNK == 0
+        return jax.shard_map(
+            body if one_head_each else shared_body,
+            mesh=mesh,
+            in_specs=(placement,) * 4,
+            out_specs=(placement,) * 4,
+            check_vma=False,
+        )(queries, keys, values, out_grad)
+
+    return layer

time: 759 us -> 149 us (0.20)
  waiting for transfers between devices: 329 us -> 50.1 us
  blocking collectives: 201 us -> 0 us
  matrix products: 103 us -> 0 us
  Pallas kernels: 0 us -> 43.3 us
  other arithmetic: 26 us -> 0 us
  local copies, waits for them, and re-layouts: 53.3 us -> 30.8 us
  between operations: 16.5 us -> 0.77 us
    psum x2 -> x0, waiting for transfers between devices: 210 us -> none  [the longest x1 169 us: share_heads(): return lax.psum(slot_mask[:, None, None] * own_matrix[None], 'seq')]
    psum x2 -> x0, blocking collectives: 119 us -> none  [the longest x1 60.2 us: body(): lax.psum(jnp.sum(key_prob * key_direct_gradient, axis=-1), 'seq')]
    dot_general x89 -> x0, matrix products: 99.8 us -> none  [the longest x18 10.8 us: newton_inverse(): product = jnp.matmul(matrix, iterate, precision=precise_setting)]
    pmax x1 -> x0, blocking collectives: 59.9 us -> none  [body(): key_max = lax.pmax(jnp.max(key_score, axis=-1), 'seq')]
    reduce_scatter x2 -> x0, waiting for transfers between devices: 57.6 us -> none  [the longest x1 57.6 us: body(): lax.psum_scatter(mark_kgrad_f, 'seq', scatter_dimension=0, tiled=True)]
    pallas_call x0 -> x7, Pallas kernels: none -> 43.3 us  [kernel_call(): pl.pallas_call(kernel, out_shape=out_shape, in_specs=[in_vmem] * len(oper...]
    all_gather x2 -> x0, waiting for transfers between devices: 40 us -> none  [the longest x1 34 us: body(): lax.all_gather(landmark(query_rows), 'seq', axis=0, tiled=True)]
    all_to_all x6 -> x4, waiting for transfers between devices: 21.8 us -> 50.1 us  [exchange(): lax.all_to_all(packed, ('seq', 'head'), split_axis=0, concat_axis=0, tile...]
  transfers between devices with their start and end apart: 12 -> 4, of which waited for: 10 -> 2; matrix products, arithmetic and copies ran while one was open for 11% -> 0% of each run, Pallas kernels for 0% -> 25%
where the time goes in v1:
time: 149 us; the launch traced here: 147 us
  waiting for transfers between devices  50.1 us (34%)
  Pallas kernels  43.3 us (29%)
  local copies, waits for them, and re-layouts  30.8 us (21%)
  starting transfers between devices  22.6 us (15%)
    all_to_all x4, waiting for transfers between devices, exchange(): lax.all_to_all(packed, ('seq', 'head'), split_axis=0, concat_axis=0, tile...  50.1 us
    pallas_call x7, Pallas kernels, kernel_call(): pl.pallas_call(kernel, out_shape=out_shape, in_specs=[in_vmem] * len(oper...  43.3 us
    unnamed x74, local copies, waits for them, and re-layouts  30.8 us
    all_to_all x4, starting transfers between devices, exchange(): lax.all_to_all(packed, ('seq', 'head'), split_axis=0, concat_axis=0, tile...  22.6 us
  transfers between devices with their start and end apart: 4, of which 2 were waited for; matrix products, arithmetic and copies ran while one was open for 0% of the time, Pallas kernels for 25%

profile of v1, /device:TPU:0, one launch (start us, length us, event | category | flops | bytes accessed | tf_op | source)
XLA Modules:
  0.0 147.5 jit_solution(12928605293636009883)
XLA Ops:
  1.7 1.0 copy-done.1
  2.7 1.2 shard_map.76
  3.9 7.3 %all-to-all-start.1 = ((bf16[32,2,64,128]{3,2,1,0:T(8,128)(2,1)}), bf16[32,2,64,128]{3,2,1,0:T(8,128)(2,1)S(1)}, u32[]{:S(2)}, u32[]{:S(2)}) async-start(bf16[32,2,64,128]{3,2,1,0:T(8,128)(2,1)} %shard_map.76), calls=%async_computation.1 | async-start | bytes 2097152 | tf_op jit(solution)/shard_map/all_to_all | solution.py:716
  11.2 1.2 shard_map.75
  12.4 25.1 %all-to-all-done.1.qk_ref = bf16[32,2,64,128]{3,2,1,0:T(8,128)(2,1)S(1)} async-done(((bf16[32,2,64,128]{3,2,1,0:T(8,128)(2,1)}), bf16[32,2,64,128]{3,2,1,0:T(8,128)(2,1)S(1)}, u32[]{:S(2)}, u32[]{:S(2)}) %all-to-all-start.1) | async-done | bytes 1048608 | tf_op jit(solution)/shard_map/all_to_all | solution.py:716
  37.4 3.6 %all-to-all-start = ((bf16[32,2,64,128]{3,2,1,0:T(8,128)(2,1)}), bf16[32,2,64,128]{3,2,1,0:T(8,128)(2,1)S(1)}, u32[]{:S(2)}, u32[]{:S(2)}) async-start(bf16[32,2,64,128]{3,2,1,0:T(8,128)(2,1)} %shard_map.75), calls=%async_computation | async-start | bytes 2097152 | tf_op jit(solution)/shard_map/all_to_all | solution.py:716
  41.1 15.8 %shard_map.77 = (bf16[256,128]{1,0:T(8,128)(2,1)S(1)}, bf16[256,128]{1,0:T(8,128)(2,1)S(1)}, f32[256,256]{1,0:T(8,128)S(1)}, f32[8,128]{1,0:T(8,128)S(1)}, f32[2...) custom-call(bf16[32,2,64,128]{3,2,1,0:T(8,128)(2,1)S(1)} %all-to-all, ...), custom_call_target="tpu_custom_call" | custom-call | flops 10000000000 | bytes 1048576 | tf_op jit(solution)/shard_map/pallas_call | solution.py:604
  61.2 1.3 copy-done.20
  62.5 1.2 copy-done.23
  63.8 1.1 copy-done.25
  68.6 1.2 copy-done.5
  69.8 1.2 copy-done.7
  71.0 1.2 copy-done.9
  74.1 3.6 %shard_map.78 = (bf16[32,2,64,128]{3,2,1,0:T(8,128)(2,1)}, bf16[256,128]{1,0:T(8,128)(2,1)S(1)}, f32[256,128]{1,0:T(8,128)S(1)}, f32[256,128]{1,0:T(8,128)S(1)}, bf16[256,128]{1,0:T(8,128)(2,1)S(1)}) custom-call(bf16[32,2,64,128]{3,2,1,0:T(8,128)(2,1)S(1)} %all-to-all-done.vg_ref, bf16[2048,256]{1,0:T(8,128)(2,1)S(1)} %get-tuple-element.31.token_low_ref, ...), custom_call_target="tpu_custom_call" | custom-call | flops 2000000000 | bytes 5898240 | tf_op jit(solution)/shard_map/pallas_call | solution.py:604
  79.6 5.8 %all-to-all-start.2 = ((bf16[32,2,64,128]{3,2,1,0:T(8,128)(2,1)}), bf16[32,2,64,128]{3,2,1,0:T(8,128)(2,1)S(1)}, u32[]{:S(2)}, u32[]{:S(2)}) async-start(bf16[32,2,64,128]{3,2,1,0:T(8,128)(2,1)} %get-tuple-element.38), calls=%async_computation.2 | async-start | bytes 2097152 | tf_op jit(solution)/shard_map/all_to_all | solution.py:716
  85.5 1.6 %copy-done.21 = f32[2048,256]{1,0:T(8,128)S(1)} copy-done((f32[2048,256]{1,0:T(8,128)S(1)}, f32[2048,256]{1,0:T(8,128)}, u32[]{:S(2)}) %copy-start.21) | copy-done | bytes 2097176
  87.1 1.6 %copy-done.22 = f32[2048,256]{1,0:T(8,128)S(1)} copy-done((f32[2048,256]{1,0:T(8,128)S(1)}, f32[2048,256]{1,0:T(8,128)}, u32[]{:S(2)}) %copy-start.22) | copy-done | bytes 2097176
  88.7 1.4 copy-done.24
  90.1 1.4 copy-done.26
  95.1 19.1 %shard_map.80 = bf16[32,2,64,128]{3,2,1,0:T(8,128)(2,1)} custom-call(bf16[32,2,64,128]{3,2,1,0:T(8,128)(2,1)S(1)} %all-to-all-done.vg_ref, bf16[256,128]{1,0:T(8,128)(2,1)S(1)} %copy-done.34, bf16[256,128]{1,0:T(8,128)(2,1)S(1)} %copy-done.36, f32[256,256]{1,0:T(8,128)S(1)} %copy-done.30, f32[8,128]{1,0:T(8,128)S(1)} %get-tuple-element.43.factor_ref, ...), custom_call_target="tpu_custom_call" | custom-call | flops 14000000000 | bytes 13635584 | tf_op jit(solution)/shard_map/pallas_call | solution.py:604
  114.2 5.8 %all-to-all-start.3 = ((bf16[32,2,64,128]{3,2,1,0:T(8,128)(2,1)}), bf16[32,2,64,128]{3,2,1,0:T(8,128)(2,1)S(1)}, u32[]{:S(2)}, u32[]{:S(2)}) async-start(bf16[32,2,64,128]{3,2,1,0:T(8,128)(2,1)} %shard_map.80), calls=%async_computation.3 | async-start | bytes 2097152 | tf_op jit(solution)/shard_map/all_to_all | solution.py:716
  120.0 1.2 shard_map.79
  121.3 25.0 %all-to-all-done.3.packed_ref = bf16[32,2,64,128]{3,2,1,0:T(8,128)(2,1)S(1)} async-done(((bf16[32,2,64,128]{3,2,1,0:T(8,128)(2,1)}), bf16[32,2,64,128]{3,2,1,0:T(8,128)(2,1)S(1)}, u32[]{:S(2)}, u32[]{:S(2)}) %all-to-all-start.3) | async-done | bytes 1048608 | tf_op jit(solution)/shard_map/all_to_all | solution.py:716
  146.3 1.2 shard_map.81
  (65 shorter events, 16.4 us)
Async XLA Ops:
  0.6 1.0 copy-start
  1.7 1.0 copy-start.1
  2.7 8.5 %copy-start.2 = (bf16[64,4096]{1,0:T(8,128)(2,1)S(1)}, bf16[64,4096]{1,0:T(8,128)(2,1)}, u32[]{:S(2)}) copy-start(bf16[64,4096]{1,0:T(8,128)(2,1)} %first_ref.2) | copy-start | bytes 1572868
  2.7 8.5 %copy-start.3 = (bf16[64,4096]{1,0:T(8,128)(2,1)S(1)}, bf16[64,4096]{1,0:T(8,128)(2,1)}, u32[]{:S(2)}) copy-start(bf16[64,4096]{1,0:T(8,128)(2,1)} %second_ref.2) | copy-start | bytes 1572868
  3.9 33.5 %all-to-all-start.1 = ((bf16[32,2,64,128]{3,2,1,0:T(8,128)(2,1)}), bf16[32,2,64,128]{3,2,1,0:T(8,128)(2,1)S(1)}, u32[]{:S(2)}, u32[]{:S(2)}) async-start(bf16[32,2,64,128]{3,2,1,0:T(8,128)(2,1)} %shard_map.76), calls=%async_computation.1 | async-start | bytes 2097152 | tf_op jit(solution)/shard_map/all_to_all | solution.py:716
  37.4 31.1 %all-to-all-start = ((bf16[32,2,64,128]{3,2,1,0:T(8,128)(2,1)}), bf16[32,2,64,128]{3,2,1,0:T(8,128)(2,1)S(1)}, u32[]{:S(2)}, u32[]{:S(2)}) async-start(bf16[32,2,64,128]{3,2,1,0:T(8,128)(2,1)} %shard_map.75), calls=%async_computation | async-start | bytes 2097152 | tf_op jit(solution)/shard_map/all_to_all | solution.py:716
  56.9 1.0 copy-start.4
  61.2 1.3 copy-start.20
  62.5 1.2 copy-start.23
  63.8 1.1 copy-start.25
  64.9 1.0 copy-start.27
  68.6 1.2 copy-start.5
  69.8 1.2 copy-start.7
  71.0 1.2 copy-start.9
  79.6 5.9 %copy-start.28 = (bf16[2,128,2048]{2,1,0:T(8,128)(2,1)S(1)}, bf16[2,128,2048]{2,1,0:T(8,128)(2,1)}, u32[]{:S(2)}) copy-start(bf16[2,128,2048]{2,1,0:T(8,128)(2,1)} %copy-done.27) | copy-start | bytes 3145732
  79.6 5.9 %copy-start.13 = (f32[256,128]{1,0:T(8,128)S(1)}, f32[256,128]{1,0:T(8,128)}, u32[]{:S(2)}) copy-start(f32[256,128]{1,0:T(8,128)} %copy-done.12) | copy-start | bytes 393220
  79.6 5.9 %copy-start.17 = (bf16[256,128]{1,0:T(8,128)(2,1)S(1)}, bf16[256,128]{1,0:T(8,128)(2,1)}, u32[]{:S(2)}) copy-start(bf16[256,128]{1,0:T(8,128)(2,1)} %copy-done.16) | copy-start | bytes 196612
  79.6 5.9 %copy-start.19 = (bf16[256,128]{1,0:T(8,128)(2,1)S(1)}, bf16[256,128]{1,0:T(8,128)(2,1)}, u32[]{:S(2)}) copy-start(bf16[256,128]{1,0:T(8,128)(2,1)} %copy-done.18) | copy-start | bytes 196612
  79.6 34.5 %all-to-all-start.2 = ((bf16[32,2,64,128]{3,2,1,0:T(8,128)(2,1)}), bf16[32,2,64,128]{3,2,1,0:T(8,128)(2,1)S(1)}, u32[]{:S(2)}, u32[]{:S(2)}) async-start(bf16[32,2,64,128]{3,2,1,0:T(8,128)(2,1)} %get-tuple-element.38), calls=%async_computation.2 | async-start | bytes 2097152 | tf_op jit(solution)/shard_map/all_to_all | solution.py:716
  85.5 1.6 %copy-start.21 = (f32[2048,256]{1,0:T(8,128)S(1)}, f32[2048,256]{1,0:T(8,128)}, u32[]{:S(2)}) copy-start(f32[2048,256]{1,0:T(8,128)} %copy-done.20) | copy-start | bytes 6291460
  87.1 1.6 %copy-start.22 = (f32[2048,256]{1,0:T(8,128)S(1)}, f32[2048,256]{1,0:T(8,128)}, u32[]{:S(2)}) copy-start(f32[2048,256]{1,0:T(8,128)} %get-tuple-element.45.key_prob_ref) | copy-start | bytes 6291460
  88.7 1.4 copy-start.24
  90.1 1.4 copy-start.26
  114.2 32.1 %all-to-all-start.3 = ((bf16[32,2,64,128]{3,2,1,0:T(8,128)(2,1)}), bf16[32,2,64,128]{3,2,1,0:T(8,128)(2,1)S(1)}, u32[]{:S(2)}, u32[]{:S(2)}) async-start(bf16[32,2,64,128]{3,2,1,0:T(8,128)(2,1)} %shard_map.80), calls=%async_computation.3 | async-start | bytes 2097152 | tf_op jit(solution)/shard_map/all_to_all | solution.py:716
  (17 other events, 13.3 us)

commit v2 on v1

--- a/solution.py
+++ b/solution.py
@@ -1,3 +1,5 @@
+import functools
+
 import jax
 import jax.numpy as jnp
 from jax import lax
@@ -9,10 +11,47 @@
 M = 256
 PINV_ITERS = 6
 CHUNK = 256
-VMEM_LIMIT = 40 * 2**20
+PACK_GROUPS = 4
+VMEM_LIMIT = 60 * 2**20
 FORWARD_FLOPS = 10 * 10**9
 MIXING_FLOPS = 2 * 10**9
 GRADIENT_FLOPS = 14 * 10**9
+MIXING_NAMES = (
+    "key_turned",
+    "token_turned",
+    "total_inverse",
+    "inverse",
+    "inverse_turned",
+    "token_low",
+    "key_plow",
+)
+GRADIENT_NAMES = (
+    "mark_q",
+    "mark_k",
+    "key_prob",
+    "columns_turned",
+    "token_prob",
+    "mark_prob",
+    "factor",
+    "pair",
+    "weight",
+    "growth",
+    "last_growth",
+)
+EARLY_NAMES = (
+    "mark_q",
+    "mark_k",
+    "mark_prob",
+    "factor",
+    "token_prob",
+    "token_low",
+    "token_turned",
+    "key_prob",
+    "key_plow",
+    "key_turned",
+    "total_inverse",
+    "columns_turned",
+)
 
 
 precise_setting = lax.Precision.HIGHEST
@@ -292,41 +331,98 @@
     return pl.ds(pl.multiple_of(index * CHUNK, CHUNK), CHUNK)
 
 
-def pack_kernel(first_ref, second_ref, out_ref):
-    for head in range(out_ref.shape[0]):
-        out_ref[head, 0] = first_ref[:, head * HD : (head + 1) * HD]
-        out_ref[head, 1] = second_ref[:, head * HD : (head + 1) * HD]
-
-
-def unpack_kernel(packed_ref, first_ref, second_ref):
-    for head in range(packed_ref.shape[0]):
-        first_ref[:, head * HD : (head + 1) * HD] = packed_ref[head, 0]
-        second_ref[:, head * HD : (head + 1) * HD] = packed_ref[head, 1]
+def pack_kernel(first_ref, second_ref, out_ref, rows_s, packed_s, in_done, out_done):
+    heads = out_ref.shape[0]
+    group = heads // PACK_GROUPS
+    reads, writes = [], []
+    for index in range(PACK_GROUPS):
+        for slot, ref in enumerate((first_ref, second_ref)):
+            place = pl.ds(index * group * HD, group * HD)
+            reads.append(
+                pltpu.make_async_copy(
+                    ref.at[:, place], rows_s.at[slot, :, place], in_done.at[slot, index]
+                )
+            )
+        place = pl.ds(index * group, group)
+        writes.append(
+            pltpu.make_async_copy(packed_s.at[place], out_ref.at[place], out_done.at[index])
+        )
+    for copy in reads:
+        copy.start()
+    for index in range(PACK_GROUPS):
+        for slot in range(2):
+            reads[2 * index + slot].wait()
+            for head in range(index * group, (index + 1) * group):
+                packed_s[head, slot] = rows_s[slot, :, head * HD : (head + 1) * HD]
+        writes[index].start()
+    for copy in writes:
+        copy.wait()
+
+
+def unpack_kernel(packed_ref, first_ref, second_ref, packed_s, rows_s, in_done, out_done):
+    heads = packed_ref.shape[0]
+    group = heads // PACK_GROUPS
+    reads, writes = [], []
+    for index in range(PACK_GROUPS):
+        place = pl.ds(index * group, group)
+        reads.append(
+            pltpu.make_async_copy(packed_ref.at[place], packed_s.at[place], in_done.at[index])
+        )
+        for slot, ref in enumerate((first_ref, second_ref)):
+            place = pl.ds(index * group * HD, group * HD)
+            writes.append(
+                pltpu.make_async_copy(
+                    rows_s.at[slot, :, place], ref.at[:, place], out_done.at[slot, index]
+                )
+            )
+    for copy in reads:
+        copy.start()
+    for index in range(PACK_GROUPS):
+        reads[index].wait()
+        for slot in range(2):
+            for head in range(index * group, (index + 1) * group):
+                rows_s[slot, :, head * HD : (head + 1) * HD] = packed_s[head, slot]
+            writes[2 * index + slot].start()
+    for copy in writes:
+        copy.wait()
 
 
 def forward_kernel(
-    qk_ref,
-    mark_q_ref,
-    mark_k_ref,
-    mark_prob_ref,
-    factor_ref,
-    token_prob_ref,
-    token_low_ref,
-    token_turned_ref,
-    key_prob_ref,
-    key_plow_ref,
-    key_turned_ref,
-    total_inverse_ref,
-    columns_turned_ref,
-    pair_ref,
-    weight_ref,
-    growth_ref,
-    inverse_ref,
-    inverse_turned_ref,
-    last_growth_ref,
-    power_s,
-    iterate_s,
+    names,
+    qk_hbm,
+    *refs,
 ):
+    count = len(names)
+    homes = dict(zip(names, refs[:count]))
+    held = dict(zip(names, refs[count : 2 * count]))
+    qk_ref, power_s, iterate_s, in_done, out_done = refs[2 * count :]
+    copies = {
+        name: pltpu.make_async_copy(held[name], homes[name], out_done.at[index])
+        for index, name in enumerate(names)
+    }
+    arrive = pltpu.make_async_copy(qk_hbm, qk_ref, in_done)
+    arrive.start()
+    arrive.wait()
+    (
+        mark_q_ref,
+        mark_k_ref,
+        mark_prob_ref,
+        factor_ref,
+        token_prob_ref,
+        token_low_ref,
+        token_turned_ref,
+        key_prob_ref,
+        key_plow_ref,
+        key_turned_ref,
+        total_inverse_ref,
+        columns_turned_ref,
+        pair_ref,
+        weight_ref,
+        growth_ref,
+        inverse_ref,
+        inverse_turned_ref,
+        last_growth_ref,
+    ) = (held[name] for name in names)
     tokens, rows, chunks = dims_of(qk_ref)
     segment_len = tokens // M
     marks_per = CHUNK // segment_len
@@ -352,34 +448,6 @@
     power_s[...] = split_dot_nt(mark_halves, mark_halves) * factor
     iterate_s[0:M] = mark_prob.T * factor
     iterate_s[M:] = identity_matrix()
-
-    def newton(sweep, carry):
-        power = power_s[...]
-        power_high, power_low = halves(power)
-        square = split_dot((power_high, power_low), (power_high, power_low))
-        square_halves = halves(square)
-        pair = (
-            jnp.concatenate([power_high, square_halves[0]], axis=0),
-            jnp.concatenate([power_low, square_halves[1]], axis=0),
-        )
-        pair_ref[sweep, 0], pair_ref[sweep, 1] = pair
-        higher = split_dot(pair, square_halves)
-        cube, fourth = higher[:M], higher[M:]
-        weight = halves(
-            0.25 * (13.0 * identity_matrix() - 15.0 * power + 7.0 * square - cube)
-        )
-        power_s[...] = 0.25 * (13.0 * power - 15.0 * square + 7.0 * cube - fourth)
-        weight_ref[sweep, 0], weight_ref[sweep, 1] = weight
-        iterate = halves(iterate_s[...])
-        growth_ref[sweep, 0], growth_ref[sweep, 1] = iterate[0][M:], iterate[1][M:]
-        iterate_s[...] = split_dot(iterate, weight)
-        return carry
-
-    lax.fori_loop(0, PINV_ITERS, newton, 0)
-    inverse = iterate_s[0:M]
-    inverse_ref[0], inverse_ref[1] = halves(inverse)
-    inverse_turned_ref[0], inverse_turned_ref[1] = halves(inverse.T)
-    last_growth_ref[0], last_growth_ref[1] = halves(iterate_s[M:])
 
     def scores(index, key_max):
         query_chunk, key_chunk = chunk_of(qk_ref, 0, index), chunk_of(qk_ref, 1, index)
@@ -418,24 +486,76 @@
         return carry
 
     lax.fori_loop(0, chunks, normalise, 0)
-
-
-def mixing_kernel(
-    vg_ref,
-    token_low_ref,
-    token_turned_ref,
-    key_plow_ref,
-    key_turned_ref,
-    total_inverse_ref,
-    inverse_ref,
-    inverse_turned_ref,
-    out_ref,
-    mixing_low_ref,
-    mixing_grad_ref,
-    mark_values_ref,
-    values_low_ref,
-):
+    for name in EARLY_NAMES:
+        copies[name].start()
+
+    def newton(sweep, carry):
+        power = power_s[...]
+        power_high, power_low = halves(power)
+        square = split_dot((power_high, power_low), (power_high, power_low))
+        square_halves = halves(square)
+        pair = (
+            jnp.concatenate([power_high, square_halves[0]], axis=0),
+            jnp.concatenate([power_low, square_halves[1]], axis=0),
+        )
+        pair_ref[sweep, 0], pair_ref[sweep, 1] = pair
+        higher = split_dot(pair, square_halves)
+        cube, fourth = higher[:M], higher[M:]
+        weight = halves(
+            0.25 * (13.0 * identity_matrix() - 15.0 * power + 7.0 * square - cube)
+        )
+        power_s[...] = 0.25 * (13.0 * power - 15.0 * square + 7.0 * cube - fourth)
+        weight_ref[sweep, 0], weight_ref[sweep, 1] = weight
+        iterate = halves(iterate_s[...])
+        growth_ref[sweep, 0], growth_ref[sweep, 1] = iterate[0][M:], iterate[1][M:]
+        iterate_s[...] = split_dot(iterate, weight)
+        return carry
+
+    lax.fori_loop(0, PINV_ITERS, newton, 0)
+    inverse = iterate_s[0:M]
+    inverse_ref[0], inverse_ref[1] = halves(inverse)
+    inverse_turned_ref[0], inverse_turned_ref[1] = halves(inverse.T)
+    last_growth_ref[0], last_growth_ref[1] = halves(iterate_s[M:])
+    for name in names:
+        if name not in EARLY_NAMES:
+            copies[name].start()
+    for name in names:
+        copies[name].wait()
+
+
+def start_reads(sources, held, done):
+    reads = [
+        pltpu.make_async_copy(source, ref, done.at[index])
+        for index, (source, ref) in enumerate(zip(sources, held))
+    ]
+    for read in reads:
+        read.start()
+    return reads
+
+
+def mixing_kernel(*refs):
+    count = len(MIXING_NAMES) + 1
+    sources, homes, held = refs[:count], refs[count : count + 5], refs[count + 5 : 2 * count + 5]
+    results, (in_done, out_done) = refs[2 * count + 5 : 2 * count + 10], refs[2 * count + 10 :]
+    reads = start_reads(sources, held, in_done)
+    (
+        vg_ref,
+        key_turned_ref,
+        token_turned_ref,
+        total_inverse_ref,
+        inverse_ref,
+        inverse_turned_ref,
+        token_low_ref,
+        key_plow_ref,
+    ) = held
+    out_ref, mixing_low_ref, mixing_grad_ref, mark_values_ref, values_low_ref = results
+    writes = [
+        pltpu.make_async_copy(result, home, out_done.at[index])
+        for index, (result, home) in enumerate(zip(results, homes))
+    ]
     tokens, rows, chunks = dims_of(vg_ref)
+    for read in reads[:6]:
+        read.wait()
     values = vg_ref[:, 0].reshape(tokens, HD)
     out_grad = vg_ref[:, 1].reshape(tokens, HD)
     landmark_values = wide_dot(key_turned_ref[...], values) * total_inverse_ref[...]
@@ -450,6 +570,10 @@
     ).astype(jnp.bfloat16)
     mixing_low_ref[...] = mixing_low
     values_low_ref[...] = values_low
+    for write in writes[1:]:
+        write.start()
+    for read in reads[6:]:
+        read.wait()
 
     def emit(index, carry):
         place = columns(index)
@@ -462,36 +586,75 @@
         return carry
 
     lax.fori_loop(0, chunks, emit, 0)
-
-
-def gradient_kernel(
-    vg_ref,
-    mark_q_ref,
-    mark_k_ref,
-    mark_prob_ref,
-    factor_ref,
-    token_prob_ref,
-    key_prob_ref,
-    columns_turned_ref,
-    pair_ref,
-    weight_ref,
-    growth_ref,
-    last_growth_ref,
-    mixing_low_ref,
-    mixing_grad_ref,
-    mark_values_ref,
-    values_low_ref,
-    out_ref,
-    power_s,
-    growth_s,
-    direct_s,
-    kept_s,
-):
+    writes[0].start()
+    for write in writes:
+        write.wait()
+
+
+def gradient_kernel(*refs):
+    count = len(GRADIENT_NAMES) + 5
+    sources, home, held = refs[:count], refs[count], refs[count + 1 : 2 * count + 1]
+    out_ref, power_s, growth_s, query_s, direct_s, kept_s, in_done, out_done = refs[2 * count + 1 :]
+    reads = start_reads(sources, held, in_done)
+    (
+        values_low_ref,
+        mixing_low_ref,
+        vg_ref,
+        mark_q_ref,
+        mark_k_ref,
+        key_prob_ref,
+        columns_turned_ref,
+        token_prob_ref,
+        mark_prob_ref,
+        factor_ref,
+        pair_ref,
+        weight_ref,
+        growth_ref,
+        last_growth_ref,
+        mixing_grad_ref,
+        mark_values_ref,
+    ) = held
     tokens, rows, chunks = dims_of(vg_ref)
     segment_len = tokens // M
     marks_per = CHUNK // segment_len
     score_scale = HD ** (-0.5)
+    for read in reads[:8]:
+        read.wait()
     landmark_q, landmark_k = mark_q_ref[...], mark_k_ref[...]
+
+    values_low = values_low_ref[...]
+
+    def key_rows(index, row_total):
+        place = columns(index)
+        key_dgrad = wide_dot_nt(chunk_of(vg_ref, 0, index), values_low)
+        kept_s[place] = key_dgrad
+        return row_total + jnp.sum(key_prob_ref[place] * key_dgrad, axis=0, keepdims=True)
+
+    row_total = lax.fori_loop(0, chunks, key_rows, jnp.zeros((1, M), jnp.float32))
+
+    def key_side(index, total):
+        place = columns(index)
+        key_sgrad = (key_prob_ref[place] * (kept_s[place] - row_total)).astype(jnp.bfloat16)
+        direct_s[place] = wide_dot(key_sgrad, landmark_q) * score_scale
+        return total + wide_dot(columns_turned_ref[1, :, place], key_sgrad)
+
+    mark_qgrad_b = lax.fori_loop(0, chunks, key_side, jnp.zeros((HD, M), jnp.float32))
+    mixing_low = mixing_low_ref[...]
+
+    def token_side(index, total):
+        place = columns(index)
+        prob = token_prob_ref[place]
+        token_grad = wide_dot_nt(chunk_of(vg_ref, 1, index), mixing_low)
+        token_sgrad = (
+            prob * (token_grad - jnp.sum(token_grad * prob, axis=1, keepdims=True))
+        ).astype(jnp.bfloat16)
+        query_s[place] = wide_dot(token_sgrad, landmark_k) * score_scale
+        return total + wide_dot(columns_turned_ref[0, :, place], token_sgrad)
+
+    mark_kgrad_f = lax.fori_loop(0, chunks, token_side, jnp.zeros((HD, M), jnp.float32))
+
+    for read in reads[8:]:
+        read.wait()
     mark_prob = mark_prob_ref[...]
     mark_halves = halves(mark_prob)
     factor = factor_ref[0:1, 0:1]
@@ -548,80 +711,67 @@
 
     mark_qgrad_a = marks_dot(mark_sgrad, landmark_k)
     mark_kgrad_a = marks_dot(mark_sgrad.T, landmark_q)
-
-    values_low = values_low_ref[...]
-
-    def key_rows(index, row_total):
-        place = columns(index)
-        key_dgrad = wide_dot_nt(chunk_of(vg_ref, 0, index), values_low)
-        kept_s[place] = key_dgrad
-        return row_total + jnp.sum(key_prob_ref[place] * key_dgrad, axis=0, keepdims=True)
-
-    row_total = lax.fori_loop(0, chunks, key_rows, jnp.zeros((1, M), jnp.float32))
-
-    def key_side(index, total):
-        place = columns(index)
-        key_sgrad = (key_prob_ref[place] * (kept_s[place] - row_total)).astype(jnp.bfloat16)
-        direct_s[place] = wide_dot(key_sgrad, landmark_q) * score_scale
-        return total + wide_dot(columns_turned_ref[1, :, place], key_sgrad)
-
-    mark_qgrad_b = lax.fori_loop(0, chunks, key_side, jnp.zeros((HD, M), jnp.float32))
-    mark_qtotal = (mark_qgrad_a + mark_qgrad_b.T) * (score_scale / segment_len)
-    mixing_low = mixing_low_ref[...]
+    kept_s[0:M, 0:HD] = (mark_qgrad_a + mark_qgrad_b.T) * (score_scale / segment_len)
+    kept_s[0:M, HD:] = (mark_kgrad_a + mark_kgrad_f.T) * (score_scale / segment_len)
 
     def spread(direct, marks):
         wide = jnp.broadcast_to(marks[:, None], (marks_per, segment_len, HD))
         return (direct + wide.reshape(CHUNK, HD)).astype(jnp.bfloat16)
 
-    kept_s[0:M, 0:HD] = mark_qtotal
-
-    def token_side(index, total):
+    def finish(index, carry):
+        marks = kept_s[pl.ds(pl.multiple_of(index * marks_per, marks_per), marks_per)]
         place = columns(index)
-        prob = token_prob_ref[place]
-        token_grad = wide_dot_nt(chunk_of(vg_ref, 1, index), mixing_low)
-        token_sgrad = (
-            prob * (token_grad - jnp.sum(token_grad * prob, axis=1, keepdims=True))
-        ).astype(jnp.bfloat16)
-        direct = wide_dot(token_sgrad, landmark_k) * score_scale
-        marks = kept_s[pl.ds(pl.multiple_of(index * marks_per, marks_per), marks_per), 0:HD]
-        store_chunk(out_ref, 0, index, spread(direct, marks))
-        return total + wide_dot(columns_turned_ref[0, :, place], token_sgrad)
-
-    mark_kgrad_f = lax.fori_loop(0, chunks, token_side, jnp.zeros((HD, M), jnp.float32))
-    kept_s[0:M, 0:HD] = (mark_kgrad_a + mark_kgrad_f.T) * (score_scale / segment_len)
-
-    def finish(index, carry):
-        marks = kept_s[pl.ds(pl.multiple_of(index * marks_per, marks_per), marks_per), 0:HD]
-        store_chunk(out_ref, 1, index, spread(direct_s[columns(index)], marks))
+        store_chunk(out_ref, 0, index, spread(query_s[place], marks[:, :HD]))
+        store_chunk(out_ref, 1, index, spread(direct_s[place], marks[:, HD:]))
         return carry
 
     lax.fori_loop(0, chunks, finish, 0)
+    write = pltpu.make_async_copy(out_ref, home, out_done)
+    write.start()
+    write.wait()
 
 
 def kernel_call(kernel, out_shape, scratch, flops, operands):
     moved = sum(x.size * x.dtype.itemsize for x in operands)
-    in_vmem = pl.BlockSpec(memory_space=pltpu.VMEM)
+    in_place = pl.BlockSpec(memory_space=pl.ANY)
     return pl.pallas_call(
         kernel,
         out_shape=out_shape,
-        in_specs=[in_vmem] * len(operands),
-        out_specs=jax.tree.map(lambda _: in_vmem, out_shape),
+        in_specs=[in_place] * len(operands),
+        out_specs=jax.tree.map(lambda _: in_place, out_shape),
         scratch_shapes=scratch,
         compiler_params=pltpu.CompilerParams(vmem_limit_bytes=VMEM_LIMIT),
         cost_estimate=pl.CostEstimate(flops=flops, bytes_accessed=moved, transcendentals=0),
     )(*operands)
 
 
+def in_vmem(array):
+    return pltpu.VMEM(array.shape, array.dtype)
+
+
 def pack(first, second):
     rows, width = first.shape
-    shape = jax.ShapeDtypeStruct((width // HD, 2, rows, HD), first.dtype)
-    return kernel_call(pack_kernel, shape, [], 0, (first, second))
+    heads = width // HD
+    shape = jax.ShapeDtypeStruct((heads, 2, rows, HD), first.dtype)
+    scratch = [
+        pltpu.VMEM((2, rows, width), first.dtype),
+        pltpu.VMEM((heads, 2, rows, HD), first.dtype),
+        pltpu.SemaphoreType.DMA((2, PACK_GROUPS)),
+        pltpu.SemaphoreType.DMA((PACK_GROUPS,)),
+    ]
+    return kernel_call(pack_kernel, shape, scratch, 0, (first, second))
 
 
 def unpack(packed):
     heads, _, rows, _ = packed.shape
     shape = jax.ShapeDtypeStruct((rows, heads * HD), packed.dtype)
-    return kernel_call(unpack_kernel, (shape, shape), [], 0, (packed,))
+    scratch = [
+        pltpu.VMEM((heads, 2, rows, HD), packed.dtype),
+        pltpu.VMEM((2, rows, heads * HD), packed.dtype),
+        pltpu.SemaphoreType.DMA((PACK_GROUPS,)),
+        pltpu.SemaphoreType.DMA((2, PACK_GROUPS)),
+    ]
+    return kernel_call(unpack_kernel, (shape, shape), scratch, 0, (packed,))
 
 
 def forward_part(qk):
@@ -653,23 +803,25 @@
         inverse_turned=low(2, M, M),
         last_growth=low(2, M, M),
     )
-    scratch = [pltpu.VMEM((M, M), jnp.float32), pltpu.VMEM((2 * M, M), jnp.float32)]
+    scratch = [
+        *(in_vmem(shape) for shape in shapes.values()),
+        in_vmem(qk),
+        pltpu.VMEM((M, M), jnp.float32),
+        pltpu.VMEM((2 * M, M), jnp.float32),
+        pltpu.SemaphoreType.DMA,
+        pltpu.SemaphoreType.DMA((len(shapes),)),
+    ]
     results = kernel_call(
-        forward_kernel, tuple(shapes.values()), scratch, FORWARD_FLOPS, (qk,)
+        functools.partial(forward_kernel, tuple(shapes)),
+        tuple(shapes.values()),
+        scratch,
+        FORWARD_FLOPS,
+        (qk,),
     )
     return dict(zip(shapes, results))
 
 
 def mixing_part(vg, kept):
-    names = (
-        "token_low",
-        "token_turned",
-        "key_plow",
-        "key_turned",
-        "total_inverse",
-        "inverse",
-        "inverse_turned",
-    )
     shapes = (
         jax.ShapeDtypeStruct(vg.shape, jnp.bfloat16),
         jax.ShapeDtypeStruct((M, HD), jnp.bfloat16),
@@ -677,39 +829,38 @@
         jax.ShapeDtypeStruct((M, HD), jnp.float32),
         jax.ShapeDtypeStruct((M, HD), jnp.bfloat16),
     )
-    return kernel_call(
-        mixing_kernel, shapes, [], MIXING_FLOPS, (vg, *(kept[name] for name in names))
-    )
+    operands = (vg, *(kept[name] for name in MIXING_NAMES))
+    scratch = [
+        *(in_vmem(array) for array in (*operands, *shapes)),
+        pltpu.SemaphoreType.DMA((len(operands),)),
+        pltpu.SemaphoreType.DMA((len(shapes),)),
+    ]
+    return kernel_call(mixing_kernel, shapes, scratch, MIXING_FLOPS, operands)
 
 
 def gradient_part(vg, kept, mixed):
-    names = (
-        "mark_q",
-        "mark_k",
-        "mark_prob",
-        "factor",
-        "token_prob",
-        "key_prob",
-        "columns_turned",
-        "pair",
-        "weight",
-        "growth",
-        "last_growth",
+    mixing_low, mixing_grad, mark_values, values_low = mixed
+    operands = (
+        values_low,
+        mixing_low,
+        vg,
+        *(kept[name] for name in GRADIENT_NAMES),
+        mixing_grad,
+        mark_values,
     )
     tokens = vg.shape[0] * vg.shape[2]
     scratch = [
+        *(in_vmem(array) for array in (*operands, vg)),
         pltpu.VMEM((M, M), jnp.float32),
         pltpu.VMEM((M, M), jnp.float32),
         pltpu.VMEM((tokens, HD), jnp.float32),
+        pltpu.VMEM((tokens, HD), jnp.float32),
         pltpu.VMEM((tokens, M), jnp.float32),
+        pltpu.SemaphoreType.DMA((len(operands),)),
+        pltpu.SemaphoreType.DMA,
     ]
-    return kernel_call(
-        gradient_kernel,
-        jax.ShapeDtypeStruct(vg.shape, jnp.bfloat16),
-        scratch,
-        GRADIENT_FLOPS,
-        (vg, *(kept[name] for name in names), *mixed),
-    )
+    shape = jax.ShapeDtypeStruct(vg.shape, jnp.bfloat16)
+    return kernel_call(gradient_kernel, shape, scratch, GRADIENT_FLOPS, operands)
 
 
 def exchange(packed):

time: 149 us -> 136 us (0.913)
  local copies, waits for them, and re-layouts: 30.8 us -> 1.97 us
  waiting for transfers between devices: 50.1 us -> 63.4 us
  Pallas kernels: 43.3 us -> 51.4 us
  starting transfers between devices: 22.6 us -> 18.2 us
    unnamed x74 -> x8, local copies, waits for them, and re-layouts: 30.8 us -> 1.97 us
    all_to_all x4, waiting for transfers between devices: 50.1 us -> 63.4 us  [exchange(): lax.all_to_all(packed, ('seq', 'head'), split_axis=0, concat_axis=0, tile...]
    pallas_call x7, Pallas kernels: 43.3 us -> 51.4 us  [kernel_call(): pl.pallas_call(kernel, out_shape=out_shape, in_specs=[in_place] * len(ope...]
    all_to_all x4, starting transfers between devices: 22.6 us -> 18.2 us  [exchange(): lax.all_to_all(packed, ('seq', 'head'), split_axis=0, concat_axis=0, tile...]
  transfers between devices with their start and end apart: 4 -> 4, of which waited for: 2 -> 4; matrix products, arithmetic and copies ran while one was open for 0% -> 0% of each run, Pallas kernels for 25% -> 31%
where the time goes in v2:
time: 136 us
  waiting for transfers between devices  63.4 us (47%)
  Pallas kernels  51.4 us (38%)
  starting transfers between devices  18.2 us (13%)
  local copies, waits for them, and re-layouts  1.97 us (1%)
    all_to_all x4, waiting for transfers between devices, exchange(): lax.all_to_all(packed, ('seq', 'head'), split_axis=0, concat_axis=0, tile...  63.4 us
    pallas_call x7, Pallas kernels, kernel_call(): pl.pallas_call(kernel, out_shape=out_shape, in_specs=[in_place] * len(ope...  51.4 us
    all_to_all x4, starting transfers between devices, exchange(): lax.all_to_all(packed, ('seq', 'head'), split_axis=0, concat_axis=0, tile...  18.2 us
  transfers between devices with their start and end apart: 4, of which 4 were waited for; matrix products, arithmetic and copies ran while one was open for 0% of the time, Pallas kernels for 31%

profile of v2, /device:TPU:0, one launch (start us, length us, event | category | flops | bytes accessed | tf_op | source)
XLA Modules:
  0.0 135.7 jit_solution(9742858051028880029)
XLA Ops:
  0.6 2.1 %shard_map.76 = bf16[32,2,64,128]{3,2,1,0:T(8,128)(2,1)} custom-call(bf16[64,4096]{1,0:T(8,128)(2,1)} %first_ref.3, bf16[64,4096]{1,0:T(8,128)(2,1)} %second_ref.3), custom_call_target="tpu_custom_call" | custom-call | bytes 1048576 | tf_op jit(solution)/shard_map/pallas_call | solution.py:737
  2.8 7.3 %all-to-all-start.1 = ((bf16[32,2,64,128]{3,2,1,0:T(8,128)(2,1)}), bf16[32,2,64,128]{3,2,1,0:T(8,128)(2,1)S(1)}, u32[]{:S(2)}, u32[]{:S(2)}) async-start(bf16[32,2,64,128]{3,2,1,0:T(8,128)(2,1)} %shard_map.76), calls=%async_computation.1 | async-start | bytes 2097152 | tf_op jit(solution)/shard_map/all_to_all | solution.py:867
  10.1 2.2 %shard_map.75 = bf16[32,2,64,128]{3,2,1,0:T(8,128)(2,1)} custom-call(bf16[64,4096]{1,0:T(8,128)(2,1)} %first_ref.2, bf16[64,4096]{1,0:T(8,128)(2,1)} %second_ref.2), custom_call_target="tpu_custom_call" | custom-call | bytes 1048576 | tf_op jit(solution)/shard_map/pallas_call | solution.py:737
  12.2 24.1 %all-to-all-done.1.qk_hbm = bf16[32,2,64,128]{3,2,1,0:T(8,128)(2,1)S(1)} async-done(((bf16[32,2,64,128]{3,2,1,0:T(8,128)(2,1)}), bf16[32,2,64,128]{3,2,1,0:T(8,128)(2,1)S(1)}, u32[]{:S(2)}, u32[]{:S(2)}) %all-to-all-start.1) | async-done | bytes 1048608 | tf_op jit(solution)/shard_map/all_to_all | solution.py:867
  36.3 0.0 copy-start.3
  36.3 3.6 %all-to-all-start = ((bf16[32,2,64,128]{3,2,1,0:T(8,128)(2,1)}), bf16[32,2,64,128]{3,2,1,0:T(8,128)(2,1)S(1)}, u32[]{:S(2)}, u32[]{:S(2)}) async-start(bf16[32,2,64,128]{3,2,1,0:T(8,128)(2,1)} %shard_map.75), calls=%async_computation | async-start | bytes 2097152 | tf_op jit(solution)/shard_map/all_to_all | solution.py:867
  39.9 0.0 copy-done.3
  40.0 16.8 %shard_map.77 = (bf16[256,128]{1,0:T(8,128)(2,1)}, bf16[256,128]{1,0:T(8,128)(2,1)}, f32[256,256]{1,0:T(8,128)}, f32[8,128]{1,0:T(8,128)}, f32[2048,256]{1,0:T(8...) custom-call(bf16[32,2,64,128]{3,2,1,0:T(8,128)(2,1)} %copy-done.3), custom_call_target="tpu_custom_call" | custom-call | flops 10000000000 | bytes 1048576 | tf_op jit(solution)/shard_map/pallas_call | solution.py:737
  56.7 9.4 %all-to-all-done.refs_0_.refs_2_ = bf16[32,2,64,128]{3,2,1,0:T(8,128)(2,1)S(1)} async-done(((bf16[32,2,64,128]{3,2,1,0:T(8,128)(2,1)}), bf16[32,2,64,128]{3,2,1,0:T(8,128)(2,1)S(1)}, u32[]{:S(2)}, u32[]{:S(2)}) %all-to-all-start) | async-done | bytes 1048608 | tf_op jit(solution)/shard_map/all_to_all | solution.py:867
  66.2 0.0 copy-start.2
  66.2 1.0 copy-done.2
  67.2 5.8 %shard_map.78 = (bf16[32,2,64,128]{3,2,1,0:T(8,128)(2,1)}, bf16[256,128]{1,0:T(8,128)(2,1)}, f32[256,128]{1,0:T(8,128)}, f32[256,128]{1,0:T(8,128)}, bf16[256,128]{1,0:T(8,128)(2,1)}) custom-call(bf16[32,2,64,128]{3,2,1,0:T(8,128)(2,1)} %copy-done.2, bf16[256,2048]{1,0:T(8,128)(2,1)} %get-tuple-element.31.refs_1_, ...), custom_call_target="tpu_custom_call" | custom-call | flops 2000000000 | bytes 5898240 | tf_op jit(solution)/shard_map/pallas_call | solution.py:737
  72.9 3.6 %all-to-all-start.2 = ((bf16[32,2,64,128]{3,2,1,0:T(8,128)(2,1)}), bf16[32,2,64,128]{3,2,1,0:T(8,128)(2,1)S(1)}, u32[]{:S(2)}, u32[]{:S(2)}) async-start(bf16[32,2,64,128]{3,2,1,0:T(8,128)(2,1)} %get-tuple-element.38), calls=%async_computation.2 | async-start | bytes 2097152 | tf_op jit(solution)/shard_map/all_to_all | solution.py:867
  76.6 20.5 %shard_map.80 = bf16[32,2,64,128]{3,2,1,0:T(8,128)(2,1)} custom-call(bf16[256,128]{1,0:T(8,128)(2,1)} %get-tuple-element.40.refs_0_, bf16[256,128]{1,0:T(8,128)(2,1)} %get-tuple-element.41.refs_1_, bf16[32,2,64,128]{3,2,1,0:T(8,128)(2,1)} %copy-done.2, bf16[256,128]{1,0:T(8,128)(2,1)} %get-tuple-element.42.refs_3_, ...), custom_call_target="tpu_custom_call" | custom-call | flops 14000000000 | bytes 13635584 | tf_op jit(solution)/shard_map/pallas_call | solution.py:737
  97.1 5.7 %all-to-all-done.2.packed_ref = bf16[32,2,64,128]{3,2,1,0:T(8,128)(2,1)S(1)} async-done(((bf16[32,2,64,128]{3,2,1,0:T(8,128)(2,1)}), bf16[32,2,64,128]{3,2,1,0:T(8,128)(2,1)S(1)}, u32[]{:S(2)}, u32[]{:S(2)}) %all-to-all-start.2) | async-done | bytes 1048608 | tf_op jit(solution)/shard_map/all_to_all | solution.py:867
  102.8 0.0 copy-start
  102.8 3.6 %all-to-all-start.3 = ((bf16[32,2,64,128]{3,2,1,0:T(8,128)(2,1)}), bf16[32,2,64,128]{3,2,1,0:T(8,128)(2,1)S(1)}, u32[]{:S(2)}, u32[]{:S(2)}) async-start(bf16[32,2,64,128]{3,2,1,0:T(8,128)(2,1)} %shard_map.80), calls=%async_computation.3 | async-start | bytes 2097152 | tf_op jit(solution)/shard_map/all_to_all | solution.py:867
  106.4 0.0 copy-done
  106.5 2.0 %shard_map.79 = (bf16[64,4096]{1,0:T(8,128)(2,1)}, bf16[64,4096]{1,0:T(8,128)(2,1)}) custom-call(bf16[32,2,64,128]{3,2,1,0:T(8,128)(2,1)} %copy-done), custom_call_target="tpu_custom_call" | custom-call | bytes 1048576 | tf_op jit(solution)/shard_map/pallas_call | solution.py:737
  108.5 24.2 %all-to-all-done.3.packed_ref = bf16[32,2,64,128]{3,2,1,0:T(8,128)(2,1)S(1)} async-done(((bf16[32,2,64,128]{3,2,1,0:T(8,128)(2,1)}), bf16[32,2,64,128]{3,2,1,0:T(8,128)(2,1)S(1)}, u32[]{:S(2)}, u32[]{:S(2)}) %all-to-all-start.3) | async-done | bytes 1048608 | tf_op jit(solution)/shard_map/all_to_all | solution.py:867
  132.7 0.0 copy-start.1
  132.7 1.0 copy-done.1
  133.7 2.0 %shard_map.81 = (bf16[64,4096]{1,0:T(8,128)(2,1)}, bf16[64,4096]{1,0:T(8,128)(2,1)}) custom-call(bf16[32,2,64,128]{3,2,1,0:T(8,128)(2,1)} %copy-done.1), custom_call_target="tpu_custom_call" | custom-call | bytes 1048576 | tf_op jit(solution)/shard_map/pallas_call | solution.py:737
Async XLA Ops:
  2.8 33.5 %all-to-all-start.1 = ((bf16[32,2,64,128]{3,2,1,0:T(8,128)(2,1)}), bf16[32,2,64,128]{3,2,1,0:T(8,128)(2,1)S(1)}, u32[]{:S(2)}, u32[]{:S(2)}) async-start(bf16[32,2,64,128]{3,2,1,0:T(8,128)(2,1)} %shard_map.76), calls=%async_computation.1 | async-start | bytes 2097152 | tf_op jit(solution)/shard_map/all_to_all | solution.py:867
  36.3 3.6 %copy-start.3 = (bf16[32,2,64,128]{3,2,1,0:T(8,128)(2,1)}, bf16[32,2,64,128]{3,2,1,0:T(8,128)(2,1)S(1)}, u32[]{:S(2)}) copy-start(bf16[32,2,64,128]{3,2,1,0:T(8,128)(2,1)S(1)} %all-to-all-done.1.qk_hbm) | copy-start | bytes 3145732
  36.3 29.9 %all-to-all-start = ((bf16[32,2,64,128]{3,2,1,0:T(8,128)(2,1)}), bf16[32,2,64,128]{3,2,1,0:T(8,128)(2,1)S(1)}, u32[]{:S(2)}, u32[]{:S(2)}) async-start(bf16[32,2,64,128]{3,2,1,0:T(8,128)(2,1)} %shard_map.75), calls=%async_computation | async-start | bytes 2097152 | tf_op jit(solution)/shard_map/all_to_all | solution.py:867
  66.2 1.0 copy-start.2
  72.9 29.9 %all-to-all-start.2 = ((bf16[32,2,64,128]{3,2,1,0:T(8,128)(2,1)}), bf16[32,2,64,128]{3,2,1,0:T(8,128)(2,1)S(1)}, u32[]{:S(2)}, u32[]{:S(2)}) async-start(bf16[32,2,64,128]{3,2,1,0:T(8,128)(2,1)} %get-tuple-element.38), calls=%async_computation.2 | async-start | bytes 2097152 | tf_op jit(solution)/shard_map/all_to_all | solution.py:867
  102.8 3.6 %copy-start = (bf16[32,2,64,128]{3,2,1,0:T(8,128)(2,1)}, bf16[32,2,64,128]{3,2,1,0:T(8,128)(2,1)S(1)}, u32[]{:S(2)}) copy-start(bf16[32,2,64,128]{3,2,1,0:T(8,128)(2,1)S(1)} %all-to-all-done.2.packed_ref) | copy-start | bytes 3145732
  102.8 29.9 %all-to-all-start.3 = ((bf16[32,2,64,128]{3,2,1,0:T(8,128)(2,1)}), bf16[32,2,64,128]{3,2,1,0:T(8,128)(2,1)S(1)}, u32[]{:S(2)}, u32[]{:S(2)}) async-start(bf16[32,2,64,128]{3,2,1,0:T(8,128)(2,1)} %shard_map.80), calls=%async_computation.3 | async-start | bytes 2097152 | tf_op jit(solution)/shard_map/all_to_all | solution.py:867
  132.7 1.0 copy-start.1

commit v3 on v0

--- a/solution.py
+++ b/solution.py
@@ -1,11 +1,21 @@
+import functools
+from types import SimpleNamespace
+
 import jax
 import jax.numpy as jnp
 from jax import lax
+from jax.experimental import pallas as pl
+from jax.experimental.pallas import tpu as pltpu
 from jax.sharding import PartitionSpec as P
 
 HD = 128
 M = 256
 PINV_ITERS = 6
+CHUNK = 256
+PACK_GROUPS = 4
+HALF = M // 2
+SWAP = ((0, 1), (1, 0))
+VMEM_LIMIT = 60 * 2**20
 
 
 precise_setting = lax.Precision.HIGHEST
@@ -31,7 +41,7 @@
     return lax.psum(slot_mask[:, None, None] * own_matrix[None], "seq")
 
 
-def body(queries, keys, values, out_grad):
+def shared_body(queries, keys, values, out_grad):
     query_rows, key_rows, value_rows, grad_rows = (
         lax.all_to_all(queries, "head", split_axis=1, concat_axis=0, tiled=True),
         lax.all_to_all(keys, "head", split_axis=1, concat_axis=0, tiled=True),
@@ -225,21 +235,855 @@
     return (attended_out, query_out, key_out, value_out)
 
 
+def halves(matrix):
+    high = matrix.astype(jnp.bfloat16)
+    return high, (matrix - high.astype(jnp.float32)).astype(jnp.bfloat16)
+
+
+def wide_dot(left, right):
+    return jnp.dot(left, right, preferred_element_type=jnp.float32)
+
+
+def wide_dot_nt(left, right):
+    return lax.dot_general(
+        left, right, (((1,), (1,)), ((), ())), preferred_element_type=jnp.float32
+    )
+
+
+def split_dot(left, right):
+    left_high, left_low = left
+    right_high, right_low = right
+    return wide_dot(
+        jnp.concatenate([left_high, left_high, left_low], axis=1),
+        jnp.concatenate([right_high, right_low, right_high], axis=0),
+    )
+
+
+def split_dot_nt(left, right):
+    left_high, left_low = left
+    right_high, right_low = right
+    return wide_dot_nt(
+        jnp.concatenate([left_high, left_high, left_low], axis=1),
+        jnp.concatenate([right_high, right_low, right_high], axis=1),
+    )
+
+
+def identity_matrix():
+    return (
+        lax.broadcasted_iota(jnp.int32, (M, M), 0) == lax.broadcasted_iota(jnp.int32, (M, M), 1)
+    ).astype(jnp.float32)
+
+
+def chunk_of(ref, array, slot, index):
+    rows = ref.shape[3]
+    per = CHUNK // rows
+    return ref[pl.ds(index * per, per), array, slot].reshape(CHUNK, HD)
+
+
+def store_chunk(ref, array, slot, index, value):
+    rows = ref.shape[3]
+    per = CHUNK // rows
+    ref[pl.ds(index * per, per), array, slot] = value.reshape(per, rows, HD)
+
+
+def all_tokens(ref, array, slot):
+    return ref[:, array, slot].reshape(ref.shape[0] * ref.shape[3], HD)
+
+
+def tokens_of(ref):
+    return ref.shape[0] * ref.shape[3]
+
+
+def columns(index):
+    return pl.ds(pl.multiple_of(index * CHUNK, CHUNK), CHUNK)
+
+
+def swap_marks(matrix):
+    return jnp.concatenate([matrix[HALF:], matrix[:HALF]], axis=0)
+
+
+def as_rows(row):
+    return [row[:, :HD], row[:, HD:]]
+
+
+def as_columns(row):
+    return jnp.broadcast_to(row, (HD, M)).T
+
+
+def own_stat(stats, slot, kind):
+    place = 4 * slot + 2 * kind
+    return jnp.concatenate([stats[place : place + 1], stats[place + 1 : place + 2]], axis=1)
+
+
+def other_stat(stats, slot, kind):
+    place = 4 * (1 - slot) + 2 * kind
+    return jnp.concatenate([stats[place + 1 : place + 2], stats[place : place + 1]], axis=1)
+
+
+def key_scales(own_stats, other_stats, slot):
+    own_max, other_max = own_stat(own_stats, slot, 0), other_stat(other_stats, slot, 0)
+    key_max = jnp.maximum(own_max, other_max)
+    own_factor, other_factor = jnp.exp(own_max - key_max), jnp.exp(other_max - key_max)
+    key_total = own_stat(own_stats, slot, 1) * own_factor + (
+        other_stat(other_stats, slot, 1) * other_factor
+    )
+    return own_factor / key_total, other_factor / key_total
+
+
+def staged_kernel(compute, in_names, out_names, *refs):
+    n_in, n_out = len(in_names), len(out_names)
+    sources, homes = refs[:n_in], refs[n_in : n_in + n_out]
+    held_in, held_out = refs[n_in + n_out : 2 * n_in + n_out], refs[2 * n_in + n_out :][:n_out]
+    *extra, in_done, out_done = refs[2 * (n_in + n_out) :]
+    reads = [
+        pltpu.make_async_copy(source, ref, in_done.at[index])
+        for index, (source, ref) in enumerate(zip(sources, held_in))
+    ]
+    writes = [
+        pltpu.make_async_copy(ref, home, out_done.at[index])
+        for index, (ref, home) in enumerate(zip(held_out, homes))
+    ]
+    for read in reads:
+        read.start()
+    arrived, written = [], []
+
+    def place_of(wanted, held):
+        return next(index for index, ref in enumerate(held) if ref is wanted)
+
+    def need(*wanted):
+        places = [place_of(ref, held_in) for ref in wanted] or range(n_in)
+        for place in places:
+            if place not in arrived:
+                reads[place].wait()
+                arrived.append(place)
+
+    def put(ref):
+        place = place_of(ref, held_out)
+        writes[place].start()
+        written.append(place)
+
+    compute(
+        SimpleNamespace(**dict(zip(in_names, held_in))),
+        SimpleNamespace(**dict(zip(out_names, held_out))),
+        need,
+        put,
+        *extra,
+    )
+    need()
+    for place in range(n_out):
+        if place not in written:
+            writes[place].start()
+    for write in writes:
+        write.wait()
+
+
+def staged_call(compute, inputs, outputs, flops, extra=(), after=(), scalar=None):
+    operands = tuple(inputs.values())
+    n_in, n_after = len(operands), len(after)
+    moved = sum(x.size * x.dtype.itemsize for x in (*operands, *outputs.values()))
+    in_place = pl.BlockSpec(memory_space=pl.ANY)
+
+    scalars = () if scalar is None else (scalar,)
+    first = len(scalars)
+
+    def kernel(*refs):
+        staged_kernel(
+            functools.partial(compute, *refs[:first]),
+            tuple(inputs),
+            tuple(outputs),
+            *refs[first : first + n_in],
+            *refs[first + n_in + n_after :],
+        )
+
+    results = pl.pallas_call(
+        kernel,
+        out_shape=tuple(outputs.values()),
+        in_specs=[pl.BlockSpec(memory_space=pltpu.SMEM)] * first + [in_place] * (n_in + n_after),
+        out_specs=(in_place,) * len(outputs),
+        scratch_shapes=[
+            *(pltpu.VMEM(x.shape, x.dtype) for x in (*operands, *outputs.values())),
+            *extra,
+            pltpu.SemaphoreType.DMA((n_in,)),
+            pltpu.SemaphoreType.DMA((len(outputs),)),
+        ],
+        compiler_params=pltpu.CompilerParams(vmem_limit_bytes=VMEM_LIMIT),
+        cost_estimate=pl.CostEstimate(
+            flops=int(flops * 10**9), bytes_accessed=moved, transcendentals=0
+        ),
+    )(*scalars, *operands, *after)
+    return SimpleNamespace(**dict(zip(outputs, results)))
+
+
+def low(*shape):
+    return jax.ShapeDtypeStruct(shape, jnp.bfloat16)
+
+
+def wide(*shape):
+    return jax.ShapeDtypeStruct(shape, jnp.float32)
+
+
+def pack_kernel(half_ref, first_ref, second_ref, out_ref, rows_s, packed_s, in_done, out_done):
+    half = half_ref[0]
+    pairs = out_ref.shape[0]
+    group = pairs // PACK_GROUPS
+    span = 2 * HD
+    reads, writes = [], []
+    for index in range(PACK_GROUPS):
+        for array, ref in enumerate((first_ref, second_ref)):
+            place = pl.ds(index * group * span, group * span)
+            reads.append(
+                pltpu.make_async_copy(
+                    ref.at[:, place], rows_s.at[array, :, place], in_done.at[array, index]
+                )
+            )
+        place = pl.ds(index * group, group)
+        writes.append(
+            pltpu.make_async_copy(packed_s.at[place], out_ref.at[place], out_done.at[index])
+        )
+    for copy in reads:
+        copy.start()
+    for index in range(PACK_GROUPS):
+        for array in range(2):
+            reads[2 * index + array].wait()
+            for pair in range(index * group, (index + 1) * group):
+                start = pair * span
+                packed_s[pair, array, half] = rows_s[array, :, start : start + HD]
+                packed_s[pair, array, 1 - half] = rows_s[array, :, start + HD : start + span]
+        writes[index].start()
+    for copy in writes:
+        copy.wait()
+
+
+def unpack_kernel(half_ref, packed_ref, *refs):
+    half = half_ref[0]
+    pairs, arrays = packed_ref.shape[:2]
+    homes, (packed_s, rows_s, in_done, out_done) = refs[:arrays], refs[arrays:]
+    group = pairs // PACK_GROUPS
+    span = 2 * HD
+    reads, writes = [], []
+    for index in range(PACK_GROUPS):
+        place = pl.ds(index * group, group)
+        reads.append(
+            pltpu.make_async_copy(packed_ref.at[place], packed_s.at[place], in_done.at[index])
+        )
+        for array, ref in enumerate(homes):
+            place = pl.ds(index * group * span, group * span)
+            writes.append(
+                pltpu.make_async_copy(
+                    rows_s.at[array, :, place], ref.at[:, place], out_done.at[array, index]
+                )
+            )
+    for copy in reads:
+        copy.start()
+    for index in range(PACK_GROUPS):
+        reads[index].wait()
+        for array in range(arrays):
+            for pair in range(index * group, (index + 1) * group):
+                start = pair * span
+                rows_s[array, :, start : start + HD] = packed_s[pair, array, half]
+                rows_s[array, :, start + HD : start + span] = packed_s[pair, array, 1 - half]
+            writes[arrays * index + array].start()
+    for copy in writes:
+        copy.wait()
+
+
+def landmark_kernel(first_ref, second_ref, out_ref, rows_s, packed_s, in_done, out_done, segment_len):
+    pairs = out_ref.shape[0] // 2
+    rows = first_ref.shape[0]
+    span = 2 * HD
+    reads = [
+        pltpu.make_async_copy(ref, rows_s.at[array], in_done.at[array])
+        for array, ref in enumerate((first_ref, second_ref))
+    ]
+    for copy in reads:
+        copy.start()
+    count = rows // segment_len
+    member = (
+        lax.broadcasted_iota(jnp.int32, (count, rows), 1) // segment_len
+        == lax.broadcasted_iota(jnp.int32, (count, rows), 0)
+    ).astype(jnp.bfloat16)
+    for copy in reads:
+        copy.wait()
+    group = pairs // PACK_GROUPS
+    for index in range(PACK_GROUPS):
+        place = slice(index * group * span, (index + 1) * group * span)
+        means = [wide_dot(member, rows_s[array, :, place]) / segment_len for array in range(2)]
+        both = jnp.concatenate(means, axis=0).astype(jnp.bfloat16)
+        for pair in range(group):
+            for head in range(2):
+                start = pair * span + head * HD
+                packed_s[index * group + pair, head] = both[:, start : start + HD]
+    writes = [
+        pltpu.make_async_copy(packed_s, out_ref.at[pl.ds(side * pairs, pairs)], out_done.at[side])
+        for side in range(2)
+    ]
+    for copy in writes:
+        copy.start()
+    for copy in writes:
+        copy.wait()
+
+
+def layout_call(kernel, scalars, operands, out_shape, scratch):
+    in_place = pl.BlockSpec(memory_space=pl.ANY)
+    moved = 2 * sum(x.size * x.dtype.itemsize for x in operands)
+    return pl.pallas_call(
+        kernel,
+        out_shape=out_shape,
+        in_specs=[pl.BlockSpec(memory_space=pltpu.SMEM)] * len(scalars)
+        + [in_place] * len(operands),
+        out_specs=jax.tree.map(lambda _: in_place, out_shape),
+        scratch_shapes=scratch,
+        compiler_params=pltpu.CompilerParams(vmem_limit_bytes=VMEM_LIMIT),
+        cost_estimate=pl.CostEstimate(flops=0, bytes_accessed=moved, transcendentals=0),
+    )(*scalars, *operands)
+
+
+def pack(half, first, second):
+    rows, width = first.shape
+    shape = low(width // (2 * HD), 2, 2, rows, HD)
+    scratch = [
+        pltpu.VMEM((2, rows, width), jnp.bfloat16),
+        pltpu.VMEM(shape.shape, jnp.bfloat16),
+        pltpu.SemaphoreType.DMA((2, PACK_GROUPS)),
+        pltpu.SemaphoreType.DMA((PACK_GROUPS,)),
+    ]
+    return layout_call(pack_kernel, (half,), (first, second), shape, scratch)
+
+
+def unpack(half, packed):
+    pairs, arrays, _, rows, _ = packed.shape
+    shape = low(rows, pairs * 2 * HD)
+    scratch = [
+        pltpu.VMEM(packed.shape, jnp.bfloat16),
+        pltpu.VMEM((arrays, *shape.shape), jnp.bfloat16),
+        pltpu.SemaphoreType.DMA((PACK_GROUPS,)),
+        pltpu.SemaphoreType.DMA((arrays, PACK_GROUPS)),
+    ]
+    return layout_call(unpack_kernel, (half,), (packed,), (shape,) * arrays, scratch)
+
+
+def local_landmarks(first, second, segment_len):
+    rows, width = first.shape
+    pairs = width // (2 * HD)
+    shape = low(2 * pairs, 2, 2 * rows // segment_len, HD)
+    scratch = [
+        pltpu.VMEM((2, rows, width), jnp.bfloat16),
+        pltpu.VMEM((pairs, *shape.shape[1:]), jnp.bfloat16),
+        pltpu.SemaphoreType.DMA((2,)),
+        pltpu.SemaphoreType.DMA((2,)),
+    ]
+    kernel = functools.partial(landmark_kernel, segment_len=segment_len)
+    return layout_call(kernel, (), (first, second), shape, scratch)
+
+
+def inverse_compute(half_ref, ins, outs, need, put, power_s, iterate_s):
+    need()
+    half = half_ref[0]
+    score_scale = HD ** (-0.5)
+    sources = ins.gathered.shape[0] // 2
+    count = ins.gathered.shape[2] // 2
+    for slot, head in ((0, half), (1, 1 - half)):
+        sides = [
+            ins.gathered[pl.ds(side * sources, sources), head].astype(jnp.float32)
+            for side in (half, 1 - half)
+        ]
+        for array in range(2):
+            parts = [
+                side[:, array * count : (array + 1) * count].reshape(HALF, HD) for side in sides
+            ]
+            outs.marks[slot, array] = jnp.concatenate(parts, axis=0).astype(jnp.bfloat16)
+    put(outs.marks)
+    landmark_q, landmark_k = outs.marks[0, 0], outs.marks[0, 1]
+    mark_score = wide_dot_nt(landmark_q, landmark_k) * score_scale
+    mark_exp = jnp.exp(mark_score - jnp.max(mark_score, axis=1, keepdims=True))
+    mark_prob = mark_exp / jnp.sum(mark_exp, axis=1, keepdims=True)
+    outs.mark_prob[...] = mark_prob
+    factor = 1.0 / jnp.max(jnp.sum(mark_prob, axis=0, keepdims=True), axis=1, keepdims=True)
+    outs.factor[...] = jnp.broadcast_to(factor, outs.factor.shape)
+    mark_halves = halves(mark_prob)
+    power_s[...] = split_dot_nt(mark_halves, mark_halves) * factor
+    iterate_s[0:M] = mark_prob.T * factor
+    iterate_s[M:] = identity_matrix()
+
+    def newton(pair_ref, weight_ref, growth_ref, sweep, carry):
+        power = power_s[...]
+        power_high, power_low = halves(power)
+        square = split_dot((power_high, power_low), (power_high, power_low))
+        square_halves = halves(square)
+        pair = (
+            jnp.concatenate([power_high, square_halves[0]], axis=0),
+            jnp.concatenate([power_low, square_halves[1]], axis=0),
+        )
+        pair_ref[sweep, 0], pair_ref[sweep, 1] = pair
+        higher = split_dot(pair, square_halves)
+        cube, fourth = higher[:M], higher[M:]
+        weight = halves(
+            0.25 * (13.0 * identity_matrix() - 15.0 * power + 7.0 * square - cube)
+        )
+        power_s[...] = 0.25 * (13.0 * power - 15.0 * square + 7.0 * cube - fourth)
+        weight_ref[sweep, 0], weight_ref[sweep, 1] = weight
+        iterate = halves(iterate_s[...])
+        growth_ref[sweep, 0], growth_ref[sweep, 1] = iterate[0][M:], iterate[1][M:]
+        iterate_s[...] = split_dot(iterate, weight)
+        return carry
+
+    for saved in ((outs.pair_a, outs.weight_a, outs.growth_a), (outs.pair_b, outs.weight_b, outs.growth_b)):
+        lax.fori_loop(0, PINV_ITERS // 2, functools.partial(newton, *saved), 0)
+        for ref in saved:
+            put(ref)
+    inverse = iterate_s[0:M]
+    outs.inverse[0], outs.inverse[1] = halves(inverse)
+    outs.inverse_turned[0], outs.inverse_turned[1] = halves(inverse.T)
+    outs.last_growth[0], outs.last_growth[1] = halves(iterate_s[M:])
+
+
+def key_probability_compute(ins, outs, need, put, low_s):
+    need()
+    kv_ref, key_exp_ref = ins.kv, outs.key_exp
+    chunks = tokens_of(kv_ref) // CHUNK
+    score_scale = HD ** (-0.5)
+    stats = []
+    for slot in (1, 0):
+        landmark_q = ins.marks[slot, 0]
+
+        def scores(index, key_max):
+            key_chunk = chunk_of(kv_ref, 0, slot, index)
+            place = columns(index)
+            outs.turned[slot, :, place] = key_chunk.T
+            key_score = wide_dot_nt(key_chunk, landmark_q) * score_scale
+            key_exp_ref[slot, place] = key_score
+            return jnp.maximum(key_max, jnp.max(key_score, axis=0, keepdims=True))
+
+        key_max = lax.fori_loop(0, chunks, scores, jnp.full((1, M), -jnp.inf, jnp.float32))
+
+        def grow(index, key_total):
+            place = columns(index)
+            grown = jnp.exp(key_exp_ref[slot, place] - key_max)
+            key_exp_ref[slot, place] = grown
+            low_s[:, place] = grown.astype(jnp.bfloat16).T
+            return key_total + jnp.sum(grown, axis=0, keepdims=True)
+
+        key_total = lax.fori_loop(0, chunks, grow, jnp.zeros((1, M), jnp.float32))
+        stats = as_rows(key_max) + as_rows(key_total) + stats
+        home = outs.send if slot == 1 else outs.keep
+        home[0:M] = wide_dot(low_s[...], all_tokens(kv_ref, 1, slot))
+    outs.stats[...] = jnp.concatenate(stats, axis=0)
+    outs.send[M:] = jnp.concatenate(stats, axis=0)
+
+
+def mixing_compute(ins, outs, need, put):
+    need()
+    own_scale, other_scale = key_scales(ins.stats[...], ins.got[M:], 0)
+    landmark_values = ins.keep[...] * as_columns(own_scale) + (
+        swap_marks(ins.got[0:M]) * as_columns(other_scale)
+    )
+    outs.share[...] = split_dot(
+        (ins.inverse[0], ins.inverse[1]), halves(landmark_values)
+    ).astype(jnp.bfloat16)
+    outs.mark_values[...] = landmark_values
+
+
+def token_probability_compute(ins, outs, need, put, low_s):
+    need()
+    qg_ref = ins.qg
+    chunks = tokens_of(qg_ref) // CHUNK
+    score_scale = HD ** (-0.5)
+    for slot in (1, 0):
+        landmark_k = ins.marks[slot, 1]
+
+        def one_chunk(index, carry):
+            query_chunk = chunk_of(qg_ref, 0, slot, index)
+            place = columns(index)
+            outs.turned[slot, :, place] = query_chunk.T
+            score = wide_dot_nt(query_chunk, landmark_k) * score_scale
+            grown = jnp.exp(score - jnp.max(score, axis=1, keepdims=True))
+            prob = grown / jnp.sum(grown, axis=1, keepdims=True)
+            outs.token_prob[slot, place] = prob
+            low_s[:, place] = prob.astype(jnp.bfloat16).T
+            return carry
+
+        lax.fori_loop(0, chunks, one_chunk, 0)
+        home = outs.send if slot == 1 else outs.keep
+        home[...] = wide_dot(low_s[...], all_tokens(qg_ref, 1, slot))
+        put(home)
+
+
+def values_compute(ins, outs, need, put):
+    need()
+    mixing_grad = ins.keep[...] + swap_marks(ins.got[...])
+    values_low = split_dot(
+        (ins.inverse_turned[0], ins.inverse_turned[1]), halves(mixing_grad)
+    ).astype(jnp.bfloat16)
+    outs.share[0:M] = values_low
+    product = (values_low.astype(jnp.float32) * ins.mark_values[...]).T
+    row_total = jnp.sum(product, axis=0, keepdims=True)
+    first = row_total.astype(jnp.bfloat16).astype(jnp.float32)
+    second = (row_total - first).astype(jnp.bfloat16).astype(jnp.float32)
+    third = row_total - first - second
+    rows = as_rows(first) + as_rows(second) + as_rows(third)
+    rows.append(jnp.zeros((10, HD), jnp.float32))
+    outs.share[M:] = jnp.concatenate(rows, axis=0).astype(jnp.bfloat16)
+    outs.mixing_grad[...] = mixing_grad
+
+
+def newton_gradient_sweeps(power, growth, pair_ref, weight_ref, growth_ref):
+    for sweep in range(PINV_ITERS // 2):
+        pair = (pair_ref[sweep, 0], pair_ref[sweep, 1])
+        first = split_dot(pair, halves(power))
+        square = first[:M] + first[:M].T
+        second = split_dot(pair, halves(square))
+        cube = first[M:].T + second[:M]
+        fourth = second[M:] + second[M:].T
+        weight = halves(0.25 * (7.0 * square - 15.0 * power - cube))
+        power = 0.25 * (13.0 * power - 15.0 * square + 7.0 * cube - fourth)
+        held = (growth_ref[sweep, 0], growth_ref[sweep, 1])
+        held_weight = (weight_ref[sweep, 0], weight_ref[sweep, 1])
+        left, right = [held[0], held[0], held[1]], [weight[0], weight[1], weight[0]]
+        if growth is not None:
+            grown_high, grown_low = halves(growth)
+            left += [grown_high, grown_high, grown_low]
+            right += [held_weight[0], held_weight[1], held_weight[0]]
+        growth = wide_dot(jnp.concatenate(left, axis=1), jnp.concatenate(right, axis=0))
+    return power, growth
+
+
+def first_gradient_compute(ins, outs, need, put):
+    need(ins.mark_prob, ins.factor, ins.mixing_grad, ins.mark_values)
+    factor = ins.factor[0:1, 0:1]
+    inverse_grad = split_dot_nt(halves(ins.mixing_grad[...]), halves(ins.mark_values[...]))
+    inverse_grad_halves = halves(inverse_grad)
+    outs.inverse_grad[0], outs.inverse_grad[1] = inverse_grad_halves
+    toward = split_dot(halves(ins.mark_prob[...]), inverse_grad_halves) * factor
+    need()
+    outs.state[0], outs.state[1] = newton_gradient_sweeps(
+        0.5 * (toward + toward.T), None, ins.pair, ins.weight, ins.growth
+    )
+
+
+def second_gradient_compute(ins, outs, need, put):
+    need()
+    _, growth = newton_gradient_sweeps(
+        ins.state[0], ins.state[1], ins.pair, ins.weight, ins.growth
+    )
+    mark_prob = ins.mark_prob[...]
+    mark_grad = ins.factor[0:1, 0:1] * (
+        split_dot_nt(
+            (ins.last_growth[0], ins.last_growth[1]), (ins.inverse_grad[0], ins.inverse_grad[1])
+        )
+        + split_dot(halves(growth + growth.T), halves(mark_prob))
+    )
+    mark_sgrad = mark_prob * (mark_grad - jnp.sum(mark_grad * mark_prob, axis=1, keepdims=True))
+
+    def marks_dot(left, right):
+        left_high, left_low = halves(left)
+        return wide_dot(
+            jnp.concatenate([left_high, left_low], axis=1), jnp.concatenate([right, right], axis=0)
+        )
+
+    totals = (
+        (ins.query_marks, marks_dot(mark_sgrad, ins.marks[0, 1])),
+        (ins.key_marks, marks_dot(mark_sgrad.T, ins.marks[0, 0])),
+    )
+    for kind, (sums_ref, own) in enumerate(totals):
+        for slot in range(2):
+            total = sums_ref[slot].T
+            if slot == 0:
+                total = total + own
+            total = total * ins.scale[0:1, 0:1]
+            outs.far[kind, slot] = total[HALF:].astype(jnp.bfloat16)
+            outs.near[kind, slot] = total[:HALF]
+    put(outs.far)
+
+
+def shared(own_ref, other_ref, slot):
+    if slot == 0:
+        return own_ref[0:M]
+    return swap_marks(other_ref[0:M])
+
+
+def token_gradient_compute(ins, outs, need, put):
+    need()
+    chunks = tokens_of(ins.qg) // CHUNK
+    score_scale = HD ** (-0.5)
+    for slot in range(2):
+        mixing_low = shared(ins.share, ins.got_share, slot)
+        landmark_k = ins.marks[slot, 1]
+
+        def one_chunk(index, total):
+            place = columns(index)
+            prob = ins.token_prob[slot, place]
+            attended = wide_dot(prob.astype(jnp.bfloat16), mixing_low)
+            store_chunk(outs.out, 0, slot, index, attended.astype(jnp.bfloat16))
+            token_grad = wide_dot_nt(chunk_of(ins.qg, 1, slot, index), mixing_low)
+            token_sgrad = (
+                prob * (token_grad - jnp.sum(token_grad * prob, axis=1, keepdims=True))
+            ).astype(jnp.bfloat16)
+            outs.direct[slot, place] = wide_dot(token_sgrad, landmark_k) * score_scale
+            return total + wide_dot(ins.turned[slot, :, place], token_sgrad)
+
+        zeros = jnp.zeros((HD, M), jnp.float32)
+        outs.marks_sum[slot] = lax.fori_loop(0, chunks, one_chunk, zeros)
+
+
+def key_gradient_compute(ins, outs, need, put):
+    need()
+    chunks = tokens_of(ins.kv) // CHUNK
+    score_scale = HD ** (-0.5)
+    for slot in range(2):
+        scale, _ = key_scales(ins.stats[...], ins.got[M:], slot)
+        values_low = shared(ins.share, ins.got_share, slot)
+        landmark_q = ins.marks[slot, 0]
+        tail = (ins.share if slot == 0 else ins.got_share)[M:].astype(jnp.float32)
+        rows = [tail[place : place + 1] for place in range(6)]
+        near = rows[0] + (rows[2] + rows[4])
+        far = rows[1] + (rows[3] + rows[5])
+        row_total = jnp.concatenate([near, far] if slot == 0 else [far, near], axis=1)
+
+        def one_chunk(index, total):
+            place = columns(index)
+            key_prob = ins.key_exp[slot, place] * scale
+            value_gradient = wide_dot(key_prob.astype(jnp.bfloat16), values_low)
+            store_chunk(outs.out, 0, slot, index, value_gradient.astype(jnp.bfloat16))
+            key_dgrad = wide_dot_nt(chunk_of(ins.kv, 1, slot, index), values_low)
+            key_sgrad = (key_prob * (key_dgrad - row_total)).astype(jnp.bfloat16)
+            outs.direct[slot, place] = wide_dot(key_sgrad, landmark_q) * score_scale
+            return total + wide_dot(ins.turned[slot, :, place], key_sgrad)
+
+        zeros = jnp.zeros((HD, M), jnp.float32)
+        outs.marks_sum[slot] = lax.fori_loop(0, chunks, one_chunk, zeros)
+
+
+def finish_compute(ins, outs, need, put):
+    need()
+    out_ref = outs.out
+    segment_len = tokens_of(out_ref) // HALF
+    directs = (ins.query_direct, ins.key_direct)
+    per = CHUNK // segment_len
+    for kind in range(2):
+        for slot in range(2):
+            for index in range(tokens_of(out_ref) // CHUNK):
+                place = slice(index * per, (index + 1) * per)
+                marks = ins.near[kind, slot, place] + ins.got_far[
+                    kind, 1 - slot, place
+                ].astype(jnp.float32)
+                spread = jnp.broadcast_to(marks[:, None], (per, segment_len, HD))
+                direct = directs[kind][slot, index * CHUNK : (index + 1) * CHUNK]
+                store_chunk(
+                    out_ref,
+                    kind,
+                    slot,
+                    index,
+                    (direct + spread.reshape(CHUNK, HD)).astype(jnp.bfloat16),
+                )
+
+
+def exchange(packed):
+    return lax.all_to_all(packed, "cube", split_axis=0, concat_axis=0, tiled=True)
+
+
+def partner(array):
+    return lax.ppermute(array, "half", SWAP)
+
+
+def spread_landmarks(queries, keys):
+    segment_len = queries.shape[0] * lax.axis_size("seq") * lax.axis_size("head") // M
+    return lax.all_to_all(
+        local_landmarks(queries, keys, segment_len),
+        ("seq", "head"),
+        split_axis=0,
+        concat_axis=0,
+        tiled=True,
+    )
+
+
+def body(gathered, queries, keys, values, out_grad):
+    half = lax.axis_index("half").reshape(1)
+    rows = queries.shape[0]
+    devices = lax.axis_size("half") * lax.axis_size("cube")
+    segment_len = rows * devices // M
+    tokens = rows * devices // 2
+    kv = exchange(pack(half, keys, values))
+    qg = exchange(pack(half, queries, out_grad))
+    square = pltpu.VMEM((M, M), jnp.float32)
+    turned_s = pltpu.VMEM((M, tokens), jnp.bfloat16)
+    sweeps = PINV_ITERS // 2
+    one_array = low(qg.shape[0], 1, *qg.shape[2:])
+
+    newton = staged_call(
+        inverse_compute,
+        dict(gathered=gathered),
+        dict(
+            marks=low(2, 2, M, HD),
+            mark_prob=wide(M, M),
+            factor=wide(8, HD),
+            pair_a=low(sweeps, 2, 2 * M, M),
+            weight_a=low(sweeps, 2, M, M),
+            growth_a=low(sweeps, 2, M, M),
+            pair_b=low(sweeps, 2, 2 * M, M),
+            weight_b=low(sweeps, 2, M, M),
+            growth_b=low(sweeps, 2, M, M),
+            inverse=low(2, M, M),
+            inverse_turned=low(2, M, M),
+            last_growth=low(2, M, M),
+        ),
+        8,
+        extra=(square, pltpu.VMEM((2 * M, M), jnp.float32)),
+        scalar=half,
+    )
+    marks = newton.marks
+    key_side = staged_call(
+        key_probability_compute,
+        dict(kv=kv, marks=marks),
+        dict(
+            send=wide(M + 8, HD),
+            keep=wide(M, HD),
+            stats=wide(8, HD),
+            key_exp=wide(2, tokens, M),
+            turned=low(2, HD, tokens),
+        ),
+        4,
+        extra=(turned_s,),
+    )
+    got = partner(key_side.send)
+    mixed = staged_call(
+        mixing_compute,
+        dict(got=got, keep=key_side.keep, stats=key_side.stats, inverse=newton.inverse),
+        dict(share=low(M, HD), mark_values=wide(M, HD)),
+        0.2,
+    )
+    got_mixing = partner(mixed.share)
+    token_side = staged_call(
+        token_probability_compute,
+        dict(qg=qg, marks=marks),
+        dict(
+            send=wide(M, HD),
+            keep=wide(M, HD),
+            token_prob=wide(2, tokens, M),
+            turned=low(2, HD, tokens),
+        ),
+        4,
+        extra=(turned_s,),
+        after=(mixed.share,),
+    )
+    got_grad = partner(token_side.send)
+    token_grads = staged_call(
+        token_gradient_compute,
+        dict(
+            qg=qg,
+            marks=marks,
+            token_prob=token_side.token_prob,
+            turned=token_side.turned,
+            share=mixed.share,
+            got_share=got_mixing,
+        ),
+        dict(out=one_array, direct=wide(2, tokens, HD), marks_sum=wide(2, HD, M)),
+        4,
+    )
+    (attended,) = unpack(half, exchange(token_grads.out))
+    lowered = staged_call(
+        values_compute,
+        dict(
+            got=got_grad,
+            keep=token_side.keep,
+            inverse_turned=newton.inverse_turned,
+            mark_values=mixed.mark_values,
+        ),
+        dict(share=low(M + 16, HD), mixing_grad=wide(M, HD)),
+        0.2,
+        after=(token_grads.marks_sum,),
+    )
+    got_values = partner(lowered.share)
+    first = staged_call(
+        first_gradient_compute,
+        dict(
+            mark_prob=newton.mark_prob,
+            factor=newton.factor,
+            mixing_grad=lowered.mixing_grad,
+            mark_values=mixed.mark_values,
+            pair=newton.pair_a,
+            weight=newton.weight_a,
+            growth=newton.growth_a,
+        ),
+        dict(state=wide(2, M, M), inverse_grad=low(2, M, M)),
+        6,
+    )
+    key_grads = staged_call(
+        key_gradient_compute,
+        dict(
+            kv=kv,
+            marks=marks,
+            key_exp=key_side.key_exp,
+            turned=key_side.turned,
+            stats=key_side.stats,
+            got=got,
+            share=lowered.share,
+            got_share=got_values,
+        ),
+        dict(out=one_array, direct=wide(2, tokens, HD), marks_sum=wide(2, HD, M)),
+        4,
+        after=(first.state,),
+    )
+    (value_gradient_array,) = unpack(half, exchange(key_grads.out))
+    second = staged_call(
+        second_gradient_compute,
+        dict(
+            state=first.state,
+            inverse_grad=first.inverse_grad,
+            mark_prob=newton.mark_prob,
+            factor=newton.factor,
+            pair=newton.pair_b,
+            weight=newton.weight_b,
+            growth=newton.growth_b,
+            last_growth=newton.last_growth,
+            marks=marks,
+            query_marks=key_grads.marks_sum,
+            key_marks=token_grads.marks_sum,
+            scale=jnp.full((8, HD), HD ** (-0.5) / segment_len, jnp.float32),
+        ),
+        dict(far=low(2, 2, HALF, HD), near=wide(2, 2, HALF, HD)),
+        6,
+    )
+    results = staged_call(
+        finish_compute,
+        dict(
+            got_far=partner(second.far),
+            near=second.near,
+            query_direct=token_grads.direct,
+            key_direct=key_grads.direct,
+        ),
+        dict(out=low(*qg.shape)),
+        0.5,
+    ).out
+    query_grad, key_grad = unpack(half, exchange(results))
+    return attended, query_grad, key_grad, value_gradient_array
+
+
 def solution(mesh):
-    return jax.shard_map(
-        body,
-        mesh=mesh,
-        in_specs=(
-            P(("seq", "head"), None),
-            P(("seq", "head"), None),
-            P(("seq", "head"), None),
-            P(("seq", "head"), None),
-        ),
-        out_specs=(
-            P(("seq", "head"), None),
-            P(("seq", "head"), None),
-            P(("seq", "head"), None),
-            P(("seq", "head"), None),
-        ),
-        check_vma=False,
-    )
+    whole = P(("seq", "head"), None)
+    blocks = P(("seq", "head"))
+    halved = P(("half", "cube"), None)
+
+    def layer(queries, keys, values, out_grad):
+        arrays = (queries, keys, values, out_grad)
+        tokens, width = queries.shape
+        if width // HD != mesh.size or tokens % (2 * CHUNK):
+            return jax.shard_map(
+                shared_body,
+                mesh=mesh,
+                in_specs=(whole,) * 4,
+                out_specs=(whole,) * 4,
+                check_vma=False,
+            )(*arrays)
+        gathered = jax.shard_map(
+            spread_landmarks, mesh=mesh, in_specs=(whole,) * 2, out_specs=blocks, check_vma=False
+        )(queries, keys)
+        split = jax.sharding.Mesh(mesh.devices.reshape(2, mesh.size // 2), ("half", "cube"))
+        return jax.shard_map(
+            body,
+            mesh=split,
+            in_specs=(P(("half", "cube")), *(halved,) * 4),
+            out_specs=(halved,) * 4,
+            check_vma=False,
+        )(gathered, *arrays)
+
+    return layer

time: 759 us -> 164 us (0.22)
  waiting for transfers between devices: 329 us -> 49.9 us
  blocking collectives: 201 us -> 0 us
  matrix products: 103 us -> 0 us
  Pallas kernels: 0 us -> 71.3 us
  local copies, waits for them, and re-layouts: 53.3 us -> 5.78 us
  other arithmetic: 26 us -> 0 us
  between operations: 16.5 us -> 1.09 us
  starting transfers between devices: 23.6 us -> 34.7 us
    psum x2 -> x0, waiting for transfers between devices: 210 us -> none  [the longest x1 169 us: share_heads(): return lax.psum(slot_mask[:, None, None] * own_matrix[None], 'seq')]
    psum x2 -> x0, blocking collectives: 119 us -> none  [the longest x1 60.2 us: body(): lax.psum(jnp.sum(key_prob * key_direct_gradient, axis=-1), 'seq')]
    dot_general x89 -> x0, matrix products: 99.8 us -> none  [the longest x18 10.8 us: newton_inverse(): product = jnp.matmul(matrix, iterate, precision=precise_setting)]
    pallas_call x0 -> x16, Pallas kernels: none -> 71.3 us  [the longest x10 59.1 us: staged_call(): pl.pallas_call(kernel, out_shape=tuple(outputs.values()), in_specs=[pl.Bl...]
    pmax x1 -> x0, blocking collectives: 59.9 us -> none  [body(): key_max = lax.pmax(jnp.max(key_score, axis=-1), 'seq')]
    reduce_scatter x2 -> x0, waiting for transfers between devices: 57.6 us -> none  [the longest x1 57.6 us: body(): lax.psum_scatter(mark_kgrad_f, 'seq', scatter_dimension=0, tiled=True)]
    all_gather x2 -> x0, waiting for transfers between devices: 40 us -> none  [the longest x1 34 us: body(): lax.all_gather(landmark(query_rows), 'seq', axis=0, tiled=True)]
    all_to_all x2 -> x0, blocking collectives: 21.6 us -> none  [the longest x1 12 us: body(): lax.all_to_all(keys, 'head', split_axis=1, concat_axis=0, tiled=True)]
  transfers between devices with their start and end apart: 12 -> 11, of which waited for: 10 -> 5; matrix products, arithmetic and copies ran while one was open for 11% -> 0% of each run, Pallas kernels for 0% -> 41%
where the time goes in v3:
time: 164 us; the launch traced here: 163 us
  Pallas kernels  71.3 us (43%)
  waiting for transfers between devices  49.9 us (30%)
  starting transfers between devices  34.7 us (21%)
  local copies, waits for them, and re-layouts  5.78 us (4%)
    pallas_call x10, Pallas kernels, staged_call(): pl.pallas_call(kernel, out_shape=tuple(outputs.values()), in_specs=[pl.Bl...  59.1 us
    all_to_all x5, waiting for transfers between devices, exchange(): lax.all_to_all(packed, 'cube', split_axis=0, concat_axis=0, tiled=True)  23.7 us
    all_to_all x5, starting transfers between devices, exchange(): lax.all_to_all(packed, 'cube', split_axis=0, concat_axis=0, tiled=True)  20.3 us
    ppermute x5, waiting for transfers between devices, partner(): return lax.ppermute(array, 'half', SWAP)  17.6 us
    pallas_call x6, Pallas kernels, layout_call(): pl.pallas_call(kernel, out_shape=out_shape, in_specs=[pl.BlockSpec(memory...  12.2 us
    all_to_all x1, waiting for transfers between devices, spread_landmarks(): lax.all_to_all(local_landmarks(queries, keys, segment_len), ('seq', 'head...  8.54 us
    all_to_all x1, starting transfers between devices, spread_landmarks(): lax.all_to_all(local_landmarks(queries, keys, segment_len), ('seq', 'head...  7.3 us
    ppermute x5, starting transfers between devices, partner(): return lax.ppermute(array, 'half', SWAP)  7.13 us
  transfers between devices with their start and end apart: 11, of which 5 were waited for; matrix products, arithmetic and copies ran while one was open for 0% of the time, Pallas kernels for 41%

profile of v3, /device:TPU:0, one launch (start us, length us, event | category | flops | bytes accessed | tf_op | source)
XLA Modules:
  0.0 162.8 jit_solution(2260211771317428718)
XLA Ops:
  0.6 2.2 %shard_map.112 = bf16[32,2,16,128]{3,2,1,0:T(8,128)(2,1)} custom-call(bf16[64,4096]{1,0:T(8,128)(2,1)} %first_ref.4, bf16[64,4096]{1,0:T(8,128)(2,1)} %first_ref.5), custom_call_target="tpu_custom_call" | custom-call | bytes 2097152 | tf_op jit(solution)/shard_map/pallas_call | solution.py:529
  2.8 7.3 %all-to-all-start = ((bf16[32,2,16,128]{3,2,1,0:T(8,128)(2,1)}), bf16[32,2,16,128]{3,2,1,0:T(8,128)(2,1)S(1)}, u32[]{:S(2)}, u32[]{:S(2)}) async-start(bf16[32,2,16,128]{3,2,1,0:T(8,128)(2,1)} %shard_map.112), calls=%async_computation | async-start | bytes 524288 | tf_op jit(solution)/shard_map/all_to_all | solution.py:890
  10.1 2.1 %shard_map.115 = bf16[16,2,2,64,128]{4,3,2,1,0:T(8,128)(2,1)} custom-call(s32[1]{0:T(128)} %bitcast.half_ref.refs_0_, bf16[64,4096]{1,0:T(8,128)(2,1)} %first_ref.5, bf16[64,4096]{1,0:T(8,128)(2,1)} %second_ref.5), custom_call_target="tpu_custom_call" | custom-call | bytes 2097152 | tf_op jit(solution)/shard_map/pallas_call | solution.py:529
  12.3 8.5 %all-to-all-done.refs_1_ = bf16[32,2,16,128]{3,2,1,0:T(8,128)(2,1)S(1)} async-done(((bf16[32,2,16,128]{3,2,1,0:T(8,128)(2,1)}), bf16[32,2,16,128]{3,2,1,0:T(8,128)(2,1)S(1)}, u32[]{:S(2)}, u32[]{:S(2)}) %all-to-all-start) | async-done | bytes 262176 | tf_op jit(solution)/shard_map/all_to_all | solution.py:890
  20.8 3.7 %all-to-all-start.2 = ((bf16[16,2,2,64,128]{4,3,2,1,0:T(8,128)(2,1)}), bf16[16,2,2,64,128]{4,3,2,1,0:T(8,128)(2,1)S(1)}, u32[]{:S(2)}, u32[]{:S(2)}) async-start(bf16[16,2,2,64,128]{4,3,2,1,0:T(8,128)(2,1)} %shard_map.115), calls=%async_computation.2 | async-start | bytes 2097152 | tf_op jit(solution)/shard_map/all_to_all | solution.py:881
  26.6 12.6 %all-to-all-done.2.refs_0_ = bf16[16,2,2,64,128]{4,3,2,1,0:T(8,128)(2,1)S(1)} async-done(((bf16[16,2,2,64,128]{4,3,2,1,0:T(8,128)(2,1)}), bf16[16,2,2,64,128]{4,3,2,1,0:T(8,128)(2,1)S(1)}, u32[]{:S(2)}, u32[]{:S(2)}) %all-to-all-start.2) | async-done | bytes 1048608 | tf_op jit(solution)/shard_map/all_to_all | solution.py:881
  39.3 3.7 %all-to-all-start.1 = ((bf16[16,2,2,64,128]{4,3,2,1,0:T(8,128)(2,1)}), bf16[16,2,2,64,128]{4,3,2,1,0:T(8,128)(2,1)S(1)}, u32[]{:S(2)}, u32[]{:S(2)}) async-start(bf16[16,2,2,64,128]{4,3,2,1,0:T(8,128)(2,1)} %shard_map.113), calls=%async_computation.1 | async-start | bytes 2097152 | tf_op jit(solution)/shard_map/all_to_all | solution.py:881
  42.9 10.5 %shard_map.114 = (bf16[2,2,256,128]{3,2,1,0:T(8,128)(2,1)}, f32[256,256]{1,0:T(8,128)}, f32[8,128]{1,0:T(8,128)}, bf16[3,2,512,256]{3,2,1,0:T(8,128)(2,1)}, bf16...) custom-call(s32[1]{0:T(128)} %bitcast.half_ref.refs_0_, ...), custom_call_target="tpu_custom_call" | custom-call | flops 8000000000 | bytes 7868416 | tf_op jit(solution)/shard_map/pallas_call | solution.py:398
  53.5 5.8 %shard_map.116 = (f32[264,128]{1,0:T(8,128)}, f32[256,128]{1,0:T(8,128)}, f32[8,128]{1,0:T(8,128)}, f32[2,1024,256]{2,1,0:T(8,128)}, bf16[2,128,1024]{2,1,0:T(8,128)(2,1)}) custom-call(bf16[16,2,2,64,128]{4,3,2,1,0:T(8,128)(2,1)} %copy-done.3, bf16[2,2,256,128]{3,2,1,0:T(8,128)(2,1)} %get-tuple-element.42.refs_1_.refs_8_), custom_call_target="tpu_custom_call" | custom-call | flops 4000000000 | bytes 4202496 | tf_op jit(solution)/shard_map/pallas_call | solution.py:398
  60.3 9.0 %collective-permute-done.refs_0_.refs_5_ = f32[264,128]{1,0:T(8,128)S(1)} collective-permute-done((f32[264,128]{1,0:T(8,128)}, f32[264,128]{1,0:T(8,128)S(1)}, u32[]{:S(2)}, u32[]{:S(2)}) %collective-permute-start) | collective-permute-done | bytes 135200 | tf_op jit(solution)/shard_map/ppermute | solution.py:885
  70.0 2.2 %shard_map.117 = (bf16[256,128]{1,0:T(8,128)(2,1)}, f32[256,128]{1,0:T(8,128)}) custom-call(f32[264,128]{1,0:T(8,128)} %copy-done.8, f32[256,128]{1,0:T(8,128)} %get-tuple-element.44.refs_1_, f32[8,128]{1,0:T(8,128)} %get-tuple-element.45.refs_2_.refs_4_, bf16[2,256,256]{2,1,0:T(8,128)(2,1)} %get-tuple-element.46.refs_3_), custom_call_target="tpu_custom_call" | custom-call | flops 200000000 | bytes 729088 | tf_op jit(solution)/shard_map/pallas_call | solution.py:398
  73.3 7.0 %shard_map.118 = (f32[256,128]{1,0:T(8,128)}, f32[256,128]{1,0:T(8,128)}, f32[2,1024,256]{2,1,0:T(8,128)}, bf16[2,128,1024]{2,1,0:T(8,128)(2,1)}) custom-call(bf16[16,2,2,64,128]{4,3,2,1,0:T(8,128)(2,1)} %copy-done.4, bf16[2,2,256,128]{3,2,1,0:T(8,128)(2,1)} %get-tuple-element.42.refs_1_.refs_8_, bf16[256,128]{1,0:T(8,128)(2,1)} %get-tuple-element.47.refs_2_.refs_4_), custom_call_target="tpu_custom_call" | custom-call | flops 4000000000 | bytes 4194304 | tf_op jit(solution)/shard_map/pallas_call | solution.py:398
  80.3 3.0 %collective-permute-start.2 = (f32[256,128]{1,0:T(8,128)}, f32[256,128]{1,0:T(8,128)S(1)}, u32[]{:S(2)}, u32[]{:S(2)}) collective-permute-start(f32[256,128]{1,0:T(8,128)} %get-tuple-element.53), channel_id=1, source_target_pairs={{0,16},{16,0},{1,17},{17,1},{2,18},{18,2},{3,19},{19,3},{4,20},{20... | collective-permute-start | bytes 393224 | tf_op jit(solution)/shard_map/ppermute | solution.py:885
  83.9 6.8 %shard_map.119 = (bf16[16,1,2,64,128]{4,3,2,1,0:T(8,128)(2,1)}, f32[2,1024,128]{2,1,0:T(8,128)}, f32[2,128,256]{2,1,0:T(8,128)}) custom-call(bf16[16,2,2,64,128]{4,3,2,1,0:T(8,128)(2,1)} %copy-done.4, bf16[2,2,256,128]{3,2,1,0:T(8,128)(2,1)} %get-tuple-element.42.refs_1_.refs_8_, f32[2,1024,256]{2,1,0:T(8,128)} %get-tuple-element.48.refs_2_, ...), custom_call_target="tpu_custom_call" | custom-call | flops 4000000000 | bytes 5898240 | tf_op jit(solution)/shard_map/pallas_call | solution.py:398
  90.7 3.9 %all-to-all-start.3 = ((bf16[16,1,2,64,128]{4,3,2,1,0:T(8,128)(2,1)}), bf16[16,1,2,64,128]{4,3,2,1,0:T(8,128)(2,1)S(1)}, u32[]{:S(2)}, u32[]{:S(2)}) async-start(bf16[16,1,2,64,128]{4,3,2,1,0:T(8,128)(2,1)} %get-tuple-element.50), calls=%async_computation.3 | async-start | bytes 1048576 | tf_op jit(solution)/shard_map/all_to_all | solution.py:881
  95.3 2.2 %shard_map.121 = (bf16[272,128]{1,0:T(8,128)(2,1)}, f32[256,128]{1,0:T(8,128)}) custom-call(f32[256,128]{1,0:T(8,128)} %copy-done.7, f32[256,128]{1,0:T(8,128)} %get-tuple-element.54.refs_1_, bf16[2,256,256]{2,1,0:T(8,128)(2,1)} %get-tuple-element.55.refs_2_, f32[256,128]{1,0:T(8,128)} %get-tuple-element.56.refs_3_, ...), custom_call_target="tpu_custom_call" | custom-call | flops 200000000 | bytes 856064 | tf_op jit(solution)/shard_map/pallas_call | solution.py:398
  99.4 7.0 %shard_map.122 = (f32[2,256,256]{2,1,0:T(8,128)}, bf16[2,256,256]{2,1,0:T(8,128)(2,1)}) custom-call(f32[256,256]{1,0:T(8,128)} %get-tuple-element.51.refs_0_.refs_2_, f32[8,128]{1,0:T(8,128)} %get-tuple-element.52.refs_1_.refs_3_, f32[256,128]{1,0:T(8,128)} %get-tuple-element.58.refs_2_, f32[256,128]{1,0:T(8,128)} %get-tuple-element.56.refs_3_, ...), custom_call_target="tpu_custom_call" | custom-call | flops 6000000000 | bytes 4460544 | tf_op jit(solution)/shard_map/pallas_call | solution.py:398
  107.1 6.3 %shard_map.123 = (bf16[16,1,2,64,128]{4,3,2,1,0:T(8,128)(2,1)}, f32[2,1024,128]{2,1,0:T(8,128)}, f32[2,128,256]{2,1,0:T(8,128)}) custom-call(bf16[16,2,2,64,128]{4,3,2,1,0:T(8,128)(2,1)} %copy-done.3, bf16[2,2,256,128]{3,2,1,0:T(8,128)(2,1)} %get-tuple-element.42.refs_1_.refs_8_, f32[2,1024,256]{2,1,0:T(8,128)} %get-tuple-element.68.refs_2_, ...), custom_call_target="tpu_custom_call" | custom-call | flops 4000000000 | bytes 6045696 | tf_op jit(solution)/shard_map/pallas_call | solution.py:398
  113.4 5.1 %all-to-all-start.5 = ((bf16[16,1,2,64,128]{4,3,2,1,0:T(8,128)(2,1)}), bf16[16,1,2,64,128]{4,3,2,1,0:T(8,128)(2,1)S(1)}, u32[]{:S(2)}, u32[]{:S(2)}) async-start(bf16[16,1,2,64,128]{4,3,2,1,0:T(8,128)(2,1)} %get-tuple-element.78), calls=%async_computation.5 | async-start | bytes 1048576 | tf_op jit(solution)/shard_map/all_to_all | solution.py:881
  119.1 8.2 %shard_map.124 = (bf16[2,2,128,128]{3,2,1,0:T(8,128)(2,1)}, f32[2,2,128,128]{3,2,1,0:T(8,128)}) custom-call(f32[2,256,256]{2,1,0:T(8,128)} %get-tuple-element.62.refs_8_.refs_0_, bf16[2,256,256]{2,1,0:T(8,128)(2,1)} %get-tuple-element.63.refs_1_, f32[256,256]{1,0:T(8,128)} %get-tuple-element.51.refs_0_.refs_2_, f32[8,128]{1,0:T(8,128)} %get-tuple-element.52.refs_1_.refs_3_, ...), custom_call_target="tpu_custom_call" | custom-call | flops 6000000000 | bytes 5644288 | tf_op jit(solution)/shard_map/pallas_call | solution.py:398
  128.5 8.7 %collective-permute-done.4.refs_0_ = bf16[2,2,128,128]{3,2,1,0:T(8,128)(2,1)S(1)} collective-permute-done((bf16[2,2,128,128]{3,2,1,0:T(8,128)(2,1)}, bf16[2,2,128,128]{3,2,1,0:T(8,128)(2,1)S(1)}, u32[]{:S(2)}, u32[]{:S(2)}) %collective-permute-start.4) | collective-permute-done | bytes 131104 | tf_op jit(solution)/shard_map/ppermute | solution.py:885
  137.8 3.0 %shard_map.125 = bf16[16,2,2,64,128]{4,3,2,1,0:T(8,128)(2,1)} custom-call(bf16[2,2,128,128]{3,2,1,0:T(8,128)(2,1)} %copy-done.6, f32[2,2,128,128]{3,2,1,0:T(8,128)} %get-tuple-element.73.refs_1_, f32[2,1024,128]{2,1,0:T(8,128)} %get-tuple-element.74.refs_2_, f32[2,1024,128]{2,1,0:T(8,128)} %get-tuple-element.75.refs_3_), custom_call_target="tpu_custom_call" | custom-call | flops 500000000 | bytes 3538944 | tf_op jit(solution)/shard_map/pallas_call | solution.py:398
  140.9 3.9 %all-to-all-start.4 = ((bf16[16,2,2,64,128]{4,3,2,1,0:T(8,128)(2,1)}), bf16[16,2,2,64,128]{4,3,2,1,0:T(8,128)(2,1)S(1)}, u32[]{:S(2)}, u32[]{:S(2)}) async-start(bf16[16,2,2,64,128]{4,3,2,1,0:T(8,128)(2,1)} %shard_map.125), calls=%async_computation.4 | async-start | bytes 2097152 | tf_op jit(solution)/shard_map/all_to_all | solution.py:881
  148.6 11.1 %all-to-all-done.4.packed_ref = bf16[16,2,2,64,128]{4,3,2,1,0:T(8,128)(2,1)S(1)} async-done(((bf16[16,2,2,64,128]{4,3,2,1,0:T(8,128)(2,1)}), bf16[16,2,2,64,128]{4,3,2,1,0:T(8,128)(2,1)S(1)}, u32[]{:S(2)}, u32[]{:S(2)}) %all-to-all-start.4) | async-done | bytes 1048608 | tf_op jit(solution)/shard_map/all_to_all | solution.py:881
  (37 shorter events, 17.8 us)
Async XLA Ops:
  2.8 18.0 %all-to-all-start = ((bf16[32,2,16,128]{3,2,1,0:T(8,128)(2,1)}), bf16[32,2,16,128]{3,2,1,0:T(8,128)(2,1)S(1)}, u32[]{:S(2)}, u32[]{:S(2)}) async-start(bf16[32,2,16,128]{3,2,1,0:T(8,128)(2,1)} %shard_map.112), calls=%async_computation | async-start | bytes 524288 | tf_op jit(solution)/shard_map/all_to_all | solution.py:890
  20.8 5.8 %copy-start.5 = (bf16[32,2,16,128]{3,2,1,0:T(8,128)(2,1)}, bf16[32,2,16,128]{3,2,1,0:T(8,128)(2,1)S(1)}, u32[]{:S(2)}) copy-start(bf16[32,2,16,128]{3,2,1,0:T(8,128)(2,1)S(1)} %all-to-all-done.refs_1_) | copy-start | bytes 786436
  20.8 18.4 %all-to-all-start.2 = ((bf16[16,2,2,64,128]{4,3,2,1,0:T(8,128)(2,1)}), bf16[16,2,2,64,128]{4,3,2,1,0:T(8,128)(2,1)S(1)}, u32[]{:S(2)}, u32[]{:S(2)}) async-start(bf16[16,2,2,64,128]{4,3,2,1,0:T(8,128)(2,1)} %shard_map.115), calls=%async_computation.2 | async-start | bytes 2097152 | tf_op jit(solution)/shard_map/all_to_all | solution.py:881
  39.3 14.2 %copy-start.3 = (bf16[16,2,2,64,128]{4,3,2,1,0:T(8,128)(2,1)}, bf16[16,2,2,64,128]{4,3,2,1,0:T(8,128)(2,1)S(1)}, u32[]{:S(2)}) copy-start(bf16[16,2,2,64,128]{4,3,2,1,0:T(8,128)(2,1)S(1)} %all-to-all-done.2.refs_0_) | copy-start | bytes 3145732
  39.3 33.0 %all-to-all-start.1 = ((bf16[16,2,2,64,128]{4,3,2,1,0:T(8,128)(2,1)}), bf16[16,2,2,64,128]{4,3,2,1,0:T(8,128)(2,1)S(1)}, u32[]{:S(2)}, u32[]{:S(2)}) async-start(bf16[16,2,2,64,128]{4,3,2,1,0:T(8,128)(2,1)} %shard_map.113), calls=%async_computation.1 | async-start | bytes 2097152 | tf_op jit(solution)/shard_map/all_to_all | solution.py:881
  59.3 10.0 %collective-permute-start = (f32[264,128]{1,0:T(8,128)}, f32[264,128]{1,0:T(8,128)S(1)}, u32[]{:S(2)}, u32[]{:S(2)}) collective-permute-start(f32[264,128]{1,0:T(8,128)} %get-tuple-element.43), channel_id=1, source_target_pairs={{0,16},{16,0},{1,17},{17,1},{2,18},{18,2},{3,19},{19,3},{4,20},{20... | collective-permute-start | bytes 405512 | tf_op jit(solution)/shard_map/ppermute | solution.py:885
  69.3 0.7 copy-start.8
  72.2 11.1 %collective-permute-start.1 = (bf16[256,128]{1,0:T(8,128)(2,1)}, bf16[256,128]{1,0:T(8,128)(2,1)S(1)}, u32[]{:S(2)}, u32[]{:S(2)}) collective-permute-start(bf16[256,128]{1,0:T(8,128)(2,1)} %get-tuple-element.47.refs_2_.refs_4_), channel_id=1, source_target_pairs={{0,16},{16,0},{1,17},{17,1},{2,18},{18,2},{3,19},{19,3},{4,20},{20... | collective-permute-start | bytes 196616 | tf_op jit(solution)/shard_map/ppermute | solution.py:885
  72.3 1.0 copy-start.4
  80.3 14.3 %collective-permute-start.2 = (f32[256,128]{1,0:T(8,128)}, f32[256,128]{1,0:T(8,128)S(1)}, u32[]{:S(2)}, u32[]{:S(2)}) collective-permute-start(f32[256,128]{1,0:T(8,128)} %get-tuple-element.53), channel_id=1, source_target_pairs={{0,16},{16,0},{1,17},{17,1},{2,18},{18,2},{3,19},{19,3},{4,20},{20... | collective-permute-start | bytes 393224 | tf_op jit(solution)/shard_map/ppermute | solution.py:885
  83.3 0.6 copy-start.10
  90.7 22.7 %all-to-all-start.3 = ((bf16[16,1,2,64,128]{4,3,2,1,0:T(8,128)(2,1)}), bf16[16,1,2,64,128]{4,3,2,1,0:T(8,128)(2,1)S(1)}, u32[]{:S(2)}, u32[]{:S(2)}) async-start(bf16[16,1,2,64,128]{4,3,2,1,0:T(8,128)(2,1)} %get-tuple-element.50), calls=%async_computation.3 | async-start | bytes 1048576 | tf_op jit(solution)/shard_map/all_to_all | solution.py:881
  94.7 0.7 copy-start.7
  97.5 8.9 %collective-permute-start.3 = (bf16[272,128]{1,0:T(8,128)(2,1)}, bf16[272,128]{1,0:T(8,128)(2,1)S(1)}, u32[]{:S(2)}, u32[]{:S(2)}) collective-permute-start(bf16[272,128]{1,0:T(8,128)(2,1)} %get-tuple-element.70.refs_6_), channel_id=1, source_target_pairs={{0,16},{16,0},{1,17},{17,1},{2,18},{18,2},{3,19},{19,3},{4,20},{20... | collective-permute-start | bytes 208904 | tf_op jit(solution)/shard_map/ppermute | solution.py:885
  106.4 0.6 copy-start.9
  113.4 14.0 %copy-start.1 = (bf16[16,1,2,64,128]{4,3,2,1,0:T(8,128)(2,1)}, bf16[16,1,2,64,128]{4,3,2,1,0:T(8,128)(2,1)S(1)}, u32[]{:S(2)}) copy-start(bf16[16,1,2,64,128]{4,3,2,1,0:T(8,128)(2,1)S(1)} %all-to-all-done.3.packed_ref) | copy-start | bytes 1572868
  113.4 27.5 %all-to-all-start.5 = ((bf16[16,1,2,64,128]{4,3,2,1,0:T(8,128)(2,1)}), bf16[16,1,2,64,128]{4,3,2,1,0:T(8,128)(2,1)S(1)}, u32[]{:S(2)}, u32[]{:S(2)}) async-start(bf16[16,1,2,64,128]{4,3,2,1,0:T(8,128)(2,1)} %get-tuple-element.78), calls=%async_computation.5 | async-start | bytes 1048576 | tf_op jit(solution)/shard_map/all_to_all | solution.py:881
  127.4 9.8 %collective-permute-start.4 = (bf16[2,2,128,128]{3,2,1,0:T(8,128)(2,1)}, bf16[2,2,128,128]{3,2,1,0:T(8,128)(2,1)S(1)}, u32[]{:S(2)}, u32[]{:S(2)}) collective-permute-start(bf16[2,2,128,128]{3,2,1,0:T(8,128)(2,1)} %get-tuple-element.72), channel_id=1, source_target_pairs={{0,16},{16,0},{1,17},{17,1},{2,18},{18,2},{3,19},{19,3},{4,20},{20... | collective-permute-start | bytes 393224 | tf_op jit(solution)/shard_map/ppermute | solution.py:885
  137.2 0.7 copy-start.6
  140.9 5.8 %copy-start.2 = (bf16[16,1,2,64,128]{4,3,2,1,0:T(8,128)(2,1)}, bf16[16,1,2,64,128]{4,3,2,1,0:T(8,128)(2,1)S(1)}, u32[]{:S(2)}) copy-start(bf16[16,1,2,64,128]{4,3,2,1,0:T(8,128)(2,1)S(1)} %all-to-all-done.5.packed_ref) | copy-start | bytes 1572868
  140.9 18.7 %all-to-all-start.4 = ((bf16[16,2,2,64,128]{4,3,2,1,0:T(8,128)(2,1)}), bf16[16,2,2,64,128]{4,3,2,1,0:T(8,128)(2,1)S(1)}, u32[]{:S(2)}, u32[]{:S(2)}) async-start(bf16[16,2,2,64,128]{4,3,2,1,0:T(8,128)(2,1)} %shard_map.125), calls=%async_computation.4 | async-start | bytes 2097152 | tf_op jit(solution)/shard_map/all_to_all | solution.py:881
  159.7 1.0 copy-start

commit v4 on v2

--- a/solution.py
+++ b/solution.py
@@ -12,16 +12,16 @@
 PINV_ITERS = 6
 CHUNK = 256
 PACK_GROUPS = 4
+MIXING_PARTS = 4
 VMEM_LIMIT = 60 * 2**20
+SMALL_LIMIT = 16 * 2**20
 FORWARD_FLOPS = 10 * 10**9
 MIXING_FLOPS = 2 * 10**9
 GRADIENT_FLOPS = 14 * 10**9
 MIXING_NAMES = (
-    "key_turned",
-    "token_turned",
+    "key_low",
     "total_inverse",
     "inverse",
-    "inverse_turned",
     "token_low",
     "key_plow",
 )
@@ -45,10 +45,9 @@
     "factor",
     "token_prob",
     "token_low",
-    "token_turned",
     "key_prob",
     "key_plow",
-    "key_turned",
+    "key_low",
     "total_inverse",
     "columns_turned",
 )
@@ -359,30 +358,20 @@
         copy.wait()
 
 
-def unpack_kernel(packed_ref, first_ref, second_ref, packed_s, rows_s, in_done, out_done):
+def unpack_kernel(packed_ref, first_ref, second_ref, rows_s, out_done):
     heads = packed_ref.shape[0]
     group = heads // PACK_GROUPS
-    reads, writes = [], []
+    writes = []
     for index in range(PACK_GROUPS):
-        place = pl.ds(index * group, group)
-        reads.append(
-            pltpu.make_async_copy(packed_ref.at[place], packed_s.at[place], in_done.at[index])
-        )
         for slot, ref in enumerate((first_ref, second_ref)):
+            for head in range(index * group, (index + 1) * group):
+                rows_s[slot, :, head * HD : (head + 1) * HD] = packed_ref[head, slot]
             place = pl.ds(index * group * HD, group * HD)
-            writes.append(
-                pltpu.make_async_copy(
-                    rows_s.at[slot, :, place], ref.at[:, place], out_done.at[slot, index]
-                )
+            write = pltpu.make_async_copy(
+                rows_s.at[slot, :, place], ref.at[:, place], out_done.at[slot, index]
             )
-    for copy in reads:
-        copy.start()
-    for index in range(PACK_GROUPS):
-        reads[index].wait()
-        for slot in range(2):
-            for head in range(index * group, (index + 1) * group):
-                rows_s[slot, :, head * HD : (head + 1) * HD] = packed_s[head, slot]
-            writes[2 * index + slot].start()
+            write.start()
+            writes.append(write)
     for copy in writes:
         copy.wait()
 
@@ -410,17 +399,15 @@
         factor_ref,
         token_prob_ref,
         token_low_ref,
-        token_turned_ref,
         key_prob_ref,
         key_plow_ref,
-        key_turned_ref,
+        key_low_ref,
         total_inverse_ref,
         columns_turned_ref,
         pair_ref,
         weight_ref,
         growth_ref,
         inverse_ref,
-        inverse_turned_ref,
         last_growth_ref,
     ) = (held[name] for name in names)
     tokens, rows, chunks = dims_of(qk_ref)
@@ -456,11 +443,9 @@
         columns_turned_ref[1, :, place] = key_chunk.T
         score = wide_dot_nt(query_chunk, landmark_k) * score_scale
         grown = jnp.exp(score - jnp.max(score, axis=1, keepdims=True))
-        prob = grown / jnp.sum(grown, axis=1, keepdims=True)
+        prob = grown * (1.0 / jnp.sum(grown, axis=1, keepdims=True))
         token_prob_ref[place] = prob
-        low = prob.astype(jnp.bfloat16)
-        token_low_ref[place] = low
-        token_turned_ref[:, place] = low.T
+        token_low_ref[place] = prob.astype(jnp.bfloat16)
         key_score = wide_dot_nt(key_chunk, landmark_q) * score_scale
         key_prob_ref[place] = key_score
         return jnp.maximum(key_max, jnp.max(key_score, axis=0, keepdims=True))
@@ -471,12 +456,12 @@
         place = columns(index)
         grown = jnp.exp(key_prob_ref[place] - key_max)
         key_prob_ref[place] = grown
-        key_turned_ref[:, place] = grown.astype(jnp.bfloat16).T
+        key_low_ref[place] = grown.astype(jnp.bfloat16)
         return key_total + jnp.sum(grown, axis=0, keepdims=True)
 
     key_total = lax.fori_loop(0, chunks, grow, jnp.zeros((1, M), jnp.float32))
     total_inverse = 1.0 / key_total
-    total_inverse_ref[...] = jnp.broadcast_to(total_inverse, (HD, M)).T
+    total_inverse_ref[...] = jnp.broadcast_to(total_inverse, total_inverse_ref.shape)
 
     def normalise(index, carry):
         place = columns(index)
@@ -514,7 +499,6 @@
     lax.fori_loop(0, PINV_ITERS, newton, 0)
     inverse = iterate_s[0:M]
     inverse_ref[0], inverse_ref[1] = halves(inverse)
-    inverse_turned_ref[0], inverse_turned_ref[1] = halves(inverse.T)
     last_growth_ref[0], last_growth_ref[1] = halves(iterate_s[M:])
     for name in names:
         if name not in EARLY_NAMES:
@@ -536,59 +520,49 @@
 def mixing_kernel(*refs):
     count = len(MIXING_NAMES) + 1
     sources, homes, held = refs[:count], refs[count : count + 5], refs[count + 5 : 2 * count + 5]
-    results, (in_done, out_done) = refs[2 * count + 5 : 2 * count + 10], refs[2 * count + 10 :]
+    results = refs[2 * count + 5 : 2 * count + 10]
+    in_done, out_done, part_done = refs[2 * count + 10 :]
+    vg_ref, key_low_ref, total_inverse_ref, inverse_ref, token_low_ref, key_plow_ref = held
     reads = start_reads(sources, held, in_done)
-    (
-        vg_ref,
-        key_turned_ref,
-        token_turned_ref,
-        total_inverse_ref,
-        inverse_ref,
-        inverse_turned_ref,
-        token_low_ref,
-        key_plow_ref,
-    ) = held
     out_ref, mixing_low_ref, mixing_grad_ref, mark_values_ref, values_low_ref = results
     writes = [
         pltpu.make_async_copy(result, home, out_done.at[index])
-        for index, (result, home) in enumerate(zip(results, homes))
+        for index, (result, home) in enumerate(zip(results[1:], homes[1:]))
     ]
     tokens, rows, chunks = dims_of(vg_ref)
-    for read in reads[:6]:
+    reads[0].wait()
+    values_turned = vg_ref[:, 0].reshape(tokens, HD).T
+    for read in reads[1:4]:
         read.wait()
-    values = vg_ref[:, 0].reshape(tokens, HD)
-    out_grad = vg_ref[:, 1].reshape(tokens, HD)
-    landmark_values = wide_dot(key_turned_ref[...], values) * total_inverse_ref[...]
-    mixing_grad = wide_dot(token_turned_ref[...], out_grad)
+    inverse = (inverse_ref[0], inverse_ref[1])
+    landmark_values = wide_dot(values_turned, key_low_ref[...]) * total_inverse_ref[0:1]
     mark_values_ref[...] = landmark_values
+    mixing_low = split_dot_nt(halves(landmark_values), inverse).astype(jnp.bfloat16)
+    mixing_low_ref[...] = mixing_low
+    grad_turned = vg_ref[:, 1].reshape(tokens, HD).T
+    reads[4].wait()
+    mixing_grad = wide_dot(grad_turned, token_low_ref[...])
     mixing_grad_ref[...] = mixing_grad
-    mixing_low = split_dot(
-        (inverse_ref[0], inverse_ref[1]), halves(landmark_values)
-    ).astype(jnp.bfloat16)
-    values_low = split_dot(
-        (inverse_turned_ref[0], inverse_turned_ref[1]), halves(mixing_grad)
-    ).astype(jnp.bfloat16)
-    mixing_low_ref[...] = mixing_low
+    values_low = split_dot(halves(mixing_grad), inverse).astype(jnp.bfloat16)
     values_low_ref[...] = values_low
-    for write in writes[1:]:
+    for write in writes:
         write.start()
-    for read in reads[6:]:
-        read.wait()
-
-    def emit(index, carry):
-        place = columns(index)
-        store_chunk(
-            out_ref, 0, index, wide_dot(token_low_ref[place], mixing_low).astype(jnp.bfloat16)
-        )
-        store_chunk(
-            out_ref, 1, index, wide_dot(key_plow_ref[place], values_low).astype(jnp.bfloat16)
-        )
-        return carry
-
-    lax.fori_loop(0, chunks, emit, 0)
-    writes[0].start()
-    for write in writes:
-        write.wait()
+    out_ref[:, 0] = (
+        wide_dot_nt(token_low_ref[...], mixing_low).astype(jnp.bfloat16).reshape(-1, rows, HD)
+    )
+    reads[5].wait()
+    for part in range(MIXING_PARTS):
+        span = tokens // MIXING_PARTS
+        group = slice(part * span // rows, (part + 1) * span // rows)
+        place = slice(part * span, (part + 1) * span)
+        value_gradient = wide_dot_nt(key_plow_ref[place], values_low).astype(jnp.bfloat16)
+        out_ref[group, 1] = value_gradient.reshape(-1, rows, HD)
+        heads = pl.ds(group.start, group.stop - group.start)
+        copy = pltpu.make_async_copy(out_ref.at[heads], homes[0].at[heads], part_done.at[part])
+        copy.start()
+        writes.append(copy)
+    for copy in writes:
+        copy.wait()
 
 
 def gradient_kernel(*refs):
@@ -626,7 +600,7 @@
 
     def key_rows(index, row_total):
         place = columns(index)
-        key_dgrad = wide_dot_nt(chunk_of(vg_ref, 0, index), values_low)
+        key_dgrad = wide_dot(chunk_of(vg_ref, 0, index), values_low)
         kept_s[place] = key_dgrad
         return row_total + jnp.sum(key_prob_ref[place] * key_dgrad, axis=0, keepdims=True)
 
@@ -644,7 +618,7 @@
     def token_side(index, total):
         place = columns(index)
         prob = token_prob_ref[place]
-        token_grad = wide_dot_nt(chunk_of(vg_ref, 1, index), mixing_low)
+        token_grad = wide_dot(chunk_of(vg_ref, 1, index), mixing_low)
         token_sgrad = (
             prob * (token_grad - jnp.sum(token_grad * prob, axis=1, keepdims=True))
         ).astype(jnp.bfloat16)
@@ -658,7 +632,7 @@
     mark_prob = mark_prob_ref[...]
     mark_halves = halves(mark_prob)
     factor = factor_ref[0:1, 0:1]
-    inverse_grad = split_dot_nt(halves(mixing_grad_ref[...]), halves(mark_values_ref[...]))
+    inverse_grad = split_dot(halves(mixing_grad_ref[...].T), halves(mark_values_ref[...]))
     inverse_grad_halves = halves(inverse_grad)
     toward = split_dot(mark_halves, inverse_grad_halves) * factor
     power_s[...] = 0.5 * (toward + toward.T)
@@ -731,16 +705,17 @@
     write.wait()
 
 
-def kernel_call(kernel, out_shape, scratch, flops, operands):
+def kernel_call(kernel, out_shape, scratch, flops, operands, limit=VMEM_LIMIT, in_place=None):
     moved = sum(x.size * x.dtype.itemsize for x in operands)
-    in_place = pl.BlockSpec(memory_space=pl.ANY)
+    anywhere = pl.BlockSpec(memory_space=pl.ANY)
+    held = pl.BlockSpec(memory_space=pltpu.VMEM)
     return pl.pallas_call(
         kernel,
         out_shape=out_shape,
-        in_specs=[in_place] * len(operands),
-        out_specs=jax.tree.map(lambda _: in_place, out_shape),
+        in_specs=[held if index == in_place else anywhere for index in range(len(operands))],
+        out_specs=jax.tree.map(lambda _: anywhere, out_shape),
         scratch_shapes=scratch,
-        compiler_params=pltpu.CompilerParams(vmem_limit_bytes=VMEM_LIMIT),
+        compiler_params=pltpu.CompilerParams(vmem_limit_bytes=limit),
         cost_estimate=pl.CostEstimate(flops=flops, bytes_accessed=moved, transcendentals=0),
     )(*operands)
 
@@ -766,12 +741,12 @@
     heads, _, rows, _ = packed.shape
     shape = jax.ShapeDtypeStruct((rows, heads * HD), packed.dtype)
     scratch = [
-        pltpu.VMEM((heads, 2, rows, HD), packed.dtype),
         pltpu.VMEM((2, rows, heads * HD), packed.dtype),
-        pltpu.SemaphoreType.DMA((PACK_GROUPS,)),
         pltpu.SemaphoreType.DMA((2, PACK_GROUPS)),
     ]
-    return kernel_call(unpack_kernel, (shape, shape), scratch, 0, (packed,))
+    return kernel_call(
+        unpack_kernel, (shape, shape), scratch, 0, (packed,), limit=SMALL_LIMIT, in_place=0
+    )
 
 
 def forward_part(qk):
@@ -790,17 +765,15 @@
         factor=wide(8, HD),
         token_prob=wide(tokens, M),
         token_low=low(tokens, M),
-        token_turned=low(M, tokens),
         key_prob=wide(tokens, M),
         key_plow=low(tokens, M),
-        key_turned=low(M, tokens),
-        total_inverse=wide(M, HD),
+        key_low=low(tokens, M),
+        total_inverse=wide(8, M),
         columns_turned=low(2, HD, tokens),
         pair=low(PINV_ITERS, 2, 2 * M, M),
         weight=low(PINV_ITERS, 2, M, M),
         growth=low(PINV_ITERS, 2, M, M),
         inverse=low(2, M, M),
-        inverse_turned=low(2, M, M),
         last_growth=low(2, M, M),
     )
     scratch = [
@@ -824,16 +797,17 @@
 def mixing_part(vg, kept):
     shapes = (
         jax.ShapeDtypeStruct(vg.shape, jnp.bfloat16),
-        jax.ShapeDtypeStruct((M, HD), jnp.bfloat16),
-        jax.ShapeDtypeStruct((M, HD), jnp.float32),
-        jax.ShapeDtypeStruct((M, HD), jnp.float32),
-        jax.ShapeDtypeStruct((M, HD), jnp.bfloat16),
+        jax.ShapeDtypeStruct((HD, M), jnp.bfloat16),
+        jax.ShapeDtypeStruct((HD, M), jnp.float32),
+        jax.ShapeDtypeStruct((HD, M), jnp.float32),
+        jax.ShapeDtypeStruct((HD, M), jnp.bfloat16),
     )
     operands = (vg, *(kept[name] for name in MIXING_NAMES))
     scratch = [
         *(in_vmem(array) for array in (*operands, *shapes)),
         pltpu.SemaphoreType.DMA((len(operands),)),
-        pltpu.SemaphoreType.DMA((len(shapes),)),
+        pltpu.SemaphoreType.DMA((len(shapes) - 1,)),
+        pltpu.SemaphoreType.DMA((MIXING_PARTS,)),
     ]
     return kernel_call(mixing_kernel, shapes, scratch, MIXING_FLOPS, operands)
 

time: 136 us -> 133 us (0.978)
  Pallas kernels: 51.4 us -> 47.3 us
  waiting for transfers between devices: 63.4 us -> 65.7 us
    pallas_call x7, Pallas kernels: 51.4 us -> 47.3 us  [kernel_call(): pl.pallas_call(kernel, out_shape=out_shape, in_specs=[held if index == in...]
    all_to_all x4, waiting for transfers between devices: 63.4 us -> 65.7 us  [exchange(): lax.all_to_all(packed, ('seq', 'head'), split_axis=0, concat_axis=0, tile...]
  transfers between devices with their start and end apart: 4 -> 4, of which waited for: 4 -> 4; matrix products, arithmetic and copies ran while one was open for 0% -> 0% of each run, Pallas kernels for 31% -> 30%
where the time goes in v4:
time: 133 us
  waiting for transfers between devices  65.7 us (49%)
  Pallas kernels  47.3 us (36%)
  starting transfers between devices  18.2 us (14%)
    all_to_all x4, waiting for transfers between devices, exchange(): lax.all_to_all(packed, ('seq', 'head'), split_axis=0, concat_axis=0, tile...  65.7 us
    pallas_call x7, Pallas kernels, kernel_call(): pl.pallas_call(kernel, out_shape=out_shape, in_specs=[held if index == in...  47.3 us
    all_to_all x4, starting transfers between devices, exchange(): lax.all_to_all(packed, ('seq', 'head'), split_axis=0, concat_axis=0, tile...  18.2 us
  transfers between devices with their start and end apart: 4, of which 4 were waited for; matrix products, arithmetic and copies ran while one was open for 0% of the time, Pallas kernels for 30%

profile of v4, /device:TPU:0, one launch (start us, length us, event | category | flops | bytes accessed | tf_op | source)
XLA Modules:
  0.0 132.9 jit_solution(10349958589484761289)
XLA Ops:
  0.6 2.1 %shard_map.76 = bf16[32,2,64,128]{3,2,1,0:T(8,128)(2,1)} custom-call(bf16[64,4096]{1,0:T(8,128)(2,1)} %first_ref.3, bf16[64,4096]{1,0:T(8,128)(2,1)} %second_ref.3), custom_call_target="tpu_custom_call" | custom-call | bytes 1048576 | tf_op jit(solution)/shard_map/pallas_call | solution.py:712
  2.8 7.3 %all-to-all-start.1 = ((bf16[32,2,64,128]{3,2,1,0:T(8,128)(2,1)}), bf16[32,2,64,128]{3,2,1,0:T(8,128)(2,1)S(1)}, u32[]{:S(2)}, u32[]{:S(2)}) async-start(bf16[32,2,64,128]{3,2,1,0:T(8,128)(2,1)} %shard_map.76), calls=%async_computation.1 | async-start | bytes 2097152 | tf_op jit(solution)/shard_map/all_to_all | solution.py:841
  10.1 2.1 %shard_map.75 = bf16[32,2,64,128]{3,2,1,0:T(8,128)(2,1)} custom-call(bf16[64,4096]{1,0:T(8,128)(2,1)} %first_ref.2, bf16[64,4096]{1,0:T(8,128)(2,1)} %second_ref.2), custom_call_target="tpu_custom_call" | custom-call | bytes 1048576 | tf_op jit(solution)/shard_map/pallas_call | solution.py:712
  12.2 24.1 %all-to-all-done.1.qk_hbm = bf16[32,2,64,128]{3,2,1,0:T(8,128)(2,1)S(1)} async-done(((bf16[32,2,64,128]{3,2,1,0:T(8,128)(2,1)}), bf16[32,2,64,128]{3,2,1,0:T(8,128)(2,1)S(1)}, u32[]{:S(2)}, u32[]{:S(2)}) %all-to-all-start.1) | async-done | bytes 1048608 | tf_op jit(solution)/shard_map/all_to_all | solution.py:841
  36.3 0.0 copy-start.1
  36.3 3.6 %all-to-all-start = ((bf16[32,2,64,128]{3,2,1,0:T(8,128)(2,1)}), bf16[32,2,64,128]{3,2,1,0:T(8,128)(2,1)S(1)}, u32[]{:S(2)}, u32[]{:S(2)}) async-start(bf16[32,2,64,128]{3,2,1,0:T(8,128)(2,1)} %shard_map.75), calls=%async_computation | async-start | bytes 2097152 | tf_op jit(solution)/shard_map/all_to_all | solution.py:841
  39.9 0.0 copy-done.1
  40.0 15.8 %shard_map.77 = (bf16[256,128]{1,0:T(8,128)(2,1)}, bf16[256,128]{1,0:T(8,128)(2,1)}, f32[256,256]{1,0:T(8,128)}, f32[8,128]{1,0:T(8,128)}, f32[2048,256]{1,0:T(8...) custom-call(bf16[32,2,64,128]{3,2,1,0:T(8,128)(2,1)} %copy-done.1), custom_call_target="tpu_custom_call" | custom-call | flops 10000000000 | bytes 1048576 | tf_op jit(solution)/shard_map/pallas_call | solution.py:712
  55.7 10.4 %all-to-all-done.refs_0_.refs_2_ = bf16[32,2,64,128]{3,2,1,0:T(8,128)(2,1)S(1)} async-done(((bf16[32,2,64,128]{3,2,1,0:T(8,128)(2,1)}), bf16[32,2,64,128]{3,2,1,0:T(8,128)(2,1)S(1)}, u32[]{:S(2)}, u32[]{:S(2)}) %all-to-all-start) | async-done | bytes 1048608 | tf_op jit(solution)/shard_map/all_to_all | solution.py:841
  66.2 0.0 copy-start
  66.2 1.0 copy-done
  67.2 4.9 %shard_map.78 = (bf16[32,2,64,128]{3,2,1,0:T(8,128)(2,1)}, bf16[128,256]{1,0:T(8,128)(2,1)}, f32[128,256]{1,0:T(8,128)}, f32[128,256]{1,0:T(8,128)}, bf16[128,256]{1,0:T(8,128)(2,1)}) custom-call(bf16[32,2,64,128]{3,2,1,0:T(8,128)(2,1)} %copy-done, bf16[2048,256]{1,0:T(8,128)(2,1)} %get-tuple-element.29.refs_1_, f32[8,256]{1,0:T(8,128)} %get-tuple-element.30.refs_2_, ...), custom_call_target="tpu_custom_call" | custom-call | flops 2000000000 | bytes 4464640 | tf_op jit(solution)/shard_map/pallas_call | solution.py:712
  72.1 3.6 %all-to-all-start.2 = ((bf16[32,2,64,128]{3,2,1,0:T(8,128)(2,1)}), bf16[32,2,64,128]{3,2,1,0:T(8,128)(2,1)S(1)}, u32[]{:S(2)}, u32[]{:S(2)}) async-start(bf16[32,2,64,128]{3,2,1,0:T(8,128)(2,1)} %get-tuple-element.34), calls=%async_computation.2 | async-start | bytes 2097152 | tf_op jit(solution)/shard_map/all_to_all | solution.py:841
  75.7 20.2 %shard_map.80 = bf16[32,2,64,128]{3,2,1,0:T(8,128)(2,1)} custom-call(bf16[128,256]{1,0:T(8,128)(2,1)} %get-tuple-element.36.refs_0_, bf16[128,256]{1,0:T(8,128)(2,1)} %get-tuple-element.37.refs_1_, bf16[32,2,64,128]{3,2,1,0:T(8,128)(2,1)} %copy-done, bf16[256,128]{1,0:T(8,128)(2,1)} %get-tuple-element.38.refs_3_, ...), custom_call_target="tpu_custom_call" | custom-call | flops 14000000000 | bytes 13635584 | tf_op jit(solution)/shard_map/pallas_call | solution.py:712
  95.9 6.0 %all-to-all-done.2.packed_ref = bf16[32,2,64,128]{3,2,1,0:T(8,128)(2,1)S(1)} async-done(((bf16[32,2,64,128]{3,2,1,0:T(8,128)(2,1)}), bf16[32,2,64,128]{3,2,1,0:T(8,128)(2,1)S(1)}, u32[]{:S(2)}, u32[]{:S(2)}) %all-to-all-start.2) | async-done | bytes 1048608 | tf_op jit(solution)/shard_map/all_to_all | solution.py:841
  101.9 3.6 %all-to-all-start.3 = ((bf16[32,2,64,128]{3,2,1,0:T(8,128)(2,1)}), bf16[32,2,64,128]{3,2,1,0:T(8,128)(2,1)S(1)}, u32[]{:S(2)}, u32[]{:S(2)}) async-start(bf16[32,2,64,128]{3,2,1,0:T(8,128)(2,1)} %shard_map.80), calls=%async_computation.3 | async-start | bytes 2097152 | tf_op jit(solution)/shard_map/all_to_all | solution.py:841
  105.6 1.1 shard_map.79
  106.6 25.2 %all-to-all-done.3.packed_ref = bf16[32,2,64,128]{3,2,1,0:T(8,128)(2,1)S(1)} async-done(((bf16[32,2,64,128]{3,2,1,0:T(8,128)(2,1)}), bf16[32,2,64,128]{3,2,1,0:T(8,128)(2,1)S(1)}, u32[]{:S(2)}, u32[]{:S(2)}) %all-to-all-start.3) | async-done | bytes 1048608 | tf_op jit(solution)/shard_map/all_to_all | solution.py:841
  131.8 1.0 shard_map.81
Async XLA Ops:
  2.8 33.5 %all-to-all-start.1 = ((bf16[32,2,64,128]{3,2,1,0:T(8,128)(2,1)}), bf16[32,2,64,128]{3,2,1,0:T(8,128)(2,1)S(1)}, u32[]{:S(2)}, u32[]{:S(2)}) async-start(bf16[32,2,64,128]{3,2,1,0:T(8,128)(2,1)} %shard_map.76), calls=%async_computation.1 | async-start | bytes 2097152 | tf_op jit(solution)/shard_map/all_to_all | solution.py:841
  36.3 3.6 %copy-start.1 = (bf16[32,2,64,128]{3,2,1,0:T(8,128)(2,1)}, bf16[32,2,64,128]{3,2,1,0:T(8,128)(2,1)S(1)}, u32[]{:S(2)}) copy-start(bf16[32,2,64,128]{3,2,1,0:T(8,128)(2,1)S(1)} %all-to-all-done.1.qk_hbm) | copy-start | bytes 3145732
  36.3 29.9 %all-to-all-start = ((bf16[32,2,64,128]{3,2,1,0:T(8,128)(2,1)}), bf16[32,2,64,128]{3,2,1,0:T(8,128)(2,1)S(1)}, u32[]{:S(2)}, u32[]{:S(2)}) async-start(bf16[32,2,64,128]{3,2,1,0:T(8,128)(2,1)} %shard_map.75), calls=%async_computation | async-start | bytes 2097152 | tf_op jit(solution)/shard_map/all_to_all | solution.py:841
  66.2 1.0 copy-start
  72.1 29.9 %all-to-all-start.2 = ((bf16[32,2,64,128]{3,2,1,0:T(8,128)(2,1)}), bf16[32,2,64,128]{3,2,1,0:T(8,128)(2,1)S(1)}, u32[]{:S(2)}, u32[]{:S(2)}) async-start(bf16[32,2,64,128]{3,2,1,0:T(8,128)(2,1)} %get-tuple-element.34), calls=%async_computation.2 | async-start | bytes 2097152 | tf_op jit(solution)/shard_map/all_to_all | solution.py:841
  101.9 29.9 %all-to-all-start.3 = ((bf16[32,2,64,128]{3,2,1,0:T(8,128)(2,1)}), bf16[32,2,64,128]{3,2,1,0:T(8,128)(2,1)S(1)}, u32[]{:S(2)}, u32[]{:S(2)}) async-start(bf16[32,2,64,128]{3,2,1,0:T(8,128)(2,1)} %shard_map.80), calls=%async_computation.3 | async-start | bytes 2097152 | tf_op jit(solution)/shard_map/all_to_all | solution.py:841

commit v5 on v0

--- a/solution.py
+++ b/solution.py
@@ -1,11 +1,22 @@
+import functools
+
 import jax
 import jax.numpy as jnp
 from jax import lax
+from jax.experimental import pallas as pl
+from jax.experimental.pallas import tpu as pltpu
 from jax.sharding import PartitionSpec as P
 
 HD = 128
 M = 256
 PINV_ITERS = 6
+CHUNK = 256
+PACK_GROUPS = 4
+SWEEP_NAMES = ("pair", "weight", "growth")
+VMEM_LIMIT = 60 * 2**20
+SMALL_LIMIT = 16 * 2**20
+FORWARD_FLOPS = 10 * 10**9
+GRADIENT_FLOPS = 14 * 10**9
 
 
 precise_setting = lax.Precision.HIGHEST
@@ -31,7 +42,7 @@
     return lax.psum(slot_mask[:, None, None] * own_matrix[None], "seq")
 
 
-def body(queries, keys, values, out_grad):
+def shared_body(queries, keys, values, out_grad):
     query_rows, key_rows, value_rows, grad_rows = (
         lax.all_to_all(queries, "head", split_axis=1, concat_axis=0, tiled=True),
         lax.all_to_all(keys, "head", split_axis=1, concat_axis=0, tiled=True),
@@ -225,21 +236,592 @@
     return (attended_out, query_out, key_out, value_out)
 
 
+def dims_of(rows):
+    tokens = rows.shape[0] * rows.shape[2]
+    return tokens, rows.shape[2], tokens // CHUNK
+
+
+def halves(matrix):
+    high = matrix.astype(jnp.bfloat16)
+    return high, (matrix - high.astype(jnp.float32)).astype(jnp.bfloat16)
+
+
+def wide_dot(left, right):
+    return jnp.dot(left, right, preferred_element_type=jnp.float32)
+
+
+def wide_dot_nt(left, right):
+    return lax.dot_general(
+        left, right, (((1,), (1,)), ((), ())), preferred_element_type=jnp.float32
+    )
+
+
+def split_dot(left, right):
+    left_high, left_low = left
+    right_high, right_low = right
+    return wide_dot(
+        jnp.concatenate([left_high, left_high, left_low], axis=1),
+        jnp.concatenate([right_high, right_low, right_high], axis=0),
+    )
+
+
+def split_dot_nt(left, right):
+    left_high, left_low = left
+    right_high, right_low = right
+    return wide_dot_nt(
+        jnp.concatenate([left_high, left_high, left_low], axis=1),
+        jnp.concatenate([right_high, right_low, right_high], axis=1),
+    )
+
+
+def identity_matrix():
+    return (
+        lax.broadcasted_iota(jnp.int32, (M, M), 0) == lax.broadcasted_iota(jnp.int32, (M, M), 1)
+    ).astype(jnp.float32)
+
+
+def chunk_of(ref, slot, index):
+    rows = ref.shape[2]
+    per = CHUNK // rows
+    return ref[pl.ds(index * per, per), slot].reshape(CHUNK, HD)
+
+
+def store_chunk(ref, slot, index, value):
+    rows = ref.shape[2]
+    per = CHUNK // rows
+    ref[pl.ds(index * per, per), slot] = value.reshape(per, rows, HD)
+
+
+def columns(index):
+    return pl.ds(pl.multiple_of(index * CHUNK, CHUNK), CHUNK)
+
+
+def pack_kernel(*refs):
+    arrays = len(refs) - 5
+    sources, (out_ref, rows_s, packed_s, in_done, out_done) = refs[:arrays], refs[arrays:]
+    group = out_ref.shape[0] // PACK_GROUPS
+    reads, writes = [], []
+    for index in range(PACK_GROUPS):
+        for slot, ref in enumerate(sources):
+            place = pl.ds(index * group * HD, group * HD)
+            reads.append(
+                pltpu.make_async_copy(
+                    ref.at[:, place], rows_s.at[slot, :, place], in_done.at[slot, index]
+                )
+            )
+        place = pl.ds(index * group, group)
+        writes.append(
+            pltpu.make_async_copy(packed_s.at[place], out_ref.at[place], out_done.at[index])
+        )
+    for copy in reads:
+        copy.start()
+    for index in range(PACK_GROUPS):
+        for slot in range(arrays):
+            reads[arrays * index + slot].wait()
+            for head in range(index * group, (index + 1) * group):
+                packed_s[head, slot] = rows_s[slot, :, head * HD : (head + 1) * HD]
+        writes[index].start()
+    for copy in writes:
+        copy.wait()
+
+
+def unpack_kernel(packed_ref, *refs):
+    homes, (rows_s, out_done) = refs[:-2], refs[-2:]
+    group = packed_ref.shape[0] // PACK_GROUPS
+    writes = []
+    for index in range(PACK_GROUPS):
+        for slot, ref in enumerate(homes):
+            for head in range(index * group, (index + 1) * group):
+                rows_s[slot, :, head * HD : (head + 1) * HD] = packed_ref[head, slot]
+            place = pl.ds(index * group * HD, group * HD)
+            write = pltpu.make_async_copy(
+                rows_s.at[slot, :, place], ref.at[:, place], out_done.at[slot, index]
+            )
+            write.start()
+            writes.append(write)
+    for copy in writes:
+        copy.wait()
+
+
+def sweep_forward(power_s, iterate_s, saved, sweep, work):
+    pair_ref, weight_ref, growth_ref = saved
+    power = power_s[...]
+    power_high, power_low = halves(power)
+    square = split_dot((power_high, power_low), (power_high, power_low))
+    next(work)()
+    square_halves = halves(square)
+    pair = (
+        jnp.concatenate([power_high, square_halves[0]], axis=0),
+        jnp.concatenate([power_low, square_halves[1]], axis=0),
+    )
+    pair_ref[sweep, 0], pair_ref[sweep, 1] = pair
+    higher = split_dot(pair, square_halves)
+    next(work)()
+    cube, fourth = higher[:M], higher[M:]
+    weight = halves(0.25 * (13.0 * identity_matrix() - 15.0 * power + 7.0 * square - cube))
+    power_s[...] = 0.25 * (13.0 * power - 15.0 * square + 7.0 * cube - fourth)
+    weight_ref[sweep, 0], weight_ref[sweep, 1] = weight
+    iterate = halves(iterate_s[...])
+    growth_ref[sweep, 0], growth_ref[sweep, 1] = iterate[0][M:], iterate[1][M:]
+    iterate_s[...] = split_dot(iterate, weight)
+
+
+def forward_kernel(names, qkv_hbm, *refs):
+    count = len(names)
+    homes, refs = dict(zip(names, refs[:count])), refs[count:]
+    held, refs = dict(zip(names, refs[:count])), refs[count:]
+    qkv_ref, power_s, iterate_s, token_low_s, key_low_s, in_done, out_done, sweep_done = refs
+    copies = {
+        name: pltpu.make_async_copy(held[name], homes[name], out_done.at[index])
+        for index, name in enumerate(names)
+        if name not in SWEEP_NAMES
+    }
+    sent = []
+
+    def send(*chosen):
+        for name in chosen:
+            copies[name].start()
+            sent.append(copies[name])
+
+    arrive = [
+        pltpu.make_async_copy(qkv_hbm.at[:, slot], qkv_ref.at[:, slot], in_done.at[slot])
+        for slot in range(3)
+    ]
+    for copy in arrive:
+        copy.start()
+    for copy in arrive[:2]:
+        copy.wait()
+    tokens, rows, chunks = dims_of(qkv_ref)
+    segment_len = tokens // M
+    marks_per = CHUNK // segment_len
+    score_scale = HD ** (-0.5)
+    member = (
+        lax.broadcasted_iota(jnp.int32, (marks_per, CHUNK), 1) // segment_len
+        == lax.broadcasted_iota(jnp.int32, (marks_per, CHUNK), 0)
+    ).astype(jnp.bfloat16)
+    for index in range(chunks):
+        both = jnp.concatenate([chunk_of(qkv_ref, 0, index), chunk_of(qkv_ref, 1, index)], axis=1)
+        mean = (wide_dot(member, both) / segment_len).astype(jnp.bfloat16)
+        held["mark_q"][index * marks_per : (index + 1) * marks_per] = mean[:, :HD]
+        held["mark_k"][index * marks_per : (index + 1) * marks_per] = mean[:, HD:]
+    landmark_q, landmark_k = held["mark_q"][...], held["mark_k"][...]
+
+    mark_score = wide_dot_nt(landmark_q, landmark_k) * score_scale
+    mark_exp = jnp.exp(mark_score - jnp.max(mark_score, axis=1, keepdims=True))
+    mark_prob = mark_exp / jnp.sum(mark_exp, axis=1, keepdims=True)
+    held["mark_prob"][...] = mark_prob
+    factor = 1.0 / jnp.max(jnp.sum(mark_prob, axis=0, keepdims=True), axis=1, keepdims=True)
+    held["factor"][...] = jnp.broadcast_to(factor, held["factor"].shape)
+    mark_halves = halves(mark_prob)
+    power_s[...] = split_dot_nt(mark_halves, mark_halves) * factor
+    iterate_s[0:M] = mark_prob.T * factor
+    iterate_s[M:] = identity_matrix()
+    send("mark_q", "mark_k", "mark_prob", "factor")
+
+    tops, totals = [], []
+    places = [slice(index * CHUNK, (index + 1) * CHUNK) for index in range(chunks)]
+
+    def scores(index):
+        query_chunk, key_chunk = chunk_of(qkv_ref, 0, index), chunk_of(qkv_ref, 1, index)
+        place = places[index]
+        held["turned"][0, :, place] = query_chunk.T
+        held["turned"][1, :, place] = key_chunk.T
+        score = wide_dot_nt(query_chunk, landmark_k) * score_scale
+        grown = jnp.exp(score - jnp.max(score, axis=1, keepdims=True))
+        prob = grown * (1.0 / jnp.sum(grown, axis=1, keepdims=True))
+        held["token_prob"][place] = prob
+        token_low_s[place] = prob.astype(jnp.bfloat16)
+        key_score = wide_dot_nt(key_chunk, landmark_q) * score_scale
+        held["key_prob"][place] = key_score
+        tops.append(jnp.max(key_score, axis=0, keepdims=True))
+
+    def grow(index):
+        if index == 0:
+            tops[0] = functools.reduce(jnp.maximum, tops)
+        place = places[index]
+        grown = jnp.exp(held["key_prob"][place] - tops[0])
+        held["key_prob"][place] = grown
+        key_low_s[place] = grown.astype(jnp.bfloat16)
+        totals.append(jnp.sum(grown, axis=0, keepdims=True))
+
+    def units():
+        half = (chunks + 3) // 4
+        for first in range(0, chunks, max(1, chunks // 8)):
+            yield functools.partial(
+                lambda start: [scores(x) for x in range(start, min(chunks, start + chunks // 8))],
+                first,
+            )
+        for first in range(0, chunks, half):
+            yield functools.partial(
+                lambda start: [grow(x) for x in range(start, min(chunks, start + half))], first
+            )
+
+    work = units()
+    saved = tuple(held[name] for name in SWEEP_NAMES)
+    for sweep in range(PINV_ITERS):
+        sweep_forward(power_s, iterate_s, saved, sweep, work)
+        for place, name in enumerate(SWEEP_NAMES):
+            copy = pltpu.make_async_copy(
+                held[name].at[sweep], homes[name].at[sweep], sweep_done.at[place, sweep]
+            )
+            copy.start()
+            sent.append(copy)
+        if sweep == 3:
+            send("token_prob", "turned")
+    inverse = halves(iterate_s[0:M])
+    held["inverse"][0], held["inverse"][1] = inverse
+    held["last_growth"][0], held["last_growth"][1] = halves(iterate_s[M:])
+    send("inverse", "last_growth")
+    total_inverse = 1.0 / sum(totals[1:], totals[0])
+    arrive[2].wait()
+    values_turned = qkv_ref[:, 2].reshape(tokens, HD).T
+    landmark_values = wide_dot(values_turned, key_low_s[...]) * total_inverse
+    held["mark_values"][...] = landmark_values
+    mixing_low = split_dot_nt(halves(landmark_values), inverse).astype(jnp.bfloat16)
+    held["mixing_low"][...] = mixing_low
+    attended = wide_dot_nt(token_low_s[...], mixing_low).astype(jnp.bfloat16)
+    held["attended"][:, 0] = attended.reshape(-1, rows, HD)
+    send("attended", "mark_values", "mixing_low")
+    for place in places:
+        held["key_prob"][place] = held["key_prob"][place] * total_inverse
+    send("key_prob")
+    for copy in sent:
+        copy.wait()
+
+
+def gradient_kernel(names, qkv_hbm, grad_hbm, *refs):
+    count = len(names)
+    sources, home, refs = dict(zip(names, refs[:count])), refs[count], refs[count + 1 :]
+    held, refs = dict(zip(names, refs[:count])), refs[count:]
+    values_s, grads_s, out_ref, query_s, direct_s, kept_s, in_done, sweep_done, out_done = refs
+    reads = {
+        name: pltpu.make_async_copy(sources[name], held[name], in_done.at[index])
+        for index, name in enumerate(names)
+        if name not in SWEEP_NAMES
+    }
+    fetch_grads = pltpu.make_async_copy(grad_hbm.at[:, 0], grads_s, in_done.at[count])
+    fetch_values = pltpu.make_async_copy(qkv_hbm.at[:, 2], values_s, in_done.at[count + 1])
+    sweeps = [
+        [
+            pltpu.make_async_copy(
+                sources[name].at[sweep], held[name].at[sweep], sweep_done.at[place, sweep]
+            )
+            for place, name in enumerate(SWEEP_NAMES)
+        ]
+        for sweep in range(PINV_ITERS)
+    ]
+
+    def start(*chosen):
+        for name in chosen:
+            reads[name].start()
+
+    def wait(*chosen):
+        for name in chosen:
+            reads[name].wait()
+
+    fetch_grads.start()
+    start("token_prob", "inverse", "mark_values", "mark_prob", "factor")
+    for copy in sweeps[0]:
+        copy.start()
+    fetch_values.start()
+    start("key_prob")
+    for copies in sweeps[1:3]:
+        for copy in copies:
+            copy.start()
+    start("mark_q", "turned", "mark_k", "mixing_low")
+    for copies in sweeps[3:]:
+        for copy in copies:
+            copy.start()
+    start("last_growth")
+
+    heads, rows, _ = values_s.shape
+    tokens = heads * rows
+    chunks, per = tokens // CHUNK, CHUNK // rows
+    segment_len = tokens // M
+    marks_per = CHUNK // segment_len
+    score_scale = HD ** (-0.5)
+    places = [slice(index * CHUNK, (index + 1) * CHUNK) for index in range(chunks)]
+
+    def block(ref, index):
+        return ref[index * per : (index + 1) * per].reshape(CHUNK, HD)
+
+    fetch_grads.wait()
+    grads_turned = grads_s[...].reshape(tokens, HD).T
+    wait("token_prob")
+    mixing_grad = wide_dot(grads_turned, held["token_prob"][...].astype(jnp.bfloat16))
+    wait("inverse", "mark_values", "mark_prob", "factor")
+    values_low = split_dot(
+        halves(mixing_grad), (held["inverse"][0], held["inverse"][1])
+    ).astype(jnp.bfloat16)
+    mark_prob = held["mark_prob"][...]
+    mark_halves = halves(mark_prob)
+    factor = held["factor"][0:1, 0:1]
+    inverse_grad = split_dot(halves(mixing_grad.T), halves(held["mark_values"][...]))
+    inverse_grad_halves = halves(inverse_grad)
+    toward = split_dot(mark_halves, inverse_grad_halves) * factor
+    power = 0.5 * (toward + toward.T)
+    growth = None
+
+    row_totals, query_sums, key_sums = [], [], []
+
+    def key_rows(index):
+        place = places[index]
+        key_prob = held["key_prob"][place]
+        value_gradient = wide_dot_nt(key_prob.astype(jnp.bfloat16), values_low)
+        out_ref[index * per : (index + 1) * per, 0] = value_gradient.astype(
+            jnp.bfloat16
+        ).reshape(per, rows, HD)
+        key_dgrad = wide_dot(block(values_s, index), values_low)
+        kept_s[place] = key_dgrad
+        row_totals.append(jnp.sum(key_prob * key_dgrad, axis=0, keepdims=True))
+
+    def key_side(index):
+        if index == 0:
+            row_totals[0] = sum(row_totals[1:], row_totals[0])
+        place = places[index]
+        key_sgrad = (held["key_prob"][place] * (kept_s[place] - row_totals[0])).astype(
+            jnp.bfloat16
+        )
+        direct_s[place] = wide_dot(key_sgrad, held["mark_q"][...]) * score_scale
+        query_sums.append(wide_dot(held["turned"][1, :, place], key_sgrad))
+
+    def token_side(index):
+        place = places[index]
+        prob = held["token_prob"][place]
+        token_grad = wide_dot(block(grads_s, index), held["mixing_low"][...])
+        token_sgrad = (
+            prob * (token_grad - jnp.sum(token_grad * prob, axis=1, keepdims=True))
+        ).astype(jnp.bfloat16)
+        query_s[place] = wide_dot(token_sgrad, held["mark_k"][...]) * score_scale
+        key_sums.append(wide_dot(held["turned"][0, :, place], token_sgrad))
+
+    span = (chunks + 3) // 4
+    work = iter(
+        [
+            (unit, range(first, min(chunks, first + span)))
+            for unit in (key_rows, key_side, token_side)
+            for first in range(0, chunks, span)
+        ]
+    )
+
+    def beside():
+        unit, indices = next(work)
+        for index in indices:
+            unit(index)
+
+    for sweep in range(PINV_ITERS):
+        if sweep == 0:
+            fetch_values.wait()
+            wait("key_prob")
+        if sweep == 2:
+            wait("mark_q", "turned", "mark_k", "mixing_low")
+        for copy in sweeps[sweep]:
+            copy.wait()
+        pair_ref, weight_ref, growth_ref = (held[name] for name in SWEEP_NAMES)
+        pair = (pair_ref[sweep, 0], pair_ref[sweep, 1])
+        first = split_dot(pair, halves(power))
+        beside()
+        square = first[:M] + first[:M].T
+        second = split_dot(pair, halves(square))
+        beside()
+        cube = first[M:].T + second[:M]
+        fourth = second[M:] + second[M:].T
+        weight = halves(0.25 * (7.0 * square - 15.0 * power - cube))
+        power = 0.25 * (13.0 * power - 15.0 * square + 7.0 * cube - fourth)
+        held_growth = (growth_ref[sweep, 0], growth_ref[sweep, 1])
+        left = [held_growth[0], held_growth[0], held_growth[1]]
+        right = [weight[0], weight[1], weight[0]]
+        if growth is not None:
+            grown = halves(growth)
+            left += [grown[0], grown[0], grown[1]]
+            right += [weight_ref[sweep, 0], weight_ref[sweep, 1], weight_ref[sweep, 0]]
+        growth = wide_dot(jnp.concatenate(left, axis=1), jnp.concatenate(right, axis=0))
+    wait("last_growth")
+    mark_grad = factor * (
+        split_dot_nt((held["last_growth"][0], held["last_growth"][1]), inverse_grad_halves)
+        + split_dot(halves(growth + growth.T), mark_halves)
+    )
+    mark_sgrad = mark_prob * (mark_grad - jnp.sum(mark_grad * mark_prob, axis=1, keepdims=True))
+
+    def marks_dot(left, right):
+        high, low = halves(left)
+        return wide_dot(
+            jnp.concatenate([high, low], axis=1), jnp.concatenate([right, right], axis=0)
+        )
+
+    marks_scale = score_scale / segment_len
+    query_marks = (
+        marks_dot(mark_sgrad, held["mark_k"][...]) + sum(query_sums[1:], query_sums[0]).T
+    ) * marks_scale
+    key_marks = (
+        marks_dot(mark_sgrad.T, held["mark_q"][...]) + sum(key_sums[1:], key_sums[0]).T
+    ) * marks_scale
+
+    writes = []
+    for index, place in enumerate(places):
+        group = slice(index * per, (index + 1) * per)
+        marked = slice(index * marks_per, (index + 1) * marks_per)
+        for slot, direct, marks in ((1, query_s, query_marks), (2, direct_s, key_marks)):
+            wide = jnp.broadcast_to(marks[marked][:, None], (marks_per, segment_len, HD))
+            total = direct[place] + wide.reshape(CHUNK, HD)
+            out_ref[group, slot] = total.astype(jnp.bfloat16).reshape(per, rows, HD)
+        write = pltpu.make_async_copy(
+            out_ref.at[pl.ds(index * per, per)],
+            home.at[pl.ds(index * per, per)],
+            out_done.at[index],
+        )
+        write.start()
+        writes.append(write)
+    for write in writes:
+        write.wait()
+
+
+def kernel_call(kernel, out_shape, scratch, flops, operands, limit=VMEM_LIMIT, in_place=None):
+    moved = sum(x.size * x.dtype.itemsize for x in operands)
+    anywhere = pl.BlockSpec(memory_space=pl.ANY)
+    held = pl.BlockSpec(memory_space=pltpu.VMEM)
+    return pl.pallas_call(
+        kernel,
+        out_shape=out_shape,
+        in_specs=[held if index == in_place else anywhere for index in range(len(operands))],
+        out_specs=jax.tree.map(lambda _: anywhere, out_shape),
+        scratch_shapes=scratch,
+        compiler_params=pltpu.CompilerParams(vmem_limit_bytes=limit),
+        cost_estimate=pl.CostEstimate(flops=flops, bytes_accessed=moved, transcendentals=0),
+    )(*operands)
+
+
+def in_vmem(array):
+    return pltpu.VMEM(array.shape, array.dtype)
+
+
+def pack(*sources):
+    rows, width = sources[0].shape
+    heads, arrays = width // HD, len(sources)
+    shape = jax.ShapeDtypeStruct((heads, arrays, rows, HD), sources[0].dtype)
+    scratch = [
+        pltpu.VMEM((arrays, rows, width), sources[0].dtype),
+        pltpu.VMEM(shape.shape, sources[0].dtype),
+        pltpu.SemaphoreType.DMA((arrays, PACK_GROUPS)),
+        pltpu.SemaphoreType.DMA((PACK_GROUPS,)),
+    ]
+    return kernel_call(pack_kernel, shape, scratch, 0, sources)
+
+
+def unpack(packed):
+    heads, arrays, rows, _ = packed.shape
+    shape = jax.ShapeDtypeStruct((rows, heads * HD), packed.dtype)
+    scratch = [
+        pltpu.VMEM((arrays, rows, heads * HD), packed.dtype),
+        pltpu.SemaphoreType.DMA((arrays, PACK_GROUPS)),
+    ]
+    return kernel_call(
+        unpack_kernel, (shape,) * arrays, scratch, 0, (packed,), limit=SMALL_LIMIT, in_place=0
+    )
+
+
+def low(*shape):
+    return jax.ShapeDtypeStruct(shape, jnp.bfloat16)
+
+
+def wide(*shape):
+    return jax.ShapeDtypeStruct(shape, jnp.float32)
+
+
+def forward_part(qkv):
+    heads, _, rows, _ = qkv.shape
+    tokens = heads * rows
+    shapes = dict(
+        attended=low(heads, 1, rows, HD),
+        mark_q=low(M, HD),
+        mark_k=low(M, HD),
+        mark_prob=wide(M, M),
+        factor=wide(8, HD),
+        token_prob=wide(tokens, M),
+        key_prob=wide(tokens, M),
+        turned=low(2, HD, tokens),
+        pair=low(PINV_ITERS, 2, 2 * M, M),
+        weight=low(PINV_ITERS, 2, M, M),
+        growth=low(PINV_ITERS, 2, M, M),
+        inverse=low(2, M, M),
+        last_growth=low(2, M, M),
+        mark_values=wide(HD, M),
+        mixing_low=low(HD, M),
+    )
+    scratch = [
+        *(in_vmem(shape) for shape in shapes.values()),
+        in_vmem(qkv),
+        pltpu.VMEM((M, M), jnp.float32),
+        pltpu.VMEM((2 * M, M), jnp.float32),
+        pltpu.VMEM((tokens, M), jnp.bfloat16),
+        pltpu.VMEM((tokens, M), jnp.bfloat16),
+        pltpu.SemaphoreType.DMA((3,)),
+        pltpu.SemaphoreType.DMA((len(shapes),)),
+        pltpu.SemaphoreType.DMA((len(SWEEP_NAMES), PINV_ITERS)),
+    ]
+    results = kernel_call(
+        functools.partial(forward_kernel, tuple(shapes)),
+        tuple(shapes.values()),
+        scratch,
+        FORWARD_FLOPS,
+        (qkv,),
+    )
+    return dict(zip(shapes, results))
+
+
+def gradient_part(qkv, grads, kept):
+    heads, _, rows, _ = qkv.shape
+    tokens = heads * rows
+    names = tuple(name for name in kept if name != "attended")
+    operands = tuple(kept[name] for name in names)
+    shape = low(heads, 3, rows, HD)
+    scratch = [
+        *(in_vmem(array) for array in operands),
+        pltpu.VMEM((heads, rows, HD), jnp.bfloat16),
+        pltpu.VMEM((heads, rows, HD), jnp.bfloat16),
+        in_vmem(shape),
+        pltpu.VMEM((tokens, HD), jnp.float32),
+        pltpu.VMEM((tokens, HD), jnp.float32),
+        pltpu.VMEM((tokens, M), jnp.float32),
+        pltpu.SemaphoreType.DMA((len(names) + 2,)),
+        pltpu.SemaphoreType.DMA((len(SWEEP_NAMES), PINV_ITERS)),
+        pltpu.SemaphoreType.DMA((tokens // CHUNK,)),
+    ]
+    return kernel_call(
+        functools.partial(gradient_kernel, names),
+        shape,
+        scratch,
+        GRADIENT_FLOPS,
+        (qkv, grads, *operands),
+    )
+
+
+def exchange(packed):
+    return lax.all_to_all(packed, ("seq", "head"), split_axis=0, concat_axis=0, tiled=True)
+
+
+def body(queries, keys, values, out_grad):
+    qkv = exchange(pack(queries, keys, values))
+    grads = exchange(pack(out_grad))
+    kept = forward_part(qkv)
+    (attended,) = unpack(exchange(kept["attended"]))
+    value_gradient_array, query_grad, key_grad = unpack(
+        exchange(gradient_part(qkv, grads, kept))
+    )
+    return attended, query_grad, key_grad, value_gradient_array
+
+
 def solution(mesh):
-    return jax.shard_map(
-        body,
-        mesh=mesh,
-        in_specs=(
-            P(("seq", "head"), None),
-            P(("seq", "head"), None),
-            P(("seq", "head"), None),
-            P(("seq", "head"), None),
-        ),
-        out_specs=(
-            P(("seq", "head"), None),
-            P(("seq", "head"), None),
-            P(("seq", "head"), None),
-            P(("seq", "head"), None),
-        ),
-        check_vma=False,
-    )
+    placement = P(("seq", "head"), None)
+
+    def layer(queries, keys, values, out_grad):
+        one_head_each = queries.shape[1] // HD == mesh.size and queries.shape[0] == 8 * CHUNK
+        return jax.shard_map(
+            body if one_head_each else shared_body,
+            mesh=mesh,
+            in_specs=(placement,) * 4,
+            out_specs=(placement,) * 4,
+            check_vma=False,
+        )(queries, keys, values, out_grad)
+
+    return layer

time: 759 us -> 132 us (0.17)
  waiting for transfers between devices: 329 us -> 75.6 us
  blocking collectives: 201 us -> 0 us
  matrix products: 103 us -> 0 us
  local copies, waits for them, and re-layouts: 53.3 us -> 0.01 us
  Pallas kernels: 0 us -> 34.3 us
  other arithmetic: 26 us -> 0 us
  between operations: 16.5 us -> 0.89 us
    psum x2 -> x0, waiting for transfers between devices: 210 us -> none  [the longest x1 169 us: share_heads(): return lax.psum(slot_mask[:, None, None] * own_matrix[None], 'seq')]
    psum x2 -> x0, blocking collectives: 119 us -> none  [the longest x1 60.2 us: body(): lax.psum(jnp.sum(key_prob * key_direct_gradient, axis=-1), 'seq')]
    dot_general x89 -> x0, matrix products: 99.8 us -> none  [the longest x18 10.8 us: newton_inverse(): product = jnp.matmul(matrix, iterate, precision=precise_setting)]
    pmax x1 -> x0, blocking collectives: 59.9 us -> none  [body(): key_max = lax.pmax(jnp.max(key_score, axis=-1), 'seq')]
    reduce_scatter x2 -> x0, waiting for transfers between devices: 57.6 us -> none  [the longest x1 57.6 us: body(): lax.psum_scatter(mark_kgrad_f, 'seq', scatter_dimension=0, tiled=True)]
    all_to_all x6 -> x4, waiting for transfers between devices: 21.8 us -> 75.6 us  [exchange(): lax.all_to_all(packed, ('seq', 'head'), split_axis=0, concat_axis=0, tile...]
    all_gather x2 -> x0, waiting for transfers between devices: 40 us -> none  [the longest x1 34 us: body(): lax.all_gather(landmark(query_rows), 'seq', axis=0, tiled=True)]
    pallas_call x0 -> x6, Pallas kernels: none -> 34.3 us  [kernel_call(): pl.pallas_call(kernel, out_shape=out_shape, in_specs=[held if index == in...]
  transfers between devices with their start and end apart: 12 -> 4, of which waited for: 10 -> 3; matrix products, arithmetic and copies ran while one was open for 11% -> 0% of each run, Pallas kernels for 0% -> 23%
where the time goes in v5:
time: 132 us; the launch traced here: 131 us
  waiting for transfers between devices  75.6 us (57%)
  Pallas kernels  34.3 us (26%)
  starting transfers between devices  20.4 us (15%)
    all_to_all x4, waiting for transfers between devices, exchange(): lax.all_to_all(packed, ('seq', 'head'), split_axis=0, concat_axis=0, tile...  75.6 us
    pallas_call x6, Pallas kernels, kernel_call(): pl.pallas_call(kernel, out_shape=out_shape, in_specs=[held if index == in...  34.3 us
    all_to_all x4, starting transfers between devices, exchange(): lax.all_to_all(packed, ('seq', 'head'), split_axis=0, concat_axis=0, tile...  20.4 us
  transfers between devices with their start and end apart: 4, of which 3 were waited for; matrix products, arithmetic and copies ran while one was open for 0% of the time, Pallas kernels for 23%

profile of v5, /device:TPU:0, one launch (start us, length us, event | category | flops | bytes accessed | tf_op | source)
XLA Modules:
  0.0 131.3 jit_solution(7968943230108454548)
XLA Ops:
  0.6 2.4 %shard_map.75 = bf16[32,3,64,128]{3,2,1,0:T(8,128)(2,1)} custom-call(bf16[64,4096]{1,0:T(8,128)(2,1)} %refs_0_.2, bf16[64,4096]{1,0:T(8,128)(2,1)} %refs_1_.1, bf16[64,4096]{1,0:T(8,128)(2,1)} %refs_2_.1), custom_call_target="tpu_custom_call" | custom-call | bytes 1572864 | tf_op jit(solution)/shard_map/pallas_call | solution.py:683
  3.0 7.3 %all-to-all-start = ((bf16[32,3,64,128]{3,2,1,0:T(8,128)(2,1)}), bf16[32,3,64,128]{3,2,1,0:T(8,128)(2,1)S(1)}, u32[]{:S(2)}, u32[]{:S(2)}) async-start(bf16[32,3,64,128]{3,2,1,0:T(8,128)(2,1)} %shard_map.75), calls=%async_computation | async-start | bytes 3145728 | tf_op jit(solution)/shard_map/all_to_all | solution.py:800
  10.3 1.8 %shard_map.78 = bf16[32,1,64,128]{3,2,1,0:T(8,128)(2,1)} custom-call(bf16[64,4096]{1,0:T(8,128)(2,1)} %refs_0_.3), custom_call_target="tpu_custom_call" | custom-call | bytes 524288 | tf_op jit(solution)/shard_map/pallas_call | solution.py:683
  12.2 35.6 %all-to-all-done.qkv_hbm = bf16[32,3,64,128]{3,2,1,0:T(8,128)(2,1)S(1)} async-done(((bf16[32,3,64,128]{3,2,1,0:T(8,128)(2,1)}), bf16[32,3,64,128]{3,2,1,0:T(8,128)(2,1)S(1)}, u32[]{:S(2)}, u32[]{:S(2)}) %all-to-all-start) | async-done | bytes 1572896 | tf_op jit(solution)/shard_map/all_to_all | solution.py:800
  47.8 0.0 copy-start
  47.8 3.6 %all-to-all-start.2 = ((bf16[32,1,64,128]{3,2,1,0:T(8,128)(2,1)}), bf16[32,1,64,128]{3,2,1,0:T(8,128)(2,1)S(1)}, u32[]{:S(2)}, u32[]{:S(2)}) async-start(bf16[32,1,64,128]{3,2,1,0:T(8,128)(2,1)} %shard_map.78), calls=%async_computation.2 | async-start | bytes 1048576 | tf_op jit(solution)/shard_map/all_to_all | solution.py:800
  51.5 0.0 copy-done
  51.5 11.6 %shard_map.76 = (bf16[32,1,64,128]{3,2,1,0:T(8,128)(2,1)}, bf16[256,128]{1,0:T(8,128)(2,1)}, bf16[256,128]{1,0:T(8,128)(2,1)}, f32[256,256]{1,0:T(8,128)}, f32[8...) custom-call(bf16[32,3,64,128]{3,2,1,0:T(8,128)(2,1)} %copy-done), custom_call_target="tpu_custom_call" | custom-call | flops 10000000000 | bytes 1572864 | tf_op jit(solution)/shard_map/pallas_call | solution.py:683
  63.1 3.4 %all-to-all-done.2.grad_hbm = bf16[32,1,64,128]{3,2,1,0:T(8,128)(2,1)S(1)} async-done(((bf16[32,1,64,128]{3,2,1,0:T(8,128)(2,1)}), bf16[32,1,64,128]{3,2,1,0:T(8,128)(2,1)S(1)}, u32[]{:S(2)}, u32[]{:S(2)}) %all-to-all-start.2) | async-done | bytes 524320 | tf_op jit(solution)/shard_map/all_to_all | solution.py:800
  66.5 0.0 copy-start.1
  66.5 3.8 %all-to-all-start.1 = ((bf16[32,1,64,128]{3,2,1,0:T(8,128)(2,1)}), bf16[32,1,64,128]{3,2,1,0:T(8,128)(2,1)S(1)}, u32[]{:S(2)}, u32[]{:S(2)}) async-start(bf16[32,1,64,128]{3,2,1,0:T(8,128)(2,1)} %get-tuple-element.22), calls=%async_computation.1 | async-start | bytes 1048576 | tf_op jit(solution)/shard_map/all_to_all | solution.py:800
  70.3 0.0 copy-done.1
  70.3 16.4 %shard_map.79 = bf16[32,3,64,128]{3,2,1,0:T(8,128)(2,1)} custom-call(bf16[32,3,64,128]{3,2,1,0:T(8,128)(2,1)} %copy-done, bf16[32,1,64,128]{3,2,1,0:T(8,128)(2,1)} %copy-done.1, bf16[256,128]{1,0:T(8,128)(2,1)} %get-tuple-element.23.refs_0_, bf16[256,128]{1,0:T(8,128)(2,1)} %get-tuple-element.24.refs_1_, f32[256,256]{1,0:T(8,128)} %get-tuple-element.25.refs_2_, ...), custom_call_target="tpu_custom_call" | custom-call | flops 14000000000 | bytes 14749696 | tf_op jit(solution)/shard_map/pallas_call | solution.py:683
  86.7 0.0 all-to-all-done.1.packed_ref
  86.7 5.7 %all-to-all-start.3 = ((bf16[32,3,64,128]{3,2,1,0:T(8,128)(2,1)}), bf16[32,3,64,128]{3,2,1,0:T(8,128)(2,1)S(1)}, u32[]{:S(2)}, u32[]{:S(2)}) async-start(bf16[32,3,64,128]{3,2,1,0:T(8,128)(2,1)} %shard_map.79), calls=%async_computation.3 | async-start | bytes 3145728 | tf_op jit(solution)/shard_map/all_to_all | solution.py:800
  92.4 0.8 shard_map.77
  93.2 36.6 %all-to-all-done.3.packed_ref = bf16[32,3,64,128]{3,2,1,0:T(8,128)(2,1)S(1)} async-done(((bf16[32,3,64,128]{3,2,1,0:T(8,128)(2,1)}), bf16[32,3,64,128]{3,2,1,0:T(8,128)(2,1)S(1)}, u32[]{:S(2)}, u32[]{:S(2)}) %all-to-all-start.3) | async-done | bytes 1572896 | tf_op jit(solution)/shard_map/all_to_all | solution.py:800
  129.9 1.3 shard_map.80
Async XLA Ops:
  3.0 44.8 %all-to-all-start = ((bf16[32,3,64,128]{3,2,1,0:T(8,128)(2,1)}), bf16[32,3,64,128]{3,2,1,0:T(8,128)(2,1)S(1)}, u32[]{:S(2)}, u32[]{:S(2)}) async-start(bf16[32,3,64,128]{3,2,1,0:T(8,128)(2,1)} %shard_map.75), calls=%async_computation | async-start | bytes 3145728 | tf_op jit(solution)/shard_map/all_to_all | solution.py:800
  47.8 3.6 %copy-start = (bf16[32,3,64,128]{3,2,1,0:T(8,128)(2,1)}, bf16[32,3,64,128]{3,2,1,0:T(8,128)(2,1)S(1)}, u32[]{:S(2)}) copy-start(bf16[32,3,64,128]{3,2,1,0:T(8,128)(2,1)S(1)} %all-to-all-done.qkv_hbm) | copy-start | bytes 4718596
  47.8 18.6 %all-to-all-start.2 = ((bf16[32,1,64,128]{3,2,1,0:T(8,128)(2,1)}), bf16[32,1,64,128]{3,2,1,0:T(8,128)(2,1)S(1)}, u32[]{:S(2)}, u32[]{:S(2)}) async-start(bf16[32,1,64,128]{3,2,1,0:T(8,128)(2,1)} %shard_map.78), calls=%async_computation.2 | async-start | bytes 1048576 | tf_op jit(solution)/shard_map/all_to_all | solution.py:800
  66.5 3.8 %copy-start.1 = (bf16[32,1,64,128]{3,2,1,0:T(8,128)(2,1)}, bf16[32,1,64,128]{3,2,1,0:T(8,128)(2,1)S(1)}, u32[]{:S(2)}) copy-start(bf16[32,1,64,128]{3,2,1,0:T(8,128)(2,1)S(1)} %all-to-all-done.2.grad_hbm) | copy-start | bytes 1572868
  66.5 20.2 %all-to-all-start.1 = ((bf16[32,1,64,128]{3,2,1,0:T(8,128)(2,1)}), bf16[32,1,64,128]{3,2,1,0:T(8,128)(2,1)S(1)}, u32[]{:S(2)}, u32[]{:S(2)}) async-start(bf16[32,1,64,128]{3,2,1,0:T(8,128)(2,1)} %get-tuple-element.22), calls=%async_computation.1 | async-start | bytes 1048576 | tf_op jit(solution)/shard_map/all_to_all | solution.py:800
  86.7 43.1 %all-to-all-start.3 = ((bf16[32,3,64,128]{3,2,1,0:T(8,128)(2,1)}), bf16[32,3,64,128]{3,2,1,0:T(8,128)(2,1)S(1)}, u32[]{:S(2)}, u32[]{:S(2)}) async-start(bf16[32,3,64,128]{3,2,1,0:T(8,128)(2,1)} %shard_map.79), calls=%async_computation.3 | async-start | bytes 3145728 | tf_op jit(solution)/shard_map/all_to_all | solution.py:800

commit v6 on v5

--- a/solution.py
+++ b/solution.py
@@ -11,7 +11,7 @@
 M = 256
 PINV_ITERS = 6
 CHUNK = 256
-PACK_GROUPS = 4
+PACK_GROUPS = 8
 SWEEP_NAMES = ("pair", "weight", "growth")
 VMEM_LIMIT = 60 * 2**20
 SMALL_LIMIT = 16 * 2**20
@@ -520,16 +520,13 @@
             reads[name].wait()
 
     fetch_grads.start()
-    start("token_prob", "inverse", "mark_values", "mark_prob", "factor")
+    start("token_prob", "mixing_low", "mark_k", "turned", "inverse")
+    start("mark_values", "mark_prob", "factor")
     for copy in sweeps[0]:
         copy.start()
     fetch_values.start()
-    start("key_prob")
-    for copies in sweeps[1:3]:
-        for copy in copies:
-            copy.start()
-    start("mark_q", "turned", "mark_k", "mixing_low")
-    for copies in sweeps[3:]:
+    start("key_prob", "mark_q")
+    for copies in sweeps[1:]:
         for copy in copies:
             copy.start()
     start("last_growth")
@@ -544,23 +541,6 @@
 
     def block(ref, index):
         return ref[index * per : (index + 1) * per].reshape(CHUNK, HD)
-
-    fetch_grads.wait()
-    grads_turned = grads_s[...].reshape(tokens, HD).T
-    wait("token_prob")
-    mixing_grad = wide_dot(grads_turned, held["token_prob"][...].astype(jnp.bfloat16))
-    wait("inverse", "mark_values", "mark_prob", "factor")
-    values_low = split_dot(
-        halves(mixing_grad), (held["inverse"][0], held["inverse"][1])
-    ).astype(jnp.bfloat16)
-    mark_prob = held["mark_prob"][...]
-    mark_halves = halves(mark_prob)
-    factor = held["factor"][0:1, 0:1]
-    inverse_grad = split_dot(halves(mixing_grad.T), halves(held["mark_values"][...]))
-    inverse_grad_halves = halves(inverse_grad)
-    toward = split_dot(mark_halves, inverse_grad_halves) * factor
-    power = 0.5 * (toward + toward.T)
-    growth = None
 
     row_totals, query_sums, key_sums = [], [], []
 
@@ -599,22 +579,45 @@
     work = iter(
         [
             (unit, range(first, min(chunks, first + span)))
-            for unit in (key_rows, key_side, token_side)
+            for unit in (token_side, key_rows, key_side)
             for first in range(0, chunks, span)
         ]
     )
 
     def beside():
-        unit, indices = next(work)
+        unit, indices = next(work, (None, ()))
         for index in indices:
             unit(index)
 
+    fetch_grads.wait()
+    grads_turned = grads_s[...].reshape(tokens, HD).T
+    wait("token_prob")
+    mixing_grad = wide_dot(grads_turned, held["token_prob"][...].astype(jnp.bfloat16))
+    wait("mixing_low", "mark_k", "turned", "inverse", "mark_values", "mark_prob", "factor")
+    beside()
+    values_low = split_dot(
+        halves(mixing_grad), (held["inverse"][0], held["inverse"][1])
+    ).astype(jnp.bfloat16)
+    mark_prob = held["mark_prob"][...]
+    mark_halves = halves(mark_prob)
+    factor = held["factor"][0:1, 0:1]
+    inverse_grad = split_dot(halves(mixing_grad.T), halves(held["mark_values"][...]))
+    inverse_grad_halves = halves(inverse_grad)
+    beside()
+    toward = split_dot(mark_halves, inverse_grad_halves) * factor
+    power = 0.5 * (toward + toward.T)
+    growth = None
+
+    sent = []
     for sweep in range(PINV_ITERS):
-        if sweep == 0:
+        if sweep == 1:
             fetch_values.wait()
-            wait("key_prob")
-        if sweep == 2:
-            wait("mark_q", "turned", "mark_k", "mixing_low")
+            wait("key_prob", "mark_q")
+        if sweep == 3:
+            sent.append(
+                pltpu.make_async_copy(out_ref.at[:, 0], home.at[:, 0], out_done.at[chunks])
+            )
+            sent[0].start()
         for copy in sweeps[sweep]:
             copy.wait()
         pair_ref, weight_ref, growth_ref = (held[name] for name in SWEEP_NAMES)
@@ -657,7 +660,6 @@
         marks_dot(mark_sgrad.T, held["mark_q"][...]) + sum(key_sums[1:], key_sums[0]).T
     ) * marks_scale
 
-    writes = []
     for index, place in enumerate(places):
         group = slice(index * per, (index + 1) * per)
         marked = slice(index * marks_per, (index + 1) * marks_per)
@@ -665,15 +667,12 @@
             wide = jnp.broadcast_to(marks[marked][:, None], (marks_per, segment_len, HD))
             total = direct[place] + wide.reshape(CHUNK, HD)
             out_ref[group, slot] = total.astype(jnp.bfloat16).reshape(per, rows, HD)
-        write = pltpu.make_async_copy(
-            out_ref.at[pl.ds(index * per, per)],
-            home.at[pl.ds(index * per, per)],
-            out_done.at[index],
-        )
-        write.start()
-        writes.append(write)
-    for write in writes:
-        write.wait()
+        ends = pl.ds(index * per, per), pl.ds(1, 2)
+        copy = pltpu.make_async_copy(out_ref.at[ends], home.at[ends], out_done.at[index])
+        copy.start()
+        sent.append(copy)
+    for copy in sent:
+        copy.wait()
 
 
 def kernel_call(kernel, out_shape, scratch, flops, operands, limit=VMEM_LIMIT, in_place=None):
@@ -785,7 +784,7 @@
         pltpu.VMEM((tokens, M), jnp.float32),
         pltpu.SemaphoreType.DMA((len(names) + 2,)),
         pltpu.SemaphoreType.DMA((len(SWEEP_NAMES), PINV_ITERS)),
-        pltpu.SemaphoreType.DMA((tokens // CHUNK,)),
+        pltpu.SemaphoreType.DMA((tokens // CHUNK + 1,)),
     ]
     return kernel_call(
         functools.partial(gradient_kernel, names),

time: 132 us -> 132 us (level)
  transfers between devices with their start and end apart: 4 -> 4, of which waited for: 3 -> 3; matrix products, arithmetic and copies ran while one was open for 0% -> 0% of each run, Pallas kernels for 23% -> 24%
where the time goes in v6:
time: 132 us
  waiting for transfers between devices  75.6 us (57%)
  Pallas kernels  34.8 us (26%)
  starting transfers between devices  20.4 us (15%)
    all_to_all x4, waiting for transfers between devices, exchange(): lax.all_to_all(packed, ('seq', 'head'), split_axis=0, concat_axis=0, tile...  75.6 us
    pallas_call x6, Pallas kernels, kernel_call(): pl.pallas_call(kernel, out_shape=out_shape, in_specs=[held if index == in...  34.8 us
    all_to_all x4, starting transfers between devices, exchange(): lax.all_to_all(packed, ('seq', 'head'), split_axis=0, concat_axis=0, tile...  20.4 us
  transfers between devices with their start and end apart: 4, of which 3 were waited for; matrix products, arithmetic and copies ran while one was open for 0% of the time, Pallas kernels for 24%

profile of v6, /device:TPU:0, one launch (start us, length us, event | category | flops | bytes accessed | tf_op | source)
XLA Modules:
  0.0 131.7 jit_solution(12098502645132586895)
XLA Ops:
  0.6 2.4 %shard_map.75 = bf16[32,3,64,128]{3,2,1,0:T(8,128)(2,1)} custom-call(bf16[64,4096]{1,0:T(8,128)(2,1)} %refs_0_.2, bf16[64,4096]{1,0:T(8,128)(2,1)} %refs_1_.1, bf16[64,4096]{1,0:T(8,128)(2,1)} %refs_2_.1), custom_call_target="tpu_custom_call" | custom-call | bytes 1572864 | tf_op jit(solution)/shard_map/pallas_call | solution.py:682
  3.1 7.3 %all-to-all-start = ((bf16[32,3,64,128]{3,2,1,0:T(8,128)(2,1)}), bf16[32,3,64,128]{3,2,1,0:T(8,128)(2,1)S(1)}, u32[]{:S(2)}, u32[]{:S(2)}) async-start(bf16[32,3,64,128]{3,2,1,0:T(8,128)(2,1)} %shard_map.75), calls=%async_computation | async-start | bytes 3145728 | tf_op jit(solution)/shard_map/all_to_all | solution.py:799
  10.4 1.8 %shard_map.78 = bf16[32,1,64,128]{3,2,1,0:T(8,128)(2,1)} custom-call(bf16[64,4096]{1,0:T(8,128)(2,1)} %refs_0_.3), custom_call_target="tpu_custom_call" | custom-call | bytes 524288 | tf_op jit(solution)/shard_map/pallas_call | solution.py:682
  12.2 35.6 %all-to-all-done.qkv_hbm = bf16[32,3,64,128]{3,2,1,0:T(8,128)(2,1)S(1)} async-done(((bf16[32,3,64,128]{3,2,1,0:T(8,128)(2,1)}), bf16[32,3,64,128]{3,2,1,0:T(8,128)(2,1)S(1)}, u32[]{:S(2)}, u32[]{:S(2)}) %all-to-all-start) | async-done | bytes 1572896 | tf_op jit(solution)/shard_map/all_to_all | solution.py:799
  47.9 0.0 copy-start
  47.9 3.6 %all-to-all-start.2 = ((bf16[32,1,64,128]{3,2,1,0:T(8,128)(2,1)}), bf16[32,1,64,128]{3,2,1,0:T(8,128)(2,1)S(1)}, u32[]{:S(2)}, u32[]{:S(2)}) async-start(bf16[32,1,64,128]{3,2,1,0:T(8,128)(2,1)} %shard_map.78), calls=%async_computation.2 | async-start | bytes 1048576 | tf_op jit(solution)/shard_map/all_to_all | solution.py:799
  51.5 0.0 copy-done
  51.5 11.6 %shard_map.76 = (bf16[32,1,64,128]{3,2,1,0:T(8,128)(2,1)}, bf16[256,128]{1,0:T(8,128)(2,1)}, bf16[256,128]{1,0:T(8,128)(2,1)}, f32[256,256]{1,0:T(8,128)}, f32[8...) custom-call(bf16[32,3,64,128]{3,2,1,0:T(8,128)(2,1)} %copy-done), custom_call_target="tpu_custom_call" | custom-call | flops 10000000000 | bytes 1572864 | tf_op jit(solution)/shard_map/pallas_call | solution.py:682
  63.1 3.4 %all-to-all-done.2.grad_hbm = bf16[32,1,64,128]{3,2,1,0:T(8,128)(2,1)S(1)} async-done(((bf16[32,1,64,128]{3,2,1,0:T(8,128)(2,1)}), bf16[32,1,64,128]{3,2,1,0:T(8,128)(2,1)S(1)}, u32[]{:S(2)}, u32[]{:S(2)}) %all-to-all-start.2) | async-done | bytes 524320 | tf_op jit(solution)/shard_map/all_to_all | solution.py:799
  66.5 0.0 copy-start.1
  66.5 3.8 %all-to-all-start.1 = ((bf16[32,1,64,128]{3,2,1,0:T(8,128)(2,1)}), bf16[32,1,64,128]{3,2,1,0:T(8,128)(2,1)S(1)}, u32[]{:S(2)}, u32[]{:S(2)}) async-start(bf16[32,1,64,128]{3,2,1,0:T(8,128)(2,1)} %get-tuple-element.22), calls=%async_computation.1 | async-start | bytes 1048576 | tf_op jit(solution)/shard_map/all_to_all | solution.py:799
  70.3 0.0 copy-done.1
  70.3 16.7 %shard_map.79 = bf16[32,3,64,128]{3,2,1,0:T(8,128)(2,1)} custom-call(bf16[32,3,64,128]{3,2,1,0:T(8,128)(2,1)} %copy-done, bf16[32,1,64,128]{3,2,1,0:T(8,128)(2,1)} %copy-done.1, bf16[256,128]{1,0:T(8,128)(2,1)} %get-tuple-element.23.refs_0_, bf16[256,128]{1,0:T(8,128)(2,1)} %get-tuple-element.24.refs_1_, f32[256,256]{1,0:T(8,128)} %get-tuple-element.25.refs_2_, ...), custom_call_target="tpu_custom_call" | custom-call | flops 14000000000 | bytes 14749696 | tf_op jit(solution)/shard_map/pallas_call | solution.py:682
  87.1 0.0 all-to-all-done.1.packed_ref
  87.1 5.7 %all-to-all-start.3 = ((bf16[32,3,64,128]{3,2,1,0:T(8,128)(2,1)}), bf16[32,3,64,128]{3,2,1,0:T(8,128)(2,1)S(1)}, u32[]{:S(2)}, u32[]{:S(2)}) async-start(bf16[32,3,64,128]{3,2,1,0:T(8,128)(2,1)} %shard_map.79), calls=%async_computation.3 | async-start | bytes 3145728 | tf_op jit(solution)/shard_map/all_to_all | solution.py:799
  92.7 0.9 shard_map.77
  93.6 36.6 %all-to-all-done.3.packed_ref = bf16[32,3,64,128]{3,2,1,0:T(8,128)(2,1)S(1)} async-done(((bf16[32,3,64,128]{3,2,1,0:T(8,128)(2,1)}), bf16[32,3,64,128]{3,2,1,0:T(8,128)(2,1)S(1)}, u32[]{:S(2)}, u32[]{:S(2)}) %all-to-all-start.3) | async-done | bytes 1572896 | tf_op jit(solution)/shard_map/all_to_all | solution.py:799
  130.2 1.3 %shard_map.80 = (bf16[64,4096]{1,0:T(8,128)(2,1)}, bf16[64,4096]{1,0:T(8,128)(2,1)}, bf16[64,4096]{1,0:T(8,128)(2,1)}) custom-call(bf16[32,3,64,128]{3,2,1,0:T(8,128)(2,1)S(1)} %all-to-all-done.3.packed_ref), custom_call_target="tpu_custom_call" | custom-call | bytes 1572864 | tf_op jit(solution)/shard_map/pallas_call | solution.py:682
Async XLA Ops:
  3.1 44.8 %all-to-all-start = ((bf16[32,3,64,128]{3,2,1,0:T(8,128)(2,1)}), bf16[32,3,64,128]{3,2,1,0:T(8,128)(2,1)S(1)}, u32[]{:S(2)}, u32[]{:S(2)}) async-start(bf16[32,3,64,128]{3,2,1,0:T(8,128)(2,1)} %shard_map.75), calls=%async_computation | async-start | bytes 3145728 | tf_op jit(solution)/shard_map/all_to_all | solution.py:799
  47.9 3.6 %copy-start = (bf16[32,3,64,128]{3,2,1,0:T(8,128)(2,1)}, bf16[32,3,64,128]{3,2,1,0:T(8,128)(2,1)S(1)}, u32[]{:S(2)}) copy-start(bf16[32,3,64,128]{3,2,1,0:T(8,128)(2,1)S(1)} %all-to-all-done.qkv_hbm) | copy-start | bytes 4718596
  47.9 18.6 %all-to-all-start.2 = ((bf16[32,1,64,128]{3,2,1,0:T(8,128)(2,1)}), bf16[32,1,64,128]{3,2,1,0:T(8,128)(2,1)S(1)}, u32[]{:S(2)}, u32[]{:S(2)}) async-start(bf16[32,1,64,128]{3,2,1,0:T(8,128)(2,1)} %shard_map.78), calls=%async_computation.2 | async-start | bytes 1048576 | tf_op jit(solution)/shard_map/all_to_all | solution.py:799
  66.5 3.8 %copy-start.1 = (bf16[32,1,64,128]{3,2,1,0:T(8,128)(2,1)}, bf16[32,1,64,128]{3,2,1,0:T(8,128)(2,1)S(1)}, u32[]{:S(2)}) copy-start(bf16[32,1,64,128]{3,2,1,0:T(8,128)(2,1)S(1)} %all-to-all-done.2.grad_hbm) | copy-start | bytes 1572868
  66.5 20.6 %all-to-all-start.1 = ((bf16[32,1,64,128]{3,2,1,0:T(8,128)(2,1)}), bf16[32,1,64,128]{3,2,1,0:T(8,128)(2,1)S(1)}, u32[]{:S(2)}, u32[]{:S(2)}) async-start(bf16[32,1,64,128]{3,2,1,0:T(8,128)(2,1)} %get-tuple-element.22), calls=%async_computation.1 | async-start | bytes 1048576 | tf_op jit(solution)/shard_map/all_to_all | solution.py:799
  87.1 43.1 %all-to-all-start.3 = ((bf16[32,3,64,128]{3,2,1,0:T(8,128)(2,1)}), bf16[32,3,64,128]{3,2,1,0:T(8,128)(2,1)S(1)}, u32[]{:S(2)}, u32[]{:S(2)}) async-start(bf16[32,3,64,128]{3,2,1,0:T(8,128)(2,1)} %shard_map.79), calls=%async_computation.3 | async-start | bytes 3145728 | tf_op jit(solution)/shard_map/all_to_all | solution.py:799

commit v7 on v0

--- a/solution.py
+++ b/solution.py
@@ -1,11 +1,24 @@
+import functools
+from types import SimpleNamespace
+
 import jax
 import jax.numpy as jnp
 from jax import lax
+from jax.experimental import pallas as pl
+from jax.experimental.pallas import tpu as pltpu
 from jax.sharding import PartitionSpec as P
 
 HD = 128
 M = 256
 PINV_ITERS = 6
+CHUNK = 256
+PACK_GROUPS = 4
+HALF = M // 2
+SWAP = ((0, 1), (1, 0))
+VMEM_LIMIT = 60 * 2**20
+SMALL_LIMIT = 16 * 2**20
+WHOLE, LEAD, GROUPS = range(3)
+SLOTS = (10, 11)
 
 
 precise_setting = lax.Precision.HIGHEST
@@ -31,7 +44,7 @@
     return lax.psum(slot_mask[:, None, None] * own_matrix[None], "seq")
 
 
-def body(queries, keys, values, out_grad):
+def shared_body(queries, keys, values, out_grad):
     query_rows, key_rows, value_rows, grad_rows = (
         lax.all_to_all(queries, "head", split_axis=1, concat_axis=0, tiled=True),
         lax.all_to_all(keys, "head", split_axis=1, concat_axis=0, tiled=True),
@@ -225,21 +238,760 @@
     return (attended_out, query_out, key_out, value_out)
 
 
+def halves(matrix):
+    high = matrix.astype(jnp.bfloat16)
+    return high, (matrix - high.astype(jnp.float32)).astype(jnp.bfloat16)
+
+
+def wide_dot(left, right):
+    return jnp.dot(left, right, preferred_element_type=jnp.float32)
+
+
+def wide_dot_nt(left, right):
+    return lax.dot_general(
+        left, right, (((1,), (1,)), ((), ())), preferred_element_type=jnp.float32
+    )
+
+
+def split_dot(left, right):
+    left_high, left_low = left
+    right_high, right_low = right
+    return wide_dot(
+        jnp.concatenate([left_high, left_high, left_low], axis=1),
+        jnp.concatenate([right_high, right_low, right_high], axis=0),
+    )
+
+
+def split_dot_nt(left, right):
+    left_high, left_low = left
+    right_high, right_low = right
+    return wide_dot_nt(
+        jnp.concatenate([left_high, left_high, left_low], axis=1),
+        jnp.concatenate([right_high, right_low, right_high], axis=1),
+    )
+
+
+def identity_matrix():
+    return (
+        lax.broadcasted_iota(jnp.int32, (M, M), 0) == lax.broadcasted_iota(jnp.int32, (M, M), 1)
+    ).astype(jnp.float32)
+
+
+def chunk_of(ref, array, slot, index):
+    per = CHUNK // ref.shape[3]
+    return ref[index * per : (index + 1) * per, array, slot].reshape(CHUNK, HD)
+
+
+def store_chunk(ref, lead, index, value):
+    rows = ref.shape[-2]
+    per = CHUNK // rows
+    ref[(slice(index * per, (index + 1) * per), *lead)] = value.reshape(per, rows, HD)
+
+
+def all_tokens(ref, array, slot):
+    return ref[:, array, slot].reshape(ref.shape[0] * ref.shape[3], HD)
+
+
+def tokens_of(ref):
+    return ref.shape[0] * ref.shape[3]
+
+
+def columns(index):
+    return pl.ds(pl.multiple_of(index * CHUNK, CHUNK), CHUNK)
+
+
+def swap_lanes(matrix):
+    return jnp.concatenate([matrix[:, HALF:], matrix[:, :HALF]], axis=1)
+
+
+def thirds(rows):
+    first = rows.astype(jnp.bfloat16).astype(jnp.float32)
+    second = (rows - first).astype(jnp.bfloat16).astype(jnp.float32)
+    return jnp.concatenate([first, second, rows - first - second], axis=0)
+
+
+def joined_thirds(rows):
+    count = rows.shape[0] // 3
+    return rows[:count] + (rows[count : 2 * count] + rows[2 * count :])
+
+
+def held_shape(kind, shape):
+    return shape[1:] if kind in SLOTS else shape
+
+
+def pieces_of(kind, shape):
+    if kind == LEAD:
+        return [(index,) for index in range(shape[0])]
+    if kind == GROUPS:
+        per = CHUNK // shape[-2]
+        return [(slice(place, place + per),) for place in range(0, shape[0], per)]
+    return [()]
+
+
+def window(ref, piece):
+    place = tuple(
+        pl.ds(part.start, part.stop - part.start) if isinstance(part, slice) else part
+        for part in piece
+    )
+    return ref.at[place] if place else ref
+
+
+class Staged:
+    def __init__(self, names, kinds, outer, inner, done, outward):
+        self.refs = SimpleNamespace(**dict(zip(names, inner)))
+        self.copies, self.order = [], []
+        count = 0
+        steps = []
+        for place, (kind, home, held) in enumerate(zip(kinds, outer, inner)):
+            home = home.at[kind - SLOTS[0]] if kind in SLOTS else home
+            copies = {}
+            for step, piece in enumerate(pieces_of(kind, held.shape)):
+                ends = (window(held, piece), window(home, piece))
+                source, target = ends if outward else ends[::-1]
+                key = tuple(
+                    part.start if isinstance(part, slice) else part for part in piece
+                )
+                copies[key] = pltpu.make_async_copy(source, target, done.at[count])
+                steps.append((step if kind != WHOLE else -1, place, key))
+                count += 1
+            self.copies.append(copies)
+        self.inner = inner
+        self.order = sorted(steps, key=lambda item: item[:2])
+        self.started, self.waited = set(), set()
+
+    def place_of(self, ref):
+        return next(index for index, held in enumerate(self.inner) if held is ref)
+
+    def start(self, ref=None, *key):
+        chosen = [
+            (place, name)
+            for _, place, name in self.order
+            if (ref is None or place == self.place_of(ref)) and (not key or name == key)
+        ]
+        for item in chosen:
+            if item not in self.started:
+                self.started.add(item)
+                self.copies[item[0]][item[1]].start()
+
+    def wait(self, ref=None, *key):
+        chosen = [
+            (place, name)
+            for _, place, name in self.order
+            if (ref is None or place == self.place_of(ref)) and (not key or name == key)
+        ]
+        for item in chosen:
+            if item not in self.waited:
+                self.waited.add(item)
+                self.copies[item[0]][item[1]].wait()
+
+
+def staged_call(compute, inputs, outputs, flops, extra=(), after=(), in_place=False):
+    names_in, names_out = tuple(inputs), tuple(outputs)
+    kinds_in = [x[1] if isinstance(x, tuple) else WHOLE for x in inputs.values()]
+    kinds_out = [x[1] if isinstance(x, tuple) else WHOLE for x in outputs.values()]
+    operands = tuple(x[0] if isinstance(x, tuple) else x for x in inputs.values())
+    shapes = tuple(x[0] if isinstance(x, tuple) else x for x in outputs.values())
+    n_in, n_out, n_after = len(operands), len(shapes), len(after)
+    moved = sum(x.size * x.dtype.itemsize for x in (*operands, *shapes))
+    anywhere = pl.BlockSpec(memory_space=pl.ANY)
+
+    def count(kinds, arrays):
+        return sum(len(pieces_of(kind, x.shape)) for kind, x in zip(kinds, arrays))
+
+    def kernel(*refs):
+        sources, refs = refs[:n_in], refs[n_in + n_after :]
+        homes, refs = refs[:n_out], refs[n_out:]
+        held_in, held_out = refs[:n_in], refs[n_in : n_in + n_out]
+        *scratch, in_done, out_done = refs[n_in + n_out :]
+        reads = Staged(names_in, kinds_in, sources, held_in, in_done, False)
+        writes = Staged(names_out, kinds_out, homes, held_out, out_done, True)
+        reads.start()
+        compute(reads.refs, writes.refs, reads.wait, writes.start, *scratch)
+        reads.wait()
+        writes.start()
+        writes.wait()
+
+    results = pl.pallas_call(
+        kernel,
+        out_shape=shapes,
+        in_specs=[anywhere] * (n_in + n_after),
+        out_specs=(anywhere,) * n_out,
+        scratch_shapes=[
+            *(
+                pltpu.VMEM(held_shape(kind, x.shape), x.dtype)
+                for kind, x in zip((*kinds_in, *kinds_out), (*operands, *shapes))
+            ),
+            *extra,
+            pltpu.SemaphoreType.DMA((count(kinds_in, operands),)),
+            pltpu.SemaphoreType.DMA((count(kinds_out, shapes),)),
+        ],
+        compiler_params=pltpu.CompilerParams(vmem_limit_bytes=VMEM_LIMIT),
+        cost_estimate=pl.CostEstimate(
+            flops=int(flops * 10**9), bytes_accessed=moved, transcendentals=0
+        ),
+    )(*operands, *after)
+    return SimpleNamespace(**dict(zip(outputs, results)))
+
+
+def low(*shape):
+    return jax.ShapeDtypeStruct(shape, jnp.bfloat16)
+
+
+def wide(*shape):
+    return jax.ShapeDtypeStruct(shape, jnp.float32)
+
+
+def pack_kernel(half_ref, first_ref, second_ref, out_ref, rows_s, packed_s, in_done, out_done):
+    half = half_ref[0]
+    pairs = out_ref.shape[0]
+    group = pairs // PACK_GROUPS
+    span = 2 * HD
+    reads, writes = [], []
+    for index in range(PACK_GROUPS):
+        for array, ref in enumerate((first_ref, second_ref)):
+            place = pl.ds(index * group * span, group * span)
+            reads.append(
+                pltpu.make_async_copy(
+                    ref.at[:, place], rows_s.at[array, :, place], in_done.at[array, index]
+                )
+            )
+        place = pl.ds(index * group, group)
+        writes.append(
+            pltpu.make_async_copy(packed_s.at[place], out_ref.at[place], out_done.at[index])
+        )
+    for copy in reads:
+        copy.start()
+    for index in range(PACK_GROUPS):
+        for array in range(2):
+            reads[2 * index + array].wait()
+            for pair in range(index * group, (index + 1) * group):
+                start = pair * span
+                packed_s[pair, array, half] = rows_s[array, :, start : start + HD]
+                packed_s[pair, array, 1 - half] = rows_s[array, :, start + HD : start + span]
+        writes[index].start()
+    for copy in writes:
+        copy.wait()
+
+
+def unpack_kernel(half_ref, packed_ref, first_ref, second_ref, rows_s, out_done):
+    half = half_ref[0]
+    pairs = packed_ref.shape[0]
+    group = pairs // PACK_GROUPS
+    span = 2 * HD
+    writes = []
+    for index in range(PACK_GROUPS):
+        for array, ref in enumerate((first_ref, second_ref)):
+            for pair in range(index * group, (index + 1) * group):
+                start = pair * span
+                rows_s[array, :, start : start + HD] = packed_ref[pair, array, half]
+                rows_s[array, :, start + HD : start + span] = packed_ref[pair, array, 1 - half]
+            place = pl.ds(index * group * span, group * span)
+            write = pltpu.make_async_copy(
+                rows_s.at[array, :, place], ref.at[:, place], out_done.at[array, index]
+            )
+            write.start()
+            writes.append(write)
+    for copy in writes:
+        copy.wait()
+
+
+def layout_call(kernel, half, operands, out_shape, scratch, in_space, limit):
+    anywhere = pl.BlockSpec(memory_space=pl.ANY)
+    moved = 2 * sum(x.size * x.dtype.itemsize for x in operands)
+    return pl.pallas_call(
+        kernel,
+        out_shape=out_shape,
+        in_specs=[pl.BlockSpec(memory_space=pltpu.SMEM)]
+        + [pl.BlockSpec(memory_space=in_space)] * len(operands),
+        out_specs=jax.tree.map(lambda _: anywhere, out_shape),
+        scratch_shapes=scratch,
+        compiler_params=pltpu.CompilerParams(vmem_limit_bytes=limit),
+        cost_estimate=pl.CostEstimate(flops=0, bytes_accessed=moved, transcendentals=0),
+    )(half, *operands)
+
+
+def pack(half, first, second):
+    rows, width = first.shape
+    shape = low(width // (2 * HD), 2, 2, rows, HD)
+    scratch = [
+        pltpu.VMEM((2, rows, width), jnp.bfloat16),
+        pltpu.VMEM(shape.shape, jnp.bfloat16),
+        pltpu.SemaphoreType.DMA((2, PACK_GROUPS)),
+        pltpu.SemaphoreType.DMA((PACK_GROUPS,)),
+    ]
+    return layout_call(
+        pack_kernel, half, (first, second), shape, scratch, pl.ANY, VMEM_LIMIT
+    )
+
+
+def unpack(half, packed):
+    pairs, _, _, rows, _ = packed.shape
+    shape = low(rows, pairs * 2 * HD)
+    scratch = [
+        pltpu.VMEM((2, *shape.shape), jnp.bfloat16),
+        pltpu.SemaphoreType.DMA((2, PACK_GROUPS)),
+    ]
+    return layout_call(
+        unpack_kernel, half, (packed,), (shape, shape), scratch, pltpu.VMEM, SMALL_LIMIT
+    )
+
+
+def landmark_kernel(qk_ref, marks_ref):
+    tokens = tokens_of(qk_ref)
+    segment_len = tokens // HALF
+    per = CHUNK // segment_len
+    member = (
+        lax.broadcasted_iota(jnp.int32, (per, CHUNK), 1) // segment_len
+        == lax.broadcasted_iota(jnp.int32, (per, CHUNK), 0)
+    ).astype(jnp.bfloat16)
+    kinds = [(slot, array) for slot in range(2) for array in range(2)]
+    for index in range(tokens // CHUNK):
+        parts = [chunk_of(qk_ref, array, slot, index) for slot, array in kinds]
+        summed = wide_dot(member, jnp.concatenate(parts, axis=1))
+        mean = (summed / segment_len).astype(jnp.bfloat16)
+        for place, (slot, array) in enumerate(kinds):
+            marks_ref[slot, array, index * per : (index + 1) * per] = mean[
+                :, place * HD : (place + 1) * HD
+            ]
+
+
+def landmarks_of(qk):
+    held = pl.BlockSpec(memory_space=pltpu.VMEM)
+    return pl.pallas_call(
+        landmark_kernel,
+        out_shape=low(2, 2, HALF, HD),
+        in_specs=[held],
+        out_specs=held,
+        compiler_params=pltpu.CompilerParams(vmem_limit_bytes=SMALL_LIMIT),
+        cost_estimate=pl.CostEstimate(
+            flops=2 * 10**8, bytes_accessed=qk.size * 2, transcendentals=0
+        ),
+    )(qk)
+
+
+def sweep_forward(power_s, iterate_s, saved, sweep, work):
+    pair_ref, weight_ref, growth_ref = saved
+    power = power_s[...]
+    power_high, power_low = halves(power)
+    square = split_dot((power_high, power_low), (power_high, power_low))
+    next(work)()
+    square_halves = halves(square)
+    pair = (
+        jnp.concatenate([power_high, square_halves[0]], axis=0),
+        jnp.concatenate([power_low, square_halves[1]], axis=0),
+    )
+    pair_ref[sweep, 0], pair_ref[sweep, 1] = pair
+    higher = split_dot(pair, square_halves)
+    next(work)()
+    cube, fourth = higher[:M], higher[M:]
+    weight = halves(0.25 * (13.0 * identity_matrix() - 15.0 * power + 7.0 * square - cube))
+    power_s[...] = 0.25 * (13.0 * power - 15.0 * square + 7.0 * cube - fourth)
+    weight_ref[sweep, 0], weight_ref[sweep, 1] = weight
+    iterate = halves(iterate_s[...])
+    growth_ref[sweep, 0], growth_ref[sweep, 1] = iterate[0][M:], iterate[1][M:]
+    iterate_s[...] = split_dot(iterate, weight)
+
+
+def probability_compute(ins, outs, need, put, power_s, iterate_s):
+    need()
+    qk_ref = ins.qk
+    chunks = tokens_of(qk_ref) // CHUNK
+    score_scale = HD ** (-0.5)
+    for slot in range(2):
+        for array in range(2):
+            outs.marks[slot, array] = jnp.concatenate(
+                [ins.mine[slot, array], ins.theirs[1 - slot, array]], axis=0
+            )
+    put(outs.marks)
+    landmark_q, landmark_k = outs.marks[0, 0], outs.marks[0, 1]
+    mark_score = wide_dot_nt(landmark_q, landmark_k) * score_scale
+    mark_exp = jnp.exp(mark_score - jnp.max(mark_score, axis=1, keepdims=True))
+    mark_prob = mark_exp / jnp.sum(mark_exp, axis=1, keepdims=True)
+    outs.mark_prob[...] = mark_prob
+    factor = 1.0 / jnp.max(jnp.sum(mark_prob, axis=0, keepdims=True), axis=1, keepdims=True)
+    outs.factor[...] = jnp.broadcast_to(factor, outs.factor.shape)
+    mark_halves = halves(mark_prob)
+    power_s[...] = split_dot_nt(mark_halves, mark_halves) * factor
+    iterate_s[0:M] = mark_prob.T * factor
+    iterate_s[M:] = identity_matrix()
+    tops, totals = [[], []], [[], []]
+
+    def scores(slot, index):
+        query_chunk, key_chunk = (chunk_of(qk_ref, array, slot, index) for array in range(2))
+        place = slice(index * CHUNK, (index + 1) * CHUNK)
+        outs.turned[slot, 0, :, place] = query_chunk.T
+        outs.turned[slot, 1, :, place] = key_chunk.T
+        score = wide_dot_nt(query_chunk, outs.marks[slot, 1]) * score_scale
+        grown = jnp.exp(score - jnp.max(score, axis=1, keepdims=True))
+        prob = grown * (1.0 / jnp.sum(grown, axis=1, keepdims=True))
+        outs.token_prob[slot, place] = prob
+        outs.token_low[slot, place] = prob.astype(jnp.bfloat16)
+        key_score = wide_dot_nt(key_chunk, outs.marks[slot, 0]) * score_scale
+        outs.key_exp[slot, place] = key_score
+        tops[slot].append(jnp.max(key_score, axis=0, keepdims=True))
+
+    def grow(slot, index):
+        if index == 0:
+            tops[slot] = functools.reduce(jnp.maximum, tops[slot])
+        place = slice(index * CHUNK, (index + 1) * CHUNK)
+        grown = jnp.exp(outs.key_exp[slot, place] - tops[slot])
+        outs.key_exp[slot, place] = grown
+        outs.key_low[slot, place] = grown.astype(jnp.bfloat16)
+        totals[slot].append(jnp.sum(grown, axis=0, keepdims=True))
+
+    def several(unit, pairs):
+        for slot, index in pairs:
+            unit(slot, index)
+
+    pairs = [(slot, index) for slot in range(2) for index in range(chunks)]
+    work = iter(
+        [functools.partial(several, scores, [pair]) for pair in pairs]
+        + [
+            functools.partial(several, grow, pairs[first : first + 2])
+            for first in range(0, len(pairs), 2)
+        ]
+    )
+    saved = (outs.pair, outs.weight, outs.growth)
+    for sweep in range(PINV_ITERS):
+        sweep_forward(power_s, iterate_s, saved, sweep, work)
+        for ref in saved:
+            put(ref, sweep)
+        if sweep == 3:
+            for ref in (outs.token_low, outs.token_prob, outs.turned):
+                put(ref)
+    put(outs.key_low)
+    put(outs.key_exp)
+    outs.inverse[0], outs.inverse[1] = halves(iterate_s[0:M])
+    outs.last_growth[0], outs.last_growth[1] = halves(iterate_s[M:])
+    stats = [x for slot in range(2) for x in (tops[slot], sum(totals[slot][1:], totals[slot][0]))]
+    outs.stats[0:4] = jnp.concatenate(stats, axis=0)
+    outs.stats[4:8] = jnp.zeros((4, M), jnp.float32)
+
+
+def partial_compute(ins, outs, need, put):
+    need(ins.vg)
+    turned = [[all_tokens(ins.vg, array, slot).T for array in range(2)] for slot in range(2)]
+    need()
+    rows = thirds(ins.stats[0:4])
+    outs.send[2 * HD :] = jnp.concatenate([rows, jnp.zeros((4, M), jnp.float32)], axis=0).astype(
+        jnp.bfloat16
+    )
+    for slot, home in ((1, outs.send), (0, outs.keep)):
+        home[0:HD] = wide_dot(turned[slot][0], ins.key_low[slot]).astype(home.dtype)
+        home[HD : 2 * HD] = wide_dot(turned[slot][1], ins.token_low[slot]).astype(home.dtype)
+        put(home)
+
+
+def mixing_compute(ins, outs, need, put):
+    need()
+    got = ins.got[...].astype(jnp.float32)
+    others = swap_lanes(joined_thirds(got[2 * HD : 2 * HD + 12]))
+    scales = []
+    for slot in range(2):
+        own_max, own_total = ins.stats[2 * slot : 2 * slot + 1], ins.stats[2 * slot + 1 : 2 * slot + 2]
+        other = 1 - slot
+        other_max, other_total = others[2 * other : 2 * other + 1], others[2 * other + 1 : 2 * other + 2]
+        key_max = jnp.maximum(own_max, other_max)
+        own_factor, other_factor = jnp.exp(own_max - key_max), jnp.exp(other_max - key_max)
+        inverse_total = 1.0 / (own_total * own_factor + other_total * other_factor)
+        scales.append((own_factor * inverse_total, other_factor * inverse_total))
+    outs.scales[...] = jnp.concatenate(
+        [scales[0][0], scales[1][0], jnp.zeros((6, M), jnp.float32)], axis=0
+    )
+    landmark_values = ins.keep[0:HD] * scales[0][0] + swap_lanes(got[0:HD]) * scales[0][1]
+    mixing_grad = ins.keep[HD : 2 * HD] + swap_lanes(got[HD : 2 * HD])
+    inverse = (ins.inverse[0], ins.inverse[1])
+    outs.share[0:HD] = split_dot_nt(halves(landmark_values), inverse).astype(jnp.bfloat16)
+    values_low = split_dot(halves(mixing_grad), inverse).astype(jnp.bfloat16)
+    outs.share[HD : 2 * HD] = values_low
+    row_total = jnp.sum(values_low.astype(jnp.float32) * landmark_values, axis=0, keepdims=True)
+    outs.share[2 * HD :] = jnp.concatenate(
+        [thirds(row_total), jnp.zeros((13, M), jnp.float32)], axis=0
+    ).astype(jnp.bfloat16)
+    put(outs.share)
+    outs.mixing_grad[...] = mixing_grad
+    outs.mark_values[...] = landmark_values
+
+
+def head_units(ins, slot, out_ref, lead, direct_ref, share):
+    score_scale = HD ** (-0.5)
+    mixing_low, values_low, row_total = share
+    query_sums, key_sums = [], []
+    scale = ins.scales[slot : slot + 1]
+
+    def token_side(index):
+        place = slice(index * CHUNK, (index + 1) * CHUNK)
+        prob = ins.token_prob[place]
+        attended = wide_dot_nt(prob.astype(jnp.bfloat16), mixing_low)
+        store_chunk(out_ref, (0, *lead), index, attended.astype(jnp.bfloat16))
+        token_grad = wide_dot(chunk_of(ins.vg, 1, slot, index), mixing_low)
+        token_sgrad = (
+            prob * (token_grad - jnp.sum(token_grad * prob, axis=1, keepdims=True))
+        ).astype(jnp.bfloat16)
+        direct_ref[0, place] = wide_dot(token_sgrad, ins.marks[slot, 1]) * score_scale
+        key_sums.append(wide_dot(ins.turned[0, :, place], token_sgrad))
+
+    def key_side(index):
+        place = slice(index * CHUNK, (index + 1) * CHUNK)
+        key_prob = ins.key_exp[place] * scale
+        value_gradient = wide_dot_nt(key_prob.astype(jnp.bfloat16), values_low)
+        store_chunk(out_ref, (1, *lead), index, value_gradient.astype(jnp.bfloat16))
+        key_dgrad = wide_dot(chunk_of(ins.vg, 0, slot, index), values_low)
+        key_sgrad = (key_prob * (key_dgrad - row_total)).astype(jnp.bfloat16)
+        direct_ref[1, place] = wide_dot(key_sgrad, ins.marks[slot, 0]) * score_scale
+        query_sums.append(wide_dot(ins.turned[1, :, place], key_sgrad))
+
+    chunks = tokens_of(ins.vg) // CHUNK
+    units = [
+        functools.partial(unit, index) for unit in (key_side, token_side) for index in range(chunks)
+    ]
+    return units, query_sums, key_sums
+
+
+def share_parts(ref, swap):
+    parts = [ref[0:HD], ref[HD : 2 * HD], joined_thirds(ref[2 * HD :].astype(jnp.float32)[0:3])]
+    return [swap_lanes(part) for part in parts] if swap else parts
+
+
+def own_gradient_compute(ins, outs, need, put):
+    for ref in (ins.mark_prob, ins.factor, ins.mixing_grad, ins.mark_values, ins.share, ins.scales):
+        need(ref)
+    mark_prob = ins.mark_prob[...]
+    mark_halves = halves(mark_prob)
+    factor = ins.factor[0:1, 0:1]
+    inverse_grad = split_dot(halves(ins.mixing_grad[...].T), halves(ins.mark_values[...]))
+    inverse_grad_halves = halves(inverse_grad)
+    toward = split_dot(mark_halves, inverse_grad_halves) * factor
+    power = 0.5 * (toward + toward.T)
+    growth = None
+    units, query_sums, key_sums = head_units(
+        ins, 0, outs.out, (), outs.direct, share_parts(ins.share, False)
+    )
+    work = iter(units)
+
+    def beside():
+        next(work, lambda: None)()
+
+    for sweep in range(PINV_ITERS):
+        if sweep == 0:
+            for ref in (ins.marks, ins.vg, ins.key_exp, ins.turned):
+                need(ref)
+        if sweep == 2:
+            need(ins.token_prob)
+        for ref in (ins.pair, ins.weight, ins.growth):
+            need(ref, sweep)
+        pair = (ins.pair[sweep, 0], ins.pair[sweep, 1])
+        first = split_dot(pair, halves(power))
+        beside()
+        square = first[:M] + first[:M].T
+        last = sweep == PINV_ITERS - 1
+        second = split_dot(tuple(x[:M] for x in pair) if last else pair, halves(square))
+        beside()
+        cube = first[M:].T + second[:M]
+        weight = halves(0.25 * (7.0 * square - 15.0 * power - cube))
+        if not last:
+            fourth = second[M:] + second[M:].T
+            power = 0.25 * (13.0 * power - 15.0 * square + 7.0 * cube - fourth)
+        left = [ins.growth[sweep, 0], ins.growth[sweep, 0], ins.growth[sweep, 1]]
+        right = [weight[0], weight[1], weight[0]]
+        if growth is not None:
+            grown = halves(growth)
+            left += [grown[0], grown[0], grown[1]]
+            right += [ins.weight[sweep, 0], ins.weight[sweep, 1], ins.weight[sweep, 0]]
+        growth = wide_dot(jnp.concatenate(left, axis=1), jnp.concatenate(right, axis=0))
+    for unit in work:
+        unit()
+    put(outs.out)
+    put(outs.direct)
+    need()
+    mark_grad = factor * (
+        split_dot_nt((ins.last_growth[0], ins.last_growth[1]), inverse_grad_halves)
+        + split_dot(halves(growth + growth.T), mark_halves)
+    )
+    mark_sgrad = mark_prob * (mark_grad - jnp.sum(mark_grad * mark_prob, axis=1, keepdims=True))
+
+    def marks_dot(left, right):
+        left_high, left_low = halves(left)
+        return wide_dot(
+            jnp.concatenate([left_high, left_low], axis=1), jnp.concatenate([right, right], axis=0)
+        )
+
+    outs.totals[0] = marks_dot(mark_sgrad, ins.marks[0, 1]) + sum(query_sums[1:], query_sums[0]).T
+    outs.totals[1] = marks_dot(mark_sgrad.T, ins.marks[0, 0]) + sum(key_sums[1:], key_sums[0]).T
+
+
+def other_gradient_compute(ins, outs, need, put):
+    need()
+    outs.out[:, :, 0] = ins.own_out[...]
+    units, query_sums, key_sums = head_units(
+        ins, 1, outs.out, (1,), outs.direct, share_parts(ins.got_share, True)
+    )
+    for unit in units:
+        unit()
+    put(outs.out)
+    marks_scale = HD ** (-0.5) / (tokens_of(ins.vg) // HALF)
+    for kind, sums in enumerate((query_sums, key_sums)):
+        for slot, total in ((0, ins.totals[kind]), (1, sum(sums[1:], sums[0]).T)):
+            total = total * marks_scale
+            outs.near[kind, slot] = total[:HALF]
+            outs.far[kind, slot] = total[HALF:].astype(jnp.bfloat16)
+
+
+def finish_compute(ins, outs, need, put):
+    need()
+    out_ref = outs.out
+    group = CHUNK // out_ref.shape[3]
+    segment_len = tokens_of(out_ref) // HALF
+    per = CHUNK // segment_len
+    for index in range(tokens_of(out_ref) // CHUNK):
+        place, start = slice(index * per, (index + 1) * per), index * CHUNK
+        for slot, direct_ref in enumerate((ins.own_direct, ins.other_direct)):
+            for kind in range(2):
+                marks = ins.near[kind, slot, place] + ins.got_far[
+                    kind, 1 - slot, place
+                ].astype(jnp.float32)
+                spread = jnp.broadcast_to(marks[:, None], (per, segment_len, HD))
+                total = direct_ref[kind, start : start + CHUNK] + spread.reshape(CHUNK, HD)
+                store_chunk(out_ref, (kind, slot), index, total.astype(jnp.bfloat16))
+        put(out_ref, index * group)
+
+
+def exchange(packed):
+    return lax.all_to_all(packed, "cube", split_axis=0, concat_axis=0, tiled=True)
+
+
+def partner(array):
+    return lax.ppermute(array, "half", SWAP)
+
+
+def body(queries, keys, values, out_grad):
+    half = lax.axis_index("half").reshape(1)
+    qk = exchange(pack(half, queries, keys))
+    tokens = qk.shape[0] * qk.shape[3]
+    mine = landmarks_of(qk)
+    theirs = partner(mine)
+    values, mine = lax.optimization_barrier((values, mine))
+    vg = exchange(pack(half, values, out_grad))
+    kept = staged_call(
+        probability_compute,
+        dict(qk=qk, mine=mine, theirs=theirs),
+        dict(
+            marks=low(2, 2, M, HD),
+            token_prob=wide(2, tokens, M),
+            token_low=low(2, tokens, M),
+            key_exp=wide(2, tokens, M),
+            key_low=low(2, tokens, M),
+            turned=low(2, 2, HD, tokens),
+            stats=wide(8, M),
+            mark_prob=wide(M, M),
+            factor=wide(8, HD),
+            pair=(low(PINV_ITERS, 2, 2 * M, M), LEAD),
+            weight=(low(PINV_ITERS, 2, M, M), LEAD),
+            growth=(low(PINV_ITERS, 2, M, M), LEAD),
+            inverse=low(2, M, M),
+            last_growth=low(2, M, M),
+        ),
+        12,
+        extra=(pltpu.VMEM((M, M), jnp.float32), pltpu.VMEM((2 * M, M), jnp.float32)),
+    )
+    sums = staged_call(
+        partial_compute,
+        dict(vg=vg, stats=kept.stats, key_low=kept.key_low, token_low=kept.token_low),
+        dict(send=low(2 * HD + 16, M), keep=wide(2 * HD, M)),
+        2,
+    )
+    mixed = staged_call(
+        mixing_compute,
+        dict(got=partner(sums.send), keep=sums.keep, stats=kept.stats, inverse=kept.inverse),
+        dict(
+            share=low(2 * HD + 16, M),
+            scales=wide(8, M),
+            mixing_grad=wide(HD, M),
+            mark_values=wide(HD, M),
+        ),
+        1,
+    )
+    got_share = partner(mixed.share)
+    own = staged_call(
+        own_gradient_compute,
+        dict(
+            mark_prob=kept.mark_prob,
+            factor=kept.factor,
+            mixing_grad=mixed.mixing_grad,
+            mark_values=mixed.mark_values,
+            share=mixed.share,
+            scales=mixed.scales,
+            marks=kept.marks,
+            vg=vg,
+            key_exp=(kept.key_exp, SLOTS[0]),
+            turned=(kept.turned, SLOTS[0]),
+            pair=(kept.pair, LEAD),
+            weight=(kept.weight, LEAD),
+            growth=(kept.growth, LEAD),
+            token_prob=(kept.token_prob, SLOTS[0]),
+            last_growth=kept.last_growth,
+        ),
+        dict(
+            out=low(qk.shape[0], 2, *qk.shape[3:]),
+            direct=wide(2, tokens, HD),
+            totals=wide(2, M, HD),
+        ),
+        14,
+    )
+    other = staged_call(
+        other_gradient_compute,
+        dict(
+            got_share=got_share,
+            scales=mixed.scales,
+            marks=kept.marks,
+            vg=vg,
+            key_exp=(kept.key_exp, SLOTS[1]),
+            turned=(kept.turned, SLOTS[1]),
+            token_prob=(kept.token_prob, SLOTS[1]),
+            own_out=own.out,
+            totals=own.totals,
+        ),
+        dict(
+            out=low(*qk.shape),
+            far=low(2, 2, HALF, HD),
+            near=wide(2, 2, HALF, HD),
+            direct=wide(2, tokens, HD),
+        ),
+        3,
+    )
+    attended, value_gradient_array = unpack(half, exchange(other.out))
+    results = staged_call(
+        finish_compute,
+        dict(
+            got_far=partner(other.far),
+            near=other.near,
+            own_direct=own.direct,
+            other_direct=other.direct,
+        ),
+        dict(out=(low(*qk.shape), GROUPS)),
+        0.5,
+    ).out
+    query_grad, key_grad = unpack(half, exchange(results))
+    return attended, query_grad, key_grad, value_gradient_array
+
+
 def solution(mesh):
-    return jax.shard_map(
-        body,
-        mesh=mesh,
-        in_specs=(
-            P(("seq", "head"), None),
-            P(("seq", "head"), None),
-            P(("seq", "head"), None),
-            P(("seq", "head"), None),
-        ),
-        out_specs=(
-            P(("seq", "head"), None),
-            P(("seq", "head"), None),
-            P(("seq", "head"), None),
-            P(("seq", "head"), None),
-        ),
-        check_vma=False,
-    )
+    whole_placement = P(("seq", "head"), None)
+    halves_placement = P(("half", "cube"), None)
+
+    def layer(queries, keys, values, out_grad):
+        tokens, width = queries.shape
+        own_head_each = width // HD == mesh.size and tokens == 8 * CHUNK
+        if own_head_each:
+            split = jax.sharding.Mesh(
+                mesh.devices.reshape(2, mesh.size // 2), ("half", "cube")
+            )
+        return jax.shard_map(
+            body if own_head_each else shared_body,
+            mesh=split if own_head_each else mesh,
+            in_specs=(halves_placement if own_head_each else whole_placement,) * 4,
+            out_specs=(halves_placement if own_head_each else whole_placement,) * 4,
+            check_vma=False,
+        )(queries, keys, values, out_grad)
+
+    return layer

time: 759 us -> 142 us (0.19)
  waiting for transfers between devices: 329 us -> 49.8 us
  blocking collectives: 201 us -> 21.1 us
  matrix products: 103 us -> 0 us
  local copies, waits for them, and re-layouts: 53.3 us -> 3.63 us
  Pallas kernels: 0 us -> 45.2 us
  other arithmetic: 26 us -> 0 us
  between operations: 16.5 us -> 0.99 us
    psum x2 -> x0, waiting for transfers between devices: 210 us -> none  [the longest x1 169 us: share_heads(): return lax.psum(slot_mask[:, None, None] * own_matrix[None], 'seq')]
    psum x2 -> x0, blocking collectives: 119 us -> none  [the longest x1 60.2 us: body(): lax.psum(jnp.sum(key_prob * key_direct_gradient, axis=-1), 'seq')]
    dot_general x89 -> x0, matrix products: 99.8 us -> none  [the longest x18 10.8 us: newton_inverse(): product = jnp.matmul(matrix, iterate, precision=precise_setting)]
    pmax x1 -> x0, blocking collectives: 59.9 us -> none  [body(): key_max = lax.pmax(jnp.max(key_score, axis=-1), 'seq')]
    reduce_scatter x2 -> x0, waiting for transfers between devices: 57.6 us -> none  [the longest x1 57.6 us: body(): lax.psum_scatter(mark_kgrad_f, 'seq', scatter_dimension=0, tiled=True)]
    pallas_call x0 -> x11, Pallas kernels: none -> 45.2 us  [the longest x6 38.4 us: staged_call(): pl.pallas_call(kernel, out_shape=shapes, in_specs=[anywhere] * (n_in + n_...]
    all_gather x2 -> x0, waiting for transfers between devices: 40 us -> none  [the longest x1 34 us: body(): lax.all_gather(landmark(query_rows), 'seq', axis=0, tiled=True)]
    ppermute x0 -> x4, waiting for transfers between devices: none -> 36.1 us  [partner(): return lax.ppermute(array, 'half', SWAP)]
  transfers between devices with their start and end apart: 12 -> 7, of which waited for: 10 -> 4; matrix products, arithmetic and copies ran while one was open for 11% -> 0% of each run, Pallas kernels for 0% -> 20%
where the time goes in v7:
time: 142 us
  waiting for transfers between devices  49.8 us (35%)
  Pallas kernels  45.2 us (32%)
  blocking collectives  21.1 us (15%)
  starting transfers between devices  21 us (15%)
  local copies, waits for them, and re-layouts  3.63 us (3%)
    pallas_call x6, Pallas kernels, staged_call(): pl.pallas_call(kernel, out_shape=shapes, in_specs=[anywhere] * (n_in + n_...  38.4 us
    ppermute x4, waiting for transfers between devices, partner(): return lax.ppermute(array, 'half', SWAP)  36.1 us
    all_to_all x1, blocking collectives, exchange(): lax.all_to_all(packed, 'cube', split_axis=0, concat_axis=0, tiled=True)  21.1 us
    all_to_all x3, starting transfers between devices, exchange(): lax.all_to_all(packed, 'cube', split_axis=0, concat_axis=0, tiled=True)  14.5 us
    all_to_all x3, waiting for transfers between devices, exchange(): lax.all_to_all(packed, 'cube', split_axis=0, concat_axis=0, tiled=True)  13.8 us
    pallas_call x4, Pallas kernels, layout_call(): pl.pallas_call(kernel, out_shape=out_shape, in_specs=[pl.BlockSpec(memory...  6.5 us
    ppermute x4, starting transfers between devices, partner(): return lax.ppermute(array, 'half', SWAP)  6.47 us
    unnamed x16, local copies, waits for them, and re-layouts  3.63 us
  transfers between devices with their start and end apart: 7, of which 4 were waited for; matrix products, arithmetic and copies ran while one was open for 0% of the time, Pallas kernels for 20%

profile of v7, /device:TPU:0, one launch (start us, length us, event | category | flops | bytes accessed | tf_op | source)
XLA Modules:
  0.0 141.7 jit_solution(6079242624575952217)
XLA Ops:
  0.6 2.1 %shard_map.75 = bf16[16,2,2,64,128]{4,3,2,1,0:T(8,128)(2,1)} custom-call(s32[1]{0:T(128)} %bitcast.half_ref, bf16[64,4096]{1,0:T(8,128)(2,1)} %first_ref.1, bf16[64,4096]{1,0:T(8,128)(2,1)} %second_ref.2), custom_call_target="tpu_custom_call" | custom-call | bytes 2097152 | tf_op jit(solution)/shard_map/pallas_call | solution.py:501
  2.8 21.1 %all_to_all.20.qk_ref.refs_0_ = bf16[16,2,2,64,128]{4,3,2,1,0:T(8,128)(2,1)S(1)} all-to-all(bf16[16,2,2,64,128]{4,3,2,1,0:T(8,128)(2,1)} %shard_map.75), channel_id=1, replica_groups=mesh['seq'=16,'head'=2] {'seq':(2)8,'head'}, dimensions={0} | all-to-all | bytes 2097152 | tf_op jit(solution)/shard_map/all_to_all | solution.py:860
  24.2 2.3 %shard_map.77 = bf16[16,2,2,64,128]{4,3,2,1,0:T(8,128)(2,1)} custom-call(s32[1]{0:T(128)} %bitcast.half_ref, bf16[64,4096]{1,0:T(8,128)(2,1)} %first_ref.2, bf16[64,4096]{1,0:T(8,128)(2,1)} %second_ref.3), custom_call_target="tpu_custom_call" | custom-call | bytes 2097152 | tf_op jit(solution)/shard_map/pallas_call | solution.py:501
  26.5 3.7 %all-to-all-start.1 = ((bf16[16,2,2,64,128]{4,3,2,1,0:T(8,128)(2,1)}), bf16[16,2,2,64,128]{4,3,2,1,0:T(8,128)(2,1)S(1)}, u32[]{:S(2)}, u32[]{:S(2)}) async-start(bf16[16,2,2,64,128]{4,3,2,1,0:T(8,128)(2,1)} %shard_map.77), calls=%async_computation.1 | async-start | bytes 2097152 | tf_op jit(solution)/shard_map/all_to_all | solution.py:860
  30.2 2.7 %collective-permute-start = (bf16[2,2,128,128]{3,2,1,0:T(8,128)(2,1)S(1)}, bf16[2,2,128,128]{3,2,1,0:T(8,128)(2,1)S(1)}, u32[]{:S(2)}, u32[]{:S(2)}) collective-permute-start(bf16[2,2,128,128]{3,2,1,0:T(8,128)(2,1)S(1)} %shard_map.76.refs_1_), channel_id=1, source_target_pairs={{0,16},{16,0},{1,17},{17,1},{2,18},{18,2},{3,19},{19,3},{4,20},{20... | collective-permute-start | bytes 393224 | tf_op jit(solution)/shard_map/ppermute | solution.py:864
  32.8 13.3 %collective-permute-done.refs_2_ = bf16[2,2,128,128]{3,2,1,0:T(8,128)(2,1)S(1)} collective-permute-done((bf16[2,2,128,128]{3,2,1,0:T(8,128)(2,1)S(1)}, bf16[2,2,128,128]{3,2,1,0:T(8,128)(2,1)S(1)}, u32[]{:S(2)}, u32[]{:S(2)}) %collective-permute-start) | collective-permute-done | bytes 131104 | tf_op jit(solution)/shard_map/ppermute | solution.py:864
  46.8 10.3 %shard_map.78 = (bf16[2,2,256,128]{3,2,1,0:T(8,128)(2,1)}, f32[2,1024,256]{2,1,0:T(8,128)}, bf16[2,1024,256]{2,1,0:T(8,128)(2,1)}, f32[2,1024,256]{2,1,0:T(8,128...) custom-call(bf16[16,2,2,64,128]{4,3,2,1,0:T(8,128)(2,1)} %copy-done,, ...), custom_call_target="tpu_custom_call" | custom-call | flops 12000000000 | bytes 16003072 | tf_op jit(solution)/shard_map/pallas_call | solution.py:414
  57.1 1.0 copy-done.2
  58.1 3.1 %shard_map.79 = (bf16[272,256]{1,0:T(8,128)(2,1)}, f32[256,256]{1,0:T(8,128)}) custom-call(bf16[16,2,2,64,128]{4,3,2,1,0:T(8,128)(2,1)} %copy-done.2, f32[8,256]{1,0:T(8,128)} %get-tuple-element.39.refs_1_.refs_2_, bf16[2,1024,256]{2,1,0:T(8,128)(2,1)} %get-tuple-element.40.refs_2_, bf16[2,1024,256]{2,1,0:T(8,128)(2,1)} %get-tuple-element.41.refs_3_), custom_call_target="tpu_custom_call" | custom-call | flops 2000000000 | bytes 3555328 | tf_op jit(solution)/shard_map/pallas_call | solution.py:414
  61.1 3.4 %collective-permute-start.1 = (bf16[272,256]{1,0:T(8,128)(2,1)}, bf16[272,256]{1,0:T(8,128)(2,1)S(1)}, u32[]{:S(2)}, u32[]{:S(2)}) collective-permute-start(bf16[272,256]{1,0:T(8,128)(2,1)} %get-tuple-element.42), channel_id=1, source_target_pairs={{0,16},{16,0},{1,17},{17,1},{2,18},{18,2},{3,19},{19,3},{4,20},{20... | collective-permute-start | bytes 417800 | tf_op jit(solution)/shard_map/ppermute | solution.py:864
  64.6 6.9 %collective-permute-done.1.refs_0_ = bf16[272,256]{1,0:T(8,128)(2,1)S(1)} collective-permute-done((bf16[272,256]{1,0:T(8,128)(2,1)}, bf16[272,256]{1,0:T(8,128)(2,1)S(1)}, u32[]{:S(2)}, u32[]{:S(2)}) %collective-permute-start.1) | collective-permute-done | bytes 139296 | tf_op jit(solution)/shard_map/ppermute | solution.py:864
  71.4 0.7 copy-done.5
  72.1 2.3 %shard_map.80 = (bf16[272,256]{1,0:T(8,128)(2,1)}, f32[8,256]{1,0:T(8,128)}, f32[128,256]{1,0:T(8,128)}, f32[128,256]{1,0:T(8,128)}) custom-call(bf16[272,256]{1,0:T(8,128)(2,1)} %copy-done.5, f32[256,256]{1,0:T(8,128)} %get-tuple-element.43.refs_1_, f32[8,256]{1,0:T(8,128)} %get-tuple-element.39.refs_1_.refs_2_, bf16[2,256,256]{2,1,0:T(8,128)(2,1)} %get-tuple-element.44.refs_3_), custom_call_target="tpu_custom_call" | custom-call | flops 1000000000 | bytes 1081344 | tf_op jit(solution)/shard_map/pallas_call | solution.py:414
  74.5 13.9 %shard_map.81 = (bf16[16,2,64,128]{3,2,1,0:T(8,128)(2,1)}, f32[2,1024,128]{2,1,0:T(8,128)}, f32[2,256,128]{2,1,0:T(8,128)}) custom-call(f32[256,256]{1,0:T(8,128)} %get-tuple-element.51.refs_0_, f32[8,128]{1,0:T(8,128)} %get-tuple-element.52.refs_1_, f32[128,256]{1,0:T(8,128)} %get-tuple-element.53.refs_2_, f32[128,256]{1,0:T(8,128)} %get-tuple-element.54.refs_3_, ...), custom_call_target="tpu_custom_call" | custom-call | flops 14000000000 | bytes 15618048 | tf_op jit(solution)/shard_map/pallas_call | solution.py:414
  88.4 0.6 copy-done.4
  89.1 6.0 %shard_map.82 = (bf16[16,2,2,64,128]{4,3,2,1,0:T(8,128)(2,1)}, bf16[2,2,128,128]{3,2,1,0:T(8,128)(2,1)}, f32[2,2,128,128]{3,2,1,0:T(8,128)}, f32[2,1024,128]{2,1,0:T(8,128)}) custom-call(bf16[272,256]{1,0:T(8,128)(2,1)} %copy-done.4, f32[8,256]{1,0:T(8,128)} %get-tuple-element.46.refs_5_.refs_1_, bf16[2,2,256,128]{3,2,1,0:T(8,128)(2,1)} %get-tuple-element.47.refs_6_.refs_2_, ...), custom_call_target="tpu_custom_call" | custom-call | flops 3000000000 | bytes 9977856 | tf_op jit(solution)/shard_map/pallas_call | solution.py:414
  95.1 6.5 %all-to-all-start.2 = ((bf16[16,2,2,64,128]{4,3,2,1,0:T(8,128)(2,1)}), bf16[16,2,2,64,128]{4,3,2,1,0:T(8,128)(2,1)S(1)}, u32[]{:S(2)}, u32[]{:S(2)}) async-start(bf16[16,2,2,64,128]{4,3,2,1,0:T(8,128)(2,1)} %get-tuple-element.61), calls=%async_computation.2 | async-start | bytes 2097152 | tf_op jit(solution)/shard_map/all_to_all | solution.py:860
  101.9 15.9 %collective-permute-done.3.refs_0_ = bf16[2,2,128,128]{3,2,1,0:T(8,128)(2,1)S(1)} collective-permute-done((bf16[2,2,128,128]{3,2,1,0:T(8,128)(2,1)S(1)}, bf16[2,2,128,128]{3,2,1,0:T(8,128)(2,1)S(1)}, u32[]{:S(2)}, u32[]{:S(2)}) %collective-permute-start.3) | collective-permute-done | bytes 131104 | tf_op jit(solution)/shard_map/ppermute | solution.py:864
  117.8 0.7 copy-done.3
  118.5 2.8 %shard_map.84 = bf16[16,2,2,64,128]{4,3,2,1,0:T(8,128)(2,1)} custom-call(bf16[2,2,128,128]{3,2,1,0:T(8,128)(2,1)} %copy-done.3, f32[2,2,128,128]{3,2,1,0:T(8,128)} %get-tuple-element.64.refs_1_, f32[2,1024,128]{2,1,0:T(8,128)} %get-tuple-element.65.refs_2_, f32[2,1024,128]{2,1,0:T(8,128)} %get-tuple-element.66.refs_3_), custom_call_target="tpu_custom_call" | custom-call | flops 500000000 | bytes 3538944 | tf_op jit(solution)/shard_map/pallas_call | solution.py:414
  121.3 4.4 %all-to-all-start.3 = ((bf16[16,2,2,64,128]{4,3,2,1,0:T(8,128)(2,1)}), bf16[16,2,2,64,128]{4,3,2,1,0:T(8,128)(2,1)S(1)}, u32[]{:S(2)}, u32[]{:S(2)}) async-start(bf16[16,2,2,64,128]{4,3,2,1,0:T(8,128)(2,1)} %shard_map.84), calls=%async_computation.3 | async-start | bytes 2097152 | tf_op jit(solution)/shard_map/all_to_all | solution.py:860
  125.7 1.1 shard_map.83
  126.8 13.7 %all-to-all-done.3.packed_ref = bf16[16,2,2,64,128]{4,3,2,1,0:T(8,128)(2,1)S(1)} async-done(((bf16[16,2,2,64,128]{4,3,2,1,0:T(8,128)(2,1)}), bf16[16,2,2,64,128]{4,3,2,1,0:T(8,128)(2,1)S(1)}, u32[]{:S(2)}, u32[]{:S(2)}) %all-to-all-start.3) | async-done | bytes 1048608 | tf_op jit(solution)/shard_map/all_to_all | solution.py:860
  140.5 1.0 shard_map.85
  (18 shorter events, 1.3 us)
Async XLA Ops:
  23.9 2.6 %copy-start = (bf16[16,2,2,64,128]{4,3,2,1,0:T(8,128)(2,1)}, bf16[16,2,2,64,128]{4,3,2,1,0:T(8,128)(2,1)S(1)}, u32[]{:S(2)}) copy-start(bf16[16,2,2,64,128]{4,3,2,1,0:T(8,128)(2,1)S(1)} %all_to_all.20.qk_ref.refs_0_) | copy-start | bytes 3145732
  24.2 6.0 %copy-start.1 = (bf16[2,2,128,128]{3,2,1,0:T(8,128)(2,1)}, bf16[2,2,128,128]{3,2,1,0:T(8,128)(2,1)S(1)}, u32[]{:S(2)}) copy-start(bf16[2,2,128,128]{3,2,1,0:T(8,128)(2,1)S(1)} %shard_map.76.refs_1_) | copy-start | bytes 393220
  26.5 30.5 %all-to-all-start.1 = ((bf16[16,2,2,64,128]{4,3,2,1,0:T(8,128)(2,1)}), bf16[16,2,2,64,128]{4,3,2,1,0:T(8,128)(2,1)S(1)}, u32[]{:S(2)}, u32[]{:S(2)}) async-start(bf16[16,2,2,64,128]{4,3,2,1,0:T(8,128)(2,1)} %shard_map.77), calls=%async_computation.1 | async-start | bytes 2097152 | tf_op jit(solution)/shard_map/all_to_all | solution.py:860
  30.2 15.9 %collective-permute-start = (bf16[2,2,128,128]{3,2,1,0:T(8,128)(2,1)S(1)}, bf16[2,2,128,128]{3,2,1,0:T(8,128)(2,1)S(1)}, u32[]{:S(2)}, u32[]{:S(2)}) collective-permute-start(bf16[2,2,128,128]{3,2,1,0:T(8,128)(2,1)S(1)} %shard_map.76.refs_1_), channel_id=1, source_target_pairs={{0,16},{16,0},{1,17},{17,1},{2,18},{18,2},{3,19},{19,3},{4,20},{20... | collective-permute-start | bytes 393224 | tf_op jit(solution)/shard_map/ppermute | solution.py:864
  46.1 0.6 copy-start.7
  57.0 1.0 copy-start.2
  61.1 10.3 %collective-permute-start.1 = (bf16[272,256]{1,0:T(8,128)(2,1)}, bf16[272,256]{1,0:T(8,128)(2,1)S(1)}, u32[]{:S(2)}, u32[]{:S(2)}) collective-permute-start(bf16[272,256]{1,0:T(8,128)(2,1)} %get-tuple-element.42), channel_id=1, source_target_pairs={{0,16},{16,0},{1,17},{17,1},{2,18},{18,2},{3,19},{19,3},{4,20},{20... | collective-permute-start | bytes 417800 | tf_op jit(solution)/shard_map/ppermute | solution.py:864
  71.4 0.7 copy-start.5
  74.4 14.0 %collective-permute-start.2 = (bf16[272,256]{1,0:T(8,128)(2,1)}, bf16[272,256]{1,0:T(8,128)(2,1)S(1)}, u32[]{:S(2)}, u32[]{:S(2)}) collective-permute-start(bf16[272,256]{1,0:T(8,128)(2,1)} %get-tuple-element.45.refs_4_), channel_id=1, source_target_pairs={{0,16},{16,0},{1,17},{17,1},{2,18},{18,2},{3,19},{19,3},{4,20},{20... | collective-permute-start | bytes 417800 | tf_op jit(solution)/shard_map/ppermute | solution.py:864
  88.4 0.7 copy-start.4
  95.1 6.5 %copy-start.6 = (bf16[2,2,128,128]{3,2,1,0:T(8,128)(2,1)S(1)}, bf16[2,2,128,128]{3,2,1,0:T(8,128)(2,1)}, u32[]{:S(2)}) copy-start(bf16[2,2,128,128]{3,2,1,0:T(8,128)(2,1)} %get-tuple-element.63) | copy-start | bytes 393220
  95.1 26.2 %all-to-all-start.2 = ((bf16[16,2,2,64,128]{4,3,2,1,0:T(8,128)(2,1)}), bf16[16,2,2,64,128]{4,3,2,1,0:T(8,128)(2,1)S(1)}, u32[]{:S(2)}, u32[]{:S(2)}) async-start(bf16[16,2,2,64,128]{4,3,2,1,0:T(8,128)(2,1)} %get-tuple-element.61), calls=%async_computation.2 | async-start | bytes 2097152 | tf_op jit(solution)/shard_map/all_to_all | solution.py:860
  101.6 16.2 %collective-permute-start.3 = (bf16[2,2,128,128]{3,2,1,0:T(8,128)(2,1)S(1)}, bf16[2,2,128,128]{3,2,1,0:T(8,128)(2,1)S(1)}, u32[]{:S(2)}, u32[]{:S(2)}) collective-permute-start(bf16[2,2,128,128]{3,2,1,0:T(8,128)(2,1)S(1)} %copy-done.6), channel_id=1, source_target_pairs={{0,16},{16,0},{1,17},{17,1},{2,18},{18,2},{3,19},{19,3},{4,20},{20... | collective-permute-start | bytes 393224 | tf_op jit(solution)/shard_map/ppermute | solution.py:864
  117.8 0.7 copy-start.3
  121.3 19.2 %all-to-all-start.3 = ((bf16[16,2,2,64,128]{4,3,2,1,0:T(8,128)(2,1)}), bf16[16,2,2,64,128]{4,3,2,1,0:T(8,128)(2,1)S(1)}, u32[]{:S(2)}, u32[]{:S(2)}) async-start(bf16[16,2,2,64,128]{4,3,2,1,0:T(8,128)(2,1)} %shard_map.84), calls=%async_computation.3 | async-start | bytes 2097152 | tf_op jit(solution)/shard_map/all_to_all | solution.py:860

commit v8 on v7

--- a/solution.py
+++ b/solution.py
@@ -19,6 +19,7 @@
 SMALL_LIMIT = 16 * 2**20
 WHOLE, LEAD, GROUPS = range(3)
 SLOTS = (10, 11)
+LONG = 200
 
 
 precise_setting = lax.Precision.HIGHEST
@@ -870,8 +871,8 @@
     tokens = qk.shape[0] * qk.shape[3]
     mine = landmarks_of(qk)
     theirs = partner(mine)
-    values, mine = lax.optimization_barrier((values, mine))
-    vg = exchange(pack(half, values, out_grad))
+    vg_packed, mine = lax.optimization_barrier((pack(half, values, out_grad), mine))
+    vg = exchange(vg_packed)
     kept = staged_call(
         probability_compute,
         dict(qk=qk, mine=mine, theirs=theirs),
@@ -891,7 +892,7 @@
             inverse=low(2, M, M),
             last_growth=low(2, M, M),
         ),
-        12,
+        LONG,
         extra=(pltpu.VMEM((M, M), jnp.float32), pltpu.VMEM((2 * M, M), jnp.float32)),
     )
     sums = staged_call(
@@ -969,7 +970,7 @@
             other_direct=other.direct,
         ),
         dict(out=(low(*qk.shape), GROUPS)),
-        0.5,
+        LONG,
     ).out
     query_grad, key_grad = unpack(half, exchange(results))
     return attended, query_grad, key_grad, value_gradient_array

time: 142 us -> 127 us (0.89)
  waiting for transfers between devices: 49.8 us -> 37.1 us
  starting transfers between devices: 21 us -> 18.7 us
    ppermute x4, waiting for transfers between devices: 36.1 us -> 10.1 us  [partner(): return lax.ppermute(array, 'half', SWAP)]
    all_to_all x3, waiting for transfers between devices: 13.8 us -> 27 us  [exchange(): lax.all_to_all(packed, 'cube', split_axis=0, concat_axis=0, tiled=True)]
    all_to_all x3, starting transfers between devices: 14.5 us -> 12.6 us  [exchange(): lax.all_to_all(packed, 'cube', split_axis=0, concat_axis=0, tiled=True)]
    unnamed x16 -> x12, local copies, waits for them, and re-layouts: 3.63 us -> 2.63 us
  transfers between devices with their start and end apart: 7 -> 7, of which waited for: 4 -> 6; matrix products, arithmetic and copies ran while one was open for 0% -> 0% of each run, Pallas kernels for 20% -> 25%
where the time goes in v8:
time: 127 us
  Pallas kernels  46.3 us (36%)
  waiting for transfers between devices  37.1 us (29%)
  blocking collectives  21.1 us (17%)
  starting transfers between devices  18.7 us (15%)
  local copies, waits for them, and re-layouts  2.63 us (2%)
    pallas_call x6, Pallas kernels, staged_call(): pl.pallas_call(kernel, out_shape=shapes, in_specs=[anywhere] * (n_in + n_...  38.4 us
    all_to_all x3, waiting for transfers between devices, exchange(): lax.all_to_all(packed, 'cube', split_axis=0, concat_axis=0, tiled=True)  27 us
    all_to_all x1, blocking collectives, exchange(): lax.all_to_all(packed, 'cube', split_axis=0, concat_axis=0, tiled=True)  21.1 us
    all_to_all x3, starting transfers between devices, exchange(): lax.all_to_all(packed, 'cube', split_axis=0, concat_axis=0, tiled=True)  12.6 us
    ppermute x4, waiting for transfers between devices, partner(): return lax.ppermute(array, 'half', SWAP)  10.1 us
    pallas_call x4, Pallas kernels, layout_call(): pl.pallas_call(kernel, out_shape=out_shape, in_specs=[pl.BlockSpec(memory...  7.59 us
    ppermute x4, starting transfers between devices, partner(): return lax.ppermute(array, 'half', SWAP)  6.09 us
    unnamed x12, local copies, waits for them, and re-layouts  2.63 us
  transfers between devices with their start and end apart: 7, of which 6 were waited for; matrix products, arithmetic and copies ran while one was open for 0% of the time, Pallas kernels for 25%

profile of v8, /device:TPU:0, one launch (start us, length us, event | category | flops | bytes accessed | tf_op | source)
XLA Modules:
  0.0 126.9 jit_solution(5146203199429191809)
XLA Ops:
  0.6 2.1 %shard_map.76 = bf16[16,2,2,64,128]{4,3,2,1,0:T(8,128)(2,1)} custom-call(s32[1]{0:T(128)} %bitcast.half_ref, bf16[64,4096]{1,0:T(8,128)(2,1)} %first_ref.3, bf16[64,4096]{1,0:T(8,128)(2,1)} %second_ref.3), custom_call_target="tpu_custom_call" | custom-call | bytes 2097152 | tf_op jit(solution)/shard_map/pallas_call | solution.py:502
  2.8 21.1 %all_to_all.20.qk_ref.refs_0_ = bf16[16,2,2,64,128]{4,3,2,1,0:T(8,128)(2,1)S(1)} all-to-all(bf16[16,2,2,64,128]{4,3,2,1,0:T(8,128)(2,1)} %shard_map.76), channel_id=1, replica_groups=mesh['seq'=16,'head'=2] {'seq':(2)8,'head'}, dimensions={0} | all-to-all | bytes 2097152 | tf_op jit(solution)/shard_map/all_to_all | solution.py:861
  24.2 2.7 %collective-permute-start = (bf16[2,2,128,128]{3,2,1,0:T(8,128)(2,1)S(1)}, bf16[2,2,128,128]{3,2,1,0:T(8,128)(2,1)S(1)}, u32[]{:S(2)}, u32[]{:S(2)}) collective-permute-start(bf16[2,2,128,128]{3,2,1,0:T(8,128)(2,1)S(1)} %shard_map.77.refs_1_), channel_id=1, source_target_pairs={{0,16},{16,0},{1,17},{17,1},{2,18},{18,2},{3,19},{19,3},{4,20},{20... | collective-permute-start | bytes 393224 | tf_op jit(solution)/shard_map/ppermute | solution.py:865
  26.9 2.1 %shard_map.75 = bf16[16,2,2,64,128]{4,3,2,1,0:T(8,128)(2,1)} custom-call(s32[1]{0:T(128)} %bitcast.half_ref, bf16[64,4096]{1,0:T(8,128)(2,1)} %first_ref.2, bf16[64,4096]{1,0:T(8,128)(2,1)} %second_ref.2), custom_call_target="tpu_custom_call" | custom-call | bytes 2097152 | tf_op jit(solution)/shard_map/pallas_call | solution.py:502
  29.0 4.4 %all-to-all-start.1 = ((bf16[16,2,2,64,128]{4,3,2,1,0:T(8,128)(2,1)}), bf16[16,2,2,64,128]{4,3,2,1,0:T(8,128)(2,1)}, u32[]{:S(2)}, u32[]{:S(2)}) async-start(bf16[16,2,2,64,128]{4,3,2,1,0:T(8,128)(2,1)} %shard_map.75), calls=%async_computation.1 | async-start | bytes 2097152 | tf_op jit(solution)/shard_map/all_to_all | solution.py:861
  33.6 0.7 copy-done.4
  34.3 10.3 %shard_map.78 = (bf16[2,2,256,128]{3,2,1,0:T(8,128)(2,1)}, f32[2,1024,256]{2,1,0:T(8,128)}, bf16[2,1024,256]{2,1,0:T(8,128)(2,1)}, f32[2,1024,256]{2,1,0:T(8,128...) custom-call(bf16[16,2,2,64,128]{4,3,2,1,0:T(8,128)(2,1)} %copy-done,, ...), custom_call_target="tpu_custom_call" | custom-call | flops 199999995904 | bytes 16003072 | tf_op jit(solution)/shard_map/pallas_call | solution.py:415
  44.6 3.6 %all-to-all-done.1.refs_0_.refs_7_.refs_3_ = bf16[16,2,2,64,128]{4,3,2,1,0:T(8,128)(2,1)} async-done(((bf16[16,2,2,64,128]{4,3,2,1,0:T(8,128)(2,1)}), bf16[16,2,2,64,128]{4,3,2,1,0:T(8,128)(2,1)}, u32[]{:S(2)}, u32[]{:S(2)}) %all-to-all-start.1) | async-done | bytes 1048608 | tf_op jit(solution)/shard_map/all_to_all | solution.py:861
  48.2 3.1 %shard_map.79 = (bf16[272,256]{1,0:T(8,128)(2,1)}, f32[256,256]{1,0:T(8,128)}) custom-call(bf16[16,2,2,64,128]{4,3,2,1,0:T(8,128)(2,1)} %all-to-all-done.1.refs_0_.refs_7_.refs_3_, f32[8,256]{1,0:T(8,128)} %get-tuple-element.39.refs_1_.refs_2_, bf16[2,1024,256]{2,1,0:T(8,128)(2,1)} %get-tuple-element.40.refs_2_, bf16[2,1024,256]{2,1,0:T(8,128)(2,1)} %get-tuple-element.41.refs_3_), custom_call_target="tpu_custom_call" | custom-call | flops 2000000000 | bytes 3555328 | tf_op jit(solution)/shard_map/pallas_call | solution.py:415
  51.7 8.5 %collective-permute-done.1.refs_0_ = bf16[272,256]{1,0:T(8,128)(2,1)S(1)} collective-permute-done((bf16[272,256]{1,0:T(8,128)(2,1)}, bf16[272,256]{1,0:T(8,128)(2,1)S(1)}, u32[]{:S(2)}, u32[]{:S(2)}) %collective-permute-start.1) | collective-permute-done | bytes 139296 | tf_op jit(solution)/shard_map/ppermute | solution.py:865
  60.2 0.7 copy-done.3
  60.9 2.3 %shard_map.80 = (bf16[272,256]{1,0:T(8,128)(2,1)}, f32[8,256]{1,0:T(8,128)}, f32[128,256]{1,0:T(8,128)}, f32[128,256]{1,0:T(8,128)}) custom-call(bf16[272,256]{1,0:T(8,128)(2,1)} %copy-done.3, f32[256,256]{1,0:T(8,128)} %get-tuple-element.43.refs_1_, f32[8,256]{1,0:T(8,128)} %get-tuple-element.39.refs_1_.refs_2_, bf16[2,256,256]{2,1,0:T(8,128)(2,1)} %get-tuple-element.44.refs_3_), custom_call_target="tpu_custom_call" | custom-call | flops 1000000000 | bytes 1081344 | tf_op jit(solution)/shard_map/pallas_call | solution.py:415
  63.3 13.9 %shard_map.81 = (bf16[16,2,64,128]{3,2,1,0:T(8,128)(2,1)}, f32[2,1024,128]{2,1,0:T(8,128)}, f32[2,256,128]{2,1,0:T(8,128)}) custom-call(f32[256,256]{1,0:T(8,128)} %get-tuple-element.51.refs_0_, f32[8,128]{1,0:T(8,128)} %get-tuple-element.52.refs_1_, f32[128,256]{1,0:T(8,128)} %get-tuple-element.53.refs_2_, f32[128,256]{1,0:T(8,128)} %get-tuple-element.54.refs_3_, ...), custom_call_target="tpu_custom_call" | custom-call | flops 14000000000 | bytes 15618048 | tf_op jit(solution)/shard_map/pallas_call | solution.py:415
  77.9 6.0 %shard_map.82 = (bf16[16,2,2,64,128]{4,3,2,1,0:T(8,128)(2,1)}, bf16[2,2,128,128]{3,2,1,0:T(8,128)(2,1)}, f32[2,2,128,128]{3,2,1,0:T(8,128)}, f32[2,1024,128]{2,1,0:T(8,128)}) custom-call(bf16[272,256]{1,0:T(8,128)(2,1)} %copy-done.2, f32[8,256]{1,0:T(8,128)} %get-tuple-element.46.refs_5_.refs_1_, bf16[2,2,256,128]{3,2,1,0:T(8,128)(2,1)} %get-tuple-element.47.refs_6_.refs_2_, ...), custom_call_target="tpu_custom_call" | custom-call | flops 3000000000 | bytes 9977856 | tf_op jit(solution)/shard_map/pallas_call | solution.py:415
  83.9 3.0 %collective-permute-start.3 = (bf16[2,2,128,128]{3,2,1,0:T(8,128)(2,1)}, bf16[2,2,128,128]{3,2,1,0:T(8,128)(2,1)S(1)}, u32[]{:S(2)}, u32[]{:S(2)}) collective-permute-start(bf16[2,2,128,128]{3,2,1,0:T(8,128)(2,1)} %get-tuple-element.63), channel_id=1, source_target_pairs={{0,16},{16,0},{1,17},{17,1},{2,18},{18,2},{3,19},{19,3},{4,20},{20... | collective-permute-start | bytes 393224 | tf_op jit(solution)/shard_map/ppermute | solution.py:865
  86.8 4.6 %all-to-all-start.2 = ((bf16[16,2,2,64,128]{4,3,2,1,0:T(8,128)(2,1)}), bf16[16,2,2,64,128]{4,3,2,1,0:T(8,128)(2,1)}, u32[]{:S(2)}, u32[]{:S(2)}) async-start(bf16[16,2,2,64,128]{4,3,2,1,0:T(8,128)(2,1)} %get-tuple-element.61), calls=%async_computation.2 | async-start | bytes 2097152 | tf_op jit(solution)/shard_map/all_to_all | solution.py:861
  91.5 1.3 %collective-permute-done.3.refs_0_ = bf16[2,2,128,128]{3,2,1,0:T(8,128)(2,1)S(1)} collective-permute-done((bf16[2,2,128,128]{3,2,1,0:T(8,128)(2,1)}, bf16[2,2,128,128]{3,2,1,0:T(8,128)(2,1)S(1)}, u32[]{:S(2)}, u32[]{:S(2)}) %collective-permute-start.3) | collective-permute-done | bytes 131104 | tf_op jit(solution)/shard_map/ppermute | solution.py:865
  92.8 0.7 copy-done.5
  93.5 2.8 %shard_map.84 = bf16[16,2,2,64,128]{4,3,2,1,0:T(8,128)(2,1)} custom-call(bf16[2,2,128,128]{3,2,1,0:T(8,128)(2,1)} %copy-done.5, f32[2,2,128,128]{3,2,1,0:T(8,128)} %get-tuple-element.64.refs_1_, f32[2,1024,128]{2,1,0:T(8,128)} %get-tuple-element.65.refs_2_, f32[2,1024,128]{2,1,0:T(8,128)} %get-tuple-element.66.refs_3_), custom_call_target="tpu_custom_call" | custom-call | flops 199999995904 | bytes 3538944 | tf_op jit(solution)/shard_map/pallas_call | solution.py:415
  96.3 10.9 %all-to-all-done.2.packed_ref = bf16[16,2,2,64,128]{4,3,2,1,0:T(8,128)(2,1)} async-done(((bf16[16,2,2,64,128]{4,3,2,1,0:T(8,128)(2,1)}), bf16[16,2,2,64,128]{4,3,2,1,0:T(8,128)(2,1)}, u32[]{:S(2)}, u32[]{:S(2)}) %all-to-all-start.2) | async-done | bytes 1048608 | tf_op jit(solution)/shard_map/all_to_all | solution.py:861
  107.2 3.7 %all-to-all-start.3 = ((bf16[16,2,2,64,128]{4,3,2,1,0:T(8,128)(2,1)}), bf16[16,2,2,64,128]{4,3,2,1,0:T(8,128)(2,1)S(1)}, u32[]{:S(2)}, u32[]{:S(2)}) async-start(bf16[16,2,2,64,128]{4,3,2,1,0:T(8,128)(2,1)} %shard_map.84), calls=%async_computation.3 | async-start | bytes 2097152 | tf_op jit(solution)/shard_map/all_to_all | solution.py:861
  110.9 2.3 %shard_map.83 = (bf16[64,4096]{1,0:T(8,128)(2,1)}, bf16[64,4096]{1,0:T(8,128)(2,1)}) custom-call(s32[1]{0:T(128)} %bitcast.half_ref, bf16[16,2,2,64,128]{4,3,2,1,0:T(8,128)(2,1)} %all-to-all-done.2.packed_ref), custom_call_target="tpu_custom_call" | custom-call | bytes 2097152 | tf_op jit(solution)/shard_map/pallas_call | solution.py:502
  113.2 12.5 %all-to-all-done.3.packed_ref = bf16[16,2,2,64,128]{4,3,2,1,0:T(8,128)(2,1)S(1)} async-done(((bf16[16,2,2,64,128]{4,3,2,1,0:T(8,128)(2,1)}), bf16[16,2,2,64,128]{4,3,2,1,0:T(8,128)(2,1)S(1)}, u32[]{:S(2)}, u32[]{:S(2)}) %all-to-all-start.3) | async-done | bytes 1048608 | tf_op jit(solution)/shard_map/all_to_all | solution.py:861
  125.7 1.0 shard_map.85
  (14 shorter events, 1.7 us)
Async XLA Ops:
  23.9 5.1 %copy-start = (bf16[16,2,2,64,128]{4,3,2,1,0:T(8,128)(2,1)}, bf16[16,2,2,64,128]{4,3,2,1,0:T(8,128)(2,1)S(1)}, u32[]{:S(2)}) copy-start(bf16[16,2,2,64,128]{4,3,2,1,0:T(8,128)(2,1)S(1)} %all_to_all.20.qk_ref.refs_0_) | copy-start | bytes 3145732
  24.2 4.8 %copy-start.1 = (bf16[2,2,128,128]{3,2,1,0:T(8,128)(2,1)}, bf16[2,2,128,128]{3,2,1,0:T(8,128)(2,1)S(1)}, u32[]{:S(2)}) copy-start(bf16[2,2,128,128]{3,2,1,0:T(8,128)(2,1)S(1)} %shard_map.77.refs_1_) | copy-start | bytes 393220
  24.2 9.4 %collective-permute-start = (bf16[2,2,128,128]{3,2,1,0:T(8,128)(2,1)S(1)}, bf16[2,2,128,128]{3,2,1,0:T(8,128)(2,1)S(1)}, u32[]{:S(2)}, u32[]{:S(2)}) collective-permute-start(bf16[2,2,128,128]{3,2,1,0:T(8,128)(2,1)S(1)} %shard_map.77.refs_1_), channel_id=1, source_target_pairs={{0,16},{16,0},{1,17},{17,1},{2,18},{18,2},{3,19},{19,3},{4,20},{20... | collective-permute-start | bytes 393224 | tf_op jit(solution)/shard_map/ppermute | solution.py:865
  29.0 19.2 %all-to-all-start.1 = ((bf16[16,2,2,64,128]{4,3,2,1,0:T(8,128)(2,1)}), bf16[16,2,2,64,128]{4,3,2,1,0:T(8,128)(2,1)}, u32[]{:S(2)}, u32[]{:S(2)}) async-start(bf16[16,2,2,64,128]{4,3,2,1,0:T(8,128)(2,1)} %shard_map.75), calls=%async_computation.1 | async-start | bytes 2097152 | tf_op jit(solution)/shard_map/all_to_all | solution.py:861
  33.6 0.7 copy-start.4
  51.3 8.9 %collective-permute-start.1 = (bf16[272,256]{1,0:T(8,128)(2,1)}, bf16[272,256]{1,0:T(8,128)(2,1)S(1)}, u32[]{:S(2)}, u32[]{:S(2)}) collective-permute-start(bf16[272,256]{1,0:T(8,128)(2,1)} %get-tuple-element.42), channel_id=1, source_target_pairs={{0,16},{16,0},{1,17},{17,1},{2,18},{18,2},{3,19},{19,3},{4,20},{20... | collective-permute-start | bytes 417800 | tf_op jit(solution)/shard_map/ppermute | solution.py:865
  60.2 0.7 copy-start.3
  63.2 14.0 %collective-permute-start.2 = (bf16[272,256]{1,0:T(8,128)(2,1)}, bf16[272,256]{1,0:T(8,128)(2,1)S(1)}, u32[]{:S(2)}, u32[]{:S(2)}) collective-permute-start(bf16[272,256]{1,0:T(8,128)(2,1)} %get-tuple-element.45.refs_4_), channel_id=1, source_target_pairs={{0,16},{16,0},{1,17},{17,1},{2,18},{18,2},{3,19},{19,3},{4,20},{20... | collective-permute-start | bytes 417800 | tf_op jit(solution)/shard_map/ppermute | solution.py:865
  77.2 0.7 copy-start.2
  83.9 9.0 %collective-permute-start.3 = (bf16[2,2,128,128]{3,2,1,0:T(8,128)(2,1)}, bf16[2,2,128,128]{3,2,1,0:T(8,128)(2,1)S(1)}, u32[]{:S(2)}, u32[]{:S(2)}) collective-permute-start(bf16[2,2,128,128]{3,2,1,0:T(8,128)(2,1)} %get-tuple-element.63), channel_id=1, source_target_pairs={{0,16},{16,0},{1,17},{17,1},{2,18},{18,2},{3,19},{19,3},{4,20},{20... | collective-permute-start | bytes 393224 | tf_op jit(solution)/shard_map/ppermute | solution.py:865
  86.8 20.4 %all-to-all-start.2 = ((bf16[16,2,2,64,128]{4,3,2,1,0:T(8,128)(2,1)}), bf16[16,2,2,64,128]{4,3,2,1,0:T(8,128)(2,1)}, u32[]{:S(2)}, u32[]{:S(2)}) async-start(bf16[16,2,2,64,128]{4,3,2,1,0:T(8,128)(2,1)} %get-tuple-element.61), calls=%async_computation.2 | async-start | bytes 2097152 | tf_op jit(solution)/shard_map/all_to_all | solution.py:861
  92.8 0.7 copy-start.5
  107.2 18.4 %all-to-all-start.3 = ((bf16[16,2,2,64,128]{4,3,2,1,0:T(8,128)(2,1)}), bf16[16,2,2,64,128]{4,3,2,1,0:T(8,128)(2,1)S(1)}, u32[]{:S(2)}, u32[]{:S(2)}) async-start(bf16[16,2,2,64,128]{4,3,2,1,0:T(8,128)(2,1)} %shard_map.84), calls=%async_computation.3 | async-start | bytes 2097152 | tf_op jit(solution)/shard_map/all_to_all | solution.py:861

commit v9 on v8

--- a/solution.py
+++ b/solution.py
@@ -714,7 +714,33 @@
     outs.mark_values[...] = landmark_values
 
 
-def head_units(ins, slot, out_ref, lead, direct_ref, share):
+def several(*units):
+    for unit in units:
+        unit()
+
+
+def out_units(ins, slot, out_ref, lead, share):
+    mixing_low, values_low, _ = share
+    scale = ins.scales[slot : slot + 1]
+
+    def token_side(index):
+        place = slice(index * CHUNK, (index + 1) * CHUNK)
+        attended = wide_dot_nt(ins.token_low[place], mixing_low)
+        store_chunk(out_ref, (0, *lead), index, attended.astype(jnp.bfloat16))
+
+    def key_side(index):
+        place = slice(index * CHUNK, (index + 1) * CHUNK)
+        key_plow = (ins.key_exp[place] * scale).astype(jnp.bfloat16)
+        value_gradient = wide_dot_nt(key_plow, values_low)
+        store_chunk(out_ref, (1, *lead), index, value_gradient.astype(jnp.bfloat16))
+
+    chunks = ins.token_low.shape[0] // CHUNK
+    return [
+        functools.partial(unit, index) for unit in (token_side, key_side) for index in range(chunks)
+    ]
+
+
+def gradient_units(ins, slot, direct_ref, share):
     score_scale = HD ** (-0.5)
     mixing_low, values_low, row_total = share
     query_sums, key_sums = [], []
@@ -722,29 +748,25 @@
 
     def token_side(index):
         place = slice(index * CHUNK, (index + 1) * CHUNK)
-        prob = ins.token_prob[place]
-        attended = wide_dot_nt(prob.astype(jnp.bfloat16), mixing_low)
-        store_chunk(out_ref, (0, *lead), index, attended.astype(jnp.bfloat16))
+        prob = ins.token_prob[slot, place]
         token_grad = wide_dot(chunk_of(ins.vg, 1, slot, index), mixing_low)
         token_sgrad = (
             prob * (token_grad - jnp.sum(token_grad * prob, axis=1, keepdims=True))
         ).astype(jnp.bfloat16)
-        direct_ref[0, place] = wide_dot(token_sgrad, ins.marks[slot, 1]) * score_scale
-        key_sums.append(wide_dot(ins.turned[0, :, place], token_sgrad))
+        direct_ref[slot, 0, place] = wide_dot(token_sgrad, ins.marks[slot, 1]) * score_scale
+        key_sums.append(wide_dot(ins.turned[slot, 0, :, place], token_sgrad))
 
     def key_side(index):
         place = slice(index * CHUNK, (index + 1) * CHUNK)
-        key_prob = ins.key_exp[place] * scale
-        value_gradient = wide_dot_nt(key_prob.astype(jnp.bfloat16), values_low)
-        store_chunk(out_ref, (1, *lead), index, value_gradient.astype(jnp.bfloat16))
+        key_prob = ins.key_exp[slot, place] * scale
         key_dgrad = wide_dot(chunk_of(ins.vg, 0, slot, index), values_low)
         key_sgrad = (key_prob * (key_dgrad - row_total)).astype(jnp.bfloat16)
-        direct_ref[1, place] = wide_dot(key_sgrad, ins.marks[slot, 0]) * score_scale
-        query_sums.append(wide_dot(ins.turned[1, :, place], key_sgrad))
+        direct_ref[slot, 1, place] = wide_dot(key_sgrad, ins.marks[slot, 0]) * score_scale
+        query_sums.append(wide_dot(ins.turned[slot, 1, :, place], key_sgrad))
 
     chunks = tokens_of(ins.vg) // CHUNK
     units = [
-        functools.partial(unit, index) for unit in (key_side, token_side) for index in range(chunks)
+        functools.partial(unit, index) for index in range(chunks) for unit in (key_side, token_side)
     ]
     return units, query_sums, key_sums
 
@@ -765,20 +787,16 @@
     toward = split_dot(mark_halves, inverse_grad_halves) * factor
     power = 0.5 * (toward + toward.T)
     growth = None
-    units, query_sums, key_sums = head_units(
-        ins, 0, outs.out, (), outs.direct, share_parts(ins.share, False)
-    )
-    work = iter(units)
+    work = iter(out_units(ins, 0, outs.out, (), share_parts(ins.share, False)))
 
     def beside():
         next(work, lambda: None)()
 
     for sweep in range(PINV_ITERS):
         if sweep == 0:
-            for ref in (ins.marks, ins.vg, ins.key_exp, ins.turned):
-                need(ref)
+            need(ins.token_low)
         if sweep == 2:
-            need(ins.token_prob)
+            need(ins.key_exp)
         for ref in (ins.pair, ins.weight, ins.growth):
             need(ref, sweep)
         pair = (ins.pair[sweep, 0], ins.pair[sweep, 1])
@@ -803,7 +821,6 @@
     for unit in work:
         unit()
     put(outs.out)
-    put(outs.direct)
     need()
     mark_grad = factor * (
         split_dot_nt((ins.last_growth[0], ins.last_growth[1]), inverse_grad_halves)
@@ -817,22 +834,37 @@
             jnp.concatenate([left_high, left_low], axis=1), jnp.concatenate([right, right], axis=0)
         )
 
-    outs.totals[0] = marks_dot(mark_sgrad, ins.marks[0, 1]) + sum(query_sums[1:], query_sums[0]).T
-    outs.totals[1] = marks_dot(mark_sgrad.T, ins.marks[0, 0]) + sum(key_sums[1:], key_sums[0]).T
-
-
-def other_gradient_compute(ins, outs, need, put):
+    outs.mark_grads[0] = marks_dot(mark_sgrad, ins.marks[0, 1])
+    outs.mark_grads[1] = marks_dot(mark_sgrad.T, ins.marks[0, 0])
+
+
+def other_out_compute(ins, outs, need, put):
+    need(ins.got_share)
+    need(ins.scales)
+    need(ins.token_low)
+    units = out_units(ins, 1, outs.out, (1,), share_parts(ins.got_share, True))
+    chunks = len(units) // 2
+    several(*units[:chunks])
     need()
+    several(*units[chunks:])
     outs.out[:, :, 0] = ins.own_out[...]
-    units, query_sums, key_sums = head_units(
-        ins, 1, outs.out, (1,), outs.direct, share_parts(ins.got_share, True)
-    )
-    for unit in units:
-        unit()
-    put(outs.out)
+
+
+def gradient_compute(ins, outs, need, put):
+    for ref in (ins.share, ins.got_share, ins.scales, ins.marks, ins.vg, ins.mark_grads):
+        need(ref)
     marks_scale = HD ** (-0.5) / (tokens_of(ins.vg) // HALF)
-    for kind, sums in enumerate((query_sums, key_sums)):
-        for slot, total in ((0, ins.totals[kind]), (1, sum(sums[1:], sums[0]).T)):
+    for slot in range(2):
+        for ref in (ins.key_exp, ins.token_prob, ins.turned):
+            need(ref, slot)
+        share = share_parts(ins.got_share if slot else ins.share, bool(slot))
+        units, query_sums, key_sums = gradient_units(ins, slot, outs.direct, share)
+        several(*units)
+        put(outs.direct, slot)
+        for kind, sums in enumerate((query_sums, key_sums)):
+            total = sum(sums[1:], sums[0]).T
+            if slot == 0:
+                total = total + ins.mark_grads[kind]
             total = total * marks_scale
             outs.near[kind, slot] = total[:HALF]
             outs.far[kind, slot] = total[HALF:].astype(jnp.bfloat16)
@@ -846,13 +878,13 @@
     per = CHUNK // segment_len
     for index in range(tokens_of(out_ref) // CHUNK):
         place, start = slice(index * per, (index + 1) * per), index * CHUNK
-        for slot, direct_ref in enumerate((ins.own_direct, ins.other_direct)):
+        for slot in range(2):
             for kind in range(2):
                 marks = ins.near[kind, slot, place] + ins.got_far[
                     kind, 1 - slot, place
                 ].astype(jnp.float32)
                 spread = jnp.broadcast_to(marks[:, None], (per, segment_len, HD))
-                total = direct_ref[kind, start : start + CHUNK] + spread.reshape(CHUNK, HD)
+                total = ins.direct[slot, kind, start : start + CHUNK] + spread.reshape(CHUNK, HD)
                 store_chunk(out_ref, (kind, slot), index, total.astype(jnp.bfloat16))
         put(out_ref, index * group)
 
@@ -867,11 +899,13 @@
 
 def body(queries, keys, values, out_grad):
     half = lax.axis_index("half").reshape(1)
-    qk = exchange(pack(half, queries, keys))
+    qk, vg_packed = lax.optimization_barrier(
+        (exchange(pack(half, queries, keys)), pack(half, values, out_grad))
+    )
     tokens = qk.shape[0] * qk.shape[3]
     mine = landmarks_of(qk)
     theirs = partner(mine)
-    vg_packed, mine = lax.optimization_barrier((pack(half, values, out_grad), mine))
+    vg_packed, mine = lax.optimization_barrier((vg_packed, mine))
     vg = exchange(vg_packed)
     kept = staged_call(
         probability_compute,
@@ -922,53 +956,54 @@
             mark_values=mixed.mark_values,
             share=mixed.share,
             scales=mixed.scales,
-            marks=kept.marks,
-            vg=vg,
-            key_exp=(kept.key_exp, SLOTS[0]),
-            turned=(kept.turned, SLOTS[0]),
+            token_low=(kept.token_low, SLOTS[0]),
             pair=(kept.pair, LEAD),
             weight=(kept.weight, LEAD),
             growth=(kept.growth, LEAD),
-            token_prob=(kept.token_prob, SLOTS[0]),
+            key_exp=(kept.key_exp, SLOTS[0]),
             last_growth=kept.last_growth,
+            marks=kept.marks,
         ),
+        dict(out=low(qk.shape[0], 2, *qk.shape[3:]), mark_grads=wide(2, M, HD)),
+        14,
+    )
+    first_results = staged_call(
+        other_out_compute,
         dict(
-            out=low(qk.shape[0], 2, *qk.shape[3:]),
-            direct=wide(2, tokens, HD),
-            totals=wide(2, M, HD),
+            got_share=got_share,
+            scales=mixed.scales,
+            token_low=(kept.token_low, SLOTS[1]),
+            key_exp=(kept.key_exp, SLOTS[1]),
+            own_out=own.out,
         ),
-        14,
-    )
-    other = staged_call(
-        other_gradient_compute,
+        dict(out=low(*qk.shape)),
+        1,
+    ).out
+    attended, value_gradient_array = unpack(half, exchange(first_results))
+    grads = staged_call(
+        gradient_compute,
         dict(
+            share=mixed.share,
             got_share=got_share,
             scales=mixed.scales,
             marks=kept.marks,
             vg=vg,
-            key_exp=(kept.key_exp, SLOTS[1]),
-            turned=(kept.turned, SLOTS[1]),
-            token_prob=(kept.token_prob, SLOTS[1]),
-            own_out=own.out,
-            totals=own.totals,
+            key_exp=(kept.key_exp, LEAD),
+            token_prob=(kept.token_prob, LEAD),
+            turned=(kept.turned, LEAD),
+            mark_grads=own.mark_grads,
         ),
         dict(
-            out=low(*qk.shape),
             far=low(2, 2, HALF, HD),
             near=wide(2, 2, HALF, HD),
-            direct=wide(2, tokens, HD),
+            direct=(wide(2, 2, tokens, HD), LEAD),
         ),
-        3,
-    )
-    attended, value_gradient_array = unpack(half, exchange(other.out))
+        LONG,
+        after=(first_results,),
+    )
     results = staged_call(
         finish_compute,
-        dict(
-            got_far=partner(other.far),
-            near=other.near,
-            own_direct=own.direct,
-            other_direct=other.direct,
-        ),
+        dict(got_far=partner(grads.far), near=grads.near, direct=grads.direct),
         dict(out=(low(*qk.shape), GROUPS)),
         LONG,
     ).out

time: 127 us -> 129 us (1.016)
  blocking collectives: 21.1 us -> 0 us
  waiting for transfers between devices: 37.1 us -> 50.3 us
  starting transfers between devices: 18.7 us -> 24.7 us
  Pallas kernels: 46.3 us -> 49.7 us
    all_to_all x1 -> x0, blocking collectives: 21.1 us -> none  [exchange(): lax.all_to_all(packed, 'cube', split_axis=0, concat_axis=0, tiled=True)]
    all_to_all x3 -> x4, waiting for transfers between devices: 27 us -> 39.1 us  [exchange(): lax.all_to_all(packed, 'cube', split_axis=0, concat_axis=0, tiled=True)]
    all_to_all x3 -> x4, starting transfers between devices: 12.6 us -> 18.9 us  [exchange(): lax.all_to_all(packed, 'cube', split_axis=0, concat_axis=0, tiled=True)]
    pallas_call x6 -> x7, Pallas kernels: 38.4 us -> 41.8 us  [staged_call(): pl.pallas_call(kernel, out_shape=shapes, in_specs=[anywhere] * (n_in + n_...]
  transfers between devices with their start and end apart: 7 -> 8, of which waited for: 6 -> 7; matrix products, arithmetic and copies ran while one was open for 0% -> 0% of each run, Pallas kernels for 25% -> 24%
where the time goes in v9:
time: 129 us; the launch traced here: 128 us
  waiting for transfers between devices  50.3 us (39%)
  Pallas kernels  49.7 us (39%)
  starting transfers between devices  24.7 us (19%)
  local copies, waits for them, and re-layouts  2.64 us (2%)
    pallas_call x7, Pallas kernels, staged_call(): pl.pallas_call(kernel, out_shape=shapes, in_specs=[anywhere] * (n_in + n_...  41.8 us
    all_to_all x4, waiting for transfers between devices, exchange(): lax.all_to_all(packed, 'cube', split_axis=0, concat_axis=0, tiled=True)  39.1 us
    all_to_all x4, starting transfers between devices, exchange(): lax.all_to_all(packed, 'cube', split_axis=0, concat_axis=0, tiled=True)  18.9 us
    ppermute x4, waiting for transfers between devices, partner(): return lax.ppermute(array, 'half', SWAP)  11.2 us
    pallas_call x4, Pallas kernels, layout_call(): pl.pallas_call(kernel, out_shape=out_shape, in_specs=[pl.BlockSpec(memory...  7.62 us
    ppermute x4, starting transfers between devices, partner(): return lax.ppermute(array, 'half', SWAP)  5.76 us
    unnamed x12, local copies, waits for them, and re-layouts  2.64 us
  transfers between devices with their start and end apart: 8, of which 7 were waited for; matrix products, arithmetic and copies ran while one was open for 0% of the time, Pallas kernels for 24%

profile of v9, /device:TPU:0, one launch (start us, length us, event | category | flops | bytes accessed | tf_op | source)
XLA Modules:
  0.0 128.3 jit_solution(10468643866028887050)
XLA Ops:
  0.6 2.1 %shard_map.75 = bf16[16,2,2,64,128]{4,3,2,1,0:T(8,128)(2,1)} custom-call(s32[1]{0:T(128)} %bitcast.half_ref, bf16[64,4096]{1,0:T(8,128)(2,1)} %first_ref.2, bf16[64,4096]{1,0:T(8,128)(2,1)} %second_ref.2), custom_call_target="tpu_custom_call" | custom-call | bytes 2097152 | tf_op jit(solution)/shard_map/pallas_call | solution.py:502
  2.8 6.3 %all-to-all-start = ((bf16[16,2,2,64,128]{4,3,2,1,0:T(8,128)(2,1)}), bf16[16,2,2,64,128]{4,3,2,1,0:T(8,128)(2,1)S(1)}, u32[]{:S(2)}, u32[]{:S(2)}) async-start(bf16[16,2,2,64,128]{4,3,2,1,0:T(8,128)(2,1)} %shard_map.75), calls=%async_computation | async-start | bytes 2097152 | tf_op jit(solution)/shard_map/all_to_all | solution.py:893
  9.1 2.2 %shard_map.76 = bf16[16,2,2,64,128]{4,3,2,1,0:T(8,128)(2,1)} custom-call(s32[1]{0:T(128)} %bitcast.half_ref, bf16[64,4096]{1,0:T(8,128)(2,1)} %first_ref.3, bf16[64,4096]{1,0:T(8,128)(2,1)} %second_ref.3), custom_call_target="tpu_custom_call" | custom-call | bytes 2097152 | tf_op jit(solution)/shard_map/pallas_call | solution.py:502
  11.3 12.6 %all-to-all-done.qk_ref.refs_0_ = bf16[16,2,2,64,128]{4,3,2,1,0:T(8,128)(2,1)S(1)} async-done(((bf16[16,2,2,64,128]{4,3,2,1,0:T(8,128)(2,1)}), bf16[16,2,2,64,128]{4,3,2,1,0:T(8,128)(2,1)S(1)}, u32[]{:S(2)}, u32[]{:S(2)}) %all-to-all-start) | async-done | bytes 1048608 | tf_op jit(solution)/shard_map/all_to_all | solution.py:893
  24.2 2.7 %collective-permute-start = (bf16[2,2,128,128]{3,2,1,0:T(8,128)(2,1)S(1)}, bf16[2,2,128,128]{3,2,1,0:T(8,128)(2,1)S(1)}, u32[]{:S(2)}, u32[]{:S(2)}) collective-permute-start(bf16[2,2,128,128]{3,2,1,0:T(8,128)(2,1)S(1)} %shard_map.77.refs_1_), channel_id=1, source_target_pairs={{0,16},{16,0},{1,17},{17,1},{2,18},{18,2},{3,19},{19,3},{4,20},{20... | collective-permute-start | bytes 393224 | tf_op jit(solution)/shard_map/ppermute | solution.py:897
  26.9 4.3 %all-to-all-start.1 = ((bf16[16,2,2,64,128]{4,3,2,1,0:T(8,128)(2,1)}), bf16[16,2,2,64,128]{4,3,2,1,0:T(8,128)(2,1)}, u32[]{:S(2)}, u32[]{:S(2)}) async-start(bf16[16,2,2,64,128]{4,3,2,1,0:T(8,128)(2,1)} %shard_map.76), calls=%async_computation.1 | async-start | bytes 2097152 | tf_op jit(solution)/shard_map/all_to_all | solution.py:893
  31.2 1.4 %collective-permute-done.refs_2_ = bf16[2,2,128,128]{3,2,1,0:T(8,128)(2,1)S(1)} collective-permute-done((bf16[2,2,128,128]{3,2,1,0:T(8,128)(2,1)S(1)}, bf16[2,2,128,128]{3,2,1,0:T(8,128)(2,1)S(1)}, u32[]{:S(2)}, u32[]{:S(2)}) %collective-permute-start) | collective-permute-done | bytes 131104 | tf_op jit(solution)/shard_map/ppermute | solution.py:897
  33.3 10.3 %shard_map.78 = (bf16[2,2,256,128]{3,2,1,0:T(8,128)(2,1)}, f32[2,1024,256]{2,1,0:T(8,128)}, bf16[2,1024,256]{2,1,0:T(8,128)(2,1)}, f32[2,1024,256]{2,1,0:T(8,128...) custom-call(bf16[16,2,2,64,128]{4,3,2,1,0:T(8,128)(2,1)} %copy-done,, ...), custom_call_target="tpu_custom_call" | custom-call | flops 199999995904 | bytes 16003072 | tf_op jit(solution)/shard_map/pallas_call | solution.py:415
  43.5 2.9 %all-to-all-done.1.refs_0_.refs_4_ = bf16[16,2,2,64,128]{4,3,2,1,0:T(8,128)(2,1)} async-done(((bf16[16,2,2,64,128]{4,3,2,1,0:T(8,128)(2,1)}), bf16[16,2,2,64,128]{4,3,2,1,0:T(8,128)(2,1)}, u32[]{:S(2)}, u32[]{:S(2)}) %all-to-all-start.1) | async-done | bytes 1048608 | tf_op jit(solution)/shard_map/all_to_all | solution.py:893
  46.5 3.1 %shard_map.79 = (bf16[272,256]{1,0:T(8,128)(2,1)}, f32[256,256]{1,0:T(8,128)}) custom-call(bf16[16,2,2,64,128]{4,3,2,1,0:T(8,128)(2,1)} %all-to-all-done.1.refs_0_.refs_4_, f32[8,256]{1,0:T(8,128)} %get-tuple-element.41.refs_1_.refs_2_, bf16[2,1024,256]{2,1,0:T(8,128)(2,1)} %get-tuple-element.42.refs_2_, ...), custom_call_target="tpu_custom_call" | custom-call | flops 2000000000 | bytes 3555328 | tf_op jit(solution)/shard_map/pallas_call | solution.py:415
  49.6 8.4 %collective-permute-done.1.refs_0_ = bf16[272,256]{1,0:T(8,128)(2,1)S(1)} collective-permute-done((bf16[272,256]{1,0:T(8,128)(2,1)}, bf16[272,256]{1,0:T(8,128)(2,1)S(1)}, u32[]{:S(2)}, u32[]{:S(2)}) %collective-permute-start.1) | collective-permute-done | bytes 139296 | tf_op jit(solution)/shard_map/ppermute | solution.py:897
  58.7 2.3 %shard_map.80 = (bf16[272,256]{1,0:T(8,128)(2,1)}, f32[8,256]{1,0:T(8,128)}, f32[128,256]{1,0:T(8,128)}, f32[128,256]{1,0:T(8,128)}) custom-call(bf16[272,256]{1,0:T(8,128)(2,1)} %copy-done.3, f32[256,256]{1,0:T(8,128)} %get-tuple-element.45.refs_1_, f32[8,256]{1,0:T(8,128)} %get-tuple-element.41.refs_1_.refs_2_, bf16[2,256,256]{2,1,0:T(8,128)(2,1)} %get-tuple-element.46.refs_3_), custom_call_target="tpu_custom_call" | custom-call | flops 1000000000 | bytes 1081344 | tf_op jit(solution)/shard_map/pallas_call | solution.py:415
  61.1 13.1 %shard_map.81 = (bf16[16,2,64,128]{3,2,1,0:T(8,128)(2,1)}, f32[2,256,128]{2,1,0:T(8,128)}) custom-call(f32[256,256]{1,0:T(8,128)} %get-tuple-element.50.refs_0_, f32[8,128]{1,0:T(8,128)} %get-tuple-element.51.refs_1_, f32[128,256]{1,0:T(8,128)} %get-tuple-element.52.refs_2_, f32[128,256]{1,0:T(8,128)} %get-tuple-element.53.refs_3_, ...), custom_call_target="tpu_custom_call" | custom-call | flops 14000000000 | bytes 11423744 | tf_op jit(solution)/shard_map/pallas_call | solution.py:415
  74.9 3.0 %shard_map.82.refs_9_ = bf16[16,2,2,64,128]{4,3,2,1,0:T(8,128)(2,1)} custom-call(bf16[272,256]{1,0:T(8,128)(2,1)} %copy-done.2, f32[8,256]{1,0:T(8,128)} %get-tuple-element.48.refs_5_.refs_1_.refs_2_, bf16[2,1024,256]{2,1,0:T(8,128)(2,1)} %get-tuple-element.43.refs_3_.refs_6_.refs_2_, f32[2,1024,256]{2,1,0:T(8,128)} %get-tuple-element.49.refs_10_.refs_3_.refs_5_, ...), custom_call_target="tpu_custom_call" | custom-call | flops 1000000000 | bytes 4866048 | tf_op jit(solution)/shard_map/pallas_call | solution.py:415
  77.9 7.1 %shard_map.84 = (bf16[2,2,128,128]{3,2,1,0:T(8,128)(2,1)}, f32[2,2,128,128]{3,2,1,0:T(8,128)}, f32[2,2,1024,128]{3,2,1,0:T(8,128)}) custom-call(bf16[272,256]{1,0:T(8,128)(2,1)} %get-tuple-element.47.refs_4_.refs_0_, bf16[272,256]{1,0:T(8,128)(2,1)} %copy-done.2, f32[8,256]{1,0:T(8,128)} %get-tuple-element.48.refs_5_.refs_1_.refs_2_, ...), custom_call_target="tpu_custom_call" | custom-call | flops 199999995904 | bytes 9592832 | tf_op jit(solution)/shard_map/pallas_call | solution.py:415
  85.1 3.0 %collective-permute-start.3 = (bf16[2,2,128,128]{3,2,1,0:T(8,128)(2,1)}, bf16[2,2,128,128]{3,2,1,0:T(8,128)(2,1)S(1)}, u32[]{:S(2)}, u32[]{:S(2)}) collective-permute-start(bf16[2,2,128,128]{3,2,1,0:T(8,128)(2,1)} %get-tuple-element.64), channel_id=1, source_target_pairs={{0,16},{16,0},{1,17},{17,1},{2,18},{18,2},{3,19},{19,3},{4,20},{20... | collective-permute-start | bytes 393224 | tf_op jit(solution)/shard_map/ppermute | solution.py:897
  88.0 4.6 %all-to-all-start.2 = ((bf16[16,2,2,64,128]{4,3,2,1,0:T(8,128)(2,1)}), bf16[16,2,2,64,128]{4,3,2,1,0:T(8,128)(2,1)}, u32[]{:S(2)}, u32[]{:S(2)}) async-start(bf16[16,2,2,64,128]{4,3,2,1,0:T(8,128)(2,1)} %shard_map.82.refs_9_), calls=%async_computation.2 | async-start | bytes 2097152 | tf_op jit(solution)/shard_map/all_to_all | solution.py:893
  92.6 1.4 %collective-permute-done.3.refs_0_ = bf16[2,2,128,128]{3,2,1,0:T(8,128)(2,1)S(1)} collective-permute-done((bf16[2,2,128,128]{3,2,1,0:T(8,128)(2,1)}, bf16[2,2,128,128]{3,2,1,0:T(8,128)(2,1)S(1)}, u32[]{:S(2)}, u32[]{:S(2)}) %collective-permute-start.3) | collective-permute-done | bytes 131104 | tf_op jit(solution)/shard_map/ppermute | solution.py:897
  94.7 2.9 %shard_map.85 = bf16[16,2,2,64,128]{4,3,2,1,0:T(8,128)(2,1)} custom-call(bf16[2,2,128,128]{3,2,1,0:T(8,128)(2,1)} %copy-done.5, f32[2,2,128,128]{3,2,1,0:T(8,128)} %get-tuple-element.65.refs_1_, f32[2,2,1024,128]{3,2,1,0:T(8,128)} %get-tuple-element.66.refs_2_), custom_call_target="tpu_custom_call" | custom-call | flops 199999995904 | bytes 3538944 | tf_op jit(solution)/shard_map/pallas_call | solution.py:415
  97.6 11.1 %all-to-all-done.2.packed_ref = bf16[16,2,2,64,128]{4,3,2,1,0:T(8,128)(2,1)} async-done(((bf16[16,2,2,64,128]{4,3,2,1,0:T(8,128)(2,1)}), bf16[16,2,2,64,128]{4,3,2,1,0:T(8,128)(2,1)}, u32[]{:S(2)}, u32[]{:S(2)}) %all-to-all-start.2) | async-done | bytes 1048608 | tf_op jit(solution)/shard_map/all_to_all | solution.py:893
  108.7 3.7 %all-to-all-start.3 = ((bf16[16,2,2,64,128]{4,3,2,1,0:T(8,128)(2,1)}), bf16[16,2,2,64,128]{4,3,2,1,0:T(8,128)(2,1)S(1)}, u32[]{:S(2)}, u32[]{:S(2)}) async-start(bf16[16,2,2,64,128]{4,3,2,1,0:T(8,128)(2,1)} %shard_map.85), calls=%async_computation.3 | async-start | bytes 2097152 | tf_op jit(solution)/shard_map/all_to_all | solution.py:893
  112.3 2.3 %shard_map.83 = (bf16[64,4096]{1,0:T(8,128)(2,1)}, bf16[64,4096]{1,0:T(8,128)(2,1)}) custom-call(s32[1]{0:T(128)} %bitcast.half_ref, bf16[16,2,2,64,128]{4,3,2,1,0:T(8,128)(2,1)} %all-to-all-done.2.packed_ref), custom_call_target="tpu_custom_call" | custom-call | bytes 2097152 | tf_op jit(solution)/shard_map/pallas_call | solution.py:502
  114.6 12.5 %all-to-all-done.3.packed_ref = bf16[16,2,2,64,128]{4,3,2,1,0:T(8,128)(2,1)S(1)} async-done(((bf16[16,2,2,64,128]{4,3,2,1,0:T(8,128)(2,1)}), bf16[16,2,2,64,128]{4,3,2,1,0:T(8,128)(2,1)S(1)}, u32[]{:S(2)}, u32[]{:S(2)}) %all-to-all-start.3) | async-done | bytes 1048608 | tf_op jit(solution)/shard_map/all_to_all | solution.py:893
  127.1 1.0 shard_map.86
  (16 shorter events, 3.1 us)
Async XLA Ops:
  2.8 21.1 %all-to-all-start = ((bf16[16,2,2,64,128]{4,3,2,1,0:T(8,128)(2,1)}), bf16[16,2,2,64,128]{4,3,2,1,0:T(8,128)(2,1)S(1)}, u32[]{:S(2)}, u32[]{:S(2)}) async-start(bf16[16,2,2,64,128]{4,3,2,1,0:T(8,128)(2,1)} %shard_map.75), calls=%async_computation | async-start | bytes 2097152 | tf_op jit(solution)/shard_map/all_to_all | solution.py:893
  23.9 8.7 %copy-start = (bf16[16,2,2,64,128]{4,3,2,1,0:T(8,128)(2,1)}, bf16[16,2,2,64,128]{4,3,2,1,0:T(8,128)(2,1)S(1)}, u32[]{:S(2)}) copy-start(bf16[16,2,2,64,128]{4,3,2,1,0:T(8,128)(2,1)S(1)} %all-to-all-done.qk_ref.refs_0_) | copy-start | bytes 3145732
  24.2 8.4 %copy-start.1 = (bf16[2,2,128,128]{3,2,1,0:T(8,128)(2,1)}, bf16[2,2,128,128]{3,2,1,0:T(8,128)(2,1)S(1)}, u32[]{:S(2)}) copy-start(bf16[2,2,128,128]{3,2,1,0:T(8,128)(2,1)S(1)} %shard_map.77.refs_1_) | copy-start | bytes 393220
  24.2 8.4 %collective-permute-start = (bf16[2,2,128,128]{3,2,1,0:T(8,128)(2,1)S(1)}, bf16[2,2,128,128]{3,2,1,0:T(8,128)(2,1)S(1)}, u32[]{:S(2)}, u32[]{:S(2)}) collective-permute-start(bf16[2,2,128,128]{3,2,1,0:T(8,128)(2,1)S(1)} %shard_map.77.refs_1_), channel_id=1, source_target_pairs={{0,16},{16,0},{1,17},{17,1},{2,18},{18,2},{3,19},{19,3},{4,20},{20... | collective-permute-start | bytes 393224 | tf_op jit(solution)/shard_map/ppermute | solution.py:897
  26.9 19.6 %all-to-all-start.1 = ((bf16[16,2,2,64,128]{4,3,2,1,0:T(8,128)(2,1)}), bf16[16,2,2,64,128]{4,3,2,1,0:T(8,128)(2,1)}, u32[]{:S(2)}, u32[]{:S(2)}) async-start(bf16[16,2,2,64,128]{4,3,2,1,0:T(8,128)(2,1)} %shard_map.76), calls=%async_computation.1 | async-start | bytes 2097152 | tf_op jit(solution)/shard_map/all_to_all | solution.py:893
  32.6 0.7 copy-start.4
  49.5 8.5 %collective-permute-start.1 = (bf16[272,256]{1,0:T(8,128)(2,1)}, bf16[272,256]{1,0:T(8,128)(2,1)S(1)}, u32[]{:S(2)}, u32[]{:S(2)}) collective-permute-start(bf16[272,256]{1,0:T(8,128)(2,1)} %get-tuple-element.44), channel_id=1, source_target_pairs={{0,16},{16,0},{1,17},{17,1},{2,18},{18,2},{3,19},{19,3},{4,20},{20... | collective-permute-start | bytes 417800 | tf_op jit(solution)/shard_map/ppermute | solution.py:897
  58.1 0.7 copy-start.3
  61.0 13.2 %collective-permute-start.2 = (bf16[272,256]{1,0:T(8,128)(2,1)}, bf16[272,256]{1,0:T(8,128)(2,1)S(1)}, u32[]{:S(2)}, u32[]{:S(2)}) collective-permute-start(bf16[272,256]{1,0:T(8,128)(2,1)} %get-tuple-element.47.refs_4_.refs_0_), channel_id=1, source_target_pairs={{0,16},{16,0},{1,17},{17,1},{2,18},{18,2},{3,19},{19,3},{4,20},{20... | collective-permute-start | bytes 417800 | tf_op jit(solution)/shard_map/ppermute | solution.py:897
  74.3 0.7 copy-start.2
  85.1 9.0 %collective-permute-start.3 = (bf16[2,2,128,128]{3,2,1,0:T(8,128)(2,1)}, bf16[2,2,128,128]{3,2,1,0:T(8,128)(2,1)S(1)}, u32[]{:S(2)}, u32[]{:S(2)}) collective-permute-start(bf16[2,2,128,128]{3,2,1,0:T(8,128)(2,1)} %get-tuple-element.64), channel_id=1, source_target_pairs={{0,16},{16,0},{1,17},{17,1},{2,18},{18,2},{3,19},{19,3},{4,20},{20... | collective-permute-start | bytes 393224 | tf_op jit(solution)/shard_map/ppermute | solution.py:897
  88.0 20.6 %all-to-all-start.2 = ((bf16[16,2,2,64,128]{4,3,2,1,0:T(8,128)(2,1)}), bf16[16,2,2,64,128]{4,3,2,1,0:T(8,128)(2,1)}, u32[]{:S(2)}, u32[]{:S(2)}) async-start(bf16[16,2,2,64,128]{4,3,2,1,0:T(8,128)(2,1)} %shard_map.82.refs_9_), calls=%async_computation.2 | async-start | bytes 2097152 | tf_op jit(solution)/shard_map/all_to_all | solution.py:893
  94.0 0.7 copy-start.5
  108.7 18.4 %all-to-all-start.3 = ((bf16[16,2,2,64,128]{4,3,2,1,0:T(8,128)(2,1)}), bf16[16,2,2,64,128]{4,3,2,1,0:T(8,128)(2,1)S(1)}, u32[]{:S(2)}, u32[]{:S(2)}) async-start(bf16[16,2,2,64,128]{4,3,2,1,0:T(8,128)(2,1)} %shard_map.85), calls=%async_computation.3 | async-start | bytes 2097152 | tf_op jit(solution)/shard_map/all_to_all | solution.py:893

commit v10 on v9

--- a/solution.py
+++ b/solution.py
@@ -1005,7 +1005,7 @@
         finish_compute,
         dict(got_far=partner(grads.far), near=grads.near, direct=grads.direct),
         dict(out=(low(*qk.shape), GROUPS)),
-        LONG,
+        0.1,
     ).out
     query_grad, key_grad = unpack(half, exchange(results))
     return attended, query_grad, key_grad, value_gradient_array

time: 129 us -> 126 us (0.977)
  waiting for transfers between devices: 50.3 us -> 45.6 us
  starting transfers between devices: 24.7 us -> 26.5 us
    all_to_all x4, waiting for transfers between devices: 39.1 us -> 28.1 us  [exchange(): lax.all_to_all(packed, 'cube', split_axis=0, concat_axis=0, tiled=True)]
    ppermute x4, waiting for transfers between devices: 11.2 us -> 17.5 us  [partner(): return lax.ppermute(array, 'half', SWAP)]
    all_to_all x4, starting transfers between devices: 18.9 us -> 22.3 us  [exchange(): lax.all_to_all(packed, 'cube', split_axis=0, concat_axis=0, tiled=True)]
    ppermute x4, starting transfers between devices: 5.76 us -> 4.26 us  [partner(): return lax.ppermute(array, 'half', SWAP)]
  transfers between devices with their start and end apart: 8 -> 8, of which waited for: 7 -> 6; matrix products, arithmetic and copies ran while one was open for 0% -> 0% of each run, Pallas kernels for 24% -> 30%
where the time goes in v10:
time: 126 us; the launch traced here: 125 us
  Pallas kernels  49.7 us (39%)
  waiting for transfers between devices  45.6 us (36%)
  starting transfers between devices  26.5 us (21%)
  local copies, waits for them, and re-layouts  2.64 us (2%)
    pallas_call x7, Pallas kernels, staged_call(): pl.pallas_call(kernel, out_shape=shapes, in_specs=[anywhere] * (n_in + n_...  41.8 us
    all_to_all x4, waiting for transfers between devices, exchange(): lax.all_to_all(packed, 'cube', split_axis=0, concat_axis=0, tiled=True)  28.1 us
    all_to_all x4, starting transfers between devices, exchange(): lax.all_to_all(packed, 'cube', split_axis=0, concat_axis=0, tiled=True)  22.3 us
    ppermute x4, waiting for transfers between devices, partner(): return lax.ppermute(array, 'half', SWAP)  17.5 us
    pallas_call x4, Pallas kernels, layout_call(): pl.pallas_call(kernel, out_shape=out_shape, in_specs=[pl.BlockSpec(memory...  7.62 us
    ppermute x4, starting transfers between devices, partner(): return lax.ppermute(array, 'half', SWAP)  4.26 us
    unnamed x12, local copies, waits for them, and re-layouts  2.64 us
  transfers between devices with their start and end apart: 8, of which 6 were waited for; matrix products, arithmetic and copies ran while one was open for 0% of the time, Pallas kernels for 30%

profile of v10, /device:TPU:0, one launch (start us, length us, event | category | flops | bytes accessed | tf_op | source)
XLA Modules:
  0.0 125.4 jit_solution(1358447076881353489)
XLA Ops:
  0.6 2.1 %shard_map.75 = bf16[16,2,2,64,128]{4,3,2,1,0:T(8,128)(2,1)} custom-call(s32[1]{0:T(128)} %bitcast.half_ref, bf16[64,4096]{1,0:T(8,128)(2,1)} %first_ref.2, bf16[64,4096]{1,0:T(8,128)(2,1)} %second_ref.2), custom_call_target="tpu_custom_call" | custom-call | bytes 2097152 | tf_op jit(solution)/shard_map/pallas_call | solution.py:502
  2.8 6.3 %all-to-all-start = ((bf16[16,2,2,64,128]{4,3,2,1,0:T(8,128)(2,1)}), bf16[16,2,2,64,128]{4,3,2,1,0:T(8,128)(2,1)S(1)}, u32[]{:S(2)}, u32[]{:S(2)}) async-start(bf16[16,2,2,64,128]{4,3,2,1,0:T(8,128)(2,1)} %shard_map.75), calls=%async_computation | async-start | bytes 2097152 | tf_op jit(solution)/shard_map/all_to_all | solution.py:893
  9.1 2.2 %shard_map.76 = bf16[16,2,2,64,128]{4,3,2,1,0:T(8,128)(2,1)} custom-call(s32[1]{0:T(128)} %bitcast.half_ref, bf16[64,4096]{1,0:T(8,128)(2,1)} %first_ref.3, bf16[64,4096]{1,0:T(8,128)(2,1)} %second_ref.3), custom_call_target="tpu_custom_call" | custom-call | bytes 2097152 | tf_op jit(solution)/shard_map/pallas_call | solution.py:502
  11.3 12.6 %all-to-all-done.qk_ref.refs_0_ = bf16[16,2,2,64,128]{4,3,2,1,0:T(8,128)(2,1)S(1)} async-done(((bf16[16,2,2,64,128]{4,3,2,1,0:T(8,128)(2,1)}), bf16[16,2,2,64,128]{4,3,2,1,0:T(8,128)(2,1)S(1)}, u32[]{:S(2)}, u32[]{:S(2)}) %all-to-all-start) | async-done | bytes 1048608 | tf_op jit(solution)/shard_map/all_to_all | solution.py:893
  24.2 2.7 %collective-permute-start = (bf16[2,2,128,128]{3,2,1,0:T(8,128)(2,1)S(1)}, bf16[2,2,128,128]{3,2,1,0:T(8,128)(2,1)S(1)}, u32[]{:S(2)}, u32[]{:S(2)}) collective-permute-start(bf16[2,2,128,128]{3,2,1,0:T(8,128)(2,1)S(1)} %shard_map.77.refs_1_), channel_id=1, source_target_pairs={{0,16},{16,0},{1,17},{17,1},{2,18},{18,2},{3,19},{19,3},{4,20},{20... | collective-permute-start | bytes 393224 | tf_op jit(solution)/shard_map/ppermute | solution.py:897
  26.9 4.3 %all-to-all-start.1 = ((bf16[16,2,2,64,128]{4,3,2,1,0:T(8,128)(2,1)}), bf16[16,2,2,64,128]{4,3,2,1,0:T(8,128)(2,1)}, u32[]{:S(2)}, u32[]{:S(2)}) async-start(bf16[16,2,2,64,128]{4,3,2,1,0:T(8,128)(2,1)} %shard_map.76), calls=%async_computation.1 | async-start | bytes 2097152 | tf_op jit(solution)/shard_map/all_to_all | solution.py:893
  31.2 1.4 %collective-permute-done.refs_2_ = bf16[2,2,128,128]{3,2,1,0:T(8,128)(2,1)S(1)} collective-permute-done((bf16[2,2,128,128]{3,2,1,0:T(8,128)(2,1)S(1)}, bf16[2,2,128,128]{3,2,1,0:T(8,128)(2,1)S(1)}, u32[]{:S(2)}, u32[]{:S(2)}) %collective-permute-start) | collective-permute-done | bytes 131104 | tf_op jit(solution)/shard_map/ppermute | solution.py:897
  33.3 10.3 %shard_map.78 = (bf16[2,2,256,128]{3,2,1,0:T(8,128)(2,1)}, f32[2,1024,256]{2,1,0:T(8,128)}, bf16[2,1024,256]{2,1,0:T(8,128)(2,1)}, f32[2,1024,256]{2,1,0:T(8,128...) custom-call(bf16[16,2,2,64,128]{4,3,2,1,0:T(8,128)(2,1)} %copy-done,, ...), custom_call_target="tpu_custom_call" | custom-call | flops 199999995904 | bytes 16003072 | tf_op jit(solution)/shard_map/pallas_call | solution.py:415
  43.5 2.9 %all-to-all-done.1.refs_0_.refs_4_ = bf16[16,2,2,64,128]{4,3,2,1,0:T(8,128)(2,1)} async-done(((bf16[16,2,2,64,128]{4,3,2,1,0:T(8,128)(2,1)}), bf16[16,2,2,64,128]{4,3,2,1,0:T(8,128)(2,1)}, u32[]{:S(2)}, u32[]{:S(2)}) %all-to-all-start.1) | async-done | bytes 1048608 | tf_op jit(solution)/shard_map/all_to_all | solution.py:893
  46.5 3.1 %shard_map.79 = (bf16[272,256]{1,0:T(8,128)(2,1)}, f32[256,256]{1,0:T(8,128)}) custom-call(bf16[16,2,2,64,128]{4,3,2,1,0:T(8,128)(2,1)} %all-to-all-done.1.refs_0_.refs_4_, f32[8,256]{1,0:T(8,128)} %get-tuple-element.41.refs_1_.refs_2_, bf16[2,1024,256]{2,1,0:T(8,128)(2,1)} %get-tuple-element.42.refs_2_, ...), custom_call_target="tpu_custom_call" | custom-call | flops 2000000000 | bytes 3555328 | tf_op jit(solution)/shard_map/pallas_call | solution.py:415
  49.6 8.4 %collective-permute-done.1.refs_0_ = bf16[272,256]{1,0:T(8,128)(2,1)S(1)} collective-permute-done((bf16[272,256]{1,0:T(8,128)(2,1)}, bf16[272,256]{1,0:T(8,128)(2,1)S(1)}, u32[]{:S(2)}, u32[]{:S(2)}) %collective-permute-start.1) | collective-permute-done | bytes 139296 | tf_op jit(solution)/shard_map/ppermute | solution.py:897
  58.1 0.7 copy-done.4
  58.7 2.3 %shard_map.80 = (bf16[272,256]{1,0:T(8,128)(2,1)}, f32[8,256]{1,0:T(8,128)}, f32[128,256]{1,0:T(8,128)}, f32[128,256]{1,0:T(8,128)}) custom-call(bf16[272,256]{1,0:T(8,128)(2,1)} %copy-done.4, f32[256,256]{1,0:T(8,128)} %get-tuple-element.45.refs_1_, f32[8,256]{1,0:T(8,128)} %get-tuple-element.41.refs_1_.refs_2_, bf16[2,256,256]{2,1,0:T(8,128)(2,1)} %get-tuple-element.46.refs_3_), custom_call_target="tpu_custom_call" | custom-call | flops 1000000000 | bytes 1081344 | tf_op jit(solution)/shard_map/pallas_call | solution.py:415
  61.1 13.1 %shard_map.81 = (bf16[16,2,64,128]{3,2,1,0:T(8,128)(2,1)}, f32[2,256,128]{2,1,0:T(8,128)}) custom-call(f32[256,256]{1,0:T(8,128)} %get-tuple-element.50.refs_0_, f32[8,128]{1,0:T(8,128)} %get-tuple-element.51.refs_1_, f32[128,256]{1,0:T(8,128)} %get-tuple-element.52.refs_2_, f32[128,256]{1,0:T(8,128)} %get-tuple-element.53.refs_3_, ...), custom_call_target="tpu_custom_call" | custom-call | flops 14000000000 | bytes 11423744 | tf_op jit(solution)/shard_map/pallas_call | solution.py:415
  74.9 3.0 %shard_map.82.refs_9_ = bf16[16,2,2,64,128]{4,3,2,1,0:T(8,128)(2,1)} custom-call(bf16[272,256]{1,0:T(8,128)(2,1)} %copy-done.2, f32[8,256]{1,0:T(8,128)} %get-tuple-element.48.refs_5_.refs_1_.refs_2_, bf16[2,1024,256]{2,1,0:T(8,128)(2,1)} %get-tuple-element.43.refs_3_.refs_6_.refs_2_, f32[2,1024,256]{2,1,0:T(8,128)} %get-tuple-element.49.refs_10_.refs_3_.refs_5_, ...), custom_call_target="tpu_custom_call" | custom-call | flops 1000000000 | bytes 4866048 | tf_op jit(solution)/shard_map/pallas_call | solution.py:415
  77.9 6.1 %all-to-all-start.2 = ((bf16[16,2,2,64,128]{4,3,2,1,0:T(8,128)(2,1)}), bf16[16,2,2,64,128]{4,3,2,1,0:T(8,128)(2,1)}, u32[]{:S(2)}, u32[]{:S(2)}) async-start(bf16[16,2,2,64,128]{4,3,2,1,0:T(8,128)(2,1)} %shard_map.82.refs_9_), calls=%async_computation.2 | async-start | bytes 2097152 | tf_op jit(solution)/shard_map/all_to_all | solution.py:893
  84.0 7.1 %shard_map.84 = (bf16[2,2,128,128]{3,2,1,0:T(8,128)(2,1)}, f32[2,2,128,128]{3,2,1,0:T(8,128)}, f32[2,2,1024,128]{3,2,1,0:T(8,128)}) custom-call(bf16[272,256]{1,0:T(8,128)(2,1)} %get-tuple-element.47.refs_4_.refs_0_, bf16[272,256]{1,0:T(8,128)(2,1)} %copy-done.2, f32[8,256]{1,0:T(8,128)} %get-tuple-element.48.refs_5_.refs_1_.refs_2_, ...), custom_call_target="tpu_custom_call" | custom-call | flops 199999995904 | bytes 9592832 | tf_op jit(solution)/shard_map/pallas_call | solution.py:415
  91.2 1.5 %collective-permute-start.3 = (bf16[2,2,128,128]{3,2,1,0:T(8,128)(2,1)}, bf16[2,2,128,128]{3,2,1,0:T(8,128)(2,1)S(1)}, u32[]{:S(2)}, u32[]{:S(2)}) collective-permute-start(bf16[2,2,128,128]{3,2,1,0:T(8,128)(2,1)} %get-tuple-element.64), channel_id=1, source_target_pairs={{0,16},{16,0},{1,17},{17,1},{2,18},{18,2},{3,19},{19,3},{4,20},{20... | collective-permute-start | bytes 393224 | tf_op jit(solution)/shard_map/ppermute | solution.py:897
  92.7 7.7 %collective-permute-done.3.refs_0_ = bf16[2,2,128,128]{3,2,1,0:T(8,128)(2,1)S(1)} collective-permute-done((bf16[2,2,128,128]{3,2,1,0:T(8,128)(2,1)}, bf16[2,2,128,128]{3,2,1,0:T(8,128)(2,1)S(1)}, u32[]{:S(2)}, u32[]{:S(2)}) %collective-permute-start.3) | collective-permute-done | bytes 131104 | tf_op jit(solution)/shard_map/ppermute | solution.py:897
  101.0 2.9 %shard_map.85 = bf16[16,2,2,64,128]{4,3,2,1,0:T(8,128)(2,1)} custom-call(bf16[2,2,128,128]{3,2,1,0:T(8,128)(2,1)} %copy-done.3, f32[2,2,128,128]{3,2,1,0:T(8,128)} %get-tuple-element.65.refs_1_, f32[2,2,1024,128]{3,2,1,0:T(8,128)} %get-tuple-element.66.refs_2_), custom_call_target="tpu_custom_call" | custom-call | flops 100000000 | bytes 3538944 | tf_op jit(solution)/shard_map/pallas_call | solution.py:415
  103.9 5.5 %all-to-all-start.3 = ((bf16[16,2,2,64,128]{4,3,2,1,0:T(8,128)(2,1)}), bf16[16,2,2,64,128]{4,3,2,1,0:T(8,128)(2,1)S(1)}, u32[]{:S(2)}, u32[]{:S(2)}) async-start(bf16[16,2,2,64,128]{4,3,2,1,0:T(8,128)(2,1)} %shard_map.85), calls=%async_computation.3 | async-start | bytes 2097152 | tf_op jit(solution)/shard_map/all_to_all | solution.py:893
  109.4 2.3 %shard_map.83 = (bf16[64,4096]{1,0:T(8,128)(2,1)}, bf16[64,4096]{1,0:T(8,128)(2,1)}) custom-call(s32[1]{0:T(128)} %bitcast.half_ref, bf16[16,2,2,64,128]{4,3,2,1,0:T(8,128)(2,1)} %all-to-all-done.2.packed_ref), custom_call_target="tpu_custom_call" | custom-call | bytes 2097152 | tf_op jit(solution)/shard_map/pallas_call | solution.py:502
  111.7 12.5 %all-to-all-done.3.packed_ref = bf16[16,2,2,64,128]{4,3,2,1,0:T(8,128)(2,1)S(1)} async-done(((bf16[16,2,2,64,128]{4,3,2,1,0:T(8,128)(2,1)}), bf16[16,2,2,64,128]{4,3,2,1,0:T(8,128)(2,1)S(1)}, u32[]{:S(2)}, u32[]{:S(2)}) %all-to-all-start.3) | async-done | bytes 1048608 | tf_op jit(solution)/shard_map/all_to_all | solution.py:893
  124.2 1.0 shard_map.86
  (16 shorter events, 2.4 us)
Async XLA Ops:
  2.8 21.1 %all-to-all-start = ((bf16[16,2,2,64,128]{4,3,2,1,0:T(8,128)(2,1)}), bf16[16,2,2,64,128]{4,3,2,1,0:T(8,128)(2,1)S(1)}, u32[]{:S(2)}, u32[]{:S(2)}) async-start(bf16[16,2,2,64,128]{4,3,2,1,0:T(8,128)(2,1)} %shard_map.75), calls=%async_computation | async-start | bytes 2097152 | tf_op jit(solution)/shard_map/all_to_all | solution.py:893
  23.9 8.7 %copy-start = (bf16[16,2,2,64,128]{4,3,2,1,0:T(8,128)(2,1)}, bf16[16,2,2,64,128]{4,3,2,1,0:T(8,128)(2,1)S(1)}, u32[]{:S(2)}) copy-start(bf16[16,2,2,64,128]{4,3,2,1,0:T(8,128)(2,1)S(1)} %all-to-all-done.qk_ref.refs_0_) | copy-start | bytes 3145732
  24.2 8.4 %copy-start.1 = (bf16[2,2,128,128]{3,2,1,0:T(8,128)(2,1)}, bf16[2,2,128,128]{3,2,1,0:T(8,128)(2,1)S(1)}, u32[]{:S(2)}) copy-start(bf16[2,2,128,128]{3,2,1,0:T(8,128)(2,1)S(1)} %shard_map.77.refs_1_) | copy-start | bytes 393220
  24.2 8.4 %collective-permute-start = (bf16[2,2,128,128]{3,2,1,0:T(8,128)(2,1)S(1)}, bf16[2,2,128,128]{3,2,1,0:T(8,128)(2,1)S(1)}, u32[]{:S(2)}, u32[]{:S(2)}) collective-permute-start(bf16[2,2,128,128]{3,2,1,0:T(8,128)(2,1)S(1)} %shard_map.77.refs_1_), channel_id=1, source_target_pairs={{0,16},{16,0},{1,17},{17,1},{2,18},{18,2},{3,19},{19,3},{4,20},{20... | collective-permute-start | bytes 393224 | tf_op jit(solution)/shard_map/ppermute | solution.py:897
  26.9 19.6 %all-to-all-start.1 = ((bf16[16,2,2,64,128]{4,3,2,1,0:T(8,128)(2,1)}), bf16[16,2,2,64,128]{4,3,2,1,0:T(8,128)(2,1)}, u32[]{:S(2)}, u32[]{:S(2)}) async-start(bf16[16,2,2,64,128]{4,3,2,1,0:T(8,128)(2,1)} %shard_map.76), calls=%async_computation.1 | async-start | bytes 2097152 | tf_op jit(solution)/shard_map/all_to_all | solution.py:893
  32.6 0.7 copy-start.5
  49.5 8.5 %collective-permute-start.1 = (bf16[272,256]{1,0:T(8,128)(2,1)}, bf16[272,256]{1,0:T(8,128)(2,1)S(1)}, u32[]{:S(2)}, u32[]{:S(2)}) collective-permute-start(bf16[272,256]{1,0:T(8,128)(2,1)} %get-tuple-element.44), channel_id=1, source_target_pairs={{0,16},{16,0},{1,17},{17,1},{2,18},{18,2},{3,19},{19,3},{4,20},{20... | collective-permute-start | bytes 417800 | tf_op jit(solution)/shard_map/ppermute | solution.py:897
  58.1 0.7 copy-start.4
  61.0 13.2 %collective-permute-start.2 = (bf16[272,256]{1,0:T(8,128)(2,1)}, bf16[272,256]{1,0:T(8,128)(2,1)S(1)}, u32[]{:S(2)}, u32[]{:S(2)}) collective-permute-start(bf16[272,256]{1,0:T(8,128)(2,1)} %get-tuple-element.47.refs_4_.refs_0_), channel_id=1, source_target_pairs={{0,16},{16,0},{1,17},{17,1},{2,18},{18,2},{3,19},{19,3},{4,20},{20... | collective-permute-start | bytes 417800 | tf_op jit(solution)/shard_map/ppermute | solution.py:897
  74.3 0.7 copy-start.2
  77.9 26.0 %all-to-all-start.2 = ((bf16[16,2,2,64,128]{4,3,2,1,0:T(8,128)(2,1)}), bf16[16,2,2,64,128]{4,3,2,1,0:T(8,128)(2,1)}, u32[]{:S(2)}, u32[]{:S(2)}) async-start(bf16[16,2,2,64,128]{4,3,2,1,0:T(8,128)(2,1)} %shard_map.82.refs_9_), calls=%async_computation.2 | async-start | bytes 2097152 | tf_op jit(solution)/shard_map/all_to_all | solution.py:893
  91.2 9.1 %collective-permute-start.3 = (bf16[2,2,128,128]{3,2,1,0:T(8,128)(2,1)}, bf16[2,2,128,128]{3,2,1,0:T(8,128)(2,1)S(1)}, u32[]{:S(2)}, u32[]{:S(2)}) collective-permute-start(bf16[2,2,128,128]{3,2,1,0:T(8,128)(2,1)} %get-tuple-element.64), channel_id=1, source_target_pairs={{0,16},{16,0},{1,17},{17,1},{2,18},{18,2},{3,19},{19,3},{4,20},{20... | collective-permute-start | bytes 393224 | tf_op jit(solution)/shard_map/ppermute | solution.py:897
  100.3 0.7 copy-start.3
  103.9 20.3 %all-to-all-start.3 = ((bf16[16,2,2,64,128]{4,3,2,1,0:T(8,128)(2,1)}), bf16[16,2,2,64,128]{4,3,2,1,0:T(8,128)(2,1)S(1)}, u32[]{:S(2)}, u32[]{:S(2)}) async-start(bf16[16,2,2,64,128]{4,3,2,1,0:T(8,128)(2,1)} %shard_map.85), calls=%async_computation.3 | async-start | bytes 2097152 | tf_op jit(solution)/shard_map/all_to_all | solution.py:893

commit v11 on v10

--- a/solution.py
+++ b/solution.py
@@ -17,9 +17,10 @@
 SWAP = ((0, 1), (1, 0))
 VMEM_LIMIT = 60 * 2**20
 SMALL_LIMIT = 16 * 2**20
-WHOLE, LEAD, GROUPS = range(3)
+WHOLE, LEAD, GROUPS, BLOCKS = range(4)
 SLOTS = (10, 11)
 LONG = 200
+EARLY_SWEEPS = PINV_ITERS // 2
 
 
 precise_setting = lax.Precision.HIGHEST
@@ -323,6 +324,13 @@
 def pieces_of(kind, shape):
     if kind == LEAD:
         return [(index,) for index in range(shape[0])]
+    if kind == BLOCKS:
+        return [
+            (first, second, slice(place, place + 2 * CHUNK))
+            for place in range(0, shape[2], 2 * CHUNK)
+            for first in range(shape[0])
+            for second in range(shape[1])
+        ]
     if kind == GROUPS:
         per = CHUNK // shape[-2]
         return [(slice(place, place + per),) for place in range(0, shape[0], per)]
@@ -652,11 +660,17 @@
             for first in range(0, len(pairs), 2)
         ]
     )
-    saved = (outs.pair, outs.weight, outs.growth)
     for sweep in range(PINV_ITERS):
-        sweep_forward(power_s, iterate_s, saved, sweep, work)
+        first = sweep < EARLY_SWEEPS
+        place = sweep if first else sweep - EARLY_SWEEPS
+        saved = (
+            (outs.pair_a, outs.weight_a, outs.growth_a)
+            if first
+            else (outs.pair_b, outs.weight_b, outs.growth_b)
+        )
+        sweep_forward(power_s, iterate_s, saved, place, work)
         for ref in saved:
-            put(ref, sweep)
+            put(ref, place)
         if sweep == 3:
             for ref in (outs.token_low, outs.token_prob, outs.turned):
                 put(ref)
@@ -776,66 +790,54 @@
     return [swap_lanes(part) for part in parts] if swap else parts
 
 
+def gradient_sweep(state, saved, place, beside, last):
+    power, growth = state
+    pair_ref, weight_ref, growth_ref = saved
+    pair = (pair_ref[place, 0], pair_ref[place, 1])
+    first = split_dot(pair, halves(power))
+    beside()
+    square = first[:M] + first[:M].T
+    second = split_dot(tuple(x[:M] for x in pair) if last else pair, halves(square))
+    beside()
+    cube = first[M:].T + second[:M]
+    weight = halves(0.25 * (7.0 * square - 15.0 * power - cube))
+    if not last:
+        fourth = second[M:] + second[M:].T
+        power = 0.25 * (13.0 * power - 15.0 * square + 7.0 * cube - fourth)
+    left = [growth_ref[place, 0], growth_ref[place, 0], growth_ref[place, 1]]
+    right = [weight[0], weight[1], weight[0]]
+    if growth is not None:
+        grown = halves(growth)
+        left += [grown[0], grown[0], grown[1]]
+        right += [weight_ref[place, 0], weight_ref[place, 1], weight_ref[place, 0]]
+    growth = wide_dot(jnp.concatenate(left, axis=1), jnp.concatenate(right, axis=0))
+    return power, growth
+
+
 def own_gradient_compute(ins, outs, need, put):
     for ref in (ins.mark_prob, ins.factor, ins.mixing_grad, ins.mark_values, ins.share, ins.scales):
         need(ref)
-    mark_prob = ins.mark_prob[...]
-    mark_halves = halves(mark_prob)
-    factor = ins.factor[0:1, 0:1]
     inverse_grad = split_dot(halves(ins.mixing_grad[...].T), halves(ins.mark_values[...]))
     inverse_grad_halves = halves(inverse_grad)
-    toward = split_dot(mark_halves, inverse_grad_halves) * factor
-    power = 0.5 * (toward + toward.T)
-    growth = None
-    work = iter(out_units(ins, 0, outs.out, (), share_parts(ins.share, False)))
+    outs.inverse_grad[0], outs.inverse_grad[1] = inverse_grad_halves
+    toward = split_dot(halves(ins.mark_prob[...]), inverse_grad_halves) * ins.factor[0:1, 0:1]
+    state = (0.5 * (toward + toward.T), None)
+    units = out_units(ins, 0, outs.out, (), share_parts(ins.share, False))
+    work = iter([units[index : index + 2] for index in range(0, len(units), 2)])
+    saved = (ins.pair, ins.weight, ins.growth)
 
     def beside():
-        next(work, lambda: None)()
-
-    for sweep in range(PINV_ITERS):
+        several(*next(work, ()))
+
+    for sweep in range(EARLY_SWEEPS):
         if sweep == 0:
             need(ins.token_low)
-        if sweep == 2:
+        if sweep == 1:
             need(ins.key_exp)
-        for ref in (ins.pair, ins.weight, ins.growth):
+        for ref in saved:
             need(ref, sweep)
-        pair = (ins.pair[sweep, 0], ins.pair[sweep, 1])
-        first = split_dot(pair, halves(power))
-        beside()
-        square = first[:M] + first[:M].T
-        last = sweep == PINV_ITERS - 1
-        second = split_dot(tuple(x[:M] for x in pair) if last else pair, halves(square))
-        beside()
-        cube = first[M:].T + second[:M]
-        weight = halves(0.25 * (7.0 * square - 15.0 * power - cube))
-        if not last:
-            fourth = second[M:] + second[M:].T
-            power = 0.25 * (13.0 * power - 15.0 * square + 7.0 * cube - fourth)
-        left = [ins.growth[sweep, 0], ins.growth[sweep, 0], ins.growth[sweep, 1]]
-        right = [weight[0], weight[1], weight[0]]
-        if growth is not None:
-            grown = halves(growth)
-            left += [grown[0], grown[0], grown[1]]
-            right += [ins.weight[sweep, 0], ins.weight[sweep, 1], ins.weight[sweep, 0]]
-        growth = wide_dot(jnp.concatenate(left, axis=1), jnp.concatenate(right, axis=0))
-    for unit in work:
-        unit()
-    put(outs.out)
-    need()
-    mark_grad = factor * (
-        split_dot_nt((ins.last_growth[0], ins.last_growth[1]), inverse_grad_halves)
-        + split_dot(halves(growth + growth.T), mark_halves)
-    )
-    mark_sgrad = mark_prob * (mark_grad - jnp.sum(mark_grad * mark_prob, axis=1, keepdims=True))
-
-    def marks_dot(left, right):
-        left_high, left_low = halves(left)
-        return wide_dot(
-            jnp.concatenate([left_high, left_low], axis=1), jnp.concatenate([right, right], axis=0)
-        )
-
-    outs.mark_grads[0] = marks_dot(mark_sgrad, ins.marks[0, 1])
-    outs.mark_grads[1] = marks_dot(mark_sgrad.T, ins.marks[0, 0])
+        state = gradient_sweep(state, saved, sweep, beside, False)
+    outs.state[0], outs.state[1] = state
 
 
 def other_out_compute(ins, outs, need, put):
@@ -851,27 +853,66 @@
 
 
 def gradient_compute(ins, outs, need, put):
-    for ref in (ins.share, ins.got_share, ins.scales, ins.marks, ins.vg, ins.mark_grads):
+    for ref in (ins.state, ins.share, ins.got_share, ins.scales, ins.marks, ins.vg):
         need(ref)
+    sides = []
+    for slot in range(2):
+        share = share_parts(ins.got_share if slot else ins.share, bool(slot))
+        sides.append(gradient_units(ins, slot, outs.direct, share))
+    units = sides[0][0] + sides[1][0]
+    sweeps = PINV_ITERS - EARLY_SWEEPS
+    span = -(-len(units) // (2 * sweeps))
+    work = iter([units[index : index + span] for index in range(0, len(units), span)])
+    saved = (ins.pair, ins.weight, ins.growth)
+    state = (ins.state[0], ins.state[1])
+
+    def beside():
+        several(*next(work, ()))
+
+    for sweep in range(sweeps):
+        if sweep < 2:
+            for ref in (ins.key_exp, ins.token_prob, ins.turned):
+                need(ref, sweep)
+        for ref in saved:
+            need(ref, sweep)
+        state = gradient_sweep(state, saved, sweep, beside, sweep == sweeps - 1)
+    put(outs.direct)
+    need()
+    growth = state[1]
+    mark_prob = ins.mark_prob[...]
+    mark_grad = ins.factor[0:1, 0:1] * (
+        split_dot_nt(
+            (ins.last_growth[0], ins.last_growth[1]), (ins.inverse_grad[0], ins.inverse_grad[1])
+        )
+        + split_dot(halves(growth + growth.T), halves(mark_prob))
+    )
+    mark_sgrad = mark_prob * (mark_grad - jnp.sum(mark_grad * mark_prob, axis=1, keepdims=True))
+
+    def marks_dot(left, right):
+        left_high, left_low = halves(left)
+        return wide_dot(
+            jnp.concatenate([left_high, left_low], axis=1), jnp.concatenate([right, right], axis=0)
+        )
+
+    own_marks = (
+        marks_dot(mark_sgrad, ins.marks[0, 1]),
+        marks_dot(mark_sgrad.T, ins.marks[0, 0]),
+    )
     marks_scale = HD ** (-0.5) / (tokens_of(ins.vg) // HALF)
-    for slot in range(2):
-        for ref in (ins.key_exp, ins.token_prob, ins.turned):
-            need(ref, slot)
-        share = share_parts(ins.got_share if slot else ins.share, bool(slot))
-        units, query_sums, key_sums = gradient_units(ins, slot, outs.direct, share)
-        several(*units)
-        put(outs.direct, slot)
+    for slot, (_, query_sums, key_sums) in enumerate(sides):
         for kind, sums in enumerate((query_sums, key_sums)):
             total = sum(sums[1:], sums[0]).T
             if slot == 0:
-                total = total + ins.mark_grads[kind]
+                total = total + own_marks[kind]
             total = total * marks_scale
+            outs.far[kind, slot] = total[HALF:].astype(jnp.bfloat16)
             outs.near[kind, slot] = total[:HALF]
-            outs.far[kind, slot] = total[HALF:].astype(jnp.bfloat16)
+    put(outs.far)
 
 
 def finish_compute(ins, outs, need, put):
-    need()
+    need(ins.near)
+    need(ins.got_far)
     out_ref = outs.out
     group = CHUNK // out_ref.shape[3]
     segment_len = tokens_of(out_ref) // HALF
@@ -880,6 +921,8 @@
         place, start = slice(index * per, (index + 1) * per), index * CHUNK
         for slot in range(2):
             for kind in range(2):
+                if index % 2 == 0:
+                    need(ins.direct, slot, kind, start)
                 marks = ins.near[kind, slot, place] + ins.got_far[
                     kind, 1 - slot, place
                 ].astype(jnp.float32)
@@ -920,9 +963,12 @@
             stats=wide(8, M),
             mark_prob=wide(M, M),
             factor=wide(8, HD),
-            pair=(low(PINV_ITERS, 2, 2 * M, M), LEAD),
-            weight=(low(PINV_ITERS, 2, M, M), LEAD),
-            growth=(low(PINV_ITERS, 2, M, M), LEAD),
+            pair_a=(low(EARLY_SWEEPS, 2, 2 * M, M), LEAD),
+            weight_a=(low(EARLY_SWEEPS, 2, M, M), LEAD),
+            growth_a=(low(EARLY_SWEEPS, 2, M, M), LEAD),
+            pair_b=(low(PINV_ITERS - EARLY_SWEEPS, 2, 2 * M, M), LEAD),
+            weight_b=(low(PINV_ITERS - EARLY_SWEEPS, 2, M, M), LEAD),
+            growth_b=(low(PINV_ITERS - EARLY_SWEEPS, 2, M, M), LEAD),
             inverse=low(2, M, M),
             last_growth=low(2, M, M),
         ),
@@ -957,15 +1003,17 @@
             share=mixed.share,
             scales=mixed.scales,
             token_low=(kept.token_low, SLOTS[0]),
-            pair=(kept.pair, LEAD),
-            weight=(kept.weight, LEAD),
-            growth=(kept.growth, LEAD),
+            pair=(kept.pair_a, LEAD),
+            weight=(kept.weight_a, LEAD),
+            growth=(kept.growth_a, LEAD),
             key_exp=(kept.key_exp, SLOTS[0]),
-            last_growth=kept.last_growth,
-            marks=kept.marks,
         ),
-        dict(out=low(qk.shape[0], 2, *qk.shape[3:]), mark_grads=wide(2, M, HD)),
-        14,
+        dict(
+            out=low(qk.shape[0], 2, *qk.shape[3:]),
+            state=wide(2, M, M),
+            inverse_grad=low(2, M, M),
+        ),
+        8,
     )
     first_results = staged_call(
         other_out_compute,
@@ -983,15 +1031,22 @@
     grads = staged_call(
         gradient_compute,
         dict(
+            state=own.state,
             share=mixed.share,
             got_share=got_share,
             scales=mixed.scales,
             marks=kept.marks,
             vg=vg,
+            pair=(kept.pair_b, LEAD),
+            weight=(kept.weight_b, LEAD),
+            growth=(kept.growth_b, LEAD),
             key_exp=(kept.key_exp, LEAD),
             token_prob=(kept.token_prob, LEAD),
             turned=(kept.turned, LEAD),
-            mark_grads=own.mark_grads,
+            inverse_grad=own.inverse_grad,
+            last_growth=kept.last_growth,
+            mark_prob=kept.mark_prob,
+            factor=kept.factor,
         ),
         dict(
             far=low(2, 2, HALF, HD),
@@ -1003,7 +1058,7 @@
     )
     results = staged_call(
         finish_compute,
-        dict(got_far=partner(grads.far), near=grads.near, direct=grads.direct),
+        dict(got_far=partner(grads.far), near=grads.near, direct=(grads.direct, BLOCKS)),
         dict(out=(low(*qk.shape), GROUPS)),
         0.1,
     ).out

time: 126 us -> 124 us (0.984)
  Pallas kernels: 49.7 us -> 48 us
  starting transfers between devices: 26.5 us -> 25 us
    all_to_all x4, starting transfers between devices: 22.3 us -> 20.2 us  [exchange(): lax.all_to_all(packed, 'cube', split_axis=0, concat_axis=0, tiled=True)]
    pallas_call x7, Pallas kernels: 41.8 us -> 40.1 us  [staged_call(): pl.pallas_call(kernel, out_shape=shapes, in_specs=[anywhere] * (n_in + n_...]
  transfers between devices with their start and end apart: 8 -> 8, of which waited for: 6 -> 7; matrix products, arithmetic and copies ran while one was open for 0% -> 0% of each run, Pallas kernels for 30% -> 29%
where the time goes in v11:
time: 124 us; the launch traced here: 123 us
  Pallas kernels  48 us (39%)
  waiting for transfers between devices  46.2 us (37%)
  starting transfers between devices  25 us (20%)
  local copies, waits for them, and re-layouts  2.63 us (2%)
    pallas_call x7, Pallas kernels, staged_call(): pl.pallas_call(kernel, out_shape=shapes, in_specs=[anywhere] * (n_in + n_...  40.1 us
    all_to_all x4, waiting for transfers between devices, exchange(): lax.all_to_all(packed, 'cube', split_axis=0, concat_axis=0, tiled=True)  28.1 us
    all_to_all x4, starting transfers between devices, exchange(): lax.all_to_all(packed, 'cube', split_axis=0, concat_axis=0, tiled=True)  20.2 us
    ppermute x4, waiting for transfers between devices, partner(): return lax.ppermute(array, 'half', SWAP)  18 us
    pallas_call x4, Pallas kernels, layout_call(): pl.pallas_call(kernel, out_shape=out_shape, in_specs=[pl.BlockSpec(memory...  7.59 us
    ppermute x4, starting transfers between devices, partner(): return lax.ppermute(array, 'half', SWAP)  4.84 us
    unnamed x12, local copies, waits for them, and re-layouts  2.63 us
  transfers between devices with their start and end apart: 8, of which 7 were waited for; matrix products, arithmetic and copies ran while one was open for 0% of the time, Pallas kernels for 29%

profile of v11, /device:TPU:0, one launch (start us, length us, event | category | flops | bytes accessed | tf_op | source)
XLA Modules:
  0.0 122.7 jit_solution(15204992563730902239)
XLA Ops:
  0.6 2.1 %shard_map.75 = bf16[16,2,2,64,128]{4,3,2,1,0:T(8,128)(2,1)} custom-call(s32[1]{0:T(128)} %bitcast.half_ref, bf16[64,4096]{1,0:T(8,128)(2,1)} %first_ref.2, bf16[64,4096]{1,0:T(8,128)(2,1)} %second_ref.2), custom_call_target="tpu_custom_call" | custom-call | bytes 2097152 | tf_op jit(solution)/shard_map/pallas_call | solution.py:510
  2.8 6.3 %all-to-all-start = ((bf16[16,2,2,64,128]{4,3,2,1,0:T(8,128)(2,1)}), bf16[16,2,2,64,128]{4,3,2,1,0:T(8,128)(2,1)S(1)}, u32[]{:S(2)}, u32[]{:S(2)}) async-start(bf16[16,2,2,64,128]{4,3,2,1,0:T(8,128)(2,1)} %shard_map.75), calls=%async_computation | async-start | bytes 2097152 | tf_op jit(solution)/shard_map/all_to_all | solution.py:936
  9.1 2.1 %shard_map.76 = bf16[16,2,2,64,128]{4,3,2,1,0:T(8,128)(2,1)} custom-call(s32[1]{0:T(128)} %bitcast.half_ref, bf16[64,4096]{1,0:T(8,128)(2,1)} %first_ref.3, bf16[64,4096]{1,0:T(8,128)(2,1)} %second_ref.3), custom_call_target="tpu_custom_call" | custom-call | bytes 2097152 | tf_op jit(solution)/shard_map/pallas_call | solution.py:510
  11.2 12.7 %all-to-all-done.qk_ref.refs_0_ = bf16[16,2,2,64,128]{4,3,2,1,0:T(8,128)(2,1)S(1)} async-done(((bf16[16,2,2,64,128]{4,3,2,1,0:T(8,128)(2,1)}), bf16[16,2,2,64,128]{4,3,2,1,0:T(8,128)(2,1)S(1)}, u32[]{:S(2)}, u32[]{:S(2)}) %all-to-all-start) | async-done | bytes 1048608 | tf_op jit(solution)/shard_map/all_to_all | solution.py:936
  24.2 2.7 %collective-permute-start = (bf16[2,2,128,128]{3,2,1,0:T(8,128)(2,1)S(1)}, bf16[2,2,128,128]{3,2,1,0:T(8,128)(2,1)S(1)}, u32[]{:S(2)}, u32[]{:S(2)}) collective-permute-start(bf16[2,2,128,128]{3,2,1,0:T(8,128)(2,1)S(1)} %shard_map.77.refs_1_), channel_id=1, source_target_pairs={{0,16},{16,0},{1,17},{17,1},{2,18},{18,2},{3,19},{19,3},{4,20},{20... | collective-permute-start | bytes 393224 | tf_op jit(solution)/shard_map/ppermute | solution.py:940
  26.8 4.3 %all-to-all-start.1 = ((bf16[16,2,2,64,128]{4,3,2,1,0:T(8,128)(2,1)}), bf16[16,2,2,64,128]{4,3,2,1,0:T(8,128)(2,1)}, u32[]{:S(2)}, u32[]{:S(2)}) async-start(bf16[16,2,2,64,128]{4,3,2,1,0:T(8,128)(2,1)} %shard_map.76), calls=%async_computation.1 | async-start | bytes 2097152 | tf_op jit(solution)/shard_map/all_to_all | solution.py:936
  31.2 1.4 %collective-permute-done.refs_2_ = bf16[2,2,128,128]{3,2,1,0:T(8,128)(2,1)S(1)} collective-permute-done((bf16[2,2,128,128]{3,2,1,0:T(8,128)(2,1)S(1)}, bf16[2,2,128,128]{3,2,1,0:T(8,128)(2,1)S(1)}, u32[]{:S(2)}, u32[]{:S(2)}) %collective-permute-start) | collective-permute-done | bytes 131104 | tf_op jit(solution)/shard_map/ppermute | solution.py:940
  32.6 0.7 copy-done.5
  33.3 10.3 %shard_map.78 = (bf16[2,2,256,128]{3,2,1,0:T(8,128)(2,1)}, f32[2,1024,256]{2,1,0:T(8,128)}, bf16[2,1024,256]{2,1,0:T(8,128)(2,1)}, f32[2,1024,256]{2,1,0:T(8,128...) custom-call(bf16[16,2,2,64,128]{4,3,2,1,0:T(8,128)(2,1)} %copy-done,, ...), custom_call_target="tpu_custom_call" | custom-call | flops 199999995904 | bytes 16003072 | tf_op jit(solution)/shard_map/pallas_call | solution.py:423
  43.5 2.9 %all-to-all-done.1.refs_0_.refs_5_ = bf16[16,2,2,64,128]{4,3,2,1,0:T(8,128)(2,1)} async-done(((bf16[16,2,2,64,128]{4,3,2,1,0:T(8,128)(2,1)}), bf16[16,2,2,64,128]{4,3,2,1,0:T(8,128)(2,1)}, u32[]{:S(2)}, u32[]{:S(2)}) %all-to-all-start.1) | async-done | bytes 1048608 | tf_op jit(solution)/shard_map/all_to_all | solution.py:936
  46.5 3.1 %shard_map.79 = (bf16[272,256]{1,0:T(8,128)(2,1)}, f32[256,256]{1,0:T(8,128)}) custom-call(bf16[16,2,2,64,128]{4,3,2,1,0:T(8,128)(2,1)} %all-to-all-done.1.refs_0_.refs_5_, f32[8,256]{1,0:T(8,128)} %get-tuple-element.45.refs_1_.refs_2_, bf16[2,1024,256]{2,1,0:T(8,128)(2,1)} %get-tuple-element.46.refs_2_, ...), custom_call_target="tpu_custom_call" | custom-call | flops 2000000000 | bytes 3555328 | tf_op jit(solution)/shard_map/pallas_call | solution.py:423
  49.6 8.4 %collective-permute-done.1.refs_0_ = bf16[272,256]{1,0:T(8,128)(2,1)S(1)} collective-permute-done((bf16[272,256]{1,0:T(8,128)(2,1)}, bf16[272,256]{1,0:T(8,128)(2,1)S(1)}, u32[]{:S(2)}, u32[]{:S(2)}) %collective-permute-start.1) | collective-permute-done | bytes 139296 | tf_op jit(solution)/shard_map/ppermute | solution.py:940
  58.7 2.4 %shard_map.80 = (bf16[272,256]{1,0:T(8,128)(2,1)}, f32[8,256]{1,0:T(8,128)}, f32[128,256]{1,0:T(8,128)}, f32[128,256]{1,0:T(8,128)}) custom-call(bf16[272,256]{1,0:T(8,128)(2,1)} %copy-done.4, f32[256,256]{1,0:T(8,128)} %get-tuple-element.49.refs_1_, f32[8,256]{1,0:T(8,128)} %get-tuple-element.45.refs_1_.refs_2_, bf16[2,256,256]{2,1,0:T(8,128)(2,1)} %get-tuple-element.50.refs_3_), custom_call_target="tpu_custom_call" | custom-call | flops 1000000000 | bytes 1081344 | tf_op jit(solution)/shard_map/pallas_call | solution.py:423
  61.1 7.4 %shard_map.81 = (bf16[16,2,64,128]{3,2,1,0:T(8,128)(2,1)}, f32[2,256,256]{2,1,0:T(8,128)}, bf16[2,256,256]{2,1,0:T(8,128)(2,1)}) custom-call(f32[256,256]{1,0:T(8,128)} %get-tuple-element.54.refs_0_.refs_14_, f32[8,128]{1,0:T(8,128)} %get-tuple-element.55.refs_1_.refs_15_, f32[128,256]{1,0:T(8,128)} %get-tuple-element.56.refs_2_, ...), custom_call_target="tpu_custom_call" | custom-call | flops 8000000000 | bytes 8278016 | tf_op jit(solution)/shard_map/pallas_call | solution.py:423
  69.8 3.0 %shard_map.82.refs_16_ = bf16[16,2,2,64,128]{4,3,2,1,0:T(8,128)(2,1)} custom-call(bf16[272,256]{1,0:T(8,128)(2,1)} %copy-done.2, f32[8,256]{1,0:T(8,128)} %get-tuple-element.52.refs_5_.refs_1_.refs_3_, bf16[2,1024,256]{2,1,0:T(8,128)(2,1)} %get-tuple-element.47.refs_3_.refs_6_.refs_2_, f32[2,1024,256]{2,1,0:T(8,128)} %get-tuple-element.53.refs_10_.refs_3_.refs_9_, ...), custom_call_target="tpu_custom_call" | custom-call | flops 1000000000 | bytes 4866048 | tf_op jit(solution)/shard_map/pallas_call | solution.py:423
  72.7 5.6 %all-to-all-start.2 = ((bf16[16,2,2,64,128]{4,3,2,1,0:T(8,128)(2,1)}), bf16[16,2,2,64,128]{4,3,2,1,0:T(8,128)(2,1)}, u32[]{:S(2)}, u32[]{:S(2)}) async-start(bf16[16,2,2,64,128]{4,3,2,1,0:T(8,128)(2,1)} %shard_map.82.refs_16_), calls=%async_computation.2 | async-start | bytes 2097152 | tf_op jit(solution)/shard_map/all_to_all | solution.py:936
  78.3 11.4 %shard_map.84 = (bf16[2,2,128,128]{3,2,1,0:T(8,128)(2,1)}, f32[2,2,128,128]{3,2,1,0:T(8,128)}, f32[2,2,1024,128]{3,2,1,0:T(8,128)}) custom-call(f32[2,256,256]{2,1,0:T(8,128)} %get-tuple-element.63.refs_0_, bf16[272,256]{1,0:T(8,128)(2,1)} %get-tuple-element.51.refs_4_.refs_1_, bf16[272,256]{1,0:T(8,128)(2,1)} %copy-done.2, ...), custom_call_target="tpu_custom_call" | custom-call | flops 199999995904 | bytes 13791232 | tf_op jit(solution)/shard_map/pallas_call | solution.py:423
  89.7 2.0 %collective-permute-start.3 = (bf16[2,2,128,128]{3,2,1,0:T(8,128)(2,1)}, bf16[2,2,128,128]{3,2,1,0:T(8,128)(2,1)S(1)}, u32[]{:S(2)}, u32[]{:S(2)}) collective-permute-start(bf16[2,2,128,128]{3,2,1,0:T(8,128)(2,1)} %get-tuple-element.72), channel_id=1, source_target_pairs={{0,16},{16,0},{1,17},{17,1},{2,18},{18,2},{3,19},{19,3},{4,20},{20... | collective-permute-start | bytes 393224 | tf_op jit(solution)/shard_map/ppermute | solution.py:940
  91.8 7.7 %collective-permute-done.3.refs_0_ = bf16[2,2,128,128]{3,2,1,0:T(8,128)(2,1)S(1)} collective-permute-done((bf16[2,2,128,128]{3,2,1,0:T(8,128)(2,1)}, bf16[2,2,128,128]{3,2,1,0:T(8,128)(2,1)S(1)}, u32[]{:S(2)}, u32[]{:S(2)}) %collective-permute-start.3) | collective-permute-done | bytes 131104 | tf_op jit(solution)/shard_map/ppermute | solution.py:940
  100.1 2.6 %shard_map.85 = bf16[16,2,2,64,128]{4,3,2,1,0:T(8,128)(2,1)} custom-call(bf16[2,2,128,128]{3,2,1,0:T(8,128)(2,1)} %copy-done.3, f32[2,2,128,128]{3,2,1,0:T(8,128)} %get-tuple-element.73.refs_1_, f32[2,2,1024,128]{3,2,1,0:T(8,128)} %get-tuple-element.74.refs_2_), custom_call_target="tpu_custom_call" | custom-call | flops 100000000 | bytes 3538944 | tf_op jit(solution)/shard_map/pallas_call | solution.py:423
  102.7 4.0 %all-to-all-start.3 = ((bf16[16,2,2,64,128]{4,3,2,1,0:T(8,128)(2,1)}), bf16[16,2,2,64,128]{4,3,2,1,0:T(8,128)(2,1)S(1)}, u32[]{:S(2)}, u32[]{:S(2)}) async-start(bf16[16,2,2,64,128]{4,3,2,1,0:T(8,128)(2,1)} %shard_map.85), calls=%async_computation.3 | async-start | bytes 2097152 | tf_op jit(solution)/shard_map/all_to_all | solution.py:936
  106.7 2.3 %shard_map.83 = (bf16[64,4096]{1,0:T(8,128)(2,1)}, bf16[64,4096]{1,0:T(8,128)(2,1)}) custom-call(s32[1]{0:T(128)} %bitcast.half_ref, bf16[16,2,2,64,128]{4,3,2,1,0:T(8,128)(2,1)} %all-to-all-done.2.packed_ref), custom_call_target="tpu_custom_call" | custom-call | bytes 2097152 | tf_op jit(solution)/shard_map/pallas_call | solution.py:510
  109.0 12.5 %all-to-all-done.3.packed_ref = bf16[16,2,2,64,128]{4,3,2,1,0:T(8,128)(2,1)S(1)} async-done(((bf16[16,2,2,64,128]{4,3,2,1,0:T(8,128)(2,1)}), bf16[16,2,2,64,128]{4,3,2,1,0:T(8,128)(2,1)S(1)}, u32[]{:S(2)}, u32[]{:S(2)}) %all-to-all-start.3) | async-done | bytes 1048608 | tf_op jit(solution)/shard_map/all_to_all | solution.py:936
  121.5 1.0 shard_map.86
  (16 shorter events, 3.0 us)
Async XLA Ops:
  2.8 21.1 %all-to-all-start = ((bf16[16,2,2,64,128]{4,3,2,1,0:T(8,128)(2,1)}), bf16[16,2,2,64,128]{4,3,2,1,0:T(8,128)(2,1)S(1)}, u32[]{:S(2)}, u32[]{:S(2)}) async-start(bf16[16,2,2,64,128]{4,3,2,1,0:T(8,128)(2,1)} %shard_map.75), calls=%async_computation | async-start | bytes 2097152 | tf_op jit(solution)/shard_map/all_to_all | solution.py:936
  23.9 8.7 %copy-start = (bf16[16,2,2,64,128]{4,3,2,1,0:T(8,128)(2,1)}, bf16[16,2,2,64,128]{4,3,2,1,0:T(8,128)(2,1)S(1)}, u32[]{:S(2)}) copy-start(bf16[16,2,2,64,128]{4,3,2,1,0:T(8,128)(2,1)S(1)} %all-to-all-done.qk_ref.refs_0_) | copy-start | bytes 3145732
  24.2 8.4 %copy-start.1 = (bf16[2,2,128,128]{3,2,1,0:T(8,128)(2,1)}, bf16[2,2,128,128]{3,2,1,0:T(8,128)(2,1)S(1)}, u32[]{:S(2)}) copy-start(bf16[2,2,128,128]{3,2,1,0:T(8,128)(2,1)S(1)} %shard_map.77.refs_1_) | copy-start | bytes 393220
  24.2 8.4 %collective-permute-start = (bf16[2,2,128,128]{3,2,1,0:T(8,128)(2,1)S(1)}, bf16[2,2,128,128]{3,2,1,0:T(8,128)(2,1)S(1)}, u32[]{:S(2)}, u32[]{:S(2)}) collective-permute-start(bf16[2,2,128,128]{3,2,1,0:T(8,128)(2,1)S(1)} %shard_map.77.refs_1_), channel_id=1, source_target_pairs={{0,16},{16,0},{1,17},{17,1},{2,18},{18,2},{3,19},{19,3},{4,20},{20... | collective-permute-start | bytes 393224 | tf_op jit(solution)/shard_map/ppermute | solution.py:940
  26.8 19.6 %all-to-all-start.1 = ((bf16[16,2,2,64,128]{4,3,2,1,0:T(8,128)(2,1)}), bf16[16,2,2,64,128]{4,3,2,1,0:T(8,128)(2,1)}, u32[]{:S(2)}, u32[]{:S(2)}) async-start(bf16[16,2,2,64,128]{4,3,2,1,0:T(8,128)(2,1)} %shard_map.76), calls=%async_computation.1 | async-start | bytes 2097152 | tf_op jit(solution)/shard_map/all_to_all | solution.py:936
  32.6 0.7 copy-start.5
  49.5 8.5 %collective-permute-start.1 = (bf16[272,256]{1,0:T(8,128)(2,1)}, bf16[272,256]{1,0:T(8,128)(2,1)S(1)}, u32[]{:S(2)}, u32[]{:S(2)}) collective-permute-start(bf16[272,256]{1,0:T(8,128)(2,1)} %get-tuple-element.48), channel_id=1, source_target_pairs={{0,16},{16,0},{1,17},{17,1},{2,18},{18,2},{3,19},{19,3},{4,20},{20... | collective-permute-start | bytes 417800 | tf_op jit(solution)/shard_map/ppermute | solution.py:940
  58.0 0.7 copy-start.4
  61.1 8.1 %collective-permute-start.2 = (bf16[272,256]{1,0:T(8,128)(2,1)}, bf16[272,256]{1,0:T(8,128)(2,1)S(1)}, u32[]{:S(2)}, u32[]{:S(2)}) collective-permute-start(bf16[272,256]{1,0:T(8,128)(2,1)} %get-tuple-element.51.refs_4_.refs_1_), channel_id=1, source_target_pairs={{0,16},{16,0},{1,17},{17,1},{2,18},{18,2},{3,19},{19,3},{4,20},{20... | collective-permute-start | bytes 417800 | tf_op jit(solution)/shard_map/ppermute | solution.py:940
  69.1 0.7 copy-start.2
  72.7 30.0 %all-to-all-start.2 = ((bf16[16,2,2,64,128]{4,3,2,1,0:T(8,128)(2,1)}), bf16[16,2,2,64,128]{4,3,2,1,0:T(8,128)(2,1)}, u32[]{:S(2)}, u32[]{:S(2)}) async-start(bf16[16,2,2,64,128]{4,3,2,1,0:T(8,128)(2,1)} %shard_map.82.refs_16_), calls=%async_computation.2 | async-start | bytes 2097152 | tf_op jit(solution)/shard_map/all_to_all | solution.py:936
  89.7 9.7 %collective-permute-start.3 = (bf16[2,2,128,128]{3,2,1,0:T(8,128)(2,1)}, bf16[2,2,128,128]{3,2,1,0:T(8,128)(2,1)S(1)}, u32[]{:S(2)}, u32[]{:S(2)}) collective-permute-start(bf16[2,2,128,128]{3,2,1,0:T(8,128)(2,1)} %get-tuple-element.72), channel_id=1, source_target_pairs={{0,16},{16,0},{1,17},{17,1},{2,18},{18,2},{3,19},{19,3},{4,20},{20... | collective-permute-start | bytes 393224 | tf_op jit(solution)/shard_map/ppermute | solution.py:940
  99.5 0.7 copy-start.3
  102.7 18.8 %all-to-all-start.3 = ((bf16[16,2,2,64,128]{4,3,2,1,0:T(8,128)(2,1)}), bf16[16,2,2,64,128]{4,3,2,1,0:T(8,128)(2,1)S(1)}, u32[]{:S(2)}, u32[]{:S(2)}) async-start(bf16[16,2,2,64,128]{4,3,2,1,0:T(8,128)(2,1)} %shard_map.85), calls=%async_computation.3 | async-start | bytes 2097152 | tf_op jit(solution)/shard_map/all_to_all | solution.py:936

commit v12 on v11

--- a/solution.py
+++ b/solution.py
@@ -17,7 +17,7 @@
 SWAP = ((0, 1), (1, 0))
 VMEM_LIMIT = 60 * 2**20
 SMALL_LIMIT = 16 * 2**20
-WHOLE, LEAD, GROUPS, BLOCKS = range(4)
+WHOLE, LEAD, GROUPS, BLOCKS, LATE, LAST = range(6)
 SLOTS = (10, 11)
 LONG = 200
 EARLY_SWEEPS = PINV_ITERS // 2
@@ -361,7 +361,7 @@
                     part.start if isinstance(part, slice) else part for part in piece
                 )
                 copies[key] = pltpu.make_async_copy(source, target, done.at[count])
-                steps.append((step if kind != WHOLE else -1, place, key))
+                steps.append(({WHOLE: -1, LAST: 9}.get(kind, step), place, key))
                 count += 1
             self.copies.append(copies)
         self.inner = inner
@@ -686,13 +686,15 @@
 def partial_compute(ins, outs, need, put):
     need(ins.vg)
     turned = [[all_tokens(ins.vg, array, slot).T for array in range(2)] for slot in range(2)]
-    need()
+    need(ins.stats)
     rows = thirds(ins.stats[0:4])
     outs.send[2 * HD :] = jnp.concatenate([rows, jnp.zeros((4, M), jnp.float32)], axis=0).astype(
         jnp.bfloat16
     )
-    for slot, home in ((1, outs.send), (0, outs.keep)):
+    for slot, home in enumerate((outs.keep, outs.send)):
+        need(ins.key_low, slot)
         home[0:HD] = wide_dot(turned[slot][0], ins.key_low[slot]).astype(home.dtype)
+        need(ins.token_low, slot)
         home[HD : 2 * HD] = wide_dot(turned[slot][1], ins.token_low[slot]).astype(home.dtype)
         put(home)
 
@@ -780,7 +782,7 @@
 
     chunks = tokens_of(ins.vg) // CHUNK
     units = [
-        functools.partial(unit, index) for index in range(chunks) for unit in (key_side, token_side)
+        [functools.partial(unit, index) for index in range(chunks)] for unit in (key_side, token_side)
     ]
     return units, query_sums, key_sums
 
@@ -841,25 +843,33 @@
 
 
 def other_out_compute(ins, outs, need, put):
-    need(ins.got_share)
-    need(ins.scales)
-    need(ins.token_low)
+    for ref in (ins.got_share, ins.scales, ins.token_low):
+        need(ref)
     units = out_units(ins, 1, outs.out, (1,), share_parts(ins.got_share, True))
     chunks = len(units) // 2
     several(*units[:chunks])
     need()
-    several(*units[chunks:])
-    outs.out[:, :, 0] = ins.own_out[...]
+    group = CHUNK // outs.out.shape[3]
+    for index, unit in enumerate(units[chunks:]):
+        unit()
+        place = slice(index * group, (index + 1) * group)
+        outs.out[place, :, 0] = ins.own_out[place]
+        put(outs.out, index * group)
 
 
 def gradient_compute(ins, outs, need, put):
-    for ref in (ins.state, ins.share, ins.got_share, ins.scales, ins.marks, ins.vg):
+    for ref in (ins.state, ins.share, ins.got_share, ins.scales, ins.marks):
         need(ref)
     sides = []
     for slot in range(2):
         share = share_parts(ins.got_share if slot else ins.share, bool(slot))
         sides.append(gradient_units(ins, slot, outs.direct, share))
-    units = sides[0][0] + sides[1][0]
+    units = [
+        (slot, kind, unit)
+        for slot in range(2)
+        for kind, side in enumerate(sides[slot][0])
+        for unit in side
+    ]
     sweeps = PINV_ITERS - EARLY_SWEEPS
     span = -(-len(units) // (2 * sweeps))
     work = iter([units[index : index + span] for index in range(0, len(units), span)])
@@ -867,12 +877,13 @@
     state = (ins.state[0], ins.state[1])
 
     def beside():
-        several(*next(work, ()))
+        for slot, kind, unit in next(work, ()):
+            need(ins.vg)
+            need(ins.turned, slot)
+            need(ins.token_prob if kind else ins.key_exp, slot)
+            unit()
 
     for sweep in range(sweeps):
-        if sweep < 2:
-            for ref in (ins.key_exp, ins.token_prob, ins.turned):
-                need(ref, sweep)
         for ref in saved:
             need(ref, sweep)
         state = gradient_sweep(state, saved, sweep, beside, sweep == sweeps - 1)
@@ -977,7 +988,12 @@
     )
     sums = staged_call(
         partial_compute,
-        dict(vg=vg, stats=kept.stats, key_low=kept.key_low, token_low=kept.token_low),
+        dict(
+            vg=vg,
+            stats=kept.stats,
+            key_low=(kept.key_low, LEAD),
+            token_low=(kept.token_low, LEAD),
+        ),
         dict(send=low(2 * HD + 16, M), keep=wide(2 * HD, M)),
         2,
     )
@@ -1024,7 +1040,7 @@
             key_exp=(kept.key_exp, SLOTS[1]),
             own_out=own.out,
         ),
-        dict(out=low(*qk.shape)),
+        dict(out=(low(*qk.shape), GROUPS)),
         1,
     ).out
     attended, value_gradient_array = unpack(half, exchange(first_results))
@@ -1036,17 +1052,17 @@
             got_share=got_share,
             scales=mixed.scales,
             marks=kept.marks,
-            vg=vg,
             pair=(kept.pair_b, LEAD),
             weight=(kept.weight_b, LEAD),
             growth=(kept.growth_b, LEAD),
+            vg=(vg, LATE),
             key_exp=(kept.key_exp, LEAD),
+            turned=(kept.turned, LEAD),
             token_prob=(kept.token_prob, LEAD),
-            turned=(kept.turned, LEAD),
-            inverse_grad=own.inverse_grad,
-            last_growth=kept.last_growth,
-            mark_prob=kept.mark_prob,
-            factor=kept.factor,
+            inverse_grad=(own.inverse_grad, LAST),
+            last_growth=(kept.last_growth, LAST),
+            mark_prob=(kept.mark_prob, LAST),
+            factor=(kept.factor, LAST),
         ),
         dict(
             far=low(2, 2, HALF, HD),

time: 124 us -> 123 us (level)
  no operation moved by 1% of the time
where the time goes in v12:
time: 123 us; the launch traced here: 122 us
  Pallas kernels  47.7 us (39%)
  waiting for transfers between devices  46.2 us (38%)
  starting transfers between devices  25 us (20%)
  local copies, waits for them, and re-layouts  2.63 us (2%)
    pallas_call x7, Pallas kernels, staged_call(): pl.pallas_call(kernel, out_shape=shapes, in_specs=[anywhere] * (n_in + n_...  39.8 us
    all_to_all x4, waiting for transfers between devices, exchange(): lax.all_to_all(packed, 'cube', split_axis=0, concat_axis=0, tiled=True)  28.1 us
    all_to_all x4, starting transfers between devices, exchange(): lax.all_to_all(packed, 'cube', split_axis=0, concat_axis=0, tiled=True)  20.2 us
    ppermute x4, waiting for transfers between devices, partner(): return lax.ppermute(array, 'half', SWAP)  18 us
    pallas_call x4, Pallas kernels, layout_call(): pl.pallas_call(kernel, out_shape=out_shape, in_specs=[pl.BlockSpec(memory...  7.59 us
    ppermute x4, starting transfers between devices, partner(): return lax.ppermute(array, 'half', SWAP)  4.84 us
    unnamed x12, local copies, waits for them, and re-layouts  2.63 us
  transfers between devices with their start and end apart: 8, of which 7 were waited for; matrix products, arithmetic and copies ran while one was open for 0% of the time, Pallas kernels for 29%

profile of v12, /device:TPU:0, one launch (start us, length us, event | category | flops | bytes accessed | tf_op | source)
XLA Modules:
  0.0 122.4 jit_solution(15461128212192283060)
XLA Ops:
  0.6 2.1 %shard_map.75 = bf16[16,2,2,64,128]{4,3,2,1,0:T(8,128)(2,1)} custom-call(s32[1]{0:T(128)} %bitcast.half_ref, bf16[64,4096]{1,0:T(8,128)(2,1)} %first_ref.2, bf16[64,4096]{1,0:T(8,128)(2,1)} %second_ref.2), custom_call_target="tpu_custom_call" | custom-call | bytes 2097152 | tf_op jit(solution)/shard_map/pallas_call | solution.py:510
  2.8 6.3 %all-to-all-start = ((bf16[16,2,2,64,128]{4,3,2,1,0:T(8,128)(2,1)}), bf16[16,2,2,64,128]{4,3,2,1,0:T(8,128)(2,1)S(1)}, u32[]{:S(2)}, u32[]{:S(2)}) async-start(bf16[16,2,2,64,128]{4,3,2,1,0:T(8,128)(2,1)} %shard_map.75), calls=%async_computation | async-start | bytes 2097152 | tf_op jit(solution)/shard_map/all_to_all | solution.py:947
  9.1 2.1 %shard_map.76 = bf16[16,2,2,64,128]{4,3,2,1,0:T(8,128)(2,1)} custom-call(s32[1]{0:T(128)} %bitcast.half_ref, bf16[64,4096]{1,0:T(8,128)(2,1)} %first_ref.3, bf16[64,4096]{1,0:T(8,128)(2,1)} %second_ref.3), custom_call_target="tpu_custom_call" | custom-call | bytes 2097152 | tf_op jit(solution)/shard_map/pallas_call | solution.py:510
  11.2 12.7 %all-to-all-done.qk_ref.refs_0_ = bf16[16,2,2,64,128]{4,3,2,1,0:T(8,128)(2,1)S(1)} async-done(((bf16[16,2,2,64,128]{4,3,2,1,0:T(8,128)(2,1)}), bf16[16,2,2,64,128]{4,3,2,1,0:T(8,128)(2,1)S(1)}, u32[]{:S(2)}, u32[]{:S(2)}) %all-to-all-start) | async-done | bytes 1048608 | tf_op jit(solution)/shard_map/all_to_all | solution.py:947
  24.2 2.7 %collective-permute-start = (bf16[2,2,128,128]{3,2,1,0:T(8,128)(2,1)S(1)}, bf16[2,2,128,128]{3,2,1,0:T(8,128)(2,1)S(1)}, u32[]{:S(2)}, u32[]{:S(2)}) collective-permute-start(bf16[2,2,128,128]{3,2,1,0:T(8,128)(2,1)S(1)} %shard_map.77.refs_1_), channel_id=1, source_target_pairs={{0,16},{16,0},{1,17},{17,1},{2,18},{18,2},{3,19},{19,3},{4,20},{20... | collective-permute-start | bytes 393224 | tf_op jit(solution)/shard_map/ppermute | solution.py:951
  26.8 4.3 %all-to-all-start.1 = ((bf16[16,2,2,64,128]{4,3,2,1,0:T(8,128)(2,1)}), bf16[16,2,2,64,128]{4,3,2,1,0:T(8,128)(2,1)}, u32[]{:S(2)}, u32[]{:S(2)}) async-start(bf16[16,2,2,64,128]{4,3,2,1,0:T(8,128)(2,1)} %shard_map.76), calls=%async_computation.1 | async-start | bytes 2097152 | tf_op jit(solution)/shard_map/all_to_all | solution.py:947
  31.2 1.4 %collective-permute-done.refs_2_ = bf16[2,2,128,128]{3,2,1,0:T(8,128)(2,1)S(1)} collective-permute-done((bf16[2,2,128,128]{3,2,1,0:T(8,128)(2,1)S(1)}, bf16[2,2,128,128]{3,2,1,0:T(8,128)(2,1)S(1)}, u32[]{:S(2)}, u32[]{:S(2)}) %collective-permute-start) | collective-permute-done | bytes 131104 | tf_op jit(solution)/shard_map/ppermute | solution.py:951
  32.6 0.7 copy-done.5
  33.3 10.3 %shard_map.78 = (bf16[2,2,256,128]{3,2,1,0:T(8,128)(2,1)}, f32[2,1024,256]{2,1,0:T(8,128)}, bf16[2,1024,256]{2,1,0:T(8,128)(2,1)}, f32[2,1024,256]{2,1,0:T(8,128...) custom-call(bf16[16,2,2,64,128]{4,3,2,1,0:T(8,128)(2,1)} %copy-done,, ...), custom_call_target="tpu_custom_call" | custom-call | flops 199999995904 | bytes 16003072 | tf_op jit(solution)/shard_map/pallas_call | solution.py:423
  43.5 2.9 %all-to-all-done.1.refs_0_.refs_8_ = bf16[16,2,2,64,128]{4,3,2,1,0:T(8,128)(2,1)} async-done(((bf16[16,2,2,64,128]{4,3,2,1,0:T(8,128)(2,1)}), bf16[16,2,2,64,128]{4,3,2,1,0:T(8,128)(2,1)}, u32[]{:S(2)}, u32[]{:S(2)}) %all-to-all-start.1) | async-done | bytes 1048608 | tf_op jit(solution)/shard_map/all_to_all | solution.py:947
  46.5 3.4 %shard_map.79 = (bf16[272,256]{1,0:T(8,128)(2,1)}, f32[256,256]{1,0:T(8,128)}) custom-call(bf16[16,2,2,64,128]{4,3,2,1,0:T(8,128)(2,1)} %all-to-all-done.1.refs_0_.refs_8_, f32[8,256]{1,0:T(8,128)} %get-tuple-element.45.refs_1_.refs_2_, bf16[2,1024,256]{2,1,0:T(8,128)(2,1)} %get-tuple-element.46.refs_2_, ...), custom_call_target="tpu_custom_call" | custom-call | flops 2000000000 | bytes 3555328 | tf_op jit(solution)/shard_map/pallas_call | solution.py:423
  50.0 8.4 %collective-permute-done.1.refs_0_ = bf16[272,256]{1,0:T(8,128)(2,1)S(1)} collective-permute-done((bf16[272,256]{1,0:T(8,128)(2,1)}, bf16[272,256]{1,0:T(8,128)(2,1)S(1)}, u32[]{:S(2)}, u32[]{:S(2)}) %collective-permute-start.1) | collective-permute-done | bytes 139296 | tf_op jit(solution)/shard_map/ppermute | solution.py:951
  59.0 2.4 %shard_map.80 = (bf16[272,256]{1,0:T(8,128)(2,1)}, f32[8,256]{1,0:T(8,128)}, f32[128,256]{1,0:T(8,128)}, f32[128,256]{1,0:T(8,128)}) custom-call(bf16[272,256]{1,0:T(8,128)(2,1)} %copy-done.4, f32[256,256]{1,0:T(8,128)} %get-tuple-element.49.refs_1_, f32[8,256]{1,0:T(8,128)} %get-tuple-element.45.refs_1_.refs_2_, bf16[2,256,256]{2,1,0:T(8,128)(2,1)} %get-tuple-element.50.refs_3_), custom_call_target="tpu_custom_call" | custom-call | flops 1000000000 | bytes 1081344 | tf_op jit(solution)/shard_map/pallas_call | solution.py:423
  61.5 7.4 %shard_map.81 = (bf16[16,2,64,128]{3,2,1,0:T(8,128)(2,1)}, f32[2,256,256]{2,1,0:T(8,128)}, bf16[2,256,256]{2,1,0:T(8,128)(2,1)}) custom-call(f32[256,256]{1,0:T(8,128)} %get-tuple-element.54.refs_0_.refs_14_, f32[8,128]{1,0:T(8,128)} %get-tuple-element.55.refs_1_.refs_15_, f32[128,256]{1,0:T(8,128)} %get-tuple-element.56.refs_2_, ...), custom_call_target="tpu_custom_call" | custom-call | flops 8000000000 | bytes 8278016 | tf_op jit(solution)/shard_map/pallas_call | solution.py:423
  70.1 2.9 %shard_map.82.refs_16_ = bf16[16,2,2,64,128]{4,3,2,1,0:T(8,128)(2,1)} custom-call(bf16[272,256]{1,0:T(8,128)(2,1)} %copy-done.2, f32[8,256]{1,0:T(8,128)} %get-tuple-element.52.refs_5_.refs_1_.refs_3_, bf16[2,1024,256]{2,1,0:T(8,128)(2,1)} %get-tuple-element.47.refs_3_.refs_6_.refs_2_, f32[2,1024,256]{2,1,0:T(8,128)} %get-tuple-element.53.refs_10_.refs_3_.refs_9_, ...), custom_call_target="tpu_custom_call" | custom-call | flops 1000000000 | bytes 4866048 | tf_op jit(solution)/shard_map/pallas_call | solution.py:423
  73.1 5.6 %all-to-all-start.2 = ((bf16[16,2,2,64,128]{4,3,2,1,0:T(8,128)(2,1)}), bf16[16,2,2,64,128]{4,3,2,1,0:T(8,128)(2,1)}, u32[]{:S(2)}, u32[]{:S(2)}) async-start(bf16[16,2,2,64,128]{4,3,2,1,0:T(8,128)(2,1)} %shard_map.82.refs_16_), calls=%async_computation.2 | async-start | bytes 2097152 | tf_op jit(solution)/shard_map/all_to_all | solution.py:947
  78.7 10.8 %shard_map.84 = (bf16[2,2,128,128]{3,2,1,0:T(8,128)(2,1)}, f32[2,2,128,128]{3,2,1,0:T(8,128)}, f32[2,2,1024,128]{3,2,1,0:T(8,128)}) custom-call(f32[2,256,256]{2,1,0:T(8,128)} %get-tuple-element.63.refs_0_, bf16[272,256]{1,0:T(8,128)(2,1)} %get-tuple-element.51.refs_4_.refs_1_, bf16[272,256]{1,0:T(8,128)(2,1)} %copy-done.2, ...), custom_call_target="tpu_custom_call" | custom-call | flops 199999995904 | bytes 13791232 | tf_op jit(solution)/shard_map/pallas_call | solution.py:423
  89.4 2.0 %collective-permute-start.3 = (bf16[2,2,128,128]{3,2,1,0:T(8,128)(2,1)}, bf16[2,2,128,128]{3,2,1,0:T(8,128)(2,1)S(1)}, u32[]{:S(2)}, u32[]{:S(2)}) collective-permute-start(bf16[2,2,128,128]{3,2,1,0:T(8,128)(2,1)} %get-tuple-element.72), channel_id=1, source_target_pairs={{0,16},{16,0},{1,17},{17,1},{2,18},{18,2},{3,19},{19,3},{4,20},{20... | collective-permute-start | bytes 393224 | tf_op jit(solution)/shard_map/ppermute | solution.py:951
  91.5 7.7 %collective-permute-done.3.refs_0_ = bf16[2,2,128,128]{3,2,1,0:T(8,128)(2,1)S(1)} collective-permute-done((bf16[2,2,128,128]{3,2,1,0:T(8,128)(2,1)}, bf16[2,2,128,128]{3,2,1,0:T(8,128)(2,1)S(1)}, u32[]{:S(2)}, u32[]{:S(2)}) %collective-permute-start.3) | collective-permute-done | bytes 131104 | tf_op jit(solution)/shard_map/ppermute | solution.py:951
  99.8 2.6 %shard_map.85 = bf16[16,2,2,64,128]{4,3,2,1,0:T(8,128)(2,1)} custom-call(bf16[2,2,128,128]{3,2,1,0:T(8,128)(2,1)} %copy-done.3, f32[2,2,128,128]{3,2,1,0:T(8,128)} %get-tuple-element.73.refs_1_, f32[2,2,1024,128]{3,2,1,0:T(8,128)} %get-tuple-element.74.refs_2_), custom_call_target="tpu_custom_call" | custom-call | flops 100000000 | bytes 3538944 | tf_op jit(solution)/shard_map/pallas_call | solution.py:423
  102.5 4.0 %all-to-all-start.3 = ((bf16[16,2,2,64,128]{4,3,2,1,0:T(8,128)(2,1)}), bf16[16,2,2,64,128]{4,3,2,1,0:T(8,128)(2,1)S(1)}, u32[]{:S(2)}, u32[]{:S(2)}) async-start(bf16[16,2,2,64,128]{4,3,2,1,0:T(8,128)(2,1)} %shard_map.85), calls=%async_computation.3 | async-start | bytes 2097152 | tf_op jit(solution)/shard_map/all_to_all | solution.py:947
  106.4 2.3 %shard_map.83 = (bf16[64,4096]{1,0:T(8,128)(2,1)}, bf16[64,4096]{1,0:T(8,128)(2,1)}) custom-call(s32[1]{0:T(128)} %bitcast.half_ref, bf16[16,2,2,64,128]{4,3,2,1,0:T(8,128)(2,1)} %all-to-all-done.2.packed_ref), custom_call_target="tpu_custom_call" | custom-call | bytes 2097152 | tf_op jit(solution)/shard_map/pallas_call | solution.py:510
  108.7 12.5 %all-to-all-done.3.packed_ref = bf16[16,2,2,64,128]{4,3,2,1,0:T(8,128)(2,1)S(1)} async-done(((bf16[16,2,2,64,128]{4,3,2,1,0:T(8,128)(2,1)}), bf16[16,2,2,64,128]{4,3,2,1,0:T(8,128)(2,1)S(1)}, u32[]{:S(2)}, u32[]{:S(2)}) %all-to-all-start.3) | async-done | bytes 1048608 | tf_op jit(solution)/shard_map/all_to_all | solution.py:947
  121.2 1.0 shard_map.86
  (16 shorter events, 3.0 us)
Async XLA Ops:
  2.8 21.1 %all-to-all-start = ((bf16[16,2,2,64,128]{4,3,2,1,0:T(8,128)(2,1)}), bf16[16,2,2,64,128]{4,3,2,1,0:T(8,128)(2,1)S(1)}, u32[]{:S(2)}, u32[]{:S(2)}) async-start(bf16[16,2,2,64,128]{4,3,2,1,0:T(8,128)(2,1)} %shard_map.75), calls=%async_computation | async-start | bytes 2097152 | tf_op jit(solution)/shard_map/all_to_all | solution.py:947
  23.9 8.7 %copy-start = (bf16[16,2,2,64,128]{4,3,2,1,0:T(8,128)(2,1)}, bf16[16,2,2,64,128]{4,3,2,1,0:T(8,128)(2,1)S(1)}, u32[]{:S(2)}) copy-start(bf16[16,2,2,64,128]{4,3,2,1,0:T(8,128)(2,1)S(1)} %all-to-all-done.qk_ref.refs_0_) | copy-start | bytes 3145732
  24.2 8.4 %copy-start.1 = (bf16[2,2,128,128]{3,2,1,0:T(8,128)(2,1)}, bf16[2,2,128,128]{3,2,1,0:T(8,128)(2,1)S(1)}, u32[]{:S(2)}) copy-start(bf16[2,2,128,128]{3,2,1,0:T(8,128)(2,1)S(1)} %shard_map.77.refs_1_) | copy-start | bytes 393220
  24.2 8.4 %collective-permute-start = (bf16[2,2,128,128]{3,2,1,0:T(8,128)(2,1)S(1)}, bf16[2,2,128,128]{3,2,1,0:T(8,128)(2,1)S(1)}, u32[]{:S(2)}, u32[]{:S(2)}) collective-permute-start(bf16[2,2,128,128]{3,2,1,0:T(8,128)(2,1)S(1)} %shard_map.77.refs_1_), channel_id=1, source_target_pairs={{0,16},{16,0},{1,17},{17,1},{2,18},{18,2},{3,19},{19,3},{4,20},{20... | collective-permute-start | bytes 393224 | tf_op jit(solution)/shard_map/ppermute | solution.py:951
  26.8 19.6 %all-to-all-start.1 = ((bf16[16,2,2,64,128]{4,3,2,1,0:T(8,128)(2,1)}), bf16[16,2,2,64,128]{4,3,2,1,0:T(8,128)(2,1)}, u32[]{:S(2)}, u32[]{:S(2)}) async-start(bf16[16,2,2,64,128]{4,3,2,1,0:T(8,128)(2,1)} %shard_map.76), calls=%async_computation.1 | async-start | bytes 2097152 | tf_op jit(solution)/shard_map/all_to_all | solution.py:947
  32.6 0.7 copy-start.5
  49.9 8.5 %collective-permute-start.1 = (bf16[272,256]{1,0:T(8,128)(2,1)}, bf16[272,256]{1,0:T(8,128)(2,1)S(1)}, u32[]{:S(2)}, u32[]{:S(2)}) collective-permute-start(bf16[272,256]{1,0:T(8,128)(2,1)} %get-tuple-element.48), channel_id=1, source_target_pairs={{0,16},{16,0},{1,17},{17,1},{2,18},{18,2},{3,19},{19,3},{4,20},{20... | collective-permute-start | bytes 417800 | tf_op jit(solution)/shard_map/ppermute | solution.py:951
  58.4 0.7 copy-start.4
  61.4 8.1 %collective-permute-start.2 = (bf16[272,256]{1,0:T(8,128)(2,1)}, bf16[272,256]{1,0:T(8,128)(2,1)S(1)}, u32[]{:S(2)}, u32[]{:S(2)}) collective-permute-start(bf16[272,256]{1,0:T(8,128)(2,1)} %get-tuple-element.51.refs_4_.refs_1_), channel_id=1, source_target_pairs={{0,16},{16,0},{1,17},{17,1},{2,18},{18,2},{3,19},{19,3},{4,20},{20... | collective-permute-start | bytes 417800 | tf_op jit(solution)/shard_map/ppermute | solution.py:951
  69.5 0.7 copy-start.2
  73.1 29.4 %all-to-all-start.2 = ((bf16[16,2,2,64,128]{4,3,2,1,0:T(8,128)(2,1)}), bf16[16,2,2,64,128]{4,3,2,1,0:T(8,128)(2,1)}, u32[]{:S(2)}, u32[]{:S(2)}) async-start(bf16[16,2,2,64,128]{4,3,2,1,0:T(8,128)(2,1)} %shard_map.82.refs_16_), calls=%async_computation.2 | async-start | bytes 2097152 | tf_op jit(solution)/shard_map/all_to_all | solution.py:947
  89.4 9.7 %collective-permute-start.3 = (bf16[2,2,128,128]{3,2,1,0:T(8,128)(2,1)}, bf16[2,2,128,128]{3,2,1,0:T(8,128)(2,1)S(1)}, u32[]{:S(2)}, u32[]{:S(2)}) collective-permute-start(bf16[2,2,128,128]{3,2,1,0:T(8,128)(2,1)} %get-tuple-element.72), channel_id=1, source_target_pairs={{0,16},{16,0},{1,17},{17,1},{2,18},{18,2},{3,19},{19,3},{4,20},{20... | collective-permute-start | bytes 393224 | tf_op jit(solution)/shard_map/ppermute | solution.py:951
  99.2 0.7 copy-start.3
  102.5 18.8 %all-to-all-start.3 = ((bf16[16,2,2,64,128]{4,3,2,1,0:T(8,128)(2,1)}), bf16[16,2,2,64,128]{4,3,2,1,0:T(8,128)(2,1)S(1)}, u32[]{:S(2)}, u32[]{:S(2)}) async-start(bf16[16,2,2,64,128]{4,3,2,1,0:T(8,128)(2,1)} %shard_map.85), calls=%async_computation.3 | async-start | bytes 2097152 | tf_op jit(solution)/shard_map/all_to_all | solution.py:947

commit v13 on v12

--- a/solution.py
+++ b/solution.py
@@ -699,35 +699,48 @@
         put(home)
 
 
-def mixing_compute(ins, outs, need, put):
-    need()
-    got = ins.got[...].astype(jnp.float32)
+def mixing_kernel(got_ref, keep_ref, stats_ref, inverse_ref, share_ref, mix_ref):
+    got = got_ref[...].astype(jnp.float32)
     others = swap_lanes(joined_thirds(got[2 * HD : 2 * HD + 12]))
     scales = []
     for slot in range(2):
-        own_max, own_total = ins.stats[2 * slot : 2 * slot + 1], ins.stats[2 * slot + 1 : 2 * slot + 2]
-        other = 1 - slot
-        other_max, other_total = others[2 * other : 2 * other + 1], others[2 * other + 1 : 2 * other + 2]
+        own, other = 2 * slot, 2 * (1 - slot)
+        own_max, own_total = stats_ref[own : own + 1], stats_ref[own + 1 : own + 2]
+        other_max, other_total = others[other : other + 1], others[other + 1 : other + 2]
         key_max = jnp.maximum(own_max, other_max)
         own_factor, other_factor = jnp.exp(own_max - key_max), jnp.exp(other_max - key_max)
         inverse_total = 1.0 / (own_total * own_factor + other_total * other_factor)
         scales.append((own_factor * inverse_total, other_factor * inverse_total))
-    outs.scales[...] = jnp.concatenate(
-        [scales[0][0], scales[1][0], jnp.zeros((6, M), jnp.float32)], axis=0
-    )
-    landmark_values = ins.keep[0:HD] * scales[0][0] + swap_lanes(got[0:HD]) * scales[0][1]
-    mixing_grad = ins.keep[HD : 2 * HD] + swap_lanes(got[HD : 2 * HD])
-    inverse = (ins.inverse[0], ins.inverse[1])
-    outs.share[0:HD] = split_dot_nt(halves(landmark_values), inverse).astype(jnp.bfloat16)
+    landmark_values = keep_ref[0:HD] * scales[0][0] + swap_lanes(got[0:HD]) * scales[0][1]
+    mixing_grad = keep_ref[HD : 2 * HD] + swap_lanes(got[HD : 2 * HD])
+    inverse = (inverse_ref[0], inverse_ref[1])
+    mixing_low = split_dot_nt(halves(landmark_values), inverse).astype(jnp.bfloat16)
     values_low = split_dot(halves(mixing_grad), inverse).astype(jnp.bfloat16)
-    outs.share[HD : 2 * HD] = values_low
     row_total = jnp.sum(values_low.astype(jnp.float32) * landmark_values, axis=0, keepdims=True)
-    outs.share[2 * HD :] = jnp.concatenate(
+    share_ref[0:HD] = mixing_low
+    share_ref[HD : 2 * HD] = values_low
+    share_ref[2 * HD :] = jnp.concatenate(
         [thirds(row_total), jnp.zeros((13, M), jnp.float32)], axis=0
     ).astype(jnp.bfloat16)
-    put(outs.share)
-    outs.mixing_grad[...] = mixing_grad
-    outs.mark_values[...] = landmark_values
+    mix_ref[0:HD] = mixing_low.astype(jnp.float32)
+    mix_ref[HD : 2 * HD] = values_low.astype(jnp.float32)
+    mix_ref[2 * HD : 2 * HD + 8] = jnp.concatenate(
+        [row_total, scales[0][0], scales[1][0], jnp.zeros((5, M), jnp.float32)], axis=0
+    )
+    mix_ref[2 * HD + 8 : 3 * HD + 8] = mixing_grad
+    mix_ref[3 * HD + 8 :] = landmark_values
+
+
+def joined_sums(*operands):
+    held = pl.BlockSpec(memory_space=pltpu.VMEM)
+    return pl.pallas_call(
+        mixing_kernel,
+        out_shape=(low(2 * HD + 16, M), wide(4 * HD + 8, M)),
+        in_specs=[held] * len(operands),
+        out_specs=(held, held),
+        compiler_params=pltpu.CompilerParams(vmem_limit_bytes=SMALL_LIMIT),
+        cost_estimate=pl.CostEstimate(flops=2 * 10**8, bytes_accessed=2**20, transcendentals=0),
+    )(*operands)
 
 
 def several(*units):
@@ -737,7 +750,7 @@
 
 def out_units(ins, slot, out_ref, lead, share):
     mixing_low, values_low, _ = share
-    scale = ins.scales[slot : slot + 1]
+    scale = ins.mix[2 * HD + 1 + slot : 2 * HD + 2 + slot]
 
     def token_side(index):
         place = slice(index * CHUNK, (index + 1) * CHUNK)
@@ -760,7 +773,7 @@
     score_scale = HD ** (-0.5)
     mixing_low, values_low, row_total = share
     query_sums, key_sums = [], []
-    scale = ins.scales[slot : slot + 1]
+    scale = ins.mix[2 * HD + 1 + slot : 2 * HD + 2 + slot]
 
     def token_side(index):
         place = slice(index * CHUNK, (index + 1) * CHUNK)
@@ -787,9 +800,17 @@
     return units, query_sums, key_sums
 
 
-def share_parts(ref, swap):
-    parts = [ref[0:HD], ref[HD : 2 * HD], joined_thirds(ref[2 * HD :].astype(jnp.float32)[0:3])]
-    return [swap_lanes(part) for part in parts] if swap else parts
+def own_parts(ref):
+    return (
+        ref[0:HD].astype(jnp.bfloat16),
+        ref[HD : 2 * HD].astype(jnp.bfloat16),
+        ref[2 * HD : 2 * HD + 1],
+    )
+
+
+def other_parts(ref):
+    parts = (ref[0:HD], ref[HD : 2 * HD], joined_thirds(ref[2 * HD :].astype(jnp.float32)[0:3]))
+    return [swap_lanes(part) for part in parts]
 
 
 def gradient_sweep(state, saved, place, beside, last):
@@ -817,14 +838,16 @@
 
 
 def own_gradient_compute(ins, outs, need, put):
-    for ref in (ins.mark_prob, ins.factor, ins.mixing_grad, ins.mark_values, ins.share, ins.scales):
+    for ref in (ins.mark_prob, ins.factor, ins.mix):
         need(ref)
-    inverse_grad = split_dot(halves(ins.mixing_grad[...].T), halves(ins.mark_values[...]))
+    inverse_grad = split_dot(
+        halves(ins.mix[2 * HD + 8 : 3 * HD + 8].T), halves(ins.mix[3 * HD + 8 :])
+    )
     inverse_grad_halves = halves(inverse_grad)
     outs.inverse_grad[0], outs.inverse_grad[1] = inverse_grad_halves
     toward = split_dot(halves(ins.mark_prob[...]), inverse_grad_halves) * ins.factor[0:1, 0:1]
     state = (0.5 * (toward + toward.T), None)
-    units = out_units(ins, 0, outs.out, (), share_parts(ins.share, False))
+    units = out_units(ins, 0, outs.out, (), own_parts(ins.mix))
     work = iter([units[index : index + 2] for index in range(0, len(units), 2)])
     saved = (ins.pair, ins.weight, ins.growth)
 
@@ -843,9 +866,9 @@
 
 
 def other_out_compute(ins, outs, need, put):
-    for ref in (ins.got_share, ins.scales, ins.token_low):
+    for ref in (ins.got_share, ins.mix, ins.token_low):
         need(ref)
-    units = out_units(ins, 1, outs.out, (1,), share_parts(ins.got_share, True))
+    units = out_units(ins, 1, outs.out, (1,), other_parts(ins.got_share))
     chunks = len(units) // 2
     several(*units[:chunks])
     need()
@@ -858,11 +881,11 @@
 
 
 def gradient_compute(ins, outs, need, put):
-    for ref in (ins.state, ins.share, ins.got_share, ins.scales, ins.marks):
+    for ref in (ins.state, ins.mix, ins.got_share, ins.marks):
         need(ref)
     sides = []
     for slot in range(2):
-        share = share_parts(ins.got_share if slot else ins.share, bool(slot))
+        share = other_parts(ins.got_share) if slot else own_parts(ins.mix)
         sides.append(gradient_units(ins, slot, outs.direct, share))
     units = [
         (slot, kind, unit)
@@ -997,27 +1020,14 @@
         dict(send=low(2 * HD + 16, M), keep=wide(2 * HD, M)),
         2,
     )
-    mixed = staged_call(
-        mixing_compute,
-        dict(got=partner(sums.send), keep=sums.keep, stats=kept.stats, inverse=kept.inverse),
-        dict(
-            share=low(2 * HD + 16, M),
-            scales=wide(8, M),
-            mixing_grad=wide(HD, M),
-            mark_values=wide(HD, M),
-        ),
-        1,
-    )
-    got_share = partner(mixed.share)
+    share, mix = joined_sums(partner(sums.send), sums.keep, kept.stats, kept.inverse)
+    got_share = partner(share)
     own = staged_call(
         own_gradient_compute,
         dict(
             mark_prob=kept.mark_prob,
             factor=kept.factor,
-            mixing_grad=mixed.mixing_grad,
-            mark_values=mixed.mark_values,
-            share=mixed.share,
-            scales=mixed.scales,
+            mix=mix,
             token_low=(kept.token_low, SLOTS[0]),
             pair=(kept.pair_a, LEAD),
             weight=(kept.weight_a, LEAD),
@@ -1035,7 +1045,7 @@
         other_out_compute,
         dict(
             got_share=got_share,
-            scales=mixed.scales,
+            mix=mix,
             token_low=(kept.token_low, SLOTS[1]),
             key_exp=(kept.key_exp, SLOTS[1]),
             own_out=own.out,
@@ -1048,9 +1058,8 @@
         gradient_compute,
         dict(
             state=own.state,
-            share=mixed.share,
             got_share=got_share,
-            scales=mixed.scales,
+            mix=mix,
             marks=kept.marks,
             pair=(kept.pair_b, LEAD),
             weight=(kept.weight_b, LEAD),

time: 123 us -> 122 us (level)
  Pallas kernels: 47.7 us -> 46 us
    pallas_call x7 -> x6, Pallas kernels: 39.8 us -> 37.7 us  [staged_call(): pl.pallas_call(kernel, out_shape=shapes, in_specs=[anywhere] * (n_in + n_...]
    unnamed x12 -> x18, local copies, waits for them, and re-layouts: 2.63 us -> 3.75 us
where the time goes in v13:
time: 122 us
  waiting for transfers between devices  46.5 us (38%)
  Pallas kernels  46 us (38%)
  starting transfers between devices  24.6 us (20%)
  local copies, waits for them, and re-layouts  3.75 us (3%)
    pallas_call x6, Pallas kernels, staged_call(): pl.pallas_call(kernel, out_shape=shapes, in_specs=[anywhere] * (n_in + n_...  37.7 us
    all_to_all x4, waiting for transfers between devices, exchange(): lax.all_to_all(packed, 'cube', split_axis=0, concat_axis=0, tiled=True)  28.1 us
    all_to_all x4, starting transfers between devices, exchange(): lax.all_to_all(packed, 'cube', split_axis=0, concat_axis=0, tiled=True)  20.1 us
    ppermute x4, waiting for transfers between devices, partner(): return lax.ppermute(array, 'half', SWAP)  18.4 us
    pallas_call x4, Pallas kernels, layout_call(): pl.pallas_call(kernel, out_shape=out_shape, in_specs=[pl.BlockSpec(memory...  7.65 us
    ppermute x4, starting transfers between devices, partner(): return lax.ppermute(array, 'half', SWAP)  4.54 us
    unnamed x18, local copies, waits for them, and re-layouts  3.75 us
  transfers between devices with their start and end apart: 8, of which 7 were waited for; matrix products, arithmetic and copies ran while one was open for 0% of the time, Pallas kernels for 29%

profile of v13, /device:TPU:0, one launch (start us, length us, event | category | flops | bytes accessed | tf_op | source)
XLA Modules:
  0.0 121.8 jit_solution(7384188640055413523)
XLA Ops:
  0.6 2.1 %shard_map.75 = bf16[16,2,2,64,128]{4,3,2,1,0:T(8,128)(2,1)} custom-call(s32[1]{0:T(128)} %bitcast.half_ref, bf16[64,4096]{1,0:T(8,128)(2,1)} %first_ref.2, bf16[64,4096]{1,0:T(8,128)(2,1)} %second_ref.2), custom_call_target="tpu_custom_call" | custom-call | bytes 2097152 | tf_op jit(solution)/shard_map/pallas_call | solution.py:510
  2.8 6.3 %all-to-all-start = ((bf16[16,2,2,64,128]{4,3,2,1,0:T(8,128)(2,1)}), bf16[16,2,2,64,128]{4,3,2,1,0:T(8,128)(2,1)S(1)}, u32[]{:S(2)}, u32[]{:S(2)}) async-start(bf16[16,2,2,64,128]{4,3,2,1,0:T(8,128)(2,1)} %shard_map.75), calls=%async_computation | async-start | bytes 2097152 | tf_op jit(solution)/shard_map/all_to_all | solution.py:970
  9.1 2.2 %shard_map.76 = bf16[16,2,2,64,128]{4,3,2,1,0:T(8,128)(2,1)} custom-call(s32[1]{0:T(128)} %bitcast.half_ref, bf16[64,4096]{1,0:T(8,128)(2,1)} %first_ref.3, bf16[64,4096]{1,0:T(8,128)(2,1)} %second_ref.3), custom_call_target="tpu_custom_call" | custom-call | bytes 2097152 | tf_op jit(solution)/shard_map/pallas_call | solution.py:510
  11.3 12.6 %all-to-all-done.qk_ref.refs_0_ = bf16[16,2,2,64,128]{4,3,2,1,0:T(8,128)(2,1)S(1)} async-done(((bf16[16,2,2,64,128]{4,3,2,1,0:T(8,128)(2,1)}), bf16[16,2,2,64,128]{4,3,2,1,0:T(8,128)(2,1)S(1)}, u32[]{:S(2)}, u32[]{:S(2)}) %all-to-all-start) | async-done | bytes 1048608 | tf_op jit(solution)/shard_map/all_to_all | solution.py:970
  24.2 2.7 %collective-permute-start = (bf16[2,2,128,128]{3,2,1,0:T(8,128)(2,1)S(1)}, bf16[2,2,128,128]{3,2,1,0:T(8,128)(2,1)S(1)}, u32[]{:S(2)}, u32[]{:S(2)}) collective-permute-start(bf16[2,2,128,128]{3,2,1,0:T(8,128)(2,1)S(1)} %shard_map.77.refs_1_), channel_id=1, source_target_pairs={{0,16},{16,0},{1,17},{17,1},{2,18},{18,2},{3,19},{19,3},{4,20},{20... | collective-permute-start | bytes 393224 | tf_op jit(solution)/shard_map/ppermute | solution.py:974
  26.9 4.3 %all-to-all-start.1 = ((bf16[16,2,2,64,128]{4,3,2,1,0:T(8,128)(2,1)}), bf16[16,2,2,64,128]{4,3,2,1,0:T(8,128)(2,1)}, u32[]{:S(2)}, u32[]{:S(2)}) async-start(bf16[16,2,2,64,128]{4,3,2,1,0:T(8,128)(2,1)} %shard_map.76), calls=%async_computation.1 | async-start | bytes 2097152 | tf_op jit(solution)/shard_map/all_to_all | solution.py:970
  31.2 1.4 %collective-permute-done.refs_2_ = bf16[2,2,128,128]{3,2,1,0:T(8,128)(2,1)S(1)} collective-permute-done((bf16[2,2,128,128]{3,2,1,0:T(8,128)(2,1)S(1)}, bf16[2,2,128,128]{3,2,1,0:T(8,128)(2,1)S(1)}, u32[]{:S(2)}, u32[]{:S(2)}) %collective-permute-start) | collective-permute-done | bytes 131104 | tf_op jit(solution)/shard_map/ppermute | solution.py:974
  33.3 10.3 %shard_map.78 = (bf16[2,2,256,128]{3,2,1,0:T(8,128)(2,1)}, f32[2,1024,256]{2,1,0:T(8,128)}, bf16[2,1024,256]{2,1,0:T(8,128)(2,1)}, f32[2,1024,256]{2,1,0:T(8,128...) custom-call(bf16[16,2,2,64,128]{4,3,2,1,0:T(8,128)(2,1)} %copy-done,, ...), custom_call_target="tpu_custom_call" | custom-call | flops 199999995904 | bytes 16003072 | tf_op jit(solution)/shard_map/pallas_call | solution.py:423
  43.6 2.9 %all-to-all-done.1.refs_0_.refs_7_ = bf16[16,2,2,64,128]{4,3,2,1,0:T(8,128)(2,1)} async-done(((bf16[16,2,2,64,128]{4,3,2,1,0:T(8,128)(2,1)}), bf16[16,2,2,64,128]{4,3,2,1,0:T(8,128)(2,1)}, u32[]{:S(2)}, u32[]{:S(2)}) %all-to-all-start.1) | async-done | bytes 1048608 | tf_op jit(solution)/shard_map/all_to_all | solution.py:970
  46.5 3.5 %shard_map.79 = (bf16[272,256]{1,0:T(8,128)(2,1)}, f32[256,256]{1,0:T(8,128)}) custom-call(bf16[16,2,2,64,128]{4,3,2,1,0:T(8,128)(2,1)} %all-to-all-done.1.refs_0_.refs_7_, f32[8,256]{1,0:T(8,128)} %get-tuple-element.43.refs_1_.stats_ref, bf16[2,1024,256]{2,1,0:T(8,128)(2,1)} %get-tuple-element.44.refs_2_, ...), custom_call_target="tpu_custom_call" | custom-call | flops 2000000000 | bytes 3555328 | tf_op jit(solution)/shard_map/pallas_call | solution.py:423
  50.0 8.5 %collective-permute-done.1.got_ref = bf16[272,256]{1,0:T(8,128)(2,1)S(1)} collective-permute-done((bf16[272,256]{1,0:T(8,128)(2,1)}, bf16[272,256]{1,0:T(8,128)(2,1)S(1)}, u32[]{:S(2)}, u32[]{:S(2)}) %collective-permute-start.1) | collective-permute-done | bytes 139296 | tf_op jit(solution)/shard_map/ppermute | solution.py:974
  58.5 0.9 copy-done.4
  59.8 0.8 copy-done.1
  60.6 7.4 %shard_map.81 = (bf16[16,2,64,128]{3,2,1,0:T(8,128)(2,1)}, f32[2,256,256]{2,1,0:T(8,128)}, bf16[2,256,256]{2,1,0:T(8,128)(2,1)}) custom-call(f32[256,256]{1,0:T(8,128)} %get-tuple-element.52.refs_0_.refs_13_, f32[8,128]{1,0:T(8,128)} %get-tuple-element.53.refs_1_.refs_14_, f32[520,256]{1,0:T(8,128)} %copy-done.1, ...), custom_call_target="tpu_custom_call" | custom-call | flops 8000000000 | bytes 8400896 | tf_op jit(solution)/shard_map/pallas_call | solution.py:423
  69.4 3.1 %shard_map.82.refs_15_ = bf16[16,2,2,64,128]{4,3,2,1,0:T(8,128)(2,1)} custom-call(bf16[272,256]{1,0:T(8,128)(2,1)} %copy-done.6, f32[520,256]{1,0:T(8,128)} %copy-done.1, bf16[2,1024,256]{2,1,0:T(8,128)(2,1)} %get-tuple-element.45.refs_3_.refs_2_, f32[2,1024,256]{2,1,0:T(8,128)} %get-tuple-element.51.refs_7_.refs_3_.refs_8_, ...), custom_call_target="tpu_custom_call" | custom-call | flops 1000000000 | bytes 5390336 | tf_op jit(solution)/shard_map/pallas_call | solution.py:423
  72.5 5.5 %all-to-all-start.2 = ((bf16[16,2,2,64,128]{4,3,2,1,0:T(8,128)(2,1)}), bf16[16,2,2,64,128]{4,3,2,1,0:T(8,128)(2,1)}, u32[]{:S(2)}, u32[]{:S(2)}) async-start(bf16[16,2,2,64,128]{4,3,2,1,0:T(8,128)(2,1)} %shard_map.82.refs_15_), calls=%async_computation.2 | async-start | bytes 2097152 | tf_op jit(solution)/shard_map/all_to_all | solution.py:970
  77.9 10.9 %shard_map.84 = (bf16[2,2,128,128]{3,2,1,0:T(8,128)(2,1)}, f32[2,2,128,128]{3,2,1,0:T(8,128)}, f32[2,2,1024,128]{3,2,1,0:T(8,128)}) custom-call(f32[2,256,256]{2,1,0:T(8,128)} %get-tuple-element.59.refs_0_, bf16[272,256]{1,0:T(8,128)(2,1)} %copy-done.6, f32[520,256]{1,0:T(8,128)} %copy-done.1, bf16[2,2,256,128]{3,2,1,0:T(8,128)(2,1)} %get-tuple-element.60.refs_3_, ...), custom_call_target="tpu_custom_call" | custom-call | flops 199999995904 | bytes 14176256 | tf_op jit(solution)/shard_map/pallas_call | solution.py:423
  88.8 1.8 %collective-permute-start.3 = (bf16[2,2,128,128]{3,2,1,0:T(8,128)(2,1)}, bf16[2,2,128,128]{3,2,1,0:T(8,128)(2,1)S(1)}, u32[]{:S(2)}, u32[]{:S(2)}) collective-permute-start(bf16[2,2,128,128]{3,2,1,0:T(8,128)(2,1)} %get-tuple-element.68), channel_id=1, source_target_pairs={{0,16},{16,0},{1,17},{17,1},{2,18},{18,2},{3,19},{19,3},{4,20},{20... | collective-permute-start | bytes 393224 | tf_op jit(solution)/shard_map/ppermute | solution.py:974
  90.6 7.9 %collective-permute-done.3.refs_0_ = bf16[2,2,128,128]{3,2,1,0:T(8,128)(2,1)S(1)} collective-permute-done((bf16[2,2,128,128]{3,2,1,0:T(8,128)(2,1)}, bf16[2,2,128,128]{3,2,1,0:T(8,128)(2,1)S(1)}, u32[]{:S(2)}, u32[]{:S(2)}) %collective-permute-start.3) | collective-permute-done | bytes 131104 | tf_op jit(solution)/shard_map/ppermute | solution.py:974
  99.2 2.6 %shard_map.85 = bf16[16,2,2,64,128]{4,3,2,1,0:T(8,128)(2,1)} custom-call(bf16[2,2,128,128]{3,2,1,0:T(8,128)(2,1)} %copy-done.7, f32[2,2,128,128]{3,2,1,0:T(8,128)} %get-tuple-element.69.refs_1_, f32[2,2,1024,128]{3,2,1,0:T(8,128)} %get-tuple-element.70.refs_2_), custom_call_target="tpu_custom_call" | custom-call | flops 100000000 | bytes 3538944 | tf_op jit(solution)/shard_map/pallas_call | solution.py:423
  101.8 3.9 %all-to-all-start.3 = ((bf16[16,2,2,64,128]{4,3,2,1,0:T(8,128)(2,1)}), bf16[16,2,2,64,128]{4,3,2,1,0:T(8,128)(2,1)S(1)}, u32[]{:S(2)}, u32[]{:S(2)}) async-start(bf16[16,2,2,64,128]{4,3,2,1,0:T(8,128)(2,1)} %shard_map.85), calls=%async_computation.3 | async-start | bytes 2097152 | tf_op jit(solution)/shard_map/all_to_all | solution.py:970
  105.8 2.3 %shard_map.83 = (bf16[64,4096]{1,0:T(8,128)(2,1)}, bf16[64,4096]{1,0:T(8,128)(2,1)}) custom-call(s32[1]{0:T(128)} %bitcast.half_ref, bf16[16,2,2,64,128]{4,3,2,1,0:T(8,128)(2,1)} %all-to-all-done.2.packed_ref), custom_call_target="tpu_custom_call" | custom-call | bytes 2097152 | tf_op jit(solution)/shard_map/pallas_call | solution.py:510
  108.1 12.5 %all-to-all-done.3.packed_ref = bf16[16,2,2,64,128]{4,3,2,1,0:T(8,128)(2,1)S(1)} async-done(((bf16[16,2,2,64,128]{4,3,2,1,0:T(8,128)(2,1)}), bf16[16,2,2,64,128]{4,3,2,1,0:T(8,128)(2,1)S(1)}, u32[]{:S(2)}, u32[]{:S(2)}) %all-to-all-start.3) | async-done | bytes 1048608 | tf_op jit(solution)/shard_map/all_to_all | solution.py:970
  120.6 1.0 shard_map.86
  (22 shorter events, 3.4 us)
Async XLA Ops:
  2.8 21.1 %all-to-all-start = ((bf16[16,2,2,64,128]{4,3,2,1,0:T(8,128)(2,1)}), bf16[16,2,2,64,128]{4,3,2,1,0:T(8,128)(2,1)S(1)}, u32[]{:S(2)}, u32[]{:S(2)}) async-start(bf16[16,2,2,64,128]{4,3,2,1,0:T(8,128)(2,1)} %shard_map.75), calls=%async_computation | async-start | bytes 2097152 | tf_op jit(solution)/shard_map/all_to_all | solution.py:970
  23.9 8.7 %copy-start = (bf16[16,2,2,64,128]{4,3,2,1,0:T(8,128)(2,1)}, bf16[16,2,2,64,128]{4,3,2,1,0:T(8,128)(2,1)S(1)}, u32[]{:S(2)}) copy-start(bf16[16,2,2,64,128]{4,3,2,1,0:T(8,128)(2,1)S(1)} %all-to-all-done.qk_ref.refs_0_) | copy-start | bytes 3145732
  24.2 8.4 %copy-start.2 = (bf16[2,2,128,128]{3,2,1,0:T(8,128)(2,1)}, bf16[2,2,128,128]{3,2,1,0:T(8,128)(2,1)S(1)}, u32[]{:S(2)}) copy-start(bf16[2,2,128,128]{3,2,1,0:T(8,128)(2,1)S(1)} %shard_map.77.refs_1_) | copy-start | bytes 393220
  24.2 8.4 %collective-permute-start = (bf16[2,2,128,128]{3,2,1,0:T(8,128)(2,1)S(1)}, bf16[2,2,128,128]{3,2,1,0:T(8,128)(2,1)S(1)}, u32[]{:S(2)}, u32[]{:S(2)}) collective-permute-start(bf16[2,2,128,128]{3,2,1,0:T(8,128)(2,1)S(1)} %shard_map.77.refs_1_), channel_id=1, source_target_pairs={{0,16},{16,0},{1,17},{17,1},{2,18},{18,2},{3,19},{19,3},{4,20},{20... | collective-permute-start | bytes 393224 | tf_op jit(solution)/shard_map/ppermute | solution.py:974
  26.9 19.6 %all-to-all-start.1 = ((bf16[16,2,2,64,128]{4,3,2,1,0:T(8,128)(2,1)}), bf16[16,2,2,64,128]{4,3,2,1,0:T(8,128)(2,1)}, u32[]{:S(2)}, u32[]{:S(2)}) async-start(bf16[16,2,2,64,128]{4,3,2,1,0:T(8,128)(2,1)} %shard_map.76), calls=%async_computation.1 | async-start | bytes 2097152 | tf_op jit(solution)/shard_map/all_to_all | solution.py:970
  32.6 0.7 copy-start.8
  46.5 12.0 %copy-start.3 = (bf16[2,256,256]{2,1,0:T(8,128)(2,1)S(1)}, bf16[2,256,256]{2,1,0:T(8,128)(2,1)}, u32[]{:S(2)}) copy-start(bf16[2,256,256]{2,1,0:T(8,128)(2,1)} %get-tuple-element.48.inverse_ref) | copy-start | bytes 786436
  46.5 12.0 %copy-start.5 = (f32[8,256]{1,0:T(8,128)S(1)}, f32[8,256]{1,0:T(8,128)}, u32[]{:S(2)}) copy-start(f32[8,256]{1,0:T(8,128)} %get-tuple-element.43.refs_1_.stats_ref) | copy-start | bytes 24580
  50.0 8.5 %collective-permute-start.1 = (bf16[272,256]{1,0:T(8,128)(2,1)}, bf16[272,256]{1,0:T(8,128)(2,1)S(1)}, u32[]{:S(2)}, u32[]{:S(2)}) collective-permute-start(bf16[272,256]{1,0:T(8,128)(2,1)} %get-tuple-element.46), channel_id=1, source_target_pairs={{0,16},{16,0},{1,17},{17,1},{2,18},{18,2},{3,19},{19,3},{4,20},{20... | collective-permute-start | bytes 417800 | tf_op jit(solution)/shard_map/ppermute | solution.py:974
  58.5 1.0 copy-start.4
  59.8 0.8 copy-start.1
  60.6 8.1 %collective-permute-start.2 = (bf16[272,256]{1,0:T(8,128)(2,1)S(1)}, bf16[272,256]{1,0:T(8,128)(2,1)S(1)}, u32[]{:S(2)}, u32[]{:S(2)}) collective-permute-start(bf16[272,256]{1,0:T(8,128)(2,1)S(1)} %get-tuple-element.49), channel_id=1, source_target_pairs={{0,16},{16,0},{1,17},{17,1},{2,18},{18,2},{3,19},{19,3},{4,20},{20... | collective-permute-start | bytes 417800 | tf_op jit(solution)/shard_map/ppermute | solution.py:974
  68.7 0.7 copy-start.6
  72.5 29.4 %all-to-all-start.2 = ((bf16[16,2,2,64,128]{4,3,2,1,0:T(8,128)(2,1)}), bf16[16,2,2,64,128]{4,3,2,1,0:T(8,128)(2,1)}, u32[]{:S(2)}, u32[]{:S(2)}) async-start(bf16[16,2,2,64,128]{4,3,2,1,0:T(8,128)(2,1)} %shard_map.82.refs_15_), calls=%async_computation.2 | async-start | bytes 2097152 | tf_op jit(solution)/shard_map/all_to_all | solution.py:970
  88.8 9.7 %collective-permute-start.3 = (bf16[2,2,128,128]{3,2,1,0:T(8,128)(2,1)}, bf16[2,2,128,128]{3,2,1,0:T(8,128)(2,1)S(1)}, u32[]{:S(2)}, u32[]{:S(2)}) collective-permute-start(bf16[2,2,128,128]{3,2,1,0:T(8,128)(2,1)} %get-tuple-element.68), channel_id=1, source_target_pairs={{0,16},{16,0},{1,17},{17,1},{2,18},{18,2},{3,19},{19,3},{4,20},{20... | collective-permute-start | bytes 393224 | tf_op jit(solution)/shard_map/ppermute | solution.py:974
  98.6 0.7 copy-start.7
  101.8 18.8 %all-to-all-start.3 = ((bf16[16,2,2,64,128]{4,3,2,1,0:T(8,128)(2,1)}), bf16[16,2,2,64,128]{4,3,2,1,0:T(8,128)(2,1)S(1)}, u32[]{:S(2)}, u32[]{:S(2)}) async-start(bf16[16,2,2,64,128]{4,3,2,1,0:T(8,128)(2,1)} %shard_map.85), calls=%async_computation.3 | async-start | bytes 2097152 | tf_op jit(solution)/shard_map/all_to_all | solution.py:970

commit v14 on v13

--- a/solution.py
+++ b/solution.py
@@ -944,26 +944,44 @@
     put(outs.far)
 
 
-def finish_compute(ins, outs, need, put):
-    need(ins.near)
-    need(ins.got_far)
-    out_ref = outs.out
+def finish_kernel(far_ref, near_ref, direct_ref, home, out_ref, done):
+    tokens = tokens_of(out_ref)
     group = CHUNK // out_ref.shape[3]
-    segment_len = tokens_of(out_ref) // HALF
+    segment_len = tokens // HALF
     per = CHUNK // segment_len
-    for index in range(tokens_of(out_ref) // CHUNK):
+    writes = []
+    for index in range(tokens // CHUNK):
         place, start = slice(index * per, (index + 1) * per), index * CHUNK
         for slot in range(2):
             for kind in range(2):
-                if index % 2 == 0:
-                    need(ins.direct, slot, kind, start)
-                marks = ins.near[kind, slot, place] + ins.got_far[
-                    kind, 1 - slot, place
-                ].astype(jnp.float32)
+                marks = near_ref[kind, slot, place] + far_ref[kind, 1 - slot, place].astype(
+                    jnp.float32
+                )
                 spread = jnp.broadcast_to(marks[:, None], (per, segment_len, HD))
-                total = ins.direct[slot, kind, start : start + CHUNK] + spread.reshape(CHUNK, HD)
+                total = direct_ref[slot, kind, start : start + CHUNK] + spread.reshape(CHUNK, HD)
                 store_chunk(out_ref, (kind, slot), index, total.astype(jnp.bfloat16))
-        put(out_ref, index * group)
+        ends = pl.ds(index * group, group)
+        write = pltpu.make_async_copy(out_ref.at[ends], home.at[ends], done.at[index])
+        write.start()
+        writes.append(write)
+    for write in writes:
+        write.wait()
+
+
+def finished(shape, *operands):
+    held = pl.BlockSpec(memory_space=pltpu.VMEM)
+    return pl.pallas_call(
+        finish_kernel,
+        out_shape=shape,
+        in_specs=[held] * len(operands),
+        out_specs=pl.BlockSpec(memory_space=pl.ANY),
+        scratch_shapes=[
+            pltpu.VMEM(shape.shape, shape.dtype),
+            pltpu.SemaphoreType.DMA((shape.shape[0] * shape.shape[3] // CHUNK,)),
+        ],
+        compiler_params=pltpu.CompilerParams(vmem_limit_bytes=SMALL_LIMIT),
+        cost_estimate=pl.CostEstimate(flops=10**8, bytes_accessed=2**20, transcendentals=0),
+    )(*operands)
 
 
 def exchange(packed):
@@ -1081,12 +1099,7 @@
         LONG,
         after=(first_results,),
     )
-    results = staged_call(
-        finish_compute,
-        dict(got_far=partner(grads.far), near=grads.near, direct=(grads.direct, BLOCKS)),
-        dict(out=(low(*qk.shape), GROUPS)),
-        0.1,
-    ).out
+    results = finished(low(*qk.shape), partner(grads.far), grads.near, grads.direct)
     query_grad, key_grad = unpack(half, exchange(results))
     return attended, query_grad, key_grad, value_gradient_array
 

time: 122 us -> 123 us (level)
  local copies, waits for them, and re-layouts: 3.75 us -> 5.64 us
  Pallas kernels: 46 us -> 44.5 us
    pallas_call x6 -> x5, Pallas kernels: 37.7 us -> 35.1 us  [staged_call(): pl.pallas_call(kernel, out_shape=shapes, in_specs=[anywhere] * (n_in + n_...]
    unnamed x18 -> x20, local copies, waits for them, and re-layouts: 3.75 us -> 5.64 us
  transfers between devices with their start and end apart: 8 -> 8, of which waited for: 7 -> 7; matrix products, arithmetic and copies ran while one was open for 0% -> 0% of each run, Pallas kernels for 29% -> 28%
where the time goes in v14:
time: 123 us; the launch traced here: 122 us
  waiting for transfers between devices  46.5 us (38%)
  Pallas kernels  44.5 us (36%)
  starting transfers between devices  24.6 us (20%)
  local copies, waits for them, and re-layouts  5.64 us (5%)
    pallas_call x5, Pallas kernels, staged_call(): pl.pallas_call(kernel, out_shape=shapes, in_specs=[anywhere] * (n_in + n_...  35.1 us
    all_to_all x4, waiting for transfers between devices, exchange(): lax.all_to_all(packed, 'cube', split_axis=0, concat_axis=0, tiled=True)  28.1 us
    all_to_all x4, starting transfers between devices, exchange(): lax.all_to_all(packed, 'cube', split_axis=0, concat_axis=0, tiled=True)  20.1 us
    ppermute x4, waiting for transfers between devices, partner(): return lax.ppermute(array, 'half', SWAP)  18.4 us
    pallas_call x4, Pallas kernels, layout_call(): pl.pallas_call(kernel, out_shape=out_shape, in_specs=[pl.BlockSpec(memory...  7.65 us
    unnamed x20, local copies, waits for them, and re-layouts  5.64 us
    ppermute x4, starting transfers between devices, partner(): return lax.ppermute(array, 'half', SWAP)  4.57 us
  transfers between devices with their start and end apart: 8, of which 7 were waited for; matrix products, arithmetic and copies ran while one was open for 0% of the time, Pallas kernels for 28%

profile of v14, /device:TPU:0, one launch (start us, length us, event | category | flops | bytes accessed | tf_op | source)
XLA Modules:
  0.0 122.2 jit_solution(4374299185143204426)
XLA Ops:
  0.6 2.1 %shard_map.75 = bf16[16,2,2,64,128]{4,3,2,1,0:T(8,128)(2,1)} custom-call(s32[1]{0:T(128)} %bitcast.half_ref, bf16[64,4096]{1,0:T(8,128)(2,1)} %first_ref.2, bf16[64,4096]{1,0:T(8,128)(2,1)} %second_ref.2), custom_call_target="tpu_custom_call" | custom-call | bytes 2097152 | tf_op jit(solution)/shard_map/pallas_call | solution.py:510
  2.8 6.3 %all-to-all-start = ((bf16[16,2,2,64,128]{4,3,2,1,0:T(8,128)(2,1)}), bf16[16,2,2,64,128]{4,3,2,1,0:T(8,128)(2,1)S(1)}, u32[]{:S(2)}, u32[]{:S(2)}) async-start(bf16[16,2,2,64,128]{4,3,2,1,0:T(8,128)(2,1)} %shard_map.75), calls=%async_computation | async-start | bytes 2097152 | tf_op jit(solution)/shard_map/all_to_all | solution.py:988
  9.1 2.2 %shard_map.76 = bf16[16,2,2,64,128]{4,3,2,1,0:T(8,128)(2,1)} custom-call(s32[1]{0:T(128)} %bitcast.half_ref, bf16[64,4096]{1,0:T(8,128)(2,1)} %first_ref.3, bf16[64,4096]{1,0:T(8,128)(2,1)} %second_ref.3), custom_call_target="tpu_custom_call" | custom-call | bytes 2097152 | tf_op jit(solution)/shard_map/pallas_call | solution.py:510
  11.3 12.6 %all-to-all-done.qk_ref.refs_0_ = bf16[16,2,2,64,128]{4,3,2,1,0:T(8,128)(2,1)S(1)} async-done(((bf16[16,2,2,64,128]{4,3,2,1,0:T(8,128)(2,1)}), bf16[16,2,2,64,128]{4,3,2,1,0:T(8,128)(2,1)S(1)}, u32[]{:S(2)}, u32[]{:S(2)}) %all-to-all-start) | async-done | bytes 1048608 | tf_op jit(solution)/shard_map/all_to_all | solution.py:988
  24.2 2.7 %collective-permute-start = (bf16[2,2,128,128]{3,2,1,0:T(8,128)(2,1)S(1)}, bf16[2,2,128,128]{3,2,1,0:T(8,128)(2,1)S(1)}, u32[]{:S(2)}, u32[]{:S(2)}) collective-permute-start(bf16[2,2,128,128]{3,2,1,0:T(8,128)(2,1)S(1)} %shard_map.77.refs_1_), channel_id=1, source_target_pairs={{0,16},{16,0},{1,17},{17,1},{2,18},{18,2},{3,19},{19,3},{4,20},{20... | collective-permute-start | bytes 393224 | tf_op jit(solution)/shard_map/ppermute | solution.py:992
  26.9 4.3 %all-to-all-start.1 = ((bf16[16,2,2,64,128]{4,3,2,1,0:T(8,128)(2,1)}), bf16[16,2,2,64,128]{4,3,2,1,0:T(8,128)(2,1)}, u32[]{:S(2)}, u32[]{:S(2)}) async-start(bf16[16,2,2,64,128]{4,3,2,1,0:T(8,128)(2,1)} %shard_map.76), calls=%async_computation.1 | async-start | bytes 2097152 | tf_op jit(solution)/shard_map/all_to_all | solution.py:988
  31.2 1.4 %collective-permute-done.refs_2_ = bf16[2,2,128,128]{3,2,1,0:T(8,128)(2,1)S(1)} collective-permute-done((bf16[2,2,128,128]{3,2,1,0:T(8,128)(2,1)S(1)}, bf16[2,2,128,128]{3,2,1,0:T(8,128)(2,1)S(1)}, u32[]{:S(2)}, u32[]{:S(2)}) %collective-permute-start) | collective-permute-done | bytes 131104 | tf_op jit(solution)/shard_map/ppermute | solution.py:992
  33.3 10.3 %shard_map.78 = (bf16[2,2,256,128]{3,2,1,0:T(8,128)(2,1)}, f32[2,1024,256]{2,1,0:T(8,128)}, bf16[2,1024,256]{2,1,0:T(8,128)(2,1)}, f32[2,1024,256]{2,1,0:T(8,128...) custom-call(bf16[16,2,2,64,128]{4,3,2,1,0:T(8,128)(2,1)} %copy-done,, ...), custom_call_target="tpu_custom_call" | custom-call | flops 199999995904 | bytes 16003072 | tf_op jit(solution)/shard_map/pallas_call | solution.py:423
  43.5 2.9 %all-to-all-done.1.refs_0_.refs_7_ = bf16[16,2,2,64,128]{4,3,2,1,0:T(8,128)(2,1)} async-done(((bf16[16,2,2,64,128]{4,3,2,1,0:T(8,128)(2,1)}), bf16[16,2,2,64,128]{4,3,2,1,0:T(8,128)(2,1)}, u32[]{:S(2)}, u32[]{:S(2)}) %all-to-all-start.1) | async-done | bytes 1048608 | tf_op jit(solution)/shard_map/all_to_all | solution.py:988
  46.5 3.5 %shard_map.79 = (bf16[272,256]{1,0:T(8,128)(2,1)}, f32[256,256]{1,0:T(8,128)}) custom-call(bf16[16,2,2,64,128]{4,3,2,1,0:T(8,128)(2,1)} %all-to-all-done.1.refs_0_.refs_7_, f32[8,256]{1,0:T(8,128)} %get-tuple-element.43.refs_1_.stats_ref, bf16[2,1024,256]{2,1,0:T(8,128)(2,1)} %get-tuple-element.44.refs_2_, ...), custom_call_target="tpu_custom_call" | custom-call | flops 2000000000 | bytes 3555328 | tf_op jit(solution)/shard_map/pallas_call | solution.py:423
  50.0 8.4 %collective-permute-done.1.got_ref = bf16[272,256]{1,0:T(8,128)(2,1)S(1)} collective-permute-done((bf16[272,256]{1,0:T(8,128)(2,1)}, bf16[272,256]{1,0:T(8,128)(2,1)S(1)}, u32[]{:S(2)}, u32[]{:S(2)}) %collective-permute-start.1) | collective-permute-done | bytes 139296 | tf_op jit(solution)/shard_map/ppermute | solution.py:992
  58.5 0.9 copy-done.6
  60.6 7.4 %shard_map.81 = (bf16[16,2,64,128]{3,2,1,0:T(8,128)(2,1)}, f32[2,256,256]{2,1,0:T(8,128)}, bf16[2,256,256]{2,1,0:T(8,128)(2,1)}) custom-call(f32[256,256]{1,0:T(8,128)} %get-tuple-element.52.refs_0_.refs_13_, f32[8,128]{1,0:T(8,128)} %get-tuple-element.53.refs_1_.refs_14_, f32[520,256]{1,0:T(8,128)} %copy-done.2, ...), custom_call_target="tpu_custom_call" | custom-call | flops 8000000000 | bytes 8400896 | tf_op jit(solution)/shard_map/pallas_call | solution.py:423
  69.4 3.1 %shard_map.82.refs_15_ = bf16[16,2,2,64,128]{4,3,2,1,0:T(8,128)(2,1)} custom-call(bf16[272,256]{1,0:T(8,128)(2,1)} %copy-done.8, f32[520,256]{1,0:T(8,128)} %copy-done.2, bf16[2,1024,256]{2,1,0:T(8,128)(2,1)} %get-tuple-element.45.refs_3_.refs_2_, f32[2,1024,256]{2,1,0:T(8,128)} %get-tuple-element.51.refs_7_.refs_3_.refs_8_, ...), custom_call_target="tpu_custom_call" | custom-call | flops 1000000000 | bytes 5390336 | tf_op jit(solution)/shard_map/pallas_call | solution.py:423
  72.4 5.5 %all-to-all-start.2 = ((bf16[16,2,2,64,128]{4,3,2,1,0:T(8,128)(2,1)}), bf16[16,2,2,64,128]{4,3,2,1,0:T(8,128)(2,1)}, u32[]{:S(2)}, u32[]{:S(2)}) async-start(bf16[16,2,2,64,128]{4,3,2,1,0:T(8,128)(2,1)} %shard_map.82.refs_15_), calls=%async_computation.2 | async-start | bytes 2097152 | tf_op jit(solution)/shard_map/all_to_all | solution.py:988
  77.9 10.9 %shard_map.84 = (bf16[2,2,128,128]{3,2,1,0:T(8,128)(2,1)}, f32[2,2,128,128]{3,2,1,0:T(8,128)}, f32[2,2,1024,128]{3,2,1,0:T(8,128)}) custom-call(f32[2,256,256]{2,1,0:T(8,128)} %get-tuple-element.59.refs_0_, bf16[272,256]{1,0:T(8,128)(2,1)} %copy-done.8, f32[520,256]{1,0:T(8,128)} %copy-done.2, bf16[2,2,256,128]{3,2,1,0:T(8,128)(2,1)} %get-tuple-element.60.refs_3_, ...), custom_call_target="tpu_custom_call" | custom-call | flops 199999995904 | bytes 14176256 | tf_op jit(solution)/shard_map/pallas_call | solution.py:423
  88.8 1.8 %collective-permute-start.3 = (bf16[2,2,128,128]{3,2,1,0:T(8,128)(2,1)}, bf16[2,2,128,128]{3,2,1,0:T(8,128)(2,1)S(1)}, u32[]{:S(2)}, u32[]{:S(2)}) collective-permute-start(bf16[2,2,128,128]{3,2,1,0:T(8,128)(2,1)} %get-tuple-element.68), channel_id=1, source_target_pairs={{0,16},{16,0},{1,17},{17,1},{2,18},{18,2},{3,19},{19,3},{4,20},{20... | collective-permute-start | bytes 393224 | tf_op jit(solution)/shard_map/ppermute | solution.py:992
  90.6 7.9 %collective-permute-done.3.far_ref = bf16[2,2,128,128]{3,2,1,0:T(8,128)(2,1)S(1)} collective-permute-done((bf16[2,2,128,128]{3,2,1,0:T(8,128)(2,1)}, bf16[2,2,128,128]{3,2,1,0:T(8,128)(2,1)S(1)}, u32[]{:S(2)}, u32[]{:S(2)}) %collective-permute-start.3) | collective-permute-done | bytes 131104 | tf_op jit(solution)/shard_map/ppermute | solution.py:992
  98.5 1.6 %copy-done.1 = f32[2,2,1024,128]{3,2,1,0:T(8,128)S(1)} copy-done((f32[2,2,1024,128]{3,2,1,0:T(8,128)S(1)}, f32[2,2,1024,128]{3,2,1,0:T(8,128)}, u32[]{:S(2)}) %copy-start.1) | copy-done | bytes 2097176
  101.1 1.1 shard_map.85
  102.2 4.0 %all-to-all-start.3 = ((bf16[16,2,2,64,128]{4,3,2,1,0:T(8,128)(2,1)}), bf16[16,2,2,64,128]{4,3,2,1,0:T(8,128)(2,1)S(1)}, u32[]{:S(2)}, u32[]{:S(2)}) async-start(bf16[16,2,2,64,128]{4,3,2,1,0:T(8,128)(2,1)} %shard_map.85), calls=%async_computation.3 | async-start | bytes 2097152 | tf_op jit(solution)/shard_map/all_to_all | solution.py:988
  106.1 2.3 %shard_map.83 = (bf16[64,4096]{1,0:T(8,128)(2,1)}, bf16[64,4096]{1,0:T(8,128)(2,1)}) custom-call(s32[1]{0:T(128)} %bitcast.half_ref, bf16[16,2,2,64,128]{4,3,2,1,0:T(8,128)(2,1)} %all-to-all-done.2.packed_ref), custom_call_target="tpu_custom_call" | custom-call | bytes 2097152 | tf_op jit(solution)/shard_map/pallas_call | solution.py:510
  108.4 12.5 %all-to-all-done.3.packed_ref = bf16[16,2,2,64,128]{4,3,2,1,0:T(8,128)(2,1)S(1)} async-done(((bf16[16,2,2,64,128]{4,3,2,1,0:T(8,128)(2,1)}), bf16[16,2,2,64,128]{4,3,2,1,0:T(8,128)(2,1)S(1)}, u32[]{:S(2)}, u32[]{:S(2)}) %all-to-all-start.3) | async-done | bytes 1048608 | tf_op jit(solution)/shard_map/all_to_all | solution.py:988
  120.9 1.0 shard_map.86
  (24 shorter events, 4.5 us)
Async XLA Ops:
  2.8 21.1 %all-to-all-start = ((bf16[16,2,2,64,128]{4,3,2,1,0:T(8,128)(2,1)}), bf16[16,2,2,64,128]{4,3,2,1,0:T(8,128)(2,1)S(1)}, u32[]{:S(2)}, u32[]{:S(2)}) async-start(bf16[16,2,2,64,128]{4,3,2,1,0:T(8,128)(2,1)} %shard_map.75), calls=%async_computation | async-start | bytes 2097152 | tf_op jit(solution)/shard_map/all_to_all | solution.py:988
  23.9 8.7 %copy-start = (bf16[16,2,2,64,128]{4,3,2,1,0:T(8,128)(2,1)}, bf16[16,2,2,64,128]{4,3,2,1,0:T(8,128)(2,1)S(1)}, u32[]{:S(2)}) copy-start(bf16[16,2,2,64,128]{4,3,2,1,0:T(8,128)(2,1)S(1)} %all-to-all-done.qk_ref.refs_0_) | copy-start | bytes 3145732
  24.2 8.4 %copy-start.4 = (bf16[2,2,128,128]{3,2,1,0:T(8,128)(2,1)}, bf16[2,2,128,128]{3,2,1,0:T(8,128)(2,1)S(1)}, u32[]{:S(2)}) copy-start(bf16[2,2,128,128]{3,2,1,0:T(8,128)(2,1)S(1)} %shard_map.77.refs_1_) | copy-start | bytes 393220
  24.2 8.4 %collective-permute-start = (bf16[2,2,128,128]{3,2,1,0:T(8,128)(2,1)S(1)}, bf16[2,2,128,128]{3,2,1,0:T(8,128)(2,1)S(1)}, u32[]{:S(2)}, u32[]{:S(2)}) collective-permute-start(bf16[2,2,128,128]{3,2,1,0:T(8,128)(2,1)S(1)} %shard_map.77.refs_1_), channel_id=1, source_target_pairs={{0,16},{16,0},{1,17},{17,1},{2,18},{18,2},{3,19},{19,3},{4,20},{20... | collective-permute-start | bytes 393224 | tf_op jit(solution)/shard_map/ppermute | solution.py:992
  26.9 19.6 %all-to-all-start.1 = ((bf16[16,2,2,64,128]{4,3,2,1,0:T(8,128)(2,1)}), bf16[16,2,2,64,128]{4,3,2,1,0:T(8,128)(2,1)}, u32[]{:S(2)}, u32[]{:S(2)}) async-start(bf16[16,2,2,64,128]{4,3,2,1,0:T(8,128)(2,1)} %shard_map.76), calls=%async_computation.1 | async-start | bytes 2097152 | tf_op jit(solution)/shard_map/all_to_all | solution.py:988
  32.6 0.7 copy-start.9
  46.5 12.0 %copy-start.5 = (bf16[2,256,256]{2,1,0:T(8,128)(2,1)S(1)}, bf16[2,256,256]{2,1,0:T(8,128)(2,1)}, u32[]{:S(2)}) copy-start(bf16[2,256,256]{2,1,0:T(8,128)(2,1)} %get-tuple-element.48.inverse_ref) | copy-start | bytes 786436
  46.5 12.0 %copy-start.7 = (f32[8,256]{1,0:T(8,128)S(1)}, f32[8,256]{1,0:T(8,128)}, u32[]{:S(2)}) copy-start(f32[8,256]{1,0:T(8,128)} %get-tuple-element.43.refs_1_.stats_ref) | copy-start | bytes 24580
  50.0 8.5 %collective-permute-start.1 = (bf16[272,256]{1,0:T(8,128)(2,1)}, bf16[272,256]{1,0:T(8,128)(2,1)S(1)}, u32[]{:S(2)}, u32[]{:S(2)}) collective-permute-start(bf16[272,256]{1,0:T(8,128)(2,1)} %get-tuple-element.46), channel_id=1, source_target_pairs={{0,16},{16,0},{1,17},{17,1},{2,18},{18,2},{3,19},{19,3},{4,20},{20... | collective-permute-start | bytes 417800 | tf_op jit(solution)/shard_map/ppermute | solution.py:992
  58.5 1.0 copy-start.6
  59.8 0.8 copy-start.2
  60.6 8.1 %collective-permute-start.2 = (bf16[272,256]{1,0:T(8,128)(2,1)S(1)}, bf16[272,256]{1,0:T(8,128)(2,1)S(1)}, u32[]{:S(2)}, u32[]{:S(2)}) collective-permute-start(bf16[272,256]{1,0:T(8,128)(2,1)S(1)} %get-tuple-element.49), channel_id=1, source_target_pairs={{0,16},{16,0},{1,17},{17,1},{2,18},{18,2},{3,19},{19,3},{4,20},{20... | collective-permute-start | bytes 417800 | tf_op jit(solution)/shard_map/ppermute | solution.py:992
  68.7 0.7 copy-start.8
  72.4 29.7 %all-to-all-start.2 = ((bf16[16,2,2,64,128]{4,3,2,1,0:T(8,128)(2,1)}), bf16[16,2,2,64,128]{4,3,2,1,0:T(8,128)(2,1)}, u32[]{:S(2)}, u32[]{:S(2)}) async-start(bf16[16,2,2,64,128]{4,3,2,1,0:T(8,128)(2,1)} %shard_map.82.refs_15_), calls=%async_computation.2 | async-start | bytes 2097152 | tf_op jit(solution)/shard_map/all_to_all | solution.py:988
  88.8 9.7 %collective-permute-start.3 = (bf16[2,2,128,128]{3,2,1,0:T(8,128)(2,1)}, bf16[2,2,128,128]{3,2,1,0:T(8,128)(2,1)S(1)}, u32[]{:S(2)}, u32[]{:S(2)}) collective-permute-start(bf16[2,2,128,128]{3,2,1,0:T(8,128)(2,1)} %get-tuple-element.68), channel_id=1, source_target_pairs={{0,16},{16,0},{1,17},{17,1},{2,18},{18,2},{3,19},{19,3},{4,20},{20... | collective-permute-start | bytes 393224 | tf_op jit(solution)/shard_map/ppermute | solution.py:992
  98.5 1.6 %copy-start.1 = (f32[2,2,1024,128]{3,2,1,0:T(8,128)S(1)}, f32[2,2,1024,128]{3,2,1,0:T(8,128)}, u32[]{:S(2)}) copy-start(f32[2,2,1024,128]{3,2,1,0:T(8,128)} %get-tuple-element.70.direct_ref) | copy-start | bytes 6291460
  100.1 0.9 copy-start.3
  102.2 18.8 %all-to-all-start.3 = ((bf16[16,2,2,64,128]{4,3,2,1,0:T(8,128)(2,1)}), bf16[16,2,2,64,128]{4,3,2,1,0:T(8,128)(2,1)S(1)}, u32[]{:S(2)}, u32[]{:S(2)}) async-start(bf16[16,2,2,64,128]{4,3,2,1,0:T(8,128)(2,1)} %shard_map.85), calls=%async_computation.3 | async-start | bytes 2097152 | tf_op jit(solution)/shard_map/all_to_all | solution.py:988

commit v15 on v13

--- a/solution.py
+++ b/solution.py
@@ -19,6 +19,7 @@
 SMALL_LIMIT = 16 * 2**20
 WHOLE, LEAD, GROUPS, BLOCKS, LATE, LAST = range(6)
 SLOTS = (10, 11)
+TOP = 12
 LONG = 200
 EARLY_SWEEPS = PINV_ITERS // 2
 
@@ -318,6 +319,8 @@
 
 
 def held_shape(kind, shape):
+    if kind == TOP:
+        return (2 * HD + 8, *shape[1:])
     return shape[1:] if kind in SLOTS else shape
 
 
@@ -353,6 +356,7 @@
         steps = []
         for place, (kind, home, held) in enumerate(zip(kinds, outer, inner)):
             home = home.at[kind - SLOTS[0]] if kind in SLOTS else home
+            home = home.at[pl.ds(0, 2 * HD + 8)] if kind == TOP else home
             copies = {}
             for step, piece in enumerate(pieces_of(kind, held.shape)):
                 ends = (window(held, piece), window(home, piece))
@@ -361,7 +365,7 @@
                     part.start if isinstance(part, slice) else part for part in piece
                 )
                 copies[key] = pltpu.make_async_copy(source, target, done.at[count])
-                steps.append(({WHOLE: -1, LAST: 9}.get(kind, step), place, key))
+                steps.append(({WHOLE: -1, TOP: -1, LAST: 9}.get(kind, step), place, key))
                 count += 1
             self.copies.append(copies)
         self.inner = inner
@@ -894,8 +898,8 @@
         for unit in side
     ]
     sweeps = PINV_ITERS - EARLY_SWEEPS
-    span = -(-len(units) // (2 * sweeps))
-    work = iter([units[index : index + span] for index in range(0, len(units), span)])
+    span = -(-len(units) // (2 * sweeps - 1))
+    work = iter([()] + [units[index : index + span] for index in range(0, len(units), span)])
     saved = (ins.pair, ins.weight, ins.growth)
     state = (ins.state[0], ins.state[1])
 
@@ -909,16 +913,22 @@
     for sweep in range(sweeps):
         for ref in saved:
             need(ref, sweep)
+        if sweep == sweeps - 1:
+            need(ins.last_growth)
+            need(ins.inverse_grad)
+            need(ins.mark_prob)
+            direct_part = split_dot_nt(
+                (ins.last_growth[0], ins.last_growth[1]),
+                (ins.inverse_grad[0], ins.inverse_grad[1]),
+            )
+            mark_prob = ins.mark_prob[...]
+            mark_halves = halves(mark_prob)
         state = gradient_sweep(state, saved, sweep, beside, sweep == sweeps - 1)
     put(outs.direct)
     need()
     growth = state[1]
-    mark_prob = ins.mark_prob[...]
     mark_grad = ins.factor[0:1, 0:1] * (
-        split_dot_nt(
-            (ins.last_growth[0], ins.last_growth[1]), (ins.inverse_grad[0], ins.inverse_grad[1])
-        )
-        + split_dot(halves(growth + growth.T), halves(mark_prob))
+        direct_part + split_dot(halves(growth + growth.T), mark_halves)
     )
     mark_sgrad = mark_prob * (mark_grad - jnp.sum(mark_grad * mark_prob, axis=1, keepdims=True))
 
@@ -1045,7 +1055,7 @@
         other_out_compute,
         dict(
             got_share=got_share,
-            mix=mix,
+            mix=(mix, TOP),
             token_low=(kept.token_low, SLOTS[1]),
             key_exp=(kept.key_exp, SLOTS[1]),
             own_out=own.out,
@@ -1059,7 +1069,7 @@
         dict(
             state=own.state,
             got_share=got_share,
-            mix=mix,
+            mix=(mix, TOP),
             marks=kept.marks,
             pair=(kept.pair_b, LEAD),
             weight=(kept.weight_b, LEAD),

time: 122 us -> 122 us (level)
  no operation moved by 1% of the time
where the time goes in v15:
time: 122 us
  waiting for transfers between devices  46.5 us (38%)
  Pallas kernels  45.9 us (38%)
  starting transfers between devices  24.6 us (20%)
  local copies, waits for them, and re-layouts  3.75 us (3%)
    pallas_call x6, Pallas kernels, staged_call(): pl.pallas_call(kernel, out_shape=shapes, in_specs=[anywhere] * (n_in + n_...  37.6 us
    all_to_all x4, waiting for transfers between devices, exchange(): lax.all_to_all(packed, 'cube', split_axis=0, concat_axis=0, tiled=True)  28.1 us
    all_to_all x4, starting transfers between devices, exchange(): lax.all_to_all(packed, 'cube', split_axis=0, concat_axis=0, tiled=True)  20.1 us
    ppermute x4, waiting for transfers between devices, partner(): return lax.ppermute(array, 'half', SWAP)  18.4 us
    pallas_call x4, Pallas kernels, layout_call(): pl.pallas_call(kernel, out_shape=out_shape, in_specs=[pl.BlockSpec(memory...  7.65 us
    ppermute x4, starting transfers between devices, partner(): return lax.ppermute(array, 'half', SWAP)  4.55 us
    unnamed x18, local copies, waits for them, and re-layouts  3.75 us
  transfers between devices with their start and end apart: 8, of which 7 were waited for; matrix products, arithmetic and copies ran while one was open for 0% of the time, Pallas kernels for 29%

profile of v15, /device:TPU:0, one launch (start us, length us, event | category | flops | bytes accessed | tf_op | source)
XLA Modules:
  0.0 121.7 jit_solution(15613841177311538976)
XLA Ops:
  0.6 2.1 %shard_map.75 = bf16[16,2,2,64,128]{4,3,2,1,0:T(8,128)(2,1)} custom-call(s32[1]{0:T(128)} %bitcast.half_ref, bf16[64,4096]{1,0:T(8,128)(2,1)} %first_ref.2, bf16[64,4096]{1,0:T(8,128)(2,1)} %second_ref.2), custom_call_target="tpu_custom_call" | custom-call | bytes 2097152 | tf_op jit(solution)/shard_map/pallas_call | solution.py:514
  2.8 6.3 %all-to-all-start = ((bf16[16,2,2,64,128]{4,3,2,1,0:T(8,128)(2,1)}), bf16[16,2,2,64,128]{4,3,2,1,0:T(8,128)(2,1)S(1)}, u32[]{:S(2)}, u32[]{:S(2)}) async-start(bf16[16,2,2,64,128]{4,3,2,1,0:T(8,128)(2,1)} %shard_map.75), calls=%async_computation | async-start | bytes 2097152 | tf_op jit(solution)/shard_map/all_to_all | solution.py:980
  9.1 2.2 %shard_map.76 = bf16[16,2,2,64,128]{4,3,2,1,0:T(8,128)(2,1)} custom-call(s32[1]{0:T(128)} %bitcast.half_ref, bf16[64,4096]{1,0:T(8,128)(2,1)} %first_ref.3, bf16[64,4096]{1,0:T(8,128)(2,1)} %second_ref.3), custom_call_target="tpu_custom_call" | custom-call | bytes 2097152 | tf_op jit(solution)/shard_map/pallas_call | solution.py:514
  11.3 12.6 %all-to-all-done.qk_ref.refs_0_ = bf16[16,2,2,64,128]{4,3,2,1,0:T(8,128)(2,1)S(1)} async-done(((bf16[16,2,2,64,128]{4,3,2,1,0:T(8,128)(2,1)}), bf16[16,2,2,64,128]{4,3,2,1,0:T(8,128)(2,1)S(1)}, u32[]{:S(2)}, u32[]{:S(2)}) %all-to-all-start) | async-done | bytes 1048608 | tf_op jit(solution)/shard_map/all_to_all | solution.py:980
  24.2 2.7 %collective-permute-start = (bf16[2,2,128,128]{3,2,1,0:T(8,128)(2,1)S(1)}, bf16[2,2,128,128]{3,2,1,0:T(8,128)(2,1)S(1)}, u32[]{:S(2)}, u32[]{:S(2)}) collective-permute-start(bf16[2,2,128,128]{3,2,1,0:T(8,128)(2,1)S(1)} %shard_map.77.refs_1_), channel_id=1, source_target_pairs={{0,16},{16,0},{1,17},{17,1},{2,18},{18,2},{3,19},{19,3},{4,20},{20... | collective-permute-start | bytes 393224 | tf_op jit(solution)/shard_map/ppermute | solution.py:984
  26.9 4.3 %all-to-all-start.1 = ((bf16[16,2,2,64,128]{4,3,2,1,0:T(8,128)(2,1)}), bf16[16,2,2,64,128]{4,3,2,1,0:T(8,128)(2,1)}, u32[]{:S(2)}, u32[]{:S(2)}) async-start(bf16[16,2,2,64,128]{4,3,2,1,0:T(8,128)(2,1)} %shard_map.76), calls=%async_computation.1 | async-start | bytes 2097152 | tf_op jit(solution)/shard_map/all_to_all | solution.py:980
  31.2 1.4 %collective-permute-done.refs_2_ = bf16[2,2,128,128]{3,2,1,0:T(8,128)(2,1)S(1)} collective-permute-done((bf16[2,2,128,128]{3,2,1,0:T(8,128)(2,1)S(1)}, bf16[2,2,128,128]{3,2,1,0:T(8,128)(2,1)S(1)}, u32[]{:S(2)}, u32[]{:S(2)}) %collective-permute-start) | collective-permute-done | bytes 131104 | tf_op jit(solution)/shard_map/ppermute | solution.py:984
  33.3 10.3 %shard_map.78 = (bf16[2,2,256,128]{3,2,1,0:T(8,128)(2,1)}, f32[2,1024,256]{2,1,0:T(8,128)}, bf16[2,1024,256]{2,1,0:T(8,128)(2,1)}, f32[2,1024,256]{2,1,0:T(8,128...) custom-call(bf16[16,2,2,64,128]{4,3,2,1,0:T(8,128)(2,1)} %copy-done,, ...), custom_call_target="tpu_custom_call" | custom-call | flops 199999995904 | bytes 16003072 | tf_op jit(solution)/shard_map/pallas_call | solution.py:427
  43.6 2.9 %all-to-all-done.1.refs_0_.refs_7_ = bf16[16,2,2,64,128]{4,3,2,1,0:T(8,128)(2,1)} async-done(((bf16[16,2,2,64,128]{4,3,2,1,0:T(8,128)(2,1)}), bf16[16,2,2,64,128]{4,3,2,1,0:T(8,128)(2,1)}, u32[]{:S(2)}, u32[]{:S(2)}) %all-to-all-start.1) | async-done | bytes 1048608 | tf_op jit(solution)/shard_map/all_to_all | solution.py:980
  46.5 3.5 %shard_map.79 = (bf16[272,256]{1,0:T(8,128)(2,1)}, f32[256,256]{1,0:T(8,128)}) custom-call(bf16[16,2,2,64,128]{4,3,2,1,0:T(8,128)(2,1)} %all-to-all-done.1.refs_0_.refs_7_, f32[8,256]{1,0:T(8,128)} %get-tuple-element.43.refs_1_.stats_ref, bf16[2,1024,256]{2,1,0:T(8,128)(2,1)} %get-tuple-element.44.refs_2_, ...), custom_call_target="tpu_custom_call" | custom-call | flops 2000000000 | bytes 3555328 | tf_op jit(solution)/shard_map/pallas_call | solution.py:427
  50.0 8.5 %collective-permute-done.1.got_ref = bf16[272,256]{1,0:T(8,128)(2,1)S(1)} collective-permute-done((bf16[272,256]{1,0:T(8,128)(2,1)}, bf16[272,256]{1,0:T(8,128)(2,1)S(1)}, u32[]{:S(2)}, u32[]{:S(2)}) %collective-permute-start.1) | collective-permute-done | bytes 139296 | tf_op jit(solution)/shard_map/ppermute | solution.py:984
  58.5 0.9 copy-done.4
  59.8 0.8 copy-done.1
  60.6 7.4 %shard_map.81 = (bf16[16,2,64,128]{3,2,1,0:T(8,128)(2,1)}, f32[2,256,256]{2,1,0:T(8,128)}, bf16[2,256,256]{2,1,0:T(8,128)(2,1)}) custom-call(f32[256,256]{1,0:T(8,128)} %get-tuple-element.52.refs_0_.refs_13_, f32[8,128]{1,0:T(8,128)} %get-tuple-element.53.refs_1_.refs_14_, f32[520,256]{1,0:T(8,128)} %copy-done.1, ...), custom_call_target="tpu_custom_call" | custom-call | flops 8000000000 | bytes 8400896 | tf_op jit(solution)/shard_map/pallas_call | solution.py:427
  69.4 3.0 %shard_map.82.refs_15_ = bf16[16,2,2,64,128]{4,3,2,1,0:T(8,128)(2,1)} custom-call(bf16[272,256]{1,0:T(8,128)(2,1)} %copy-done.6, f32[520,256]{1,0:T(8,128)} %copy-done.1, bf16[2,1024,256]{2,1,0:T(8,128)(2,1)} %get-tuple-element.45.refs_3_.refs_2_, f32[2,1024,256]{2,1,0:T(8,128)} %get-tuple-element.51.refs_7_.refs_3_.refs_8_, ...), custom_call_target="tpu_custom_call" | custom-call | flops 1000000000 | bytes 5390336 | tf_op jit(solution)/shard_map/pallas_call | solution.py:427
  72.4 5.5 %all-to-all-start.2 = ((bf16[16,2,2,64,128]{4,3,2,1,0:T(8,128)(2,1)}), bf16[16,2,2,64,128]{4,3,2,1,0:T(8,128)(2,1)}, u32[]{:S(2)}, u32[]{:S(2)}) async-start(bf16[16,2,2,64,128]{4,3,2,1,0:T(8,128)(2,1)} %shard_map.82.refs_15_), calls=%async_computation.2 | async-start | bytes 2097152 | tf_op jit(solution)/shard_map/all_to_all | solution.py:980
  77.9 10.8 %shard_map.84 = (bf16[2,2,128,128]{3,2,1,0:T(8,128)(2,1)}, f32[2,2,128,128]{3,2,1,0:T(8,128)}, f32[2,2,1024,128]{3,2,1,0:T(8,128)}) custom-call(f32[2,256,256]{2,1,0:T(8,128)} %get-tuple-element.59.refs_0_, bf16[272,256]{1,0:T(8,128)(2,1)} %copy-done.6, f32[520,256]{1,0:T(8,128)} %copy-done.1, bf16[2,2,256,128]{3,2,1,0:T(8,128)(2,1)} %get-tuple-element.60.refs_3_, ...), custom_call_target="tpu_custom_call" | custom-call | flops 199999995904 | bytes 14176256 | tf_op jit(solution)/shard_map/pallas_call | solution.py:427
  88.7 1.8 %collective-permute-start.3 = (bf16[2,2,128,128]{3,2,1,0:T(8,128)(2,1)}, bf16[2,2,128,128]{3,2,1,0:T(8,128)(2,1)S(1)}, u32[]{:S(2)}, u32[]{:S(2)}) collective-permute-start(bf16[2,2,128,128]{3,2,1,0:T(8,128)(2,1)} %get-tuple-element.68), channel_id=1, source_target_pairs={{0,16},{16,0},{1,17},{17,1},{2,18},{18,2},{3,19},{19,3},{4,20},{20... | collective-permute-start | bytes 393224 | tf_op jit(solution)/shard_map/ppermute | solution.py:984
  90.5 7.9 %collective-permute-done.3.refs_0_ = bf16[2,2,128,128]{3,2,1,0:T(8,128)(2,1)S(1)} collective-permute-done((bf16[2,2,128,128]{3,2,1,0:T(8,128)(2,1)}, bf16[2,2,128,128]{3,2,1,0:T(8,128)(2,1)S(1)}, u32[]{:S(2)}, u32[]{:S(2)}) %collective-permute-start.3) | collective-permute-done | bytes 131104 | tf_op jit(solution)/shard_map/ppermute | solution.py:984
  99.1 2.6 %shard_map.85 = bf16[16,2,2,64,128]{4,3,2,1,0:T(8,128)(2,1)} custom-call(bf16[2,2,128,128]{3,2,1,0:T(8,128)(2,1)} %copy-done.7, f32[2,2,128,128]{3,2,1,0:T(8,128)} %get-tuple-element.69.refs_1_, f32[2,2,1024,128]{3,2,1,0:T(8,128)} %get-tuple-element.70.refs_2_), custom_call_target="tpu_custom_call" | custom-call | flops 100000000 | bytes 3538944 | tf_op jit(solution)/shard_map/pallas_call | solution.py:427
  101.7 4.0 %all-to-all-start.3 = ((bf16[16,2,2,64,128]{4,3,2,1,0:T(8,128)(2,1)}), bf16[16,2,2,64,128]{4,3,2,1,0:T(8,128)(2,1)S(1)}, u32[]{:S(2)}, u32[]{:S(2)}) async-start(bf16[16,2,2,64,128]{4,3,2,1,0:T(8,128)(2,1)} %shard_map.85), calls=%async_computation.3 | async-start | bytes 2097152 | tf_op jit(solution)/shard_map/all_to_all | solution.py:980
  105.7 2.3 %shard_map.83 = (bf16[64,4096]{1,0:T(8,128)(2,1)}, bf16[64,4096]{1,0:T(8,128)(2,1)}) custom-call(s32[1]{0:T(128)} %bitcast.half_ref, bf16[16,2,2,64,128]{4,3,2,1,0:T(8,128)(2,1)} %all-to-all-done.2.packed_ref), custom_call_target="tpu_custom_call" | custom-call | bytes 2097152 | tf_op jit(solution)/shard_map/pallas_call | solution.py:514
  108.0 12.5 %all-to-all-done.3.packed_ref = bf16[16,2,2,64,128]{4,3,2,1,0:T(8,128)(2,1)S(1)} async-done(((bf16[16,2,2,64,128]{4,3,2,1,0:T(8,128)(2,1)}), bf16[16,2,2,64,128]{4,3,2,1,0:T(8,128)(2,1)S(1)}, u32[]{:S(2)}, u32[]{:S(2)}) %all-to-all-start.3) | async-done | bytes 1048608 | tf_op jit(solution)/shard_map/all_to_all | solution.py:980
  120.5 1.0 shard_map.86
  (22 shorter events, 3.4 us)
Async XLA Ops:
  2.8 21.1 %all-to-all-start = ((bf16[16,2,2,64,128]{4,3,2,1,0:T(8,128)(2,1)}), bf16[16,2,2,64,128]{4,3,2,1,0:T(8,128)(2,1)S(1)}, u32[]{:S(2)}, u32[]{:S(2)}) async-start(bf16[16,2,2,64,128]{4,3,2,1,0:T(8,128)(2,1)} %shard_map.75), calls=%async_computation | async-start | bytes 2097152 | tf_op jit(solution)/shard_map/all_to_all | solution.py:980
  23.9 8.7 %copy-start = (bf16[16,2,2,64,128]{4,3,2,1,0:T(8,128)(2,1)}, bf16[16,2,2,64,128]{4,3,2,1,0:T(8,128)(2,1)S(1)}, u32[]{:S(2)}) copy-start(bf16[16,2,2,64,128]{4,3,2,1,0:T(8,128)(2,1)S(1)} %all-to-all-done.qk_ref.refs_0_) | copy-start | bytes 3145732
  24.2 8.4 %copy-start.2 = (bf16[2,2,128,128]{3,2,1,0:T(8,128)(2,1)}, bf16[2,2,128,128]{3,2,1,0:T(8,128)(2,1)S(1)}, u32[]{:S(2)}) copy-start(bf16[2,2,128,128]{3,2,1,0:T(8,128)(2,1)S(1)} %shard_map.77.refs_1_) | copy-start | bytes 393220
  24.2 8.4 %collective-permute-start = (bf16[2,2,128,128]{3,2,1,0:T(8,128)(2,1)S(1)}, bf16[2,2,128,128]{3,2,1,0:T(8,128)(2,1)S(1)}, u32[]{:S(2)}, u32[]{:S(2)}) collective-permute-start(bf16[2,2,128,128]{3,2,1,0:T(8,128)(2,1)S(1)} %shard_map.77.refs_1_), channel_id=1, source_target_pairs={{0,16},{16,0},{1,17},{17,1},{2,18},{18,2},{3,19},{19,3},{4,20},{20... | collective-permute-start | bytes 393224 | tf_op jit(solution)/shard_map/ppermute | solution.py:984
  26.9 19.6 %all-to-all-start.1 = ((bf16[16,2,2,64,128]{4,3,2,1,0:T(8,128)(2,1)}), bf16[16,2,2,64,128]{4,3,2,1,0:T(8,128)(2,1)}, u32[]{:S(2)}, u32[]{:S(2)}) async-start(bf16[16,2,2,64,128]{4,3,2,1,0:T(8,128)(2,1)} %shard_map.76), calls=%async_computation.1 | async-start | bytes 2097152 | tf_op jit(solution)/shard_map/all_to_all | solution.py:980
  32.6 0.7 copy-start.8
  46.5 12.0 %copy-start.3 = (bf16[2,256,256]{2,1,0:T(8,128)(2,1)S(1)}, bf16[2,256,256]{2,1,0:T(8,128)(2,1)}, u32[]{:S(2)}) copy-start(bf16[2,256,256]{2,1,0:T(8,128)(2,1)} %get-tuple-element.48.inverse_ref) | copy-start | bytes 786436
  46.5 12.0 %copy-start.5 = (f32[8,256]{1,0:T(8,128)S(1)}, f32[8,256]{1,0:T(8,128)}, u32[]{:S(2)}) copy-start(f32[8,256]{1,0:T(8,128)} %get-tuple-element.43.refs_1_.stats_ref) | copy-start | bytes 24580
  50.0 8.5 %collective-permute-start.1 = (bf16[272,256]{1,0:T(8,128)(2,1)}, bf16[272,256]{1,0:T(8,128)(2,1)S(1)}, u32[]{:S(2)}, u32[]{:S(2)}) collective-permute-start(bf16[272,256]{1,0:T(8,128)(2,1)} %get-tuple-element.46), channel_id=1, source_target_pairs={{0,16},{16,0},{1,17},{17,1},{2,18},{18,2},{3,19},{19,3},{4,20},{20... | collective-permute-start | bytes 417800 | tf_op jit(solution)/shard_map/ppermute | solution.py:984
  58.5 1.0 copy-start.4
  59.8 0.8 copy-start.1
  60.6 8.1 %collective-permute-start.2 = (bf16[272,256]{1,0:T(8,128)(2,1)S(1)}, bf16[272,256]{1,0:T(8,128)(2,1)S(1)}, u32[]{:S(2)}, u32[]{:S(2)}) collective-permute-start(bf16[272,256]{1,0:T(8,128)(2,1)S(1)} %get-tuple-element.49), channel_id=1, source_target_pairs={{0,16},{16,0},{1,17},{17,1},{2,18},{18,2},{3,19},{19,3},{4,20},{20... | collective-permute-start | bytes 417800 | tf_op jit(solution)/shard_map/ppermute | solution.py:984
  68.7 0.7 copy-start.6
  72.4 29.3 %all-to-all-start.2 = ((bf16[16,2,2,64,128]{4,3,2,1,0:T(8,128)(2,1)}), bf16[16,2,2,64,128]{4,3,2,1,0:T(8,128)(2,1)}, u32[]{:S(2)}, u32[]{:S(2)}) async-start(bf16[16,2,2,64,128]{4,3,2,1,0:T(8,128)(2,1)} %shard_map.82.refs_15_), calls=%async_computation.2 | async-start | bytes 2097152 | tf_op jit(solution)/shard_map/all_to_all | solution.py:980
  88.7 9.7 %collective-permute-start.3 = (bf16[2,2,128,128]{3,2,1,0:T(8,128)(2,1)}, bf16[2,2,128,128]{3,2,1,0:T(8,128)(2,1)S(1)}, u32[]{:S(2)}, u32[]{:S(2)}) collective-permute-start(bf16[2,2,128,128]{3,2,1,0:T(8,128)(2,1)} %get-tuple-element.68), channel_id=1, source_target_pairs={{0,16},{16,0},{1,17},{17,1},{2,18},{18,2},{3,19},{19,3},{4,20},{20... | collective-permute-start | bytes 393224 | tf_op jit(solution)/shard_map/ppermute | solution.py:984
  98.4 0.7 copy-start.7
  101.7 18.8 %all-to-all-start.3 = ((bf16[16,2,2,64,128]{4,3,2,1,0:T(8,128)(2,1)}), bf16[16,2,2,64,128]{4,3,2,1,0:T(8,128)(2,1)S(1)}, u32[]{:S(2)}, u32[]{:S(2)}) async-start(bf16[16,2,2,64,128]{4,3,2,1,0:T(8,128)(2,1)} %shard_map.85), calls=%async_computation.3 | async-start | bytes 2097152 | tf_op jit(solution)/shard_map/all_to_all | solution.py:980

commit v16 on v15

--- a/solution.py
+++ b/solution.py
@@ -20,6 +20,7 @@
 WHOLE, LEAD, GROUPS, BLOCKS, LATE, LAST = range(6)
 SLOTS = (10, 11)
 TOP = 12
+SIDES = (20, 21)
 LONG = 200
 EARLY_SWEEPS = PINV_ITERS // 2
 
@@ -321,6 +322,8 @@
 def held_shape(kind, shape):
     if kind == TOP:
         return (2 * HD + 8, *shape[1:])
+    if kind in SIDES:
+        return (shape[0], *shape[2:])
     return shape[1:] if kind in SLOTS else shape
 
 
@@ -357,6 +360,7 @@
         for place, (kind, home, held) in enumerate(zip(kinds, outer, inner)):
             home = home.at[kind - SLOTS[0]] if kind in SLOTS else home
             home = home.at[pl.ds(0, 2 * HD + 8)] if kind == TOP else home
+            home = home.at[:, kind - SIDES[0]] if kind in SIDES else home
             copies = {}
             for step, piece in enumerate(pieces_of(kind, held.shape)):
                 ends = (window(held, piece), window(home, piece))
@@ -688,24 +692,28 @@
 
 
 def partial_compute(ins, outs, need, put):
-    need(ins.vg)
-    turned = [[all_tokens(ins.vg, array, slot).T for array in range(2)] for slot in range(2)]
+    need(ins.rows)
+    heads, _, rows, _ = ins.rows.shape
+    turned = [ins.rows[:, slot].reshape(heads * rows, HD).T for slot in range(2)]
+    for slot, home in enumerate((outs.keep, outs.send)):
+        need(ins.lowered, slot)
+        home[0:HD] = wide_dot(turned[slot], ins.lowered[slot]).astype(home.dtype)
+
+
+def stats_partial_compute(ins, outs, need, put):
+    partial_compute(ins, outs, need, put)
     need(ins.stats)
     rows = thirds(ins.stats[0:4])
-    outs.send[2 * HD :] = jnp.concatenate([rows, jnp.zeros((4, M), jnp.float32)], axis=0).astype(
+    outs.send[HD:] = jnp.concatenate([rows, jnp.zeros((4, M), jnp.float32)], axis=0).astype(
         jnp.bfloat16
     )
-    for slot, home in enumerate((outs.keep, outs.send)):
-        need(ins.key_low, slot)
-        home[0:HD] = wide_dot(turned[slot][0], ins.key_low[slot]).astype(home.dtype)
-        need(ins.token_low, slot)
-        home[HD : 2 * HD] = wide_dot(turned[slot][1], ins.token_low[slot]).astype(home.dtype)
-        put(home)
-
-
-def mixing_kernel(got_ref, keep_ref, stats_ref, inverse_ref, share_ref, mix_ref):
+
+
+def mixing_kernel(
+    got_ref, got_grad_ref, keep_ref, keep_grad_ref, stats_ref, inverse_ref, share_ref, mix_ref
+):
     got = got_ref[...].astype(jnp.float32)
-    others = swap_lanes(joined_thirds(got[2 * HD : 2 * HD + 12]))
+    others = swap_lanes(joined_thirds(got[HD : HD + 12]))
     scales = []
     for slot in range(2):
         own, other = 2 * slot, 2 * (1 - slot)
@@ -715,8 +723,8 @@
         own_factor, other_factor = jnp.exp(own_max - key_max), jnp.exp(other_max - key_max)
         inverse_total = 1.0 / (own_total * own_factor + other_total * other_factor)
         scales.append((own_factor * inverse_total, other_factor * inverse_total))
-    landmark_values = keep_ref[0:HD] * scales[0][0] + swap_lanes(got[0:HD]) * scales[0][1]
-    mixing_grad = keep_ref[HD : 2 * HD] + swap_lanes(got[HD : 2 * HD])
+    landmark_values = keep_ref[...] * scales[0][0] + swap_lanes(got[0:HD]) * scales[0][1]
+    mixing_grad = keep_grad_ref[...] + swap_lanes(got_grad_ref[...].astype(jnp.float32))
     inverse = (inverse_ref[0], inverse_ref[1])
     mixing_low = split_dot_nt(halves(landmark_values), inverse).astype(jnp.bfloat16)
     values_low = split_dot(halves(mixing_grad), inverse).astype(jnp.bfloat16)
@@ -1020,17 +1028,22 @@
         extra=(pltpu.VMEM((M, M), jnp.float32), pltpu.VMEM((2 * M, M), jnp.float32)),
     )
     sums = staged_call(
+        stats_partial_compute,
+        dict(rows=(vg, SIDES[0]), lowered=(kept.key_low, LEAD), stats=kept.stats),
+        dict(send=low(HD + 16, M), keep=wide(HD, M)),
+        1,
+    )
+    got = partner(sums.send)
+    grad_sums = staged_call(
         partial_compute,
-        dict(
-            vg=vg,
-            stats=kept.stats,
-            key_low=(kept.key_low, LEAD),
-            token_low=(kept.token_low, LEAD),
-        ),
-        dict(send=low(2 * HD + 16, M), keep=wide(2 * HD, M)),
-        2,
-    )
-    share, mix = joined_sums(partner(sums.send), sums.keep, kept.stats, kept.inverse)
+        dict(rows=(vg, SIDES[1]), lowered=(kept.token_low, LEAD)),
+        dict(send=low(HD, M), keep=wide(HD, M)),
+        1,
+        after=(sums.keep,),
+    )
+    share, mix = joined_sums(
+        got, partner(grad_sums.send), sums.keep, grad_sums.keep, kept.stats, kept.inverse
+    )
     got_share = partner(share)
     own = staged_call(
         own_gradient_compute,

time: 122 us -> 122 us (level)
  waiting for transfers between devices: 46.5 us -> 41.1 us
  starting transfers between devices: 24.6 us -> 28.1 us
  Pallas kernels: 45.9 us -> 47.5 us
    ppermute x4 -> x5, waiting for transfers between devices: 18.4 us -> 13 us  [partner(): return lax.ppermute(array, 'half', SWAP)]
    ppermute x4 -> x5, starting transfers between devices: 4.55 us -> 8.97 us  [partner(): return lax.ppermute(array, 'half', SWAP)]
    pallas_call x6 -> x7, Pallas kernels: 37.6 us -> 39.3 us  [staged_call(): pl.pallas_call(kernel, out_shape=shapes, in_specs=[anywhere] * (n_in + n_...]
    unnamed x18 -> x20, local copies, waits for them, and re-layouts: 3.75 us -> 3.66 us
  transfers between devices with their start and end apart: 8 -> 9, of which waited for: 7 -> 6; matrix products, arithmetic and copies ran while one was open for 0% -> 0% of each run, Pallas kernels for 29% -> 31%
where the time goes in v16:
time: 122 us; the launch traced here: 121 us
  Pallas kernels  47.5 us (39%)
  waiting for transfers between devices  41.1 us (34%)
  starting transfers between devices  28.1 us (23%)
  local copies, waits for them, and re-layouts  3.66 us (3%)
    pallas_call x7, Pallas kernels, staged_call(): pl.pallas_call(kernel, out_shape=shapes, in_specs=[anywhere] * (n_in + n_...  39.3 us
    all_to_all x4, waiting for transfers between devices, exchange(): lax.all_to_all(packed, 'cube', split_axis=0, concat_axis=0, tiled=True)  28.1 us
    all_to_all x4, starting transfers between devices, exchange(): lax.all_to_all(packed, 'cube', split_axis=0, concat_axis=0, tiled=True)  19.1 us
    ppermute x5, waiting for transfers between devices, partner(): return lax.ppermute(array, 'half', SWAP)  13 us
    ppermute x5, starting transfers between devices, partner(): return lax.ppermute(array, 'half', SWAP)  8.97 us
    pallas_call x4, Pallas kernels, layout_call(): pl.pallas_call(kernel, out_shape=out_shape, in_specs=[pl.BlockSpec(memory...  7.61 us
    unnamed x20, local copies, waits for them, and re-layouts  3.66 us
  transfers between devices with their start and end apart: 9, of which 6 were waited for; matrix products, arithmetic and copies ran while one was open for 0% of the time, Pallas kernels for 31%

profile of v16, /device:TPU:0, one launch (start us, length us, event | category | flops | bytes accessed | tf_op | source)
XLA Modules:
  0.0 121.4 jit_solution(6768754979149669298)
XLA Ops:
  0.6 2.1 %shard_map.75 = bf16[16,2,2,64,128]{4,3,2,1,0:T(8,128)(2,1)} custom-call(s32[1]{0:T(128)} %bitcast.half_ref, bf16[64,4096]{1,0:T(8,128)(2,1)} %first_ref.2, bf16[64,4096]{1,0:T(8,128)(2,1)} %second_ref.2), custom_call_target="tpu_custom_call" | custom-call | bytes 2097152 | tf_op jit(solution)/shard_map/pallas_call | solution.py:518
  2.8 6.3 %all-to-all-start = ((bf16[16,2,2,64,128]{4,3,2,1,0:T(8,128)(2,1)}), bf16[16,2,2,64,128]{4,3,2,1,0:T(8,128)(2,1)S(1)}, u32[]{:S(2)}, u32[]{:S(2)}) async-start(bf16[16,2,2,64,128]{4,3,2,1,0:T(8,128)(2,1)} %shard_map.75), calls=%async_computation | async-start | bytes 2097152 | tf_op jit(solution)/shard_map/all_to_all | solution.py:988
  9.1 2.1 %shard_map.76 = bf16[16,2,2,64,128]{4,3,2,1,0:T(8,128)(2,1)} custom-call(s32[1]{0:T(128)} %bitcast.half_ref, bf16[64,4096]{1,0:T(8,128)(2,1)} %first_ref.3, bf16[64,4096]{1,0:T(8,128)(2,1)} %second_ref.3), custom_call_target="tpu_custom_call" | custom-call | bytes 2097152 | tf_op jit(solution)/shard_map/pallas_call | solution.py:518
  11.2 12.7 %all-to-all-done.qk_ref.refs_0_ = bf16[16,2,2,64,128]{4,3,2,1,0:T(8,128)(2,1)S(1)} async-done(((bf16[16,2,2,64,128]{4,3,2,1,0:T(8,128)(2,1)}), bf16[16,2,2,64,128]{4,3,2,1,0:T(8,128)(2,1)S(1)}, u32[]{:S(2)}, u32[]{:S(2)}) %all-to-all-start) | async-done | bytes 1048608 | tf_op jit(solution)/shard_map/all_to_all | solution.py:988
  24.2 2.7 %collective-permute-start = (bf16[2,2,128,128]{3,2,1,0:T(8,128)(2,1)S(1)}, bf16[2,2,128,128]{3,2,1,0:T(8,128)(2,1)S(1)}, u32[]{:S(2)}, u32[]{:S(2)}) collective-permute-start(bf16[2,2,128,128]{3,2,1,0:T(8,128)(2,1)S(1)} %shard_map.77.refs_1_), channel_id=1, source_target_pairs={{0,16},{16,0},{1,17},{17,1},{2,18},{18,2},{3,19},{19,3},{4,20},{20... | collective-permute-start | bytes 393224 | tf_op jit(solution)/shard_map/ppermute | solution.py:992
  26.9 4.3 %all-to-all-start.1 = ((bf16[16,2,2,64,128]{4,3,2,1,0:T(8,128)(2,1)}), bf16[16,2,2,64,128]{4,3,2,1,0:T(8,128)(2,1)}, u32[]{:S(2)}, u32[]{:S(2)}) async-start(bf16[16,2,2,64,128]{4,3,2,1,0:T(8,128)(2,1)} %shard_map.76), calls=%async_computation.1 | async-start | bytes 2097152 | tf_op jit(solution)/shard_map/all_to_all | solution.py:988
  31.2 1.4 %collective-permute-done.refs_2_ = bf16[2,2,128,128]{3,2,1,0:T(8,128)(2,1)S(1)} collective-permute-done((bf16[2,2,128,128]{3,2,1,0:T(8,128)(2,1)S(1)}, bf16[2,2,128,128]{3,2,1,0:T(8,128)(2,1)S(1)}, u32[]{:S(2)}, u32[]{:S(2)}) %collective-permute-start) | collective-permute-done | bytes 131104 | tf_op jit(solution)/shard_map/ppermute | solution.py:992
  33.3 10.3 %shard_map.78 = (bf16[2,2,256,128]{3,2,1,0:T(8,128)(2,1)}, f32[2,1024,256]{2,1,0:T(8,128)}, bf16[2,1024,256]{2,1,0:T(8,128)(2,1)}, f32[2,1024,256]{2,1,0:T(8,128...) custom-call(bf16[16,2,2,64,128]{4,3,2,1,0:T(8,128)(2,1)} %copy-done,, ...), custom_call_target="tpu_custom_call" | custom-call | flops 199999995904 | bytes 16003072 | tf_op jit(solution)/shard_map/pallas_call | solution.py:431
  43.5 2.9 %all-to-all-done.1.refs_0_.refs_7_ = bf16[16,2,2,64,128]{4,3,2,1,0:T(8,128)(2,1)} async-done(((bf16[16,2,2,64,128]{4,3,2,1,0:T(8,128)(2,1)}), bf16[16,2,2,64,128]{4,3,2,1,0:T(8,128)(2,1)}, u32[]{:S(2)}, u32[]{:S(2)}) %all-to-all-start.1) | async-done | bytes 1048608 | tf_op jit(solution)/shard_map/all_to_all | solution.py:988
  46.5 2.6 %shard_map.79 = (bf16[144,256]{1,0:T(8,128)(2,1)}, f32[128,256]{1,0:T(8,128)}) custom-call(bf16[16,2,2,64,128]{4,3,2,1,0:T(8,128)(2,1)} %all-to-all-done.1.refs_0_.refs_7_, bf16[2,1024,256]{2,1,0:T(8,128)(2,1)} %get-tuple-element.45.refs_1_, f32[8,256]{1,0:T(8,128)} %get-tuple-element.46.refs_2_.stats_ref), custom_call_target="tpu_custom_call" | custom-call | flops 1000000000 | bytes 2310144 | tf_op jit(solution)/shard_map/pallas_call | solution.py:431
  49.1 2.6 %shard_map.80 = (bf16[128,256]{1,0:T(8,128)(2,1)}, f32[128,256]{1,0:T(8,128)}) custom-call(bf16[16,2,2,64,128]{4,3,2,1,0:T(8,128)(2,1)} %all-to-all-done.1.refs_0_.refs_7_, bf16[2,1024,256]{2,1,0:T(8,128)(2,1)} %get-tuple-element.48.refs_1_.refs_3_.refs_2_, f32[128,256]{1,0:T(8,128)} %get-tuple-element.49.refs_2_.keep_ref), custom_call_target="tpu_custom_call" | custom-call | flops 1000000000 | bytes 2293760 | tf_op jit(solution)/shard_map/pallas_call | solution.py:431
  51.7 2.9 %collective-permute-start.2 = (bf16[128,256]{1,0:T(8,128)(2,1)}, bf16[128,256]{1,0:T(8,128)(2,1)S(1)}, u32[]{:S(2)}, u32[]{:S(2)}) collective-permute-start(bf16[128,256]{1,0:T(8,128)(2,1)} %get-tuple-element.50), channel_id=1, source_target_pairs={{0,16},{16,0},{1,17},{17,1},{2,18},{18,2},{3,19},{19,3},{4,20},{20... | collective-permute-start | bytes 196616 | tf_op jit(solution)/shard_map/ppermute | solution.py:992
  54.6 2.8 %collective-permute-done.2.got_grad_ref = bf16[128,256]{1,0:T(8,128)(2,1)S(1)} collective-permute-done((bf16[128,256]{1,0:T(8,128)(2,1)}, bf16[128,256]{1,0:T(8,128)(2,1)S(1)}, u32[]{:S(2)}, u32[]{:S(2)}) %collective-permute-start.2) | collective-permute-done | bytes 65568 | tf_op jit(solution)/shard_map/ppermute | solution.py:992
  59.6 2.5 %collective-permute-start.3 = (bf16[272,256]{1,0:T(8,128)(2,1)S(1)}, bf16[272,256]{1,0:T(8,128)(2,1)S(1)}, u32[]{:S(2)}, u32[]{:S(2)}) collective-permute-start(bf16[272,256]{1,0:T(8,128)(2,1)S(1)} %get-tuple-element.53), channel_id=1, source_target_pairs={{0,16},{16,0},{1,17},{17,1},{2,18},{18,2},{3,19},{19,3},{4,20},{20... | collective-permute-start | bytes 417800 | tf_op jit(solution)/shard_map/ppermute | solution.py:992
  62.1 7.4 %shard_map.82 = (bf16[16,2,64,128]{3,2,1,0:T(8,128)(2,1)}, f32[2,256,256]{2,1,0:T(8,128)}, bf16[2,256,256]{2,1,0:T(8,128)(2,1)}) custom-call(f32[256,256]{1,0:T(8,128)} %get-tuple-element.56.refs_0_.refs_13_, f32[8,128]{1,0:T(8,128)} %get-tuple-element.57.refs_1_.refs_14_, f32[520,256]{1,0:T(8,128)} %copy-done.1, ...), custom_call_target="tpu_custom_call" | custom-call | flops 8000000000 | bytes 8400896 | tf_op jit(solution)/shard_map/pallas_call | solution.py:431
  70.2 3.0 %shard_map.83.refs_15_ = bf16[16,2,2,64,128]{4,3,2,1,0:T(8,128)(2,1)} custom-call(bf16[272,256]{1,0:T(8,128)(2,1)} %copy-done.7, f32[520,256]{1,0:T(8,128)} %copy-done.1, bf16[2,1024,256]{2,1,0:T(8,128)(2,1)} %get-tuple-element.48.refs_1_.refs_3_.refs_2_, f32[2,1024,256]{2,1,0:T(8,128)} %get-tuple-element.55.refs_7_.refs_3_.refs_8_, ...), custom_call_target="tpu_custom_call" | custom-call | flops 1000000000 | bytes 5390336 | tf_op jit(solution)/shard_map/pallas_call | solution.py:431
  73.2 4.5 %all-to-all-start.2 = ((bf16[16,2,2,64,128]{4,3,2,1,0:T(8,128)(2,1)}), bf16[16,2,2,64,128]{4,3,2,1,0:T(8,128)(2,1)}, u32[]{:S(2)}, u32[]{:S(2)}) async-start(bf16[16,2,2,64,128]{4,3,2,1,0:T(8,128)(2,1)} %shard_map.83.refs_15_), calls=%async_computation.2 | async-start | bytes 2097152 | tf_op jit(solution)/shard_map/all_to_all | solution.py:988
  77.7 10.8 %shard_map.85 = (bf16[2,2,128,128]{3,2,1,0:T(8,128)(2,1)}, f32[2,2,128,128]{3,2,1,0:T(8,128)}, f32[2,2,1024,128]{3,2,1,0:T(8,128)}) custom-call(f32[2,256,256]{2,1,0:T(8,128)} %get-tuple-element.63.refs_0_, bf16[272,256]{1,0:T(8,128)(2,1)} %copy-done.7, f32[520,256]{1,0:T(8,128)} %copy-done.1, bf16[2,2,256,128]{3,2,1,0:T(8,128)(2,1)} %get-tuple-element.64.refs_3_, ...), custom_call_target="tpu_custom_call" | custom-call | flops 199999995904 | bytes 14176256 | tf_op jit(solution)/shard_map/pallas_call | solution.py:431
  89.4 8.7 %collective-permute-done.4.refs_0_ = bf16[2,2,128,128]{3,2,1,0:T(8,128)(2,1)S(1)} collective-permute-done((bf16[2,2,128,128]{3,2,1,0:T(8,128)(2,1)}, bf16[2,2,128,128]{3,2,1,0:T(8,128)(2,1)S(1)}, u32[]{:S(2)}, u32[]{:S(2)}) %collective-permute-start.4) | collective-permute-done | bytes 131104 | tf_op jit(solution)/shard_map/ppermute | solution.py:992
  98.7 2.6 %shard_map.86 = bf16[16,2,2,64,128]{4,3,2,1,0:T(8,128)(2,1)} custom-call(bf16[2,2,128,128]{3,2,1,0:T(8,128)(2,1)} %copy-done.8, f32[2,2,128,128]{3,2,1,0:T(8,128)} %get-tuple-element.73.refs_1_, f32[2,2,1024,128]{3,2,1,0:T(8,128)} %get-tuple-element.74.refs_2_), custom_call_target="tpu_custom_call" | custom-call | flops 100000000 | bytes 3538944 | tf_op jit(solution)/shard_map/pallas_call | solution.py:431
  101.4 4.0 %all-to-all-start.3 = ((bf16[16,2,2,64,128]{4,3,2,1,0:T(8,128)(2,1)}), bf16[16,2,2,64,128]{4,3,2,1,0:T(8,128)(2,1)S(1)}, u32[]{:S(2)}, u32[]{:S(2)}) async-start(bf16[16,2,2,64,128]{4,3,2,1,0:T(8,128)(2,1)} %shard_map.86), calls=%async_computation.3 | async-start | bytes 2097152 | tf_op jit(solution)/shard_map/all_to_all | solution.py:988
  105.4 2.3 %shard_map.84 = (bf16[64,4096]{1,0:T(8,128)(2,1)}, bf16[64,4096]{1,0:T(8,128)(2,1)}) custom-call(s32[1]{0:T(128)} %bitcast.half_ref, bf16[16,2,2,64,128]{4,3,2,1,0:T(8,128)(2,1)} %all-to-all-done.2.packed_ref), custom_call_target="tpu_custom_call" | custom-call | bytes 2097152 | tf_op jit(solution)/shard_map/pallas_call | solution.py:518
  107.6 12.5 %all-to-all-done.3.packed_ref = bf16[16,2,2,64,128]{4,3,2,1,0:T(8,128)(2,1)S(1)} async-done(((bf16[16,2,2,64,128]{4,3,2,1,0:T(8,128)(2,1)}), bf16[16,2,2,64,128]{4,3,2,1,0:T(8,128)(2,1)S(1)}, u32[]{:S(2)}, u32[]{:S(2)}) %all-to-all-start.3) | async-done | bytes 1048608 | tf_op jit(solution)/shard_map/all_to_all | solution.py:988
  120.2 1.0 shard_map.87
  (27 shorter events, 5.2 us)
Async XLA Ops:
  2.8 21.1 %all-to-all-start = ((bf16[16,2,2,64,128]{4,3,2,1,0:T(8,128)(2,1)}), bf16[16,2,2,64,128]{4,3,2,1,0:T(8,128)(2,1)S(1)}, u32[]{:S(2)}, u32[]{:S(2)}) async-start(bf16[16,2,2,64,128]{4,3,2,1,0:T(8,128)(2,1)} %shard_map.75), calls=%async_computation | async-start | bytes 2097152 | tf_op jit(solution)/shard_map/all_to_all | solution.py:988
  23.9 8.7 %copy-start = (bf16[16,2,2,64,128]{4,3,2,1,0:T(8,128)(2,1)}, bf16[16,2,2,64,128]{4,3,2,1,0:T(8,128)(2,1)S(1)}, u32[]{:S(2)}) copy-start(bf16[16,2,2,64,128]{4,3,2,1,0:T(8,128)(2,1)S(1)} %all-to-all-done.qk_ref.refs_0_) | copy-start | bytes 3145732
  24.2 8.4 %copy-start.2 = (bf16[2,2,128,128]{3,2,1,0:T(8,128)(2,1)}, bf16[2,2,128,128]{3,2,1,0:T(8,128)(2,1)S(1)}, u32[]{:S(2)}) copy-start(bf16[2,2,128,128]{3,2,1,0:T(8,128)(2,1)S(1)} %shard_map.77.refs_1_) | copy-start | bytes 393220
  24.2 8.4 %collective-permute-start = (bf16[2,2,128,128]{3,2,1,0:T(8,128)(2,1)S(1)}, bf16[2,2,128,128]{3,2,1,0:T(8,128)(2,1)S(1)}, u32[]{:S(2)}, u32[]{:S(2)}) collective-permute-start(bf16[2,2,128,128]{3,2,1,0:T(8,128)(2,1)S(1)} %shard_map.77.refs_1_), channel_id=1, source_target_pairs={{0,16},{16,0},{1,17},{17,1},{2,18},{18,2},{3,19},{19,3},{4,20},{20... | collective-permute-start | bytes 393224 | tf_op jit(solution)/shard_map/ppermute | solution.py:992
  26.9 19.6 %all-to-all-start.1 = ((bf16[16,2,2,64,128]{4,3,2,1,0:T(8,128)(2,1)}), bf16[16,2,2,64,128]{4,3,2,1,0:T(8,128)(2,1)}, u32[]{:S(2)}, u32[]{:S(2)}) async-start(bf16[16,2,2,64,128]{4,3,2,1,0:T(8,128)(2,1)} %shard_map.76), calls=%async_computation.1 | async-start | bytes 2097152 | tf_op jit(solution)/shard_map/all_to_all | solution.py:988
  32.6 0.6 copy-start.9
  49.0 8.5 %copy-start.3 = (bf16[2,256,256]{2,1,0:T(8,128)(2,1)S(1)}, bf16[2,256,256]{2,1,0:T(8,128)(2,1)}, u32[]{:S(2)}) copy-start(bf16[2,256,256]{2,1,0:T(8,128)(2,1)} %get-tuple-element.52.inverse_ref) | copy-start | bytes 786436
  49.0 8.5 %copy-start.4 = (f32[128,256]{1,0:T(8,128)S(1)}, f32[128,256]{1,0:T(8,128)}, u32[]{:S(2)}) copy-start(f32[128,256]{1,0:T(8,128)} %get-tuple-element.49.refs_2_.keep_ref) | copy-start | bytes 393220
  49.1 8.4 %copy-start.6 = (f32[8,256]{1,0:T(8,128)S(1)}, f32[8,256]{1,0:T(8,128)}, u32[]{:S(2)}) copy-start(f32[8,256]{1,0:T(8,128)} %get-tuple-element.46.refs_2_.stats_ref) | copy-start | bytes 24580
  49.1 8.4 %collective-permute-start.1 = (bf16[144,256]{1,0:T(8,128)(2,1)}, bf16[144,256]{1,0:T(8,128)(2,1)S(1)}, u32[]{:S(2)}, u32[]{:S(2)}) collective-permute-start(bf16[144,256]{1,0:T(8,128)(2,1)} %get-tuple-element.47), channel_id=1, source_target_pairs={{0,16},{16,0},{1,17},{17,1},{2,18},{18,2},{3,19},{19,3},{4,20},{20... | collective-permute-start | bytes 221192 | tf_op jit(solution)/shard_map/ppermute | solution.py:992
  51.7 5.8 %collective-permute-start.2 = (bf16[128,256]{1,0:T(8,128)(2,1)}, bf16[128,256]{1,0:T(8,128)(2,1)S(1)}, u32[]{:S(2)}, u32[]{:S(2)}) collective-permute-start(bf16[128,256]{1,0:T(8,128)(2,1)} %get-tuple-element.50), channel_id=1, source_target_pairs={{0,16},{16,0},{1,17},{17,1},{2,18},{18,2},{3,19},{19,3},{4,20},{20... | collective-permute-start | bytes 196616 | tf_op jit(solution)/shard_map/ppermute | solution.py:992
  57.5 0.9 copy-start.5
  58.8 0.8 copy-start.1
  59.6 10.0 %collective-permute-start.3 = (bf16[272,256]{1,0:T(8,128)(2,1)S(1)}, bf16[272,256]{1,0:T(8,128)(2,1)S(1)}, u32[]{:S(2)}, u32[]{:S(2)}) collective-permute-start(bf16[272,256]{1,0:T(8,128)(2,1)S(1)} %get-tuple-element.53), channel_id=1, source_target_pairs={{0,16},{16,0},{1,17},{17,1},{2,18},{18,2},{3,19},{19,3},{4,20},{20... | collective-permute-start | bytes 417800 | tf_op jit(solution)/shard_map/ppermute | solution.py:992
  69.6 0.6 copy-start.7
  73.2 28.2 %all-to-all-start.2 = ((bf16[16,2,2,64,128]{4,3,2,1,0:T(8,128)(2,1)}), bf16[16,2,2,64,128]{4,3,2,1,0:T(8,128)(2,1)}, u32[]{:S(2)}, u32[]{:S(2)}) async-start(bf16[16,2,2,64,128]{4,3,2,1,0:T(8,128)(2,1)} %shard_map.83.refs_15_), calls=%async_computation.2 | async-start | bytes 2097152 | tf_op jit(solution)/shard_map/all_to_all | solution.py:988
  88.6 9.5 %collective-permute-start.4 = (bf16[2,2,128,128]{3,2,1,0:T(8,128)(2,1)}, bf16[2,2,128,128]{3,2,1,0:T(8,128)(2,1)S(1)}, u32[]{:S(2)}, u32[]{:S(2)}) collective-permute-start(bf16[2,2,128,128]{3,2,1,0:T(8,128)(2,1)} %get-tuple-element.72), channel_id=1, source_target_pairs={{0,16},{16,0},{1,17},{17,1},{2,18},{18,2},{3,19},{19,3},{4,20},{20... | collective-permute-start | bytes 393224 | tf_op jit(solution)/shard_map/ppermute | solution.py:992
  98.1 0.7 copy-start.8
  101.4 18.8 %all-to-all-start.3 = ((bf16[16,2,2,64,128]{4,3,2,1,0:T(8,128)(2,1)}), bf16[16,2,2,64,128]{4,3,2,1,0:T(8,128)(2,1)S(1)}, u32[]{:S(2)}, u32[]{:S(2)}) async-start(bf16[16,2,2,64,128]{4,3,2,1,0:T(8,128)(2,1)} %shard_map.86), calls=%async_computation.3 | async-start | bytes 2097152 | tf_op jit(solution)/shard_map/all_to_all | solution.py:988

commit v17 on v16

--- a/solution.py
+++ b/solution.py
@@ -22,6 +22,7 @@
 TOP = 12
 SIDES = (20, 21)
 LONG = 200
+SPAN = 2 * CHUNK
 EARLY_SWEEPS = PINV_ITERS // 2
 
 
@@ -281,14 +282,14 @@
     ).astype(jnp.float32)
 
 
-def chunk_of(ref, array, slot, index):
-    per = CHUNK // ref.shape[3]
-    return ref[index * per : (index + 1) * per, array, slot].reshape(CHUNK, HD)
+def chunk_of(ref, array, slot, index, size=CHUNK):
+    per = size // ref.shape[3]
+    return ref[index * per : (index + 1) * per, array, slot].reshape(size, HD)
 
 
 def store_chunk(ref, lead, index, value):
     rows = ref.shape[-2]
-    per = CHUNK // rows
+    per = value.shape[0] // rows
     ref[(slice(index * per, (index + 1) * per), *lead)] = value.reshape(per, rows, HD)
 
 
@@ -765,17 +766,17 @@
     scale = ins.mix[2 * HD + 1 + slot : 2 * HD + 2 + slot]
 
     def token_side(index):
-        place = slice(index * CHUNK, (index + 1) * CHUNK)
+        place = slice(index * SPAN, (index + 1) * SPAN)
         attended = wide_dot_nt(ins.token_low[place], mixing_low)
         store_chunk(out_ref, (0, *lead), index, attended.astype(jnp.bfloat16))
 
     def key_side(index):
-        place = slice(index * CHUNK, (index + 1) * CHUNK)
+        place = slice(index * SPAN, (index + 1) * SPAN)
         key_plow = (ins.key_exp[place] * scale).astype(jnp.bfloat16)
         value_gradient = wide_dot_nt(key_plow, values_low)
         store_chunk(out_ref, (1, *lead), index, value_gradient.astype(jnp.bfloat16))
 
-    chunks = ins.token_low.shape[0] // CHUNK
+    chunks = ins.token_low.shape[0] // SPAN
     return [
         functools.partial(unit, index) for unit in (token_side, key_side) for index in range(chunks)
     ]
@@ -788,9 +789,9 @@
     scale = ins.mix[2 * HD + 1 + slot : 2 * HD + 2 + slot]
 
     def token_side(index):
-        place = slice(index * CHUNK, (index + 1) * CHUNK)
+        place = slice(index * SPAN, (index + 1) * SPAN)
         prob = ins.token_prob[slot, place]
-        token_grad = wide_dot(chunk_of(ins.vg, 1, slot, index), mixing_low)
+        token_grad = wide_dot(chunk_of(ins.vg, 1, slot, index, SPAN), mixing_low)
         token_sgrad = (
             prob * (token_grad - jnp.sum(token_grad * prob, axis=1, keepdims=True))
         ).astype(jnp.bfloat16)
@@ -798,14 +799,14 @@
         key_sums.append(wide_dot(ins.turned[slot, 0, :, place], token_sgrad))
 
     def key_side(index):
-        place = slice(index * CHUNK, (index + 1) * CHUNK)
+        place = slice(index * SPAN, (index + 1) * SPAN)
         key_prob = ins.key_exp[slot, place] * scale
-        key_dgrad = wide_dot(chunk_of(ins.vg, 0, slot, index), values_low)
+        key_dgrad = wide_dot(chunk_of(ins.vg, 0, slot, index, SPAN), values_low)
         key_sgrad = (key_prob * (key_dgrad - row_total)).astype(jnp.bfloat16)
         direct_ref[slot, 1, place] = wide_dot(key_sgrad, ins.marks[slot, 0]) * score_scale
         query_sums.append(wide_dot(ins.turned[slot, 1, :, place], key_sgrad))
 
-    chunks = tokens_of(ins.vg) // CHUNK
+    chunks = tokens_of(ins.vg) // SPAN
     units = [
         [functools.partial(unit, index) for index in range(chunks)] for unit in (key_side, token_side)
     ]
@@ -860,7 +861,7 @@
     toward = split_dot(halves(ins.mark_prob[...]), inverse_grad_halves) * ins.factor[0:1, 0:1]
     state = (0.5 * (toward + toward.T), None)
     units = out_units(ins, 0, outs.out, (), own_parts(ins.mix))
-    work = iter([units[index : index + 2] for index in range(0, len(units), 2)])
+    work = iter([[unit] for unit in units])
     saved = (ins.pair, ins.weight, ins.growth)
 
     def beside():
@@ -884,12 +885,13 @@
     chunks = len(units) // 2
     several(*units[:chunks])
     need()
-    group = CHUNK // outs.out.shape[3]
+    group = SPAN // outs.out.shape[3]
     for index, unit in enumerate(units[chunks:]):
         unit()
         place = slice(index * group, (index + 1) * group)
         outs.out[place, :, 0] = ins.own_out[place]
-        put(outs.out, index * group)
+        for start in range(index * group, (index + 1) * group, CHUNK // outs.out.shape[3]):
+            put(outs.out, start)
 
 
 def gradient_compute(ins, outs, need, put):

time: 122 us -> 122 us (level)
  no operation moved by 1% of the time
where the time goes in v17:
time: 122 us; the launch traced here: 121 us
  Pallas kernels  47.4 us (39%)
  waiting for transfers between devices  41.1 us (34%)
  starting transfers between devices  28.1 us (23%)
  local copies, waits for them, and re-layouts  3.66 us (3%)
    pallas_call x7, Pallas kernels, staged_call(): pl.pallas_call(kernel, out_shape=shapes, in_specs=[anywhere] * (n_in + n_...  39.1 us
    all_to_all x4, waiting for transfers between devices, exchange(): lax.all_to_all(packed, 'cube', split_axis=0, concat_axis=0, tiled=True)  28.1 us
    all_to_all x4, starting transfers between devices, exchange(): lax.all_to_all(packed, 'cube', split_axis=0, concat_axis=0, tiled=True)  19.1 us
    ppermute x5, waiting for transfers between devices, partner(): return lax.ppermute(array, 'half', SWAP)  13 us
    ppermute x5, starting transfers between devices, partner(): return lax.ppermute(array, 'half', SWAP)  8.97 us
    pallas_call x4, Pallas kernels, layout_call(): pl.pallas_call(kernel, out_shape=out_shape, in_specs=[pl.BlockSpec(memory...  7.61 us
    unnamed x20, local copies, waits for them, and re-layouts  3.66 us
  transfers between devices with their start and end apart: 9, of which 6 were waited for; matrix products, arithmetic and copies ran while one was open for 0% of the time, Pallas kernels for 31%

profile of v17, /device:TPU:0, one launch (start us, length us, event | category | flops | bytes accessed | tf_op | source)
XLA Modules:
  0.0 121.2 jit_solution(5994295017784069490)
XLA Ops:
  0.6 2.1 %shard_map.75 = bf16[16,2,2,64,128]{4,3,2,1,0:T(8,128)(2,1)} custom-call(s32[1]{0:T(128)} %bitcast.half_ref, bf16[64,4096]{1,0:T(8,128)(2,1)} %first_ref.2, bf16[64,4096]{1,0:T(8,128)(2,1)} %second_ref.2), custom_call_target="tpu_custom_call" | custom-call | bytes 2097152 | tf_op jit(solution)/shard_map/pallas_call | solution.py:519
  2.8 6.3 %all-to-all-start = ((bf16[16,2,2,64,128]{4,3,2,1,0:T(8,128)(2,1)}), bf16[16,2,2,64,128]{4,3,2,1,0:T(8,128)(2,1)S(1)}, u32[]{:S(2)}, u32[]{:S(2)}) async-start(bf16[16,2,2,64,128]{4,3,2,1,0:T(8,128)(2,1)} %shard_map.75), calls=%async_computation | async-start | bytes 2097152 | tf_op jit(solution)/shard_map/all_to_all | solution.py:990
  9.1 2.1 %shard_map.76 = bf16[16,2,2,64,128]{4,3,2,1,0:T(8,128)(2,1)} custom-call(s32[1]{0:T(128)} %bitcast.half_ref, bf16[64,4096]{1,0:T(8,128)(2,1)} %first_ref.3, bf16[64,4096]{1,0:T(8,128)(2,1)} %second_ref.3), custom_call_target="tpu_custom_call" | custom-call | bytes 2097152 | tf_op jit(solution)/shard_map/pallas_call | solution.py:519
  11.2 12.7 %all-to-all-done.qk_ref.refs_0_ = bf16[16,2,2,64,128]{4,3,2,1,0:T(8,128)(2,1)S(1)} async-done(((bf16[16,2,2,64,128]{4,3,2,1,0:T(8,128)(2,1)}), bf16[16,2,2,64,128]{4,3,2,1,0:T(8,128)(2,1)S(1)}, u32[]{:S(2)}, u32[]{:S(2)}) %all-to-all-start) | async-done | bytes 1048608 | tf_op jit(solution)/shard_map/all_to_all | solution.py:990
  24.2 2.7 %collective-permute-start = (bf16[2,2,128,128]{3,2,1,0:T(8,128)(2,1)S(1)}, bf16[2,2,128,128]{3,2,1,0:T(8,128)(2,1)S(1)}, u32[]{:S(2)}, u32[]{:S(2)}) collective-permute-start(bf16[2,2,128,128]{3,2,1,0:T(8,128)(2,1)S(1)} %shard_map.77.refs_1_), channel_id=1, source_target_pairs={{0,16},{16,0},{1,17},{17,1},{2,18},{18,2},{3,19},{19,3},{4,20},{20... | collective-permute-start | bytes 393224 | tf_op jit(solution)/shard_map/ppermute | solution.py:994
  26.9 4.3 %all-to-all-start.1 = ((bf16[16,2,2,64,128]{4,3,2,1,0:T(8,128)(2,1)}), bf16[16,2,2,64,128]{4,3,2,1,0:T(8,128)(2,1)}, u32[]{:S(2)}, u32[]{:S(2)}) async-start(bf16[16,2,2,64,128]{4,3,2,1,0:T(8,128)(2,1)} %shard_map.76), calls=%async_computation.1 | async-start | bytes 2097152 | tf_op jit(solution)/shard_map/all_to_all | solution.py:990
  31.2 1.4 %collective-permute-done.refs_2_ = bf16[2,2,128,128]{3,2,1,0:T(8,128)(2,1)S(1)} collective-permute-done((bf16[2,2,128,128]{3,2,1,0:T(8,128)(2,1)S(1)}, bf16[2,2,128,128]{3,2,1,0:T(8,128)(2,1)S(1)}, u32[]{:S(2)}, u32[]{:S(2)}) %collective-permute-start) | collective-permute-done | bytes 131104 | tf_op jit(solution)/shard_map/ppermute | solution.py:994
  33.3 10.3 %shard_map.78 = (bf16[2,2,256,128]{3,2,1,0:T(8,128)(2,1)}, f32[2,1024,256]{2,1,0:T(8,128)}, bf16[2,1024,256]{2,1,0:T(8,128)(2,1)}, f32[2,1024,256]{2,1,0:T(8,128...) custom-call(bf16[16,2,2,64,128]{4,3,2,1,0:T(8,128)(2,1)} %copy-done,, ...), custom_call_target="tpu_custom_call" | custom-call | flops 199999995904 | bytes 16003072 | tf_op jit(solution)/shard_map/pallas_call | solution.py:432
  43.5 2.9 %all-to-all-done.1.refs_0_.refs_7_ = bf16[16,2,2,64,128]{4,3,2,1,0:T(8,128)(2,1)} async-done(((bf16[16,2,2,64,128]{4,3,2,1,0:T(8,128)(2,1)}), bf16[16,2,2,64,128]{4,3,2,1,0:T(8,128)(2,1)}, u32[]{:S(2)}, u32[]{:S(2)}) %all-to-all-start.1) | async-done | bytes 1048608 | tf_op jit(solution)/shard_map/all_to_all | solution.py:990
  46.5 2.6 %shard_map.79 = (bf16[144,256]{1,0:T(8,128)(2,1)}, f32[128,256]{1,0:T(8,128)}) custom-call(bf16[16,2,2,64,128]{4,3,2,1,0:T(8,128)(2,1)} %all-to-all-done.1.refs_0_.refs_7_, bf16[2,1024,256]{2,1,0:T(8,128)(2,1)} %get-tuple-element.45.refs_1_, f32[8,256]{1,0:T(8,128)} %get-tuple-element.46.refs_2_.stats_ref), custom_call_target="tpu_custom_call" | custom-call | flops 1000000000 | bytes 2310144 | tf_op jit(solution)/shard_map/pallas_call | solution.py:432
  49.1 2.6 %shard_map.80 = (bf16[128,256]{1,0:T(8,128)(2,1)}, f32[128,256]{1,0:T(8,128)}) custom-call(bf16[16,2,2,64,128]{4,3,2,1,0:T(8,128)(2,1)} %all-to-all-done.1.refs_0_.refs_7_, bf16[2,1024,256]{2,1,0:T(8,128)(2,1)} %get-tuple-element.48.refs_1_.refs_3_.refs_2_, f32[128,256]{1,0:T(8,128)} %get-tuple-element.49.refs_2_.keep_ref), custom_call_target="tpu_custom_call" | custom-call | flops 1000000000 | bytes 2293760 | tf_op jit(solution)/shard_map/pallas_call | solution.py:432
  51.7 2.9 %collective-permute-start.2 = (bf16[128,256]{1,0:T(8,128)(2,1)}, bf16[128,256]{1,0:T(8,128)(2,1)S(1)}, u32[]{:S(2)}, u32[]{:S(2)}) collective-permute-start(bf16[128,256]{1,0:T(8,128)(2,1)} %get-tuple-element.50), channel_id=1, source_target_pairs={{0,16},{16,0},{1,17},{17,1},{2,18},{18,2},{3,19},{19,3},{4,20},{20... | collective-permute-start | bytes 196616 | tf_op jit(solution)/shard_map/ppermute | solution.py:994
  54.6 2.8 %collective-permute-done.2.got_grad_ref = bf16[128,256]{1,0:T(8,128)(2,1)S(1)} collective-permute-done((bf16[128,256]{1,0:T(8,128)(2,1)}, bf16[128,256]{1,0:T(8,128)(2,1)S(1)}, u32[]{:S(2)}, u32[]{:S(2)}) %collective-permute-start.2) | collective-permute-done | bytes 65568 | tf_op jit(solution)/shard_map/ppermute | solution.py:994
  59.6 2.5 %collective-permute-start.3 = (bf16[272,256]{1,0:T(8,128)(2,1)S(1)}, bf16[272,256]{1,0:T(8,128)(2,1)S(1)}, u32[]{:S(2)}, u32[]{:S(2)}) collective-permute-start(bf16[272,256]{1,0:T(8,128)(2,1)S(1)} %get-tuple-element.53), channel_id=1, source_target_pairs={{0,16},{16,0},{1,17},{17,1},{2,18},{18,2},{3,19},{19,3},{4,20},{20... | collective-permute-start | bytes 417800 | tf_op jit(solution)/shard_map/ppermute | solution.py:994
  62.1 7.4 %shard_map.82 = (bf16[16,2,64,128]{3,2,1,0:T(8,128)(2,1)}, f32[2,256,256]{2,1,0:T(8,128)}, bf16[2,256,256]{2,1,0:T(8,128)(2,1)}) custom-call(f32[256,256]{1,0:T(8,128)} %get-tuple-element.56.refs_0_.refs_13_, f32[8,128]{1,0:T(8,128)} %get-tuple-element.57.refs_1_.refs_14_, f32[520,256]{1,0:T(8,128)} %copy-done.1, ...), custom_call_target="tpu_custom_call" | custom-call | flops 8000000000 | bytes 8400896 | tf_op jit(solution)/shard_map/pallas_call | solution.py:432
  70.2 3.1 %shard_map.83.refs_15_ = bf16[16,2,2,64,128]{4,3,2,1,0:T(8,128)(2,1)} custom-call(bf16[272,256]{1,0:T(8,128)(2,1)} %copy-done.7, f32[520,256]{1,0:T(8,128)} %copy-done.1, bf16[2,1024,256]{2,1,0:T(8,128)(2,1)} %get-tuple-element.48.refs_1_.refs_3_.refs_2_, f32[2,1024,256]{2,1,0:T(8,128)} %get-tuple-element.55.refs_7_.refs_3_.refs_8_, ...), custom_call_target="tpu_custom_call" | custom-call | flops 1000000000 | bytes 5390336 | tf_op jit(solution)/shard_map/pallas_call | solution.py:432
  73.3 4.5 %all-to-all-start.2 = ((bf16[16,2,2,64,128]{4,3,2,1,0:T(8,128)(2,1)}), bf16[16,2,2,64,128]{4,3,2,1,0:T(8,128)(2,1)}, u32[]{:S(2)}, u32[]{:S(2)}) async-start(bf16[16,2,2,64,128]{4,3,2,1,0:T(8,128)(2,1)} %shard_map.83.refs_15_), calls=%async_computation.2 | async-start | bytes 2097152 | tf_op jit(solution)/shard_map/all_to_all | solution.py:990
  77.8 10.6 %shard_map.85 = (bf16[2,2,128,128]{3,2,1,0:T(8,128)(2,1)}, f32[2,2,128,128]{3,2,1,0:T(8,128)}, f32[2,2,1024,128]{3,2,1,0:T(8,128)}) custom-call(f32[2,256,256]{2,1,0:T(8,128)} %get-tuple-element.63.refs_0_, bf16[272,256]{1,0:T(8,128)(2,1)} %copy-done.7, f32[520,256]{1,0:T(8,128)} %copy-done.1, bf16[2,2,256,128]{3,2,1,0:T(8,128)(2,1)} %get-tuple-element.64.refs_3_, ...), custom_call_target="tpu_custom_call" | custom-call | flops 199999995904 | bytes 14176256 | tf_op jit(solution)/shard_map/pallas_call | solution.py:432
  89.2 8.7 %collective-permute-done.4.refs_0_ = bf16[2,2,128,128]{3,2,1,0:T(8,128)(2,1)S(1)} collective-permute-done((bf16[2,2,128,128]{3,2,1,0:T(8,128)(2,1)}, bf16[2,2,128,128]{3,2,1,0:T(8,128)(2,1)S(1)}, u32[]{:S(2)}, u32[]{:S(2)}) %collective-permute-start.4) | collective-permute-done | bytes 131104 | tf_op jit(solution)/shard_map/ppermute | solution.py:994
  98.6 2.6 %shard_map.86 = bf16[16,2,2,64,128]{4,3,2,1,0:T(8,128)(2,1)} custom-call(bf16[2,2,128,128]{3,2,1,0:T(8,128)(2,1)} %copy-done.8, f32[2,2,128,128]{3,2,1,0:T(8,128)} %get-tuple-element.73.refs_1_, f32[2,2,1024,128]{3,2,1,0:T(8,128)} %get-tuple-element.74.refs_2_), custom_call_target="tpu_custom_call" | custom-call | flops 100000000 | bytes 3538944 | tf_op jit(solution)/shard_map/pallas_call | solution.py:432
  101.2 4.0 %all-to-all-start.3 = ((bf16[16,2,2,64,128]{4,3,2,1,0:T(8,128)(2,1)}), bf16[16,2,2,64,128]{4,3,2,1,0:T(8,128)(2,1)S(1)}, u32[]{:S(2)}, u32[]{:S(2)}) async-start(bf16[16,2,2,64,128]{4,3,2,1,0:T(8,128)(2,1)} %shard_map.86), calls=%async_computation.3 | async-start | bytes 2097152 | tf_op jit(solution)/shard_map/all_to_all | solution.py:990
  105.2 2.3 %shard_map.84 = (bf16[64,4096]{1,0:T(8,128)(2,1)}, bf16[64,4096]{1,0:T(8,128)(2,1)}) custom-call(s32[1]{0:T(128)} %bitcast.half_ref, bf16[16,2,2,64,128]{4,3,2,1,0:T(8,128)(2,1)} %all-to-all-done.2.packed_ref), custom_call_target="tpu_custom_call" | custom-call | bytes 2097152 | tf_op jit(solution)/shard_map/pallas_call | solution.py:519
  107.5 12.5 %all-to-all-done.3.packed_ref = bf16[16,2,2,64,128]{4,3,2,1,0:T(8,128)(2,1)S(1)} async-done(((bf16[16,2,2,64,128]{4,3,2,1,0:T(8,128)(2,1)}), bf16[16,2,2,64,128]{4,3,2,1,0:T(8,128)(2,1)S(1)}, u32[]{:S(2)}, u32[]{:S(2)}) %all-to-all-start.3) | async-done | bytes 1048608 | tf_op jit(solution)/shard_map/all_to_all | solution.py:990
  120.0 1.0 shard_map.87
  (27 shorter events, 5.2 us)
Async XLA Ops:
  2.8 21.1 %all-to-all-start = ((bf16[16,2,2,64,128]{4,3,2,1,0:T(8,128)(2,1)}), bf16[16,2,2,64,128]{4,3,2,1,0:T(8,128)(2,1)S(1)}, u32[]{:S(2)}, u32[]{:S(2)}) async-start(bf16[16,2,2,64,128]{4,3,2,1,0:T(8,128)(2,1)} %shard_map.75), calls=%async_computation | async-start | bytes 2097152 | tf_op jit(solution)/shard_map/all_to_all | solution.py:990
  23.9 8.7 %copy-start = (bf16[16,2,2,64,128]{4,3,2,1,0:T(8,128)(2,1)}, bf16[16,2,2,64,128]{4,3,2,1,0:T(8,128)(2,1)S(1)}, u32[]{:S(2)}) copy-start(bf16[16,2,2,64,128]{4,3,2,1,0:T(8,128)(2,1)S(1)} %all-to-all-done.qk_ref.refs_0_) | copy-start | bytes 3145732
  24.2 8.4 %copy-start.2 = (bf16[2,2,128,128]{3,2,1,0:T(8,128)(2,1)}, bf16[2,2,128,128]{3,2,1,0:T(8,128)(2,1)S(1)}, u32[]{:S(2)}) copy-start(bf16[2,2,128,128]{3,2,1,0:T(8,128)(2,1)S(1)} %shard_map.77.refs_1_) | copy-start | bytes 393220
  24.2 8.4 %collective-permute-start = (bf16[2,2,128,128]{3,2,1,0:T(8,128)(2,1)S(1)}, bf16[2,2,128,128]{3,2,1,0:T(8,128)(2,1)S(1)}, u32[]{:S(2)}, u32[]{:S(2)}) collective-permute-start(bf16[2,2,128,128]{3,2,1,0:T(8,128)(2,1)S(1)} %shard_map.77.refs_1_), channel_id=1, source_target_pairs={{0,16},{16,0},{1,17},{17,1},{2,18},{18,2},{3,19},{19,3},{4,20},{20... | collective-permute-start | bytes 393224 | tf_op jit(solution)/shard_map/ppermute | solution.py:994
  26.9 19.6 %all-to-all-start.1 = ((bf16[16,2,2,64,128]{4,3,2,1,0:T(8,128)(2,1)}), bf16[16,2,2,64,128]{4,3,2,1,0:T(8,128)(2,1)}, u32[]{:S(2)}, u32[]{:S(2)}) async-start(bf16[16,2,2,64,128]{4,3,2,1,0:T(8,128)(2,1)} %shard_map.76), calls=%async_computation.1 | async-start | bytes 2097152 | tf_op jit(solution)/shard_map/all_to_all | solution.py:990
  32.6 0.6 copy-start.9
  49.0 8.5 %copy-start.3 = (bf16[2,256,256]{2,1,0:T(8,128)(2,1)S(1)}, bf16[2,256,256]{2,1,0:T(8,128)(2,1)}, u32[]{:S(2)}) copy-start(bf16[2,256,256]{2,1,0:T(8,128)(2,1)} %get-tuple-element.52.inverse_ref) | copy-start | bytes 786436
  49.0 8.5 %copy-start.4 = (f32[128,256]{1,0:T(8,128)S(1)}, f32[128,256]{1,0:T(8,128)}, u32[]{:S(2)}) copy-start(f32[128,256]{1,0:T(8,128)} %get-tuple-element.49.refs_2_.keep_ref) | copy-start | bytes 393220
  49.1 8.4 %copy-start.6 = (f32[8,256]{1,0:T(8,128)S(1)}, f32[8,256]{1,0:T(8,128)}, u32[]{:S(2)}) copy-start(f32[8,256]{1,0:T(8,128)} %get-tuple-element.46.refs_2_.stats_ref) | copy-start | bytes 24580
  49.1 8.4 %collective-permute-start.1 = (bf16[144,256]{1,0:T(8,128)(2,1)}, bf16[144,256]{1,0:T(8,128)(2,1)S(1)}, u32[]{:S(2)}, u32[]{:S(2)}) collective-permute-start(bf16[144,256]{1,0:T(8,128)(2,1)} %get-tuple-element.47), channel_id=1, source_target_pairs={{0,16},{16,0},{1,17},{17,1},{2,18},{18,2},{3,19},{19,3},{4,20},{20... | collective-permute-start | bytes 221192 | tf_op jit(solution)/shard_map/ppermute | solution.py:994
  51.7 5.8 %collective-permute-start.2 = (bf16[128,256]{1,0:T(8,128)(2,1)}, bf16[128,256]{1,0:T(8,128)(2,1)S(1)}, u32[]{:S(2)}, u32[]{:S(2)}) collective-permute-start(bf16[128,256]{1,0:T(8,128)(2,1)} %get-tuple-element.50), channel_id=1, source_target_pairs={{0,16},{16,0},{1,17},{17,1},{2,18},{18,2},{3,19},{19,3},{4,20},{20... | collective-permute-start | bytes 196616 | tf_op jit(solution)/shard_map/ppermute | solution.py:994
  57.5 0.9 copy-start.5
  58.8 0.8 copy-start.1
  59.6 10.0 %collective-permute-start.3 = (bf16[272,256]{1,0:T(8,128)(2,1)S(1)}, bf16[272,256]{1,0:T(8,128)(2,1)S(1)}, u32[]{:S(2)}, u32[]{:S(2)}) collective-permute-start(bf16[272,256]{1,0:T(8,128)(2,1)S(1)} %get-tuple-element.53), channel_id=1, source_target_pairs={{0,16},{16,0},{1,17},{17,1},{2,18},{18,2},{3,19},{19,3},{4,20},{20... | collective-permute-start | bytes 417800 | tf_op jit(solution)/shard_map/ppermute | solution.py:994
  69.6 0.6 copy-start.7
  73.3 28.0 %all-to-all-start.2 = ((bf16[16,2,2,64,128]{4,3,2,1,0:T(8,128)(2,1)}), bf16[16,2,2,64,128]{4,3,2,1,0:T(8,128)(2,1)}, u32[]{:S(2)}, u32[]{:S(2)}) async-start(bf16[16,2,2,64,128]{4,3,2,1,0:T(8,128)(2,1)} %shard_map.83.refs_15_), calls=%async_computation.2 | async-start | bytes 2097152 | tf_op jit(solution)/shard_map/all_to_all | solution.py:990
  88.4 9.5 %collective-permute-start.4 = (bf16[2,2,128,128]{3,2,1,0:T(8,128)(2,1)}, bf16[2,2,128,128]{3,2,1,0:T(8,128)(2,1)S(1)}, u32[]{:S(2)}, u32[]{:S(2)}) collective-permute-start(bf16[2,2,128,128]{3,2,1,0:T(8,128)(2,1)} %get-tuple-element.72), channel_id=1, source_target_pairs={{0,16},{16,0},{1,17},{17,1},{2,18},{18,2},{3,19},{19,3},{4,20},{20... | collective-permute-start | bytes 393224 | tf_op jit(solution)/shard_map/ppermute | solution.py:994
  97.9 0.7 copy-start.8
  101.2 18.8 %all-to-all-start.3 = ((bf16[16,2,2,64,128]{4,3,2,1,0:T(8,128)(2,1)}), bf16[16,2,2,64,128]{4,3,2,1,0:T(8,128)(2,1)S(1)}, u32[]{:S(2)}, u32[]{:S(2)}) async-start(bf16[16,2,2,64,128]{4,3,2,1,0:T(8,128)(2,1)} %shard_map.86), calls=%async_computation.3 | async-start | bytes 2097152 | tf_op jit(solution)/shard_map/all_to_all | solution.py:990
